TPU v7x, 32 devices: a whole 2x2x4 slice. The times are simulated.
32 devices in a mesh: groups: 2 (over y), ctx: 4 (over z), head: 2 (over x), sub: 2 (over core).
Axes of the slice: x: 2, y: 2, z: 4, core: 2. Of those that a mesh axis runs over, the one named last changes fastest.
Arguments:
- key_cache: bfloat16 [8, 8192, 8, 128], P('groups', ('ctx', 'sub'), 'head'), parts along dimension 0, may hold values from -70 to 70
- value_cache: bfloat16 [8, 8192, 8, 128], P('groups', ('ctx', 'sub'), 'head'), parts along dimension 0, may hold values from -6 to 6
- lengths: int32 [8], P('groups'), parts along dimension 0, may hold values from 1 to 8192, 16384 in all
- owner_order: int32 [8], P('groups'), parts along dimension 0, may hold values from 0 to 3, each once
- first_tokens: bfloat16 [8, 8192], P(('groups', 'head', 'sub'), 'ctx'), parts along dimension 0, may hold values from -250 to 250
- second_tokens: bfloat16 [8, 8192], P(('groups', 'head', 'sub'), 'ctx'), parts along dimension 0, may hold values from -250 to 250
- norm_gain: bfloat16 [8192], P('ctx'), may hold values from 0.099609375 to 1.8984375
- w_query: bfloat16 [8192, 8192], P('ctx', ('head', 'sub')), may hold values from -1 to 1
- w_key: bfloat16 [8192, 1024], P('ctx', ('head', 'sub')), may hold values from -16 to 16
- w_value: bfloat16 [8192, 1024], P('ctx', ('head', 'sub')), may hold values from -0.0625 to 0.0625
- w_out: bfloat16 [8192, 8192], P(('head', 'sub'), 'ctx'), may hold values from -0.0625 to 0.0625
Outputs:
- key_cache_decode: bfloat16 [8, 8192, 8, 128], P(('groups', 'ctx'), None, ('head', 'sub')), parts along dimension 0
- value_cache_decode: bfloat16 [8, 8192, 8, 128], P(('groups', 'ctx'), None, ('head', 'sub')), parts along dimension 0
- first_out: bfloat16 [8, 8192], P(('groups', 'head', 'sub'), 'ctx'), parts along dimension 0
- second_out: bfloat16 [8, 8192], P(('groups', 'head', 'sub'), 'ctx'), parts along dimension 0
There are 2 independent parts, one for each index of `groups`. A program takes and returns all parts, laid end to end along the dimension named above; an argument that names none is the same for every part. Nothing has to cross between parts.
Inputs may be any that keep to these rules, and one draw needn't show every extreme that they name: `lengths`: some request has a prompt of exactly 8192 positions. A permutation of the requests; with R = 4 / 4 requests an owner, decode owner c (the index along ctx) serves the requests owner_order[c * R] to owner_order[c * R + R - 1], in that order.
All inputs are finite; a program needn't handle non-finite values.
Results may differ from a plain program's by a relative error of at most 0.0039.
Values may be sent and summed in bfloat16 or wider, within the bound.
No kernel may reach another device: no remote copies, remote signals or barrier semaphores. Data moves between devices by JAX's collectives and lax.ppermute only.
A program may use at most 128 MiB of HBM per device.

v0:
```python
import jax
import jax.numpy as jnp
from jax import lax
from jax.sharding import PartitionSpec as P

D = 8192
SEQ = 8192


theta_base = 500000.0
eps_norm = 1e-05
masked_score = -1e30


def rotate(vectors, positions):
    half_dim = vectors.shape[-1] // 2
    exponents = jnp.arange(half_dim, dtype=jnp.float32) * (2.0 / vectors.shape[-1])
    frequency = theta_base ** (-exponents)
    angles = positions[:, None, None] * frequency[None, None, :]
    cosines = jnp.cos(angles)
    sines = jnp.sin(angles)
    lower_part = vectors[..., :half_dim]
    upper_part = vectors[..., half_dim:]
    return jnp.concatenate(
        [lower_part * cosines - upper_part * sines, upper_part * cosines + lower_part * sines],
        axis=-1,
    )


def attend_masked(
    grouped_heads, keys_all, values_all, fresh_keys, fresh_values, own_lengths, score_factor
):
    logit_scores = (
        jnp.einsum("bgrd,btgd->bgrt", grouped_heads, keys_all, preferred_element_type=jnp.float32)
        * score_factor
    )
    places = lax.iota(jnp.int32, keys_all.shape[1])
    live_mask = places[None, :] < own_lengths[:, None]
    logit_scores = jnp.where(live_mask[:, None, None, :], logit_scores, masked_score)
    fresh_scores = (
        jnp.einsum("bgrd,bngd->bgrn", grouped_heads, fresh_keys, preferred_element_type=jnp.float32)
        * score_factor
    )
    row_max = jnp.maximum(jnp.max(logit_scores, axis=3), jnp.max(fresh_scores, axis=3))[..., None]
    weights = jnp.exp(logit_scores - row_max)
    fresh_weights = jnp.exp(fresh_scores - row_max)
    denominator = jnp.sum(weights, axis=3) + jnp.sum(fresh_weights, axis=3)
    weighted_numerator = jnp.einsum(
        "bgrt,btgd->bgrd",
        weights.astype(jnp.bfloat16),
        values_all,
        preferred_element_type=jnp.float32,
    )
    weighted_numerator = weighted_numerator + jnp.einsum(
        "bgrn,bngd->bgrd",
        fresh_weights.astype(jnp.bfloat16),
        fresh_values,
        preferred_element_type=jnp.float32,
    )
    return weighted_numerator / denominator[..., None]


def local(
    key_cache,
    value_cache,
    lengths,
    owner_order,
    first_tokens,
    second_tokens,
    norm_gain,
    w_query,
    w_key,
    w_value,
    w_out,
):
    ctx_count = lax.axis_size("ctx")
    sub_count = lax.axis_size("sub")
    total_requests = lengths.shape[0]
    per_owner = total_requests // ctx_count
    shard_length = key_cache.shape[1]
    heads_decode = key_cache.shape[2] // sub_count
    head_dim = key_cache.shape[3]

    def arrange(cache):
        picked = jnp.take(cache, owner_order, axis=0)
        picked = picked.reshape(
            ctx_count, per_owner, shard_length, sub_count, heads_decode, head_dim
        )
        return jnp.transpose(picked, (0, 3, 1, 2, 4, 5))

    direct_shape = (ctx_count * sub_count, per_owner, shard_length, heads_decode, head_dim)
    moved_keys, moved_values = (
        lax.all_to_all(
            arrange(key_cache).reshape(direct_shape),
            ("ctx", "sub"),
            split_axis=0,
            concat_axis=2,
            tiled=True,
        ),
        lax.all_to_all(
            arrange(value_cache).reshape(direct_shape),
            ("ctx", "sub"),
            split_axis=0,
            concat_axis=2,
            tiled=True,
        ),
    )
    final_shape = (per_owner, SEQ, heads_decode, head_dim)
    moved_keys = moved_keys.reshape(final_shape)
    moved_values = moved_values.reshape(final_shape)
    ctx_index = lax.axis_index("ctx")
    own_ids = lax.dynamic_slice_in_dim(owner_order, ctx_index * per_owner, per_owner)
    own_lengths = jnp.take(lengths, own_ids)
    query_width = w_query.shape[1]
    key_width = w_key.shape[1]
    queries_local = query_width // head_dim
    group_size = queries_local // heads_decode
    score_factor = head_dim ** (-0.5)
    gain_wide = norm_gain.astype(jnp.float32)
    rows_local = first_tokens.shape[0]
    row_start = lax.axis_index(("head", "sub")) * rows_local

    def decode_step(tokens, position_shift, earlier_keys, earlier_values):
        rows_all = lax.all_gather(tokens, ("head", "sub"), axis=0, tiled=True)
        wide = jnp.take(rows_all, owner_order, axis=0).astype(jnp.float32)
        row_squares = lax.psum(jnp.sum(wide * wide, axis=1), "ctx")
        normed = (
            wide * lax.rsqrt(row_squares / D + eps_norm)[:, None] * gain_wide[None, :]
        ).astype(jnp.bfloat16)
        projected = lax.psum_scatter(
            jnp.concatenate(
                [
                    jnp.dot(normed, w_query, preferred_element_type=jnp.float32),
                    jnp.dot(normed, w_key, preferred_element_type=jnp.float32),
                    jnp.dot(normed, w_value, preferred_element_type=jnp.float32),
                ],
                axis=1,
            ),
            "ctx",
            scatter_dimension=0,
            tiled=True,
        )
        positions = own_lengths.astype(jnp.float32) + position_shift
        queries = rotate(
            projected[:, :query_width].reshape(per_owner, queries_local, head_dim), positions
        ).astype(jnp.bfloat16)
        new_keys = rotate(
            projected[:, query_width : query_width + key_width].reshape(
                per_owner, heads_decode, head_dim
            ),
            positions,
        ).astype(jnp.bfloat16)
        new_values = (
            projected[:, query_width + key_width :]
            .reshape(per_owner, heads_decode, head_dim)
            .astype(jnp.bfloat16)
        )
        fresh_keys = jnp.stack(earlier_keys + [new_keys], axis=1)
        fresh_values = jnp.stack(earlier_values + [new_values], axis=1)
        grouped_heads = queries.reshape(per_owner, heads_decode, group_size, head_dim)
        attended = attend_masked(
            grouped_heads,
            moved_keys,
            moved_values,
            fresh_keys,
            fresh_values,
            own_lengths,
            score_factor,
        )
        attended = attended.reshape(per_owner, query_width).astype(jnp.bfloat16)
        branch = jnp.dot(
            lax.all_gather(attended, "ctx", axis=0, tiled=True),
            w_out,
            preferred_element_type=jnp.float32,
        )
        summed = lax.psum_scatter(branch, ("head", "sub"), scatter_dimension=0, tiled=True)
        residual_rows = lax.dynamic_slice_in_dim(wide, row_start, rows_local, 0)
        result = (residual_rows + summed).astype(jnp.bfloat16)
        return (result, new_keys, new_values)

    first_out, first_key, first_value = decode_step(first_tokens, 0.0, [], [])
    second_out = decode_step(second_tokens, 1.0, [first_key], [first_value])[0]
    return (moved_keys, moved_values, first_out, second_out)


def solution(mesh):
    return jax.shard_map(
        local,
        mesh=mesh,
        in_specs=(
            P("groups", ("ctx", "sub"), "head", None),
            P("groups", ("ctx", "sub"), "head", None),
            P("groups"),
            P("groups"),
            P(("groups", "head", "sub"), "ctx"),
            P(("groups", "head", "sub"), "ctx"),
            P("ctx"),
            P("ctx", ("head", "sub")),
            P("ctx", ("head", "sub")),
            P("ctx", ("head", "sub")),
            P(("head", "sub"), "ctx"),
        ),
        out_specs=(
            P(("groups", "ctx"), None, ("head", "sub"), None),
            P(("groups", "ctx"), None, ("head", "sub"), None),
            P(("groups", "head", "sub"), "ctx"),
            P(("groups", "head", "sub"), "ctx"),
        ),
        check_vma=False,
    )
```

profile of v0, /device:TPU:0, one launch (start us, length us, event | category | flops | bytes accessed | tf_op | source)
XLA Modules:
  0.0 397.3 jit_solution(12813869123792318369)
XLA Ops:
  7.2 0.8 compare_and_fusion
  7.9 0.7 compare_select_fusion
  8.6 7.5 %gather_fusion.1 = bf16[4,1024,4,128]{3,2,1,0:T(4,128)(2,1)} fusion(bf16[4,1024,4,128]{3,2,1,0:T(4,128)(2,1)} %param.16, s32[1024]{0:T(1024)S(1)} %pad_clamp_fusion), kind=kCustom, calls=%fused_computation.2.clone | custom fusion | bytes 8388624 | tf_op jit(solution)/shard_map/jit(_take)/gather | solution.py:85
  16.1 7.5 %gather_fusion = bf16[4,1024,4,128]{3,2,1,0:T(4,128)(2,1)} fusion(bf16[4,1024,4,128]{3,2,1,0:T(4,128)(2,1)} %param.15, s32[1024]{0:T(1024)S(1)} %pad_clamp_fusion), kind=kCustom, calls=%fused_computation.clone | custom fusion | bytes 8388624 | tf_op jit(solution)/shard_map/jit(_take)/gather | solution.py:85
  23.6 9.1 %broadcast_select_fusion = (bf16[4,1024,4,128]{3,2,1,0:T(4,128)(2,1)}, bf16[4,1024,4,128]{3,2,1,0:T(4,128)(2,1)S(1)}) fusion(bf16[4,1024,4,128]{3,2,1,0:T(4,128)(2,1)} %gather_fusion.1, pred[4]{0:T(512)(128)(4,1)S(1)} %compare_and_fusion, bf16[4,1024,4,128]{3,2,1,0:T(4,128)(2,1)} %gather_fusion), kind=kLoop, calls=%fused_computation.8 | loop fusion | flops 4194304 | bytes 16777220 | tf_op jit(solution)/shard_map/jit(_take)/select_n | solution.py:85
  32.7 3.0 copy.45
  35.7 6.3 %all-to-all-start = ((bf16[8,1,1024,2,128]{4,2,3,1,0:T(8,128)(2,1)}), bf16[8,1,1024,2,128]{4,2,3,1,0:T(8,128)(2,1)}, u32[]{:S(2)}, u32[]{:S(2)}) async-start(bf16[8,1,1024,2,128]{4,2,3,1,0:T(8,128)(2,1)} %bitcast.92), calls=%async_computation | async-start | bytes 8388608 | tf_op jit(solution)/shard_map/all_to_all | solution.py:93
  42.0 5.1 %copy.47 = bf16[4,1,1024,2,2,128]{5,2,4,3,0,1:T(8,128)(2,1)} copy(bf16[4,1,1024,2,2,128]{5,4,3,2,0,1:T(2,128)(2,1)} %bitcast.89) | data formatting | bytes 8388608 | tf_op jit(solution)/shard_map/reshape | solution.py:86
  47.1 89.1 %all-to-all-done = bf16[8,1,1024,2,128]{4,2,3,1,0:T(8,128)(2,1)} async-done(((bf16[8,1,1024,2,128]{4,2,3,1,0:T(8,128)(2,1)}), bf16[8,1,1024,2,128]{4,2,3,1,0:T(8,128)(2,1)}, u32[]{:S(2)}, u32[]{:S(2)}) %all-to-all-start) | async-done | bytes 4194336 | tf_op jit(solution)/shard_map/all_to_all | solution.py:93
  136.1 4.7 %all-to-all-start.1 = ((bf16[8,1,1024,2,128]{4,2,3,1,0:T(8,128)(2,1)}), bf16[8,1,1024,2,128]{4,2,3,1,0:T(8,128)(2,1)}, u32[]{:S(2)}, u32[]{:S(2)}) async-start(bf16[8,1,1024,2,128]{4,2,3,1,0:T(8,128)(2,1)} %bitcast.91), calls=%async_computation.1 | async-start | bytes 8388608 | tf_op jit(solution)/shard_map/all_to_all | solution.py:100
  140.9 5.2 %all-gather = bf16[4,1,2048]{2,1,0:T(2,128)(2,1)S(1)} all-gather(bf16[1,1,2048]{2,1,0:T(2,128)(2,1)S(1)} %bitcast.100), channel_id=1, replica_groups=mesh['groups'=2,'ctx'=4,'head'=2,'sub'=2] {'head','sub'}, dimensions={0}, use_global_device_ids=true | all-gather | bytes 20480 | tf_op jit(solution)/shard_map/all_gather | solution.py:124
  146.1 0.6 gather_fusion.2
  146.7 5.2 %all-gather.2 = bf16[4,1,2048]{2,1,0:T(2,128)(2,1)S(1)} all-gather(bf16[1,1,2048]{2,1,0:T(2,128)(2,1)S(1)} %bitcast.101), channel_id=1, replica_groups=mesh['groups'=2,'ctx'=4,'head'=2,'sub'=2] {'head','sub'}, dimensions={0}, use_global_device_ids=true | all-gather | bytes 20480 | tf_op jit(solution)/shard_map/all_gather | solution.py:124
  151.9 0.6 gather_fusion.3
  152.5 0.2 multiply_reduce_fusion
  152.7 62.8 %all-reduce.6 = (f32[4]{0:T(128)S(1)}, f32[4]{0:T(128)S(1)}) all-reduce(f32[4]{0:T(128)S(1)} %get-tuple-element.22, f32[4]{0:T(128)S(1)} %get-tuple-element.21), channel_id=1, replica_groups=mesh['groups'=2,'ctx'=4,'head'=2,'sub'=2] {'ctx'}, use_global_device_ids=true, to_apply=%region_1.4 | all-reduce | flops 8 | bytes 64 | tf_op jit(solution)/shard_map/psum | solution.py:126
  215.5 0.3 fusion.56
  215.8 0.3 fusion.55
  216.1 0.3 fusion.53
  216.4 0.3 fusion.52
  216.7 4.8 %fusion.54 = f32[4,2048]{1,0:T(4,128)S(1)} fusion(bf16[2048,2048]{1,0:T(8,128)(2,1)} %param.22, f32[2048]{0:T(1024)S(1)} %convert_element_type.133, f32[4]{0:T(128)S(1)} %get-tuple-element.52, bf16[4,2048]{1,0:T(4,128)(2,1)S(1)} %gather_fusion.2, pred[4]{0:T(512)(128)(4,1)S(1)} %compare_and_fusion), kind=kOutput, calls=%fused_computation.108 | convolution fusion | flops 33595392 | bytes 8445972 | tf_op jit(solution)/shard_map/dot_general | solution.py:133
  221.4 0.6 pad_maximum_fusion
  222.1 0.2 slice-done.1
  222.3 1.2 fusion.57
  223.5 0.6 pad_maximum_fusion.1
  224.3 0.6 dynamic_slice.10
  226.8 0.6 dynamic-slice.2
  228.1 0.6 dynamic-slice.3
  228.7 0.1 multiply_sine_fusion
  228.8 50.4 %all-reduce.12.cloned.1.call-done = (f32[4,2560]{1,0:T(4,128)}, f32[4,2560]{1,0:T(4,128)}) async-done(((f32[4,2560]{1,0:T(4,128)}, f32[4,2560]{1,0:T(4,128)}), (f32[4,2560]{1,0:T(4,128)}, f32[4,2560]{1,0:T(4,128)})) %all-reduce.12.cloned.1.call-update) | async-done | bytes 81936
  279.2 1.4 dynamic-slice.12
  280.6 1.4 dynamic-slice.15
  282.0 0.1 fusion.42
  282.1 0.1 subtract_convert_fusion.3
  282.2 0.1 maximum_bitcast_fusion.4
  282.3 1.4 fusion.30
  283.7 1.4 fusion.44
  285.1 1.4 constant_dynamic-slice_fusion.1
  286.5 0.1 fusion.25
  286.6 0.2 fusion.60
  286.8 1.4 constant_dynamic-slice_fusion
  288.2 0.1 fusion.23
  288.3 0.2 fusion.40
  288.5 2.5 copy.46
  291.0 1.3 fusion.59
  292.3 0.3 fusion.8
  292.6 0.4 copy-done.3
  293.0 1.3 fusion.58
  294.3 2.5 copy.48
  296.8 1.9 copy-done.2
  298.8 0.7 fusion.10
  299.5 0.2 fusion.4
  299.7 13.2 %all-gather.3 = bf16[4,1,2048]{2,1,0:T(2,128)(2,1)S(1)} all-gather(bf16[1,1,2048]{2,1,0:T(2,128)(2,1)S(1)} %reshape.519), channel_id=1, replica_groups=mesh['groups'=2,'ctx'=4,'head'=2,'sub'=2] {'ctx'}, dimensions={0}, use_global_device_ids=true | all-gather | bytes 20480 | tf_op jit(solution)/shard_map/all_gather | solution.py:172
  312.9 0.3 fusion.6
  313.2 2.9 fusion.5
  316.1 13.3 %all-gather.1 = bf16[4,1,2048]{2,1,0:T(2,128)(2,1)S(1)} all-gather(bf16[1,1,2048]{2,1,0:T(2,128)(2,1)S(1)} %reshape.515), channel_id=1, replica_groups=mesh['groups'=2,'ctx'=4,'head'=2,'sub'=2] {'ctx'}, dimensions={0}, use_global_device_ids=true | all-gather | bytes 20480 | tf_op jit(solution)/shard_map/all_gather | solution.py:172
  329.4 5.2 %fusion.15 = f32[4,2048]{1,0:T(4,128)} fusion(bf16[2048,2048]{1,0:T(8,128)(2,1)} %param.25, bf16[4,1,2048]{2,1,0:T(2,128)(2,1)S(1)} %all-gather.3), kind=kOutput, calls=%fused_computation.33 | convolution fusion | flops 33554432 | bytes 8437760 | tf_op jit(solution)/shard_map/dot_general | solution.py:171
  334.6 5.2 %fusion.18 = f32[4,2048]{1,0:T(4,128)} fusion(bf16[2048,2048]{1,0:T(8,128)(2,1)} %param.25, bf16[4,1,2048]{2,1,0:T(2,128)(2,1)S(1)} %all-gather.1), kind=kOutput, calls=%fused_computation.37 | convolution fusion | flops 33554432 | bytes 8437760 | tf_op jit(solution)/shard_map/dot_general | solution.py:171
  339.9 0.1 select_convert_fusion
  340.0 0.7 dynamic-slice.5
  340.6 10.2 %copy.56 = bf16[1,8192,2,128]{3,2,1,0:T(2,128)(2,1)} copy(bf16[1,8192,2,128]{3,1,2,0:T(8,128)(2,1)} %bitcast.85) | data formatting | bytes 8388608
  350.9 35.4 %copy.55 = bf16[1,8192,2,128]{3,2,1,0:T(2,128)(2,1)} copy(bf16[1,8192,2,128]{3,1,2,0:T(8,128)(2,1)S(1)} %bitcast.88) | data formatting | bytes 8388608
  386.3 2.1 fusion.21
  388.3 2.1 fusion.22
  (52 shorter events, 0.4 us)
Async XLA Ops:
  7.2 208.3 %copy-start = (bf16[2048,256]{1,0:T(8,128)(2,1)S(1)}, bf16[2048,256]{1,0:T(8,128)(2,1)}, u32[]{:S(2)}) copy-start(bf16[2048,256]{1,0:T(8,128)(2,1)} %param.23) | copy-start | bytes 3145732
  35.7 100.4 %all-to-all-start = ((bf16[8,1,1024,2,128]{4,2,3,1,0:T(8,128)(2,1)}), bf16[8,1,1024,2,128]{4,2,3,1,0:T(8,128)(2,1)}, u32[]{:S(2)}, u32[]{:S(2)}) async-start(bf16[8,1,1024,2,128]{4,2,3,1,0:T(8,128)(2,1)} %bitcast.92), calls=%async_computation | async-start | bytes 8388608 | tf_op jit(solution)/shard_map/all_to_all | solution.py:93
  136.1 4.8 %copy-start.5 = (bf16[1,2048]{1,0:T(2,128)(2,1)S(1)}, bf16[1,2048]{1,0:T(2,128)(2,1)}, u32[]{:S(2)}) copy-start(bf16[1,2048]{1,0:T(2,128)(2,1)} %param.19) | copy-start | bytes 12292
  136.1 10.6 %copy-start.6 = (bf16[1,2048]{1,0:T(2,128)(2,1)S(1)}, bf16[1,2048]{1,0:T(2,128)(2,1)}, u32[]{:S(2)}) copy-start(bf16[1,2048]{1,0:T(2,128)(2,1)} %param.20) | copy-start | bytes 12292
  136.1 79.4 %copy-start.7 = (bf16[2048]{0:T(1024)(128)(2,1)S(1)}, bf16[2048]{0:T(1024)(128)(2,1)}, u32[]{:S(2)}) copy-start(bf16[2048]{0:T(1024)(128)(2,1)} %param.21) | copy-start | bytes 12292
  136.1 79.7 %copy-start.8 = (bf16[2048,256]{1,0:T(8,128)(2,1)S(1)}, bf16[2048,256]{1,0:T(8,128)(2,1)}, u32[]{:S(2)}) copy-start(bf16[2048,256]{1,0:T(8,128)(2,1)} %param.24) | copy-start | bytes 3145732
  136.1 158.2 %all-to-all-start.1 = ((bf16[8,1,1024,2,128]{4,2,3,1,0:T(8,128)(2,1)}), bf16[8,1,1024,2,128]{4,2,3,1,0:T(8,128)(2,1)}, u32[]{:S(2)}, u32[]{:S(2)}) async-start(bf16[8,1,1024,2,128]{4,2,3,1,0:T(8,128)(2,1)} %bitcast.91), calls=%async_computation.1 | async-start | bytes 8388608 | tf_op jit(solution)/shard_map/all_to_all | solution.py:100
  140.8 138.3 %all-reduce.12.cloned.1.call-start = ((), (), s32[]{:S(2)}) async-start(), calls=%async_computation.3 | async-start | bytes 163840
  216.4 5.7 %slice-start = ((s8[8388608]{0:T(1024)(128)(4,1)}), s8[4194304]{0:T(1024)(128)(4,1)S(1)}, s32[]{:S(2)}) async-start(s8[8388608]{0:T(1024)(128)(4,1)} %bitcast.81), calls=%async_computation.4 | async-start | bytes 8388608
  216.7 5.6 %slice-start.1 = ((s8[8388608]{0:T(1024)(128)(4,1)}), s8[4194304]{0:T(1024)(128)(4,1)S(1)}, s32[]{:S(2)}) async-start(s8[8388608]{0:T(1024)(128)(4,1)} %bitcast.81), calls=%async_computation.5 | async-start | bytes 8388608
  222.3 2.0 copy-start.9
  222.3 4.5 %copy-start.10 = (s32[4]{0:T(128)S(1)}, s32[4]{0:T(128)}, u32[]{:S(2)}) copy-start(s32[4]{0:T(128)} %param.17) | copy-start | bytes 52
  222.3 5.8 %copy-start.12 = (u32[32]{0:T(128)S(1)}, u32[32]{0:T(128)}, u32[]{:S(2)}) copy-start(u32[32]{0:T(128)} %constant.100) | copy-start | bytes 388
  224.2 162.1 %all-reduce.10.cloned.1.call-start = ((), (), s32[]{:S(2)}) async-start(), calls=%async_computation.2 | async-start | bytes 131072
  291.0 2.0 copy-start.3
  296.8 1.9 copy-start.2
  334.6 5.3 %copy-start.11 = (u32[32]{0:T(128)S(1)}, u32[32]{0:T(128)}, u32[]{:S(2)}) copy-start(u32[32]{0:T(128)} %constant.104) | copy-start | bytes 388
  340.6 10.2 %copy-start.4 = (bf16[8,1,1024,2,128]{4,2,0,3,1:T(8,128)(2,1)S(1)}, bf16[8,1,1024,2,128]{4,2,0,3,1:T(8,128)(2,1)}, u32[]{:S(2)}) copy-start(bf16[8,1,1024,2,128]{4,2,0,3,1:T(8,128)(2,1)} %copy-done.3) | copy-start | bytes 12582916
  350.9 39.5 %copy-start.1 = (bf16[2048,256]{1,0:T(8,128)(2,1)S(1)}, bf16[2048,256]{1,0:T(8,128)(2,1)}, u32[]{:S(2)}) copy-start(bf16[2048,256]{1,0:T(8,128)(2,1)} %param.23) | copy-start | bytes 3145732
Sparse Core Ops, SparseCore 0:
  224.3 54.8 all-reduce.11
  340.0 31.0 all-reduce.9
where the time goes:
time: 399 us; the launch traced here: 397 us
  waiting for transfers between devices  139 us (35%)
  blocking collectives  99.7 us (25%)
  local copies, waits for them, and re-layouts  87 us (22%)
  matrix products  24.3 us (6%)
  other arithmetic  18.7 us (5%)
  between operations  16.9 us (4%)
  starting transfers between devices  11.1 us (3%)
    all_to_all x1, waiting for transfers between devices, local(): lax.all_to_all(arrange(key_cache).reshape(direct_shape), ('ctx', 'sub'),...  89.1 us
    psum x1, blocking collectives, decode_step(): row_squares = lax.psum(jnp.sum(wide * wide, axis=1), 'ctx')  62.8 us
    unnamed x4, waiting for transfers between devices  50.4 us
    unnamed x38, local copies, waits for them, and re-layouts  49.6 us
    all_gather x2, blocking collectives, decode_step(): lax.all_gather(attended, 'ctx', axis=0, tiled=True)  26.6 us
    gather x2, local copies, waits for them, and re-layouts, arrange(): picked = jnp.take(cache, owner_order, axis=0)  15 us
    dot_general x2, matrix products, decode_step(): jnp.dot(lax.all_gather(attended, 'ctx', axis=0, tiled=True), w_out, prefe...  10.4 us
    all_gather x2, blocking collectives, decode_step(): rows_all = lax.all_gather(tokens, ('head', 'sub'), axis=0, tiled=True)  10.4 us
  transfers between devices with their start and end apart: 4, of which 2 were waited for; matrix products, arithmetic and copies ran while one was open for 20% of the time, Pallas kernels for 0%

commit v1 on v0

v1 whole, which is shorter than its diff:
```python
import functools

import jax
import jax.numpy as jnp
from jax import lax
from jax.experimental import pallas as pl
from jax.experimental.pallas import tpu as pltpu
from jax.sharding import PartitionSpec as P

theta_base = 500000.0
eps_norm = 1e-05
masked_score = -1e30
LANES = 128
VMEM_BYTES = 48 * 1024 * 1024


def rotate(vectors, positions):
    half_dim = vectors.shape[-1] // 2
    exponents = jnp.arange(half_dim, dtype=jnp.float32) * (2.0 / vectors.shape[-1])
    frequency = theta_base ** (-exponents)
    angles = positions[..., None, None] * frequency
    cosines = jnp.cos(angles)
    sines = jnp.sin(angles)
    lower_part = vectors[..., :half_dim]
    upper_part = vectors[..., half_dim:]
    return jnp.concatenate(
        [lower_part * cosines - upper_part * sines, upper_part * cosines + lower_part * sines],
        axis=-1,
    )


def arrange(cache, owner_order, sub_count):
    requests, shard_length, heads, head_dim = cache.shape
    heads_decode = heads // sub_count
    split = cache.reshape(requests, shard_length, sub_count, heads_decode, head_dim)

    def kernel(order_ref, in_ref, out_ref, sems):
        copies = []
        for i in range(requests):
            for s in range(sub_count):
                copy = pltpu.make_async_copy(
                    in_ref.at[order_ref[i], :, s], out_ref.at[i, s], sems.at[i, s]
                )
                copy.start()
                copies.append(copy)
        for copy in copies:
            copy.wait()

    return pl.pallas_call(
        kernel,
        out_shape=jax.ShapeDtypeStruct(
            (requests, sub_count, shard_length, heads_decode, head_dim), cache.dtype
        ),
        in_specs=[
            pl.BlockSpec(memory_space=pltpu.SMEM),
            pl.BlockSpec(memory_space=pltpu.HBM),
        ],
        out_specs=pl.BlockSpec(memory_space=pltpu.HBM),
        scratch_shapes=[pltpu.SemaphoreType.DMA((requests, sub_count))],
        cost_estimate=pl.CostEstimate(
            flops=0, transcendentals=0, bytes_accessed=2 * cache.size * cache.dtype.itemsize
        ),
        name="arrange",
    )(owner_order, split)


def attend_shard(queries, keys, values, lengths, first_place, score_factor):
    requests, shard_length, heads, head_dim = keys.shape
    rows = queries.shape[1]
    per_head = rows // heads
    columns = shard_length * heads
    flat_keys = keys.reshape(requests, columns, head_dim)
    flat_values = values.reshape(requests, columns, head_dim)

    def kernel(lengths_ref, place_ref, q_ref, k_ref, v_ref, acc_ref, max_ref, sum_ref):
        request = pl.program_id(0)
        scores = (
            lax.dot_general(
                q_ref[0], k_ref[0], (((1,), (1,)), ((), ())), preferred_element_type=jnp.float32
            )
            * score_factor
        )
        row = lax.broadcasted_iota(jnp.int32, (rows, columns), 0)
        column = lax.broadcasted_iota(jnp.int32, (rows, columns), 1)
        live_columns = (lengths_ref[request] - place_ref[0]) * heads
        live = (lax.rem(column, heads) == lax.div(row, per_head)) & (column < live_columns)
        scores = jnp.where(live, scores, masked_score)
        row_max = jnp.max(scores, axis=1, keepdims=True)
        weights = jnp.where(live, jnp.exp(scores - row_max), 0.0)
        acc_ref[0] = jnp.dot(
            weights.astype(jnp.bfloat16), v_ref[0], preferred_element_type=jnp.float32
        )
        max_ref[0] = jnp.broadcast_to(row_max, (rows, head_dim))
        sum_ref[0] = jnp.broadcast_to(
            jnp.sum(weights, axis=1, keepdims=True), (rows, head_dim)
        )

    small = pl.BlockSpec((1, rows, head_dim), lambda r, *_: (r, 0, 0))
    large = pl.BlockSpec((1, columns, head_dim), lambda r, *_: (r, 0, 0))
    result = jax.ShapeDtypeStruct((requests, rows, head_dim), jnp.float32)
    return pl.pallas_call(
        kernel,
        out_shape=(result, result, result),
        grid_spec=pltpu.PrefetchScalarGridSpec(
            num_scalar_prefetch=2,
            grid=(requests,),
            in_specs=[small, large, large],
            out_specs=(small, small, small),
        ),
        compiler_params=pltpu.CompilerParams(vmem_limit_bytes=VMEM_BYTES),
        cost_estimate=pl.CostEstimate(
            flops=4 * requests * rows * columns * head_dim,
            transcendentals=requests * rows * columns,
            bytes_accessed=4 * keys.size,
        ),
        name="attend_shard",
    )(lengths, first_place, queries, flat_keys, flat_values)


def local(
    width,
    key_cache,
    value_cache,
    lengths,
    owner_order,
    first_tokens,
    second_tokens,
    norm_gain,
    w_query,
    w_key,
    w_value,
    w_out,
):
    ctx_count = lax.axis_size("ctx")
    sub_count = lax.axis_size("sub")
    requests, shard_length, heads, head_dim = key_cache.shape
    per_owner = requests // ctx_count
    heads_decode = heads // sub_count
    ctx_index = lax.axis_index("ctx")
    sub_index = lax.axis_index("sub")
    take = functools.partial(jnp.take, mode="clip")

    def hand_off(cache):
        blocks = arrange(cache, owner_order, sub_count)
        blocks = blocks.reshape(ctx_count, per_owner, sub_count, shard_length, heads_decode, head_dim)
        blocks = jnp.swapaxes(blocks, 1, 2)
        moved = lax.all_to_all(
            blocks.reshape(
                ctx_count * sub_count, per_owner, shard_length, heads_decode, head_dim
            ),
            ("ctx", "sub"),
            split_axis=0,
            concat_axis=2,
            tiled=True,
        )
        return moved.reshape(per_owner, -1, heads_decode, head_dim)

    moved_keys = hand_off(key_cache)
    moved_values = hand_off(value_cache)

    query_width = w_query.shape[1]
    key_width = w_key.shape[1]
    group_size = query_width // head_dim // heads_decode
    score_factor = head_dim ** (-0.5)
    rows_local = first_tokens.shape[0]
    tokens = lax.all_gather(
        jnp.stack([first_tokens, second_tokens]), ("head", "sub"), axis=1, tiled=True
    )
    wide = tokens.astype(jnp.float32).reshape(2 * requests, -1)
    gained = wide * norm_gain.astype(jnp.float32)
    upper = lax.reduce_precision(gained, 8, 7)
    lower = gained - upper
    halves = jnp.concatenate([upper, lower]).astype(jnp.bfloat16)
    products = jnp.concatenate(
        [
            jnp.dot(halves, weight, preferred_element_type=jnp.float32)
            for weight in (w_query, w_key, w_value)
        ],
        axis=1,
    )
    squares = jnp.sum(wide * wide, axis=1, keepdims=True)
    partial = jnp.concatenate(
        [
            products[: 2 * requests] + products[2 * requests :],
            jnp.broadcast_to(squares, (2 * requests, LANES)),
        ],
        axis=1,
    )
    summed = jnp.sum(lax.all_gather(partial, "ctx", axis=0), axis=0)
    raw = summed[:, :-LANES] * lax.rsqrt(summed[:, -LANES:][:, :1] / width + eps_norm)
    raw = raw.reshape(2, requests, -1, head_dim)
    positions = lengths.astype(jnp.float32)[None, :] + jnp.arange(2, dtype=jnp.float32)[:, None]
    query_heads = query_width // head_dim
    key_heads = key_width // head_dim
    rotated = rotate(raw[:, :, : query_heads + key_heads], positions).astype(jnp.bfloat16)
    queries = rotated[:, :, :query_heads].reshape(2, requests, heads_decode, group_size, head_dim)
    fresh_keys = rotated[:, :, query_heads:]
    fresh_values = raw[:, :, query_heads + key_heads :].astype(jnp.bfloat16)

    per_head = 2 * group_size
    own_queries = jnp.transpose(queries, (1, 2, 0, 3, 4)).reshape(
        requests, heads_decode * per_head, head_dim
    )
    all_queries = lax.all_gather(own_queries, "sub", axis=1, tiled=True)
    shard_index = ctx_index * sub_count + sub_index
    first_place = jnp.reshape(shard_index * shard_length, (1,)).astype(jnp.int32)
    sums, maxima, totals = attend_shard(
        all_queries, key_cache, value_cache, lengths, first_place, score_factor
    )

    own_rows = heads_decode * per_head

    def pack(core):
        part = lambda x: lax.dynamic_slice_in_dim(x, core * own_rows, own_rows, 1)
        return (part(sums), part(maxima)[:, :, 0], part(totals)[:, :, 0])

    def send_form(sums, maxima, totals):
        return jnp.concatenate(
            [x.reshape(-1, head_dim) for x in (sums, maxima, totals)], axis=0
        )

    count = requests * own_rows
    extra = count // head_dim

    def unpack(packed):
        lead = packed.shape[:-2]
        shape = lead + (requests, own_rows)
        return (
            packed[..., :count, :].reshape(shape + (head_dim,)),
            packed[..., count : count + extra, :].reshape(shape),
            packed[..., count + extra :, :].reshape(shape),
        )

    def merge(sums, maxima, totals):
        largest = jnp.max(maxima, axis=0)
        scale = jnp.exp(maxima - largest)
        return (
            jnp.sum(sums * scale[..., None], axis=0),
            largest,
            jnp.sum(totals * scale, axis=0),
        )

    kept = pack(sub_index)
    for shift in range(1, sub_count):
        pairs = [(i, (i + shift) % sub_count) for i in range(sub_count)]
        sent = send_form(*pack(lax.rem(sub_index + shift, sub_count)))
        received = unpack(lax.ppermute(sent, "sub", pairs))
        kept = merge(*(jnp.stack([a, b]) for a, b in zip(kept, received)))
    gathered = unpack(lax.all_gather(send_form(*kept), "ctx", axis=0))
    sums, maxima, totals = merge(*gathered)

    grouped = own_queries.reshape(requests, heads_decode, 2, group_size, head_dim).astype(
        jnp.float32
    )
    keys_wide = jnp.transpose(fresh_keys, (1, 2, 0, 3)).astype(jnp.float32)
    values_wide = jnp.transpose(fresh_values, (1, 2, 0, 3)).astype(jnp.float32)
    fresh_scores = (
        jnp.sum(grouped[:, :, :, :, None, :] * keys_wide[:, :, None, None, :, :], axis=-1)
        * score_factor
    )
    step = jnp.arange(2)
    seen = (step[None, :] <= step[:, None])[None, None, :, None, :]
    fresh_scores = jnp.where(seen, fresh_scores, masked_score)
    shape = (requests, heads_decode, 2, group_size)
    maxima = maxima.reshape(shape)
    largest = jnp.maximum(maxima, jnp.max(fresh_scores, axis=-1))
    old_scale = jnp.exp(maxima - largest)
    fresh_weights = jnp.where(seen, jnp.exp(fresh_scores - largest[..., None]), 0.0)
    denominator = totals.reshape(shape) * old_scale + jnp.sum(fresh_weights, axis=-1)
    numerator = sums.reshape(shape + (head_dim,)) * old_scale[..., None] + jnp.sum(
        lax.reduce_precision(fresh_weights, 8, 7)[..., None]
        * values_wide[:, :, None, None, :, :],
        axis=-2,
    )
    attended = (numerator / denominator[..., None]).astype(jnp.bfloat16)

    attended = take(attended, owner_order, axis=0)
    attended = jnp.transpose(attended, (2, 0, 1, 3, 4)).reshape(2 * requests, query_width)
    branch = jnp.dot(attended, w_out, preferred_element_type=jnp.float32)
    branch = branch.reshape(2, requests, -1)
    row_start = lax.axis_index(("head", "sub")) * rows_local
    parts = lax.all_gather(branch, ("head", "sub"), axis=0)
    parts = lax.dynamic_slice_in_dim(parts, row_start, rows_local, 2)
    own_ids = lax.dynamic_slice_in_dim(owner_order, row_start, rows_local)
    residual = take(tokens, own_ids, axis=1).astype(jnp.float32)
    result = (residual + jnp.sum(parts, axis=0)).astype(jnp.bfloat16)
    return (moved_keys, moved_values, result[0], result[1])


def solution(mesh):
    def whole(*arrays):
        return jax.shard_map(
            functools.partial(local, arrays[6].shape[0]),
            mesh=mesh,
            in_specs=(
                P("groups", ("ctx", "sub"), "head", None),
                P("groups", ("ctx", "sub"), "head", None),
                P("groups"),
                P("groups"),
                P(("groups", "head", "sub"), "ctx"),
                P(("groups", "head", "sub"), "ctx"),
                P("ctx"),
                P("ctx", ("head", "sub")),
                P("ctx", ("head", "sub")),
                P("ctx", ("head", "sub")),
                P(("head", "sub"), "ctx"),
            ),
            out_specs=(
                P(("groups", "ctx"), None, ("head", "sub"), None),
                P(("groups", "ctx"), None, ("head", "sub"), None),
                P(("groups", "head", "sub"), "ctx"),
                P(("groups", "head", "sub"), "ctx"),
            ),
            check_vma=False,
        )(*arrays)

    return whole
```

time: 399 us -> 440 us (1.10)
  Pallas kernels: 0 us -> 264 us
  waiting for transfers between devices: 139 us -> 0.01 us
  local copies, waits for them, and re-layouts: 87 us -> 20.7 us
  blocking collectives: 99.7 us -> 129 us
  other arithmetic: 18.7 us -> 2.62 us
  between operations: 16.9 us -> 1.04 us
  matrix products: 24.3 us -> 9.73 us
    pallas_call x0 -> x3, Pallas kernels: none -> 264 us  [the longest x2 258 us: arrange(): pl.pallas_call(kernel, out_shape=jax.ShapeDtypeStruct((requests, sub_coun...]
    all_gather x4 -> x5, blocking collectives: 37 us -> 129 us  [the longest x1 102 us: local(): summed = jnp.sum(lax.all_gather(partial, 'ctx', axis=0), axis=0)]
    all_to_all x2, waiting for transfers between devices: 89.1 us -> 0.01 us  [hand_off(): lax.all_to_all(blocks.reshape(ctx_count * sub_count, per_owner, shard_len...]
    psum x1 -> x0, blocking collectives: 62.8 us -> none  [decode_step(): row_squares = lax.psum(jnp.sum(wide * wide, axis=1), 'ctx')]
    unnamed x4 -> x0, waiting for transfers between devices: 50.4 us -> none
    unnamed x38 -> x18, local copies, waits for them, and re-layouts: 49.6 us -> 17.6 us
    gather x5 -> x1, local copies, waits for them, and re-layouts: 16.7 us -> 0.56 us  [local(): attended = take(attended, owner_order, axis=0)]
    dot_general x15 -> x4, matrix products: 24.3 us -> 9.73 us  [the longest x3 5.09 us: local(): jnp.dot(halves, weight, preferred_element_type=jnp.float32)]
  transfers between devices with their start and end apart: 4 -> 3, of which waited for: 2 -> 0; matrix products, arithmetic and copies ran while one was open for 20% -> 4% of each run, Pallas kernels for 0% -> 31%
where the time goes in v1:
time: 440 us; the launch traced here: 439 us
  Pallas kernels  264 us (60%)
  blocking collectives  129 us (29%)
  local copies, waits for them, and re-layouts  20.7 us (5%)
  starting transfers between devices  11.8 us (3%)
  matrix products  9.73 us (2%)
    pallas_call x2, Pallas kernels, arrange(): pl.pallas_call(kernel, out_shape=jax.ShapeDtypeStruct((requests, sub_coun...  258 us
    all_gather x1, blocking collectives, local(): summed = jnp.sum(lax.all_gather(partial, 'ctx', axis=0), axis=0)  102 us
    unnamed x18, local copies, waits for them, and re-layouts  17.6 us
    all_gather x1, blocking collectives, local(): gathered = unpack(lax.all_gather(send_form(*kept), 'ctx', axis=0))  14 us
    all_to_all x2, starting transfers between devices, hand_off(): lax.all_to_all(blocks.reshape(ctx_count * sub_count, per_owner, shard_len...  11.6 us
  transfers between devices with their start and end apart: 3, of which 0 were waited for; matrix products, arithmetic and copies ran while one was open for 4% of the time, Pallas kernels for 31%

profile of v1, /device:TPU:0, one launch (start us, length us, event | category | flops | bytes accessed | tf_op | source)
XLA Modules:
  0.0 438.9 jit_solution(977409560836172421)
XLA Ops:
  0.6 0.0 copy-start
  0.6 129.0 %arrange.2 = bf16[4,2,1024,2,128]{4,3,2,1,0:T(2,128)(2,1)} custom-call(s32[4]{0:T(128)} %order_ref.3, bf16[4,1024,2,2,128]{4,3,2,1,0:T(2,128)(2,1)} %bitcast.61), custom_call_target="tpu_custom_call" | custom-call | bytes 8388608 | tf_op jit(solution)/shard_map/arrange/pallas_call | solution.py:49
  129.7 0.0 copy-start.4
  129.7 0.0 copy-start.5
  129.7 0.0 copy-start.7
  129.7 0.0 copy-start.3
  129.7 6.5 %all-to-all-start = ((bf16[8,1,1024,2,128]{4,3,2,1,0:T(2,128)(2,1)}), bf16[8,1,1024,2,128]{4,3,2,1,0:T(2,128)(2,1)}, u32[]{:S(2)}, u32[]{:S(2)}) async-start(bf16[8,1,1024,2,128]{4,3,2,1,0:T(2,128)(2,1)} %bitcast.66), calls=%async_computation | async-start | bytes 8388608 | tf_op jit(solution)/shard_map/all_to_all | solution.py:147
  136.2 128.9 %arrange.3 = bf16[4,2,1024,2,128]{4,3,2,1,0:T(2,128)(2,1)} custom-call(s32[4]{0:T(128)} %order_ref.3, bf16[4,1024,2,2,128]{4,3,2,1,0:T(2,128)(2,1)} %bitcast.63), custom_call_target="tpu_custom_call" | custom-call | bytes 8388608 | tf_op jit(solution)/shard_map/arrange/pallas_call | solution.py:49
  265.1 0.0 copy-done.4
  265.1 0.0 copy-done.5
  265.2 5.2 %all_gather.21 = bf16[2,4,2048]{2,0,1:T(2,128)(2,1)S(1)} all-gather(bf16[2,1,2048]{2,0,1:T(2,128)(2,1)S(1)} %pad_maximum_fusion.7), channel_id=1, replica_groups=mesh['groups'=2,'ctx'=4,'head'=2,'sub'=2] {'head','sub'}, dimensions={1}, use_global_device_ids=true | all-gather | bytes 40960 | tf_op jit(solution)/shard_map/all_gather | solution.py:166
  270.4 0.1 multiply_reduce_fusion.2
  270.5 0.1 copy.53
  270.6 0.1 broadcast_in_dim.31
  270.7 0.0 copy-done.7
  270.7 0.0 copy-done
  270.8 0.2 fusion.7
  271.0 0.3 fusion.8
  271.3 4.6 %fusion.9 = f32[16,2048]{1,0:T(8,128)S(1)} fusion(bf16[2048,2048]{1,0:T(8,128)(2,1)} %param.18, bf16[8,2048]{1,0:T(8,128)(2,1)S(1)} %get-tuple-element.38, bf16[8,2048]{1,0:T(8,128)(2,1)S(1)} %get-tuple-element.37), kind=kOutput, calls=%fused_computation.36 | convolution fusion | flops 134348800 | bytes 8585216 | tf_op jit(solution)/shard_map/dot_general | solution.py:176
  275.9 0.0 all-to-all-done
  275.9 0.0 copy-start.6
  275.9 5.1 %all-to-all-start.1 = ((bf16[8,1,1024,2,128]{4,3,2,1,0:T(2,128)(2,1)}), bf16[8,1,1024,2,128]{4,3,2,1,0:T(2,128)(2,1)}, u32[]{:S(2)}, u32[]{:S(2)}) async-start(bf16[8,1,1024,2,128]{4,3,2,1,0:T(2,128)(2,1)} %bitcast.65), calls=%async_computation.1 | async-start | bytes 8388608 | tf_op jit(solution)/shard_map/all_to_all | solution.py:147
  281.0 0.1 broadcast_in_dim.33
  281.1 102.0 %all-gather = f32[32,2688]{1,0:T(8,128)S(1)} all-gather(f32[8,2688]{1,0:T(8,128)S(1)} %pad_maximum_fusion.1), channel_id=2, replica_groups=mesh['groups'=2,'ctx'=4,'head'=2,'sub'=2] {'ctx'}, dimensions={0}, use_global_device_ids=true | all-gather | bytes 430080 | tf_op jit(solution)/shard_map/all_gather | solution.py:189
  383.1 0.1 fusion.14
  383.2 0.1 slice_multiply_fusion.1
  383.4 0.1 multiply_cosine_fusion
  383.5 0.1 subtract_convert_fusion
  383.6 0.1 fusion.6
  383.7 1.9 all_gather.24.q_ref
  385.6 2.2 copy-done.1
  387.8 6.3 %attend_shard.1 = (f32[4,64,128]{2,1,0:T(8,128)S(1)}, f32[4,64,128]{2,1,0:T(8,128)S(1)}, f32[4,64,128]{2,1,0:T(8,128)S(1)}) custom-call(s32[4]{0:T(128)S(1)} %copy-done.2, s32[1]{0:T(128)} %bitcast.11.place_ref, bf16[4,64,128]{2,1,0:T(8,128)(2,1)S(1)} %all_gather.24.q_ref, bf16[4,4096,128]{2,1,0:T(8,128)(2,1)S(1)} %bitcast.62, bf16[4,4096,128]{2,1,0:T(8,128)(2,1)} %bitcast.64), custom_call_target="tpu_custom_call" | custom-call | flops 536870912 | bytes 8388608 | tf_op jit(solution)/shard_map/attend_shard/pallas_call | solution.py:101
  394.1 0.2 dynamic-slice_reduce_fusion
  394.2 0.1 reshape_squeeze.7
  394.3 0.1 reshape_squeeze.6
  394.4 0.2 collective-permute-start
  394.7 0.1 convert_bitcast_fusion.1
  394.8 0.1 reduce_max.35
  394.8 0.0 copy-done.6
  394.8 0.6 dynamic_slice.24
  395.4 0.2 multiply_reduce_fusion.1
  395.6 0.1 fusion.11
  395.8 0.0 collective-permute-done
  395.8 0.1 stack_reshape.11
  395.9 0.1 stack_reshape.10
  396.0 0.1 stack.31
  396.1 0.1 reshape.261
  396.2 0.1 fusion.3
  396.3 14.0 %all-gather.3 = f32[4,130,128]{2,1,0:T(8,128)S(1)} all-gather(f32[1,130,128]{2,1,0:T(8,128)S(1)} %maximum_bitcast_fusion), channel_id=3, replica_groups=mesh['groups'=2,'ctx'=4,'head'=2,'sub'=2] {'ctx'}, dimensions={0}, use_global_device_ids=true | all-gather | bytes 332800 | tf_op jit(solution)/shard_map/all_gather | solution.py:249
  410.3 0.1 reshape.264
  410.5 0.1 reshape.265
  410.6 0.1 fusion.21
  410.8 0.1 fusion.2
  410.9 0.1 multiply_reduce_fusion
  411.0 0.1 divide_convert_fusion
  411.1 0.6 gather_fusion
  411.7 4.6 %fusion = f32[2,4,2048]{2,1,0:T(4,128)S(1)} fusion(bf16[2,4,2048]{2,1,0:T(4,128)(2,1)S(1)} %reshape.266, bf16[2048,2048]{1,0:T(8,128)(2,1)} %param.21), kind=kOutput, calls=%fused_computation.1 | convolution fusion | flops 67108864 | bytes 8486912 | tf_op jit(solution)/shard_map/dot_general | solution.py:279
  416.3 5.8 %all-gather.2 = f32[8,4,2048]{2,1,0:T(4,128)S(1)} all-gather(f32[2,4,2048]{2,1,0:T(4,128)S(1)} %fusion), channel_id=4, replica_groups=mesh['groups'=2,'ctx'=4,'head'=2,'sub'=2] {'head','sub'}, dimensions={0}, use_global_device_ids=true | all-gather | bytes 327680 | tf_op jit(solution)/shard_map/all_gather | solution.py:282
  422.1 0.1 dynamic-slice_reduce_fusion.4
  422.2 0.7 fusion.10
  422.9 0.6 slice_bitcast_fusion
  423.5 0.0 all-to-all-done.1
  423.5 7.7 %copy.86 = bf16[1,8192,2,128]{3,2,1,0:T(2,128)(2,1)} copy(bf16[1,8192,2,128]{3,2,1,0:T(2,128)(2,1)} %bitcast.3) | data formatting | bytes 8388608
  431.2 7.7 %copy.87 = bf16[1,8192,2,128]{3,2,1,0:T(2,128)(2,1)} copy(bf16[1,8192,2,128]{3,2,1,0:T(2,128)(2,1)} %bitcast.7) | data formatting | bytes 8388608
  (40 shorter events, 0.4 us)
Async XLA Ops:
  0.6 270.1 %copy-start = (bf16[2048,256]{1,0:T(8,128)(2,1)S(1)}, bf16[2048,256]{1,0:T(8,128)(2,1)}, u32[]{:S(2)}) copy-start(bf16[2048,256]{1,0:T(8,128)(2,1)} %param.20) | copy-start | bytes 3145732
  129.7 135.4 %copy-start.4 = (bf16[1,2048]{1,0:T(2,128)(2,1)S(1)}, bf16[1,2048]{1,0:T(2,128)(2,1)}, u32[]{:S(2)}) copy-start(bf16[1,2048]{1,0:T(2,128)(2,1)} %param.16) | copy-start | bytes 12292
  129.7 135.4 %copy-start.5 = (bf16[1,2048]{1,0:T(2,128)(2,1)S(1)}, bf16[1,2048]{1,0:T(2,128)(2,1)}, u32[]{:S(2)}) copy-start(bf16[1,2048]{1,0:T(2,128)(2,1)} %param.15) | copy-start | bytes 12292
  129.7 141.0 %copy-start.7 = (bf16[2048]{0:T(1024)(128)(2,1)S(1)}, bf16[2048]{0:T(1024)(128)(2,1)}, u32[]{:S(2)}) copy-start(bf16[2048]{0:T(1024)(128)(2,1)} %param.17) | copy-start | bytes 12292
  129.7 141.3 %copy-start.3 = (bf16[2048,256]{1,0:T(8,128)(2,1)S(1)}, bf16[2048,256]{1,0:T(8,128)(2,1)}, u32[]{:S(2)}) copy-start(bf16[2048,256]{1,0:T(8,128)(2,1)} %param.19) | copy-start | bytes 3145732
  129.7 146.2 %all-to-all-start = ((bf16[8,1,1024,2,128]{4,3,2,1,0:T(2,128)(2,1)}), bf16[8,1,1024,2,128]{4,3,2,1,0:T(2,128)(2,1)}, u32[]{:S(2)}, u32[]{:S(2)}) async-start(bf16[8,1,1024,2,128]{4,3,2,1,0:T(2,128)(2,1)} %bitcast.66), calls=%async_computation | async-start | bytes 8388608 | tf_op jit(solution)/shard_map/all_to_all | solution.py:147
  275.9 107.5 %copy-start.2 = (s32[4]{0:T(128)S(1)}, s32[4]{0:T(128)}, u32[]{:S(2)}) copy-start(s32[4]{0:T(128)} %lengths_ref.1) | copy-start | bytes 52
  275.9 118.9 %copy-start.6 = (s32[4]{0:T(128)S(1)}, s32[4]{0:T(128)}, u32[]{:S(2)}) copy-start(s32[4]{0:T(128)} %order_ref.3) | copy-start | bytes 52
  275.9 147.6 %all-to-all-start.1 = ((bf16[8,1,1024,2,128]{4,3,2,1,0:T(2,128)(2,1)}), bf16[8,1,1024,2,128]{4,3,2,1,0:T(2,128)(2,1)}, u32[]{:S(2)}, u32[]{:S(2)}) async-start(bf16[8,1,1024,2,128]{4,3,2,1,0:T(2,128)(2,1)} %bitcast.65), calls=%async_computation.1 | async-start | bytes 8388608 | tf_op jit(solution)/shard_map/all_to_all | solution.py:147
  385.6 2.2 copy-start.1
  394.4 1.3 collective-permute-start

commit v2 on v1

--- a/solution.py
+++ b/solution.py
@@ -29,39 +29,93 @@
     )
 
 
-def arrange(cache, owner_order, sub_count):
-    requests, shard_length, heads, head_dim = cache.shape
-    heads_decode = heads // sub_count
-    split = cache.reshape(requests, shard_length, sub_count, heads_decode, head_dim)
-
-    def kernel(order_ref, in_ref, out_ref, sems):
-        copies = []
-        for i in range(requests):
-            for s in range(sub_count):
-                copy = pltpu.make_async_copy(
-                    in_ref.at[order_ref[i], :, s], out_ref.at[i, s], sems.at[i, s]
-                )
-                copy.start()
-                copies.append(copy)
-        for copy in copies:
+def arrange(cache, request, core, core_count, after):
+    _, shard_length, heads, head_dim = cache.shape
+    heads_decode = heads // core_count
+    steps = 4
+    places = shard_length // steps
+    block = jax.ShapeDtypeStruct((shard_length, heads_decode, head_dim), cache.dtype)
+
+    def kernel(request_ref, core_ref, in_ref, *rest):
+        out_refs = rest[len(after) :]
+        for own in range(core_count):
+
+            @pl.when(core_ref[0] == own)
+            def _():
+                for f, out_ref in enumerate(out_refs):
+                    low = (own + f) % core_count * heads_decode
+                    out_ref[...] = in_ref[0, :, low : low + heads_decode, :]
+
+    blocks = pl.pallas_call(
+        kernel,
+        out_shape=(block,) * core_count,
+        grid_spec=pltpu.PrefetchScalarGridSpec(
+            num_scalar_prefetch=2,
+            grid=(steps,),
+            in_specs=[
+                pl.BlockSpec((1, places, heads, head_dim), lambda i, r, c: (r[0], i, 0, 0))
+            ]
+            + [pl.BlockSpec(memory_space=pl.ANY)] * len(after),
+            out_specs=(pl.BlockSpec((places, heads_decode, head_dim), lambda i, r, c: (i, 0, 0)),)
+            * core_count,
+        ),
+        compiler_params=pltpu.CompilerParams(vmem_limit_bytes=VMEM_BYTES),
+        cost_estimate=pl.CostEstimate(
+            flops=0,
+            transcendentals=0,
+            bytes_accessed=4 * shard_length * heads * head_dim,
+        ),
+        name="arrange",
+    )(request, core, cache, *after)
+    return [x.reshape(shard_length * heads_decode, head_dim) for x in blocks]
+
+
+def assemble(blocks, places, rows, filled=None):
+    block_rows, head_dim = blocks[0].shape
+    count = len(blocks)
+    extra = [] if filled is None else [filled]
+
+    def kernel(places_ref, *refs):
+        in_refs = refs[:count]
+        out_ref, held, in_sems, out_sems = refs[count + len(extra) :]
+        into = [
+            pltpu.make_async_copy(in_refs[i], held.at[i], in_sems.at[i]) for i in range(count)
+        ]
+        out_of = [
+            pltpu.make_async_copy(
+                held.at[i],
+                out_ref.at[pl.ds(pl.multiple_of(places_ref[i], block_rows), block_rows)],
+                out_sems.at[i],
+            )
+            for i in range(count)
+        ]
+        for copy in into:
+            copy.start()
+        for i in range(count):
+            into[i].wait()
+            out_of[i].start()
+        for copy in out_of:
             copy.wait()
 
     return pl.pallas_call(
         kernel,
-        out_shape=jax.ShapeDtypeStruct(
-            (requests, sub_count, shard_length, heads_decode, head_dim), cache.dtype
+        out_shape=jax.ShapeDtypeStruct((rows, head_dim), blocks[0].dtype),
+        in_specs=[pl.BlockSpec(memory_space=pltpu.SMEM)]
+        + [pl.BlockSpec(memory_space=pl.ANY)] * count
+        + [pl.BlockSpec(memory_space=pltpu.HBM)] * len(extra),
+        out_specs=pl.BlockSpec(memory_space=pltpu.HBM),
+        scratch_shapes=[
+            pltpu.VMEM((count, block_rows, head_dim), blocks[0].dtype),
+            pltpu.SemaphoreType.DMA((count,)),
+            pltpu.SemaphoreType.DMA((count,)),
+        ],
+        input_output_aliases={1 + count: 0} if extra else {},
+        compiler_params=pltpu.CompilerParams(vmem_limit_bytes=VMEM_BYTES),
+        cost_estimate=pl.CostEstimate(
+            flops=0, transcendentals=0, bytes_accessed=4 * count * block_rows * head_dim
         ),
-        in_specs=[
-            pl.BlockSpec(memory_space=pltpu.SMEM),
-            pl.BlockSpec(memory_space=pltpu.HBM),
-        ],
-        out_specs=pl.BlockSpec(memory_space=pltpu.HBM),
-        scratch_shapes=[pltpu.SemaphoreType.DMA((requests, sub_count))],
-        cost_estimate=pl.CostEstimate(
-            flops=0, transcendentals=0, bytes_accessed=2 * cache.size * cache.dtype.itemsize
-        ),
-        name="arrange",
-    )(owner_order, split)
+        name="assemble",
+    )(places, *blocks, *extra)
 
 
 def attend_shard(queries, keys, values, lengths, first_place, score_factor):
@@ -134,29 +188,54 @@
     ctx_count = lax.axis_size("ctx")
     sub_count = lax.axis_size("sub")
     requests, shard_length, heads, head_dim = key_cache.shape
-    per_owner = requests // ctx_count
+    assert requests == ctx_count
     heads_decode = heads // sub_count
     ctx_index = lax.axis_index("ctx")
     sub_index = lax.axis_index("sub")
     take = functools.partial(jnp.take, mode="clip")
 
-    def hand_off(cache):
-        blocks = arrange(cache, owner_order, sub_count)
-        blocks = blocks.reshape(ctx_count, per_owner, sub_count, shard_length, heads_decode, head_dim)
-        blocks = jnp.swapaxes(blocks, 1, 2)
-        moved = lax.all_to_all(
-            blocks.reshape(
-                ctx_count * sub_count, per_owner, shard_length, heads_decode, head_dim
-            ),
-            ("ctx", "sub"),
-            split_axis=0,
-            concat_axis=2,
-            tiled=True,
-        )
-        return moved.reshape(per_owner, -1, heads_decode, head_dim)
-
-    moved_keys = hand_off(key_cache)
-    moved_values = hand_off(value_cache)
+    device_rows = shard_length * heads_decode
+    core = jnp.reshape(sub_index, (1,)).astype(jnp.int32)
+    received = ({}, {})
+
+    def place_of(shift, flip):
+        source = lax.rem(ctx_index - shift + ctx_count, ctx_count) * sub_count + lax.rem(
+            sub_index - flip + sub_count, sub_count
+        )
+        return source * device_rows
+
+    def hand_off(which, shift, after=()):
+        owner = lax.rem(ctx_index + shift, ctx_count)
+        request = lax.dynamic_slice_in_dim(owner_order, owner, 1)
+        blocks = arrange(
+            (key_cache, value_cache)[which], request, core, sub_count, after
+        )
+        for flip, block in enumerate(blocks):
+            if shift or flip:
+                pairs = [
+                    (
+                        c * sub_count + s,
+                        (c + shift) % ctx_count * sub_count + (s + flip) % sub_count,
+                    )
+                    for c in range(ctx_count)
+                    for s in range(sub_count)
+                ]
+                block = lax.ppermute(block, ("ctx", "sub"), pairs)
+            received[which][shift, flip] = block
+
+    def sum_shifted(values, combine):
+        return combine(
+            [values]
+            + [
+                lax.ppermute(
+                    values, "ctx", [(c, (c + shift) % ctx_count) for c in range(ctx_count)]
+                )
+                for shift in range(1, ctx_count)
+            ]
+        )
+
+    middle = ctx_count // 2
+    hand_off(0, middle)
 
     query_width = w_query.shape[1]
     key_width = w_key.shape[1]
@@ -186,7 +265,11 @@
         ],
         axis=1,
     )
-    summed = jnp.sum(lax.all_gather(partial, "ctx", axis=0), axis=0)
+    summed = sum_shifted(partial, lambda parts: functools.reduce(jnp.add, parts))
+    for which in (0, 1):
+        for shift in range(1, middle):
+            hand_off(which, shift, (partial,))
+        hand_off(which, 0, (partial,))
     raw = summed[:, :-LANES] * lax.rsqrt(summed[:, -LANES:][:, :1] / width + eps_norm)
     raw = raw.reshape(2, requests, -1, head_dim)
     positions = lengths.astype(jnp.float32)[None, :] + jnp.arange(2, dtype=jnp.float32)[:, None]
@@ -244,10 +327,15 @@
     for shift in range(1, sub_count):
         pairs = [(i, (i + shift) % sub_count) for i in range(sub_count)]
         sent = send_form(*pack(lax.rem(sub_index + shift, sub_count)))
-        received = unpack(lax.ppermute(sent, "sub", pairs))
-        kept = merge(*(jnp.stack([a, b]) for a, b in zip(kept, received)))
-    gathered = unpack(lax.all_gather(send_form(*kept), "ctx", axis=0))
+        other = unpack(lax.ppermute(sent, "sub", pairs))
+        kept = merge(*(jnp.stack([a, b]) for a, b in zip(kept, other)))
+    stats = send_form(*kept)
+    gathered = unpack(sum_shifted(stats, jnp.stack))
     sums, maxima, totals = merge(*gathered)
+    for which in (0, 1):
+        for shift in range(middle + 1, ctx_count):
+            hand_off(which, shift, (stats,))
+    hand_off(1, middle, (stats,))
 
     grouped = own_queries.reshape(requests, heads_decode, 2, group_size, head_dim).astype(
         jnp.float32
@@ -284,6 +372,22 @@
     own_ids = lax.dynamic_slice_in_dim(owner_order, row_start, rows_local)
     residual = take(tokens, own_ids, axis=1).astype(jnp.float32)
     result = (residual + jnp.sum(parts, axis=0)).astype(jnp.bfloat16)
+
+    def outcome(which, last):
+        early = [key for key in received[which] if key not in last]
+        whole = None
+        for keys in (early, last):
+            if keys:
+                whole = assemble(
+                    [received[which][key] for key in keys],
+                    jnp.stack([place_of(*key) for key in keys]).astype(jnp.int32),
+                    ctx_count * sub_count * device_rows,
+                    whole,
+                )
+        return whole.reshape(1, -1, heads_decode, head_dim)
+
+    moved_keys = outcome(0, [])
+    moved_values = outcome(1, [(middle, flip) for flip in range(sub_count)])
     return (moved_keys, moved_values, result[0], result[1])
 
 

time: 440 us -> 243 us (0.55)
  Pallas kernels: 264 us -> 30.9 us
  waiting for transfers between devices: 0.01 us -> 128 us
  blocking collectives: 129 us -> 13.8 us
  starting transfers between devices: 11.8 us -> 30.6 us
    pallas_call x2 -> x11, Pallas kernels: 258 us -> 24.6 us  [the longest x8 16.8 us: arrange(): pl.pallas_call(kernel, out_shape=(block,) * core_count, grid_spec=pltpu.P...]
    ppermute x1 -> x21, waiting for transfers between devices: 0.01 us -> 128 us  [the longest x14 127 us: hand_off(): block = lax.ppermute(block, ('ctx', 'sub'), pairs)]
    all_gather x2 -> x0, blocking collectives: 116 us -> none  [the longest x1 102 us: local(): summed = jnp.sum(lax.all_gather(partial, 'ctx', axis=0), axis=0)]
    ppermute x1 -> x21, starting transfers between devices: 0.23 us -> 30.6 us  [the longest x14 18 us: hand_off(): block = lax.ppermute(block, ('ctx', 'sub'), pairs)]
    all_to_all x2 -> x0, starting transfers between devices: 11.6 us -> none  [hand_off(): lax.all_to_all(blocks.reshape(ctx_count * sub_count, per_owner, shard_len...]
    unnamed x18 -> x58, local copies, waits for them, and re-layouts: 17.6 us -> 21.1 us
  transfers between devices with their start and end apart: 3 -> 21, of which waited for: 0 -> 9; matrix products, arithmetic and copies ran while one was open for 4% -> 4% of each run, Pallas kernels for 31% -> 12%
where the time goes in v2:
time: 243 us
  waiting for transfers between devices  128 us (53%)
  Pallas kernels  30.9 us (13%)
  starting transfers between devices  30.6 us (13%)
  local copies, waits for them, and re-layouts  24.4 us (10%)
  blocking collectives  13.8 us (6%)
  matrix products  9.81 us (4%)
  other arithmetic  4.13 us (2%)
    ppermute x14, waiting for transfers between devices, hand_off(): block = lax.ppermute(block, ('ctx', 'sub'), pairs)  127 us
    unnamed x58, local copies, waits for them, and re-layouts  21.1 us
    ppermute x14, starting transfers between devices, hand_off(): block = lax.ppermute(block, ('ctx', 'sub'), pairs)  18 us
    pallas_call x8, Pallas kernels, arrange(): pl.pallas_call(kernel, out_shape=(block,) * core_count, grid_spec=pltpu.P...  16.8 us
    ppermute x6, starting transfers between devices, sum_shifted(): lax.ppermute(values, 'ctx', [(c, (c + shift) % ctx_count) for c in range(...  12.4 us
    pallas_call x3, Pallas kernels, assemble(): pl.pallas_call(kernel, out_shape=jax.ShapeDtypeStruct((rows, head_dim), b...  7.87 us
    pallas_call x1, Pallas kernels, attend_shard(): pl.pallas_call(kernel, out_shape=(result, result, result), grid_spec=pltp...  6.29 us
    all_gather x1, blocking collectives, local(): lax.all_gather(jnp.stack([first_tokens, second_tokens]), ('head', 'sub'),...  6.17 us
  transfers between devices with their start and end apart: 21, of which 9 were waited for; matrix products, arithmetic and copies ran while one was open for 4% of the time, Pallas kernels for 12%

profile of v2, /device:TPU:0, one launch (start us, length us, event | category | flops | bytes accessed | tf_op | source)
XLA Modules:
  0.0 242.7 jit_solution(9429556768676249353)
XLA Ops:
  0.6 0.8 pad_maximum_fusion.9
  1.5 6.2 %all_gather.9 = bf16[2,4,2048]{2,0,1:T(2,128)(2,1)S(1)} all-gather(bf16[2,1,2048]{2,0,1:T(2,128)(2,1)S(1)} %pad_maximum_fusion.9), channel_id=1, replica_groups=mesh['groups'=2,'ctx'=4,'head'=2,'sub'=2] {'head','sub'}, dimensions={1}, use_global_device_ids=true | all-gather | bytes 40960 | tf_op jit(solution)/shard_map/all_gather | solution.py:245
  7.8 0.7 convert_element_type.53
  8.6 4.7 %fusion.9 = f32[16,2048]{1,0:T(8,128)S(1)} fusion(bf16[2048,2048]{1,0:T(8,128)(2,1)} %param.18, bf16[8,2048]{1,0:T(8,128)(2,1)S(1)} %get-tuple-element.70, bf16[8,2048]{1,0:T(8,128)(2,1)S(1)} %get-tuple-element.69), kind=kOutput, calls=%fused_computation.38 | convolution fusion | flops 134348800 | bytes 8585216 | tf_op jit(solution)/shard_map/dot_general | solution.py:255
  13.2 0.3 fusion.7
  13.5 0.3 fusion.8
  14.0 2.1 collective-permute-start.5
  16.1 2.6 %collective-permute-start.6 = (f32[8,2688]{1,0:T(8,128)S(1)}, f32[8,2688]{1,0:T(8,128)S(1)}, u32[]{:S(2)}, u32[]{:S(2)}) collective-permute-start(f32[8,2688]{1,0:T(8,128)S(1)} %pad_maximum_fusion.2.rest_0_), channel_id=1, source_target_pairs={{0,8},{4,12},{8,0},{12,4},{1,9},{5,13},{9,1},{13,5},{2,10},{6,14},... | collective-permute-start | bytes 258056 | tf_op jit(solution)/shard_map/ppermute | solution.py:230
  18.7 1.3 collective-permute-start.7
  20.0 0.7 fusion.26
  20.7 2.2 copy-done.1
  22.9 2.8 %arrange.13 = (bf16[1024,2,128]{2,1,0:T(2,128)(2,1)}, bf16[1024,2,128]{2,1,0:T(2,128)(2,1)}) custom-call(s32[1]{0:T(128)} %get-tuple-element.86.request_ref, s32[1]{0:T(128)} %bitcast.8.core_ref, bf16[4,1024,4,128]{3,2,1,0:T(4,128)(2,1)S(1)} %copy-done.1, f32[8,2688]{1,0:T(8,128)S(1)} %pad_maximum_fusion.2.rest_0_), custom_call_target="tpu_custom_call" | custom-call | bytes 2097152 | tf_op jit(solution)/shard_map/arrange/pallas_call | solution.py:49
  25.7 0.7 collective-permute-start.13
  26.5 2.2 copy-done.2
  28.7 2.7 %arrange.14 = (bf16[1024,2,128]{2,1,0:T(2,128)(2,1)S(1)}, bf16[1024,2,128]{2,1,0:T(2,128)(2,1)}) custom-call(s32[1]{0:T(128)} %get-tuple-element.85.request_ref, s32[1]{0:T(128)} %bitcast.8.core_ref, bf16[4,1024,4,128]{3,2,1,0:T(4,128)(2,1)S(1)} %copy-done.2, f32[8,2688]{1,0:T(8,128)S(1)} %pad_maximum_fusion.2.rest_0_), custom_call_target="tpu_custom_call" | custom-call | bytes 2097152 | tf_op jit(solution)/shard_map/arrange/pallas_call | solution.py:49
  31.4 0.8 copy-done.9
  32.2 2.2 copy-done.5
  34.4 2.7 %arrange.9 = (bf16[1024,2,128]{2,1,0:T(2,128)(2,1)}, bf16[1024,2,128]{2,1,0:T(2,128)(2,1)S(1)}) custom-call(s32[1]{0:T(128)} %get-tuple-element.86.request_ref, s32[1]{0:T(128)} %bitcast.8.core_ref, bf16[4,1024,4,128]{3,2,1,0:T(4,128)(2,1)S(1)} %copy-done.5, f32[8,2688]{1,0:T(8,128)S(1)} %pad_maximum_fusion.2.rest_0_), custom_call_target="tpu_custom_call" | custom-call | bytes 2097152 | tf_op jit(solution)/shard_map/arrange/pallas_call | solution.py:49
  37.1 1.7 arrange.10
  38.8 2.3 copy-done.6
  41.1 1.7 arrange.8
  42.8 0.8 copy-done.14
  43.6 0.8 copy-done.16
  45.3 1.9 all_gather.10.q_ref
  47.2 2.2 copy-done.7
  49.4 6.3 %attend_shard.1 = (f32[4,64,128]{2,1,0:T(8,128)S(1)}, f32[4,64,128]{2,1,0:T(8,128)S(1)}, f32[4,64,128]{2,1,0:T(8,128)S(1)}) custom-call(s32[4]{0:T(128)S(1)} %copy-done.11, s32[1]{0:T(128)} %bitcast.17.place_ref, bf16[4,64,128]{2,1,0:T(8,128)(2,1)S(1)} %all_gather.10.q_ref, bf16[4,4096,128]{2,1,0:T(8,128)(2,1)S(1)} %bitcast.80, bf16[4,4096,128]{2,1,0:T(8,128)(2,1)} %bitcast.79), custom_call_target="tpu_custom_call" | custom-call | flops 536870912 | bytes 8388608 | tf_op jit(solution)/shard_map/attend_shard/pallas_call | solution.py:155
  55.7 0.2 dynamic-slice_reduce_fusion
  56.0 0.2 collective-permute-start.8
  56.5 0.9 collective-permute-done.8
  57.9 0.7 collective-permute-start.18
  58.6 3.5 %collective-permute-start.19 = (f32[130,128]{1,0:T(8,128)S(1)}, f32[130,128]{1,0:T(8,128)S(1)}, u32[]{:S(2)}, u32[]{:S(2)}) collective-permute-start(f32[130,128]{1,0:T(8,128)S(1)} %get-tuple-element.74.rest_0_), channel_id=1, source_target_pairs={{0,8},{4,12},{8,0},{12,4},{1,9},{5,13},{9,1},{13,5},{2,10},{6,14},... | collective-permute-start | bytes 199688 | tf_op jit(solution)/shard_map/ppermute | solution.py:230
  62.0 2.2 collective-permute-start.20
  64.4 2.2 copy-done.3
  66.6 1.8 arrange.12
  68.4 0.8 copy-done.23
  69.2 0.8 copy-done.24
  70.0 2.2 copy-done.4
  72.2 1.7 arrange.15
  74.0 1.7 arrange.11
  75.7 0.8 copy-done.19
  76.5 0.8 copy-done.21
  78.0 0.1 fusion.2
  78.3 0.6 gather_fusion
  79.0 3.9 %collective-permute-start.16 = (bf16[2048,128]{1,0:T(8,128)(2,1)}, bf16[2048,128]{1,0:T(8,128)(2,1)S(1)}, u32[]{:S(2)}, u32[]{:S(2)}) collective-permute-start(bf16[2048,128]{1,0:T(8,128)(2,1)} %bitcast.92), channel_id=1, source_target_pairs={{0,12},{1,13},{4,0},{5,1},{8,4},{9,5},{12,8},{13,9},{2,14},{3,15},... | collective-permute-start | bytes 1572872 | tf_op jit(solution)/shard_map/ppermute | solution.py:223
  82.9 1.4 collective-permute-start.17
  84.3 10.0 %collective-permute-done.2.refs_2_ = bf16[2048,128]{1,0:T(8,128)(2,1)S(1)} collective-permute-done((bf16[2048,128]{1,0:T(8,128)(2,1)}, bf16[2048,128]{1,0:T(8,128)(2,1)S(1)}, u32[]{:S(2)}, u32[]{:S(2)}) %collective-permute-start.2) | collective-permute-done | bytes 524320 | tf_op jit(solution)/shard_map/ppermute | solution.py:223
  94.3 4.6 %fusion = f32[2,4,2048]{2,1,0:T(4,128)S(1)} fusion(bf16[2,4,2048]{2,1,0:T(4,128)(2,1)S(1)} %reshape.318, bf16[2048,2048]{1,0:T(8,128)(2,1)} %param.21), kind=kOutput, calls=%fused_computation.1 | convolution fusion | flops 67108864 | bytes 8486912 | tf_op jit(solution)/shard_map/dot_general | solution.py:367
  98.9 5.8 %all-gather = f32[8,4,2048]{2,1,0:T(4,128)S(1)} all-gather(f32[2,4,2048]{2,1,0:T(4,128)S(1)} %fusion), channel_id=2, replica_groups=mesh['groups'=2,'ctx'=4,'head'=2,'sub'=2] {'head','sub'}, dimensions={0}, use_global_device_ids=true | all-gather | bytes 327680 | tf_op jit(solution)/shard_map/all_gather | solution.py:370
  104.8 0.4 collective-permute-start.4
  105.2 11.0 %collective-permute-done.16.refs_4_ = bf16[2048,128]{1,0:T(8,128)(2,1)S(1)} collective-permute-done((bf16[2048,128]{1,0:T(8,128)(2,1)}, bf16[2048,128]{1,0:T(8,128)(2,1)S(1)}, u32[]{:S(2)}, u32[]{:S(2)}) %collective-permute-start.16) | collective-permute-done | bytes 524320 | tf_op jit(solution)/shard_map/ppermute | solution.py:223
  116.2 1.0 collective-permute-start
  117.2 9.8 %collective-permute-done.17.refs_5_ = bf16[2048,128]{1,0:T(8,128)(2,1)S(1)} collective-permute-done((bf16[2048,128]{1,0:T(8,128)(2,1)}, bf16[2048,128]{1,0:T(8,128)(2,1)S(1)}, u32[]{:S(2)}, u32[]{:S(2)}) %collective-permute-start.17) | collective-permute-done | bytes 524320 | tf_op jit(solution)/shard_map/ppermute | solution.py:223
  127.0 1.2 collective-permute-start.1
  128.2 55.4 %collective-permute-done.11.refs_0_ = bf16[2048,128]{1,0:T(8,128)(2,1)S(1)} collective-permute-done((bf16[2048,128]{1,0:T(8,128)(2,1)}, bf16[2048,128]{1,0:T(8,128)(2,1)S(1)}, u32[]{:S(2)}, u32[]{:S(2)}) %collective-permute-start.11) | collective-permute-done | bytes 524320 | tf_op jit(solution)/shard_map/ppermute | solution.py:223
  183.6 11.3 %collective-permute-done.12.refs_1_ = bf16[2048,128]{1,0:T(8,128)(2,1)S(1)} collective-permute-done((bf16[2048,128]{1,0:T(8,128)(2,1)}, bf16[2048,128]{1,0:T(8,128)(2,1)S(1)}, u32[]{:S(2)}, u32[]{:S(2)}) %collective-permute-start.12) | collective-permute-done | bytes 524320 | tf_op jit(solution)/shard_map/ppermute | solution.py:223
  194.9 9.3 %collective-permute-start.9 = (bf16[2048,128]{1,0:T(8,128)(2,1)S(1)}, bf16[2048,128]{1,0:T(8,128)(2,1)S(1)}, u32[]{:S(2)}, u32[]{:S(2)}) collective-permute-start(bf16[2048,128]{1,0:T(8,128)(2,1)S(1)} %bitcast.87), channel_id=1, source_target_pairs={{0,12},{1,13},{4,0},{5,1},{8,4},{9,5},{12,8},{13,9},{2,14},{3,15},... | collective-permute-start | bytes 1572872 | tf_op jit(solution)/shard_map/ppermute | solution.py:223
  204.2 0.6 fusion.10
  204.8 0.6 slice_bitcast_fusion
  205.4 3.3 %assemble.4.refs_2_ = bf16[16384,128]{1,0:T(8,128)(2,1)} custom-call(s32[6]{0:T(128)S(1)} %stack.100.places_ref, bf16[2048,128]{1,0:T(8,128)(2,1)S(1)} %collective-permute-done.13.refs_0_, bf16[2048,128]{1,0:T(8,128)(2,1)} %collective-permute-done.14.refs_1_, bf16[2048,128]{1,0:T(8,128)(2,1)S(1)} %bitcast.82, ...), custom_call_target="tpu_custom_call" | custom-call | bytes 6291456 | tf_op jit(solution)/shard_map/assemble/pallas_call | solution.py:100
  208.7 1.6 assemble.5
  210.4 7.0 %collective-permute-done.1.refs_1_ = bf16[2048,128]{1,0:T(8,128)(2,1)S(1)} collective-permute-done((bf16[2048,128]{1,0:T(8,128)(2,1)S(1)}, bf16[2048,128]{1,0:T(8,128)(2,1)S(1)}, u32[]{:S(2)}, u32[]{:S(2)}) %collective-permute-start.1) | collective-permute-done | bytes 524320 | tf_op jit(solution)/shard_map/ppermute | solution.py:223
  217.3 11.1 %collective-permute-done.10.refs_7_ = bf16[2048,128]{1,0:T(8,128)(2,1)S(1)} collective-permute-done((bf16[2048,128]{1,0:T(8,128)(2,1)S(1)}, bf16[2048,128]{1,0:T(8,128)(2,1)S(1)}, u32[]{:S(2)}, u32[]{:S(2)}) %collective-permute-start.10) | collective-permute-done | bytes 524320 | tf_op jit(solution)/shard_map/ppermute | solution.py:223
  228.5 11.3 %collective-permute-done.9.refs_6_ = bf16[2048,128]{1,0:T(8,128)(2,1)S(1)} collective-permute-done((bf16[2048,128]{1,0:T(8,128)(2,1)S(1)}, bf16[2048,128]{1,0:T(8,128)(2,1)S(1)}, u32[]{:S(2)}, u32[]{:S(2)}) %collective-permute-start.9) | collective-permute-done | bytes 524320 | tf_op jit(solution)/shard_map/ppermute | solution.py:223
  239.8 3.0 %assemble.3 = bf16[16384,128]{1,0:T(8,128)(2,1)} custom-call(s32[8]{0:T(128)S(1)} %stack.89.places_ref, bf16[2048,128]{1,0:T(8,128)(2,1)S(1)} %collective-permute-done.refs_0_, bf16[2048,128]{1,0:T(8,128)(2,1)S(1)} %collective-permute-done.1.refs_1_, bf16[2048,128]{1,0:T(8,128)(2,1)S(1)} %collective-permute-done.2.refs_2_, ...), custom_call_target="tpu_custom_call" | custom-call | bytes 8388608 | tf_op jit(solution)/shard_map/assemble/pallas_call | solution.py:100
  (126 shorter events, 3.4 us)
Async XLA Ops:
  0.6 12.6 %copy-start = (bf16[2048,256]{1,0:T(8,128)(2,1)S(1)}, bf16[2048,256]{1,0:T(8,128)(2,1)}, u32[]{:S(2)}) copy-start(bf16[2048,256]{1,0:T(8,128)(2,1)} %param.20) | copy-start | bytes 3145732
  8.5 5.0 %copy-start.27 = (bf16[2048,256]{1,0:T(8,128)(2,1)S(1)}, bf16[2048,256]{1,0:T(8,128)(2,1)}, u32[]{:S(2)}) copy-start(bf16[2048,256]{1,0:T(8,128)(2,1)} %param.19) | copy-start | bytes 3145732
  8.5 11.5 %copy-start.28 = (s32[4]{0:T(128)S(1)}, s32[4]{0:T(128)}, u32[]{:S(2)}) copy-start(s32[4]{0:T(128)} %param.14) | copy-start | bytes 52
  14.0 30.7 %collective-permute-start.5 = (f32[8,2688]{1,0:T(8,128)S(1)}, f32[8,2688]{1,0:T(8,128)S(1)}, u32[]{:S(2)}, u32[]{:S(2)}) collective-permute-start(f32[8,2688]{1,0:T(8,128)S(1)} %pad_maximum_fusion.2.rest_0_), channel_id=1, source_target_pairs={{0,4},{4,8},{8,12},{12,0},{1,5},{5,9},{9,13},{13,1},{2,6},{6,10},{... | collective-permute-start | bytes 258056 | tf_op jit(solution)/shard_map/ppermute | solution.py:230
  16.1 28.7 %collective-permute-start.6 = (f32[8,2688]{1,0:T(8,128)S(1)}, f32[8,2688]{1,0:T(8,128)S(1)}, u32[]{:S(2)}, u32[]{:S(2)}) collective-permute-start(f32[8,2688]{1,0:T(8,128)S(1)} %pad_maximum_fusion.2.rest_0_), channel_id=1, source_target_pairs={{0,8},{4,12},{8,0},{12,4},{1,9},{5,13},{9,1},{13,5},{2,10},{6,14},... | collective-permute-start | bytes 258056 | tf_op jit(solution)/shard_map/ppermute | solution.py:230
  18.7 26.1 %collective-permute-start.7 = (f32[8,2688]{1,0:T(8,128)S(1)}, f32[8,2688]{1,0:T(8,128)S(1)}, u32[]{:S(2)}, u32[]{:S(2)}) collective-permute-start(f32[8,2688]{1,0:T(8,128)S(1)} %pad_maximum_fusion.2.rest_0_), channel_id=1, source_target_pairs={{0,12},{4,0},{8,4},{12,8},{1,13},{5,1},{9,5},{13,9},{2,14},{6,2},{... | collective-permute-start | bytes 258056 | tf_op jit(solution)/shard_map/ppermute | solution.py:230
  20.7 2.2 copy-start.1
  22.9 15.8 %copy-start.11 = (s32[4]{0:T(128)S(1)}, s32[4]{0:T(128)}, u32[]{:S(2)}) copy-start(s32[4]{0:T(128)} %lengths_ref.1) | copy-start | bytes 52
  25.7 53.2 %collective-permute-start.13 = (bf16[2048,128]{1,0:T(8,128)(2,1)}, bf16[2048,128]{1,0:T(8,128)(2,1)S(1)}, u32[]{:S(2)}, u32[]{:S(2)}) collective-permute-start(bf16[2048,128]{1,0:T(8,128)(2,1)} %bitcast.32), channel_id=1, source_target_pairs={{0,4},{1,5},{4,8},{5,9},{8,12},{9,13},{12,0},{13,1},{2,6},{3,7},{6... | collective-permute-start | bytes 1572872 | tf_op jit(solution)/shard_map/ppermute | solution.py:223
  26.4 56.5 %collective-permute-start.14 = (bf16[2048,128]{1,0:T(8,128)(2,1)}, bf16[2048,128]{1,0:T(8,128)(2,1)}, u32[]{:S(2)}, u32[]{:S(2)}) collective-permute-start(bf16[2048,128]{1,0:T(8,128)(2,1)} %bitcast.33), channel_id=1, source_target_pairs={{0,5},{1,4},{4,9},{5,8},{8,13},{9,12},{12,1},{13,0},{2,7},{3,6},{6... | collective-permute-start | bytes 1572872 | tf_op jit(solution)/shard_map/ppermute | solution.py:223
  26.5 2.2 copy-start.2
  31.4 0.8 copy-start.9
  32.2 2.2 copy-start.5
  37.1 1.7 copy-start.18
  38.7 29.6 %copy-start.12 = (bf16[1024,2,128]{2,1,0:T(2,128)(2,1)}, bf16[1024,2,128]{2,1,0:T(2,128)(2,1)S(1)}, u32[]{:S(2)}) copy-start(bf16[1024,2,128]{2,1,0:T(2,128)(2,1)S(1)} %get-tuple-element.28) | copy-start | bytes 1572868
  38.8 2.4 copy-start.6
  42.8 0.8 copy-start.14
  43.6 0.8 copy-start.16
  47.2 2.2 copy-start.7
  56.0 1.3 collective-permute-start.8
  57.9 19.4 %collective-permute-start.18 = (f32[130,128]{1,0:T(8,128)S(1)}, f32[130,128]{1,0:T(8,128)S(1)}, u32[]{:S(2)}, u32[]{:S(2)}) collective-permute-start(f32[130,128]{1,0:T(8,128)S(1)} %get-tuple-element.74.rest_0_), channel_id=1, source_target_pairs={{0,4},{4,8},{8,12},{12,0},{1,5},{5,9},{9,13},{13,1},{2,6},{6,10},{... | collective-permute-start | bytes 199688 | tf_op jit(solution)/shard_map/ppermute | solution.py:230
  58.6 18.7 %collective-permute-start.19 = (f32[130,128]{1,0:T(8,128)S(1)}, f32[130,128]{1,0:T(8,128)S(1)}, u32[]{:S(2)}, u32[]{:S(2)}) collective-permute-start(f32[130,128]{1,0:T(8,128)S(1)} %get-tuple-element.74.rest_0_), channel_id=1, source_target_pairs={{0,8},{4,12},{8,0},{12,4},{1,9},{5,13},{9,1},{13,5},{2,10},{6,14},... | collective-permute-start | bytes 199688 | tf_op jit(solution)/shard_map/ppermute | solution.py:230
  62.0 15.3 %collective-permute-start.20 = (f32[130,128]{1,0:T(8,128)S(1)}, f32[130,128]{1,0:T(8,128)S(1)}, u32[]{:S(2)}, u32[]{:S(2)}) collective-permute-start(f32[130,128]{1,0:T(8,128)S(1)} %get-tuple-element.74.rest_0_), channel_id=1, source_target_pairs={{0,12},{4,0},{8,4},{12,8},{1,13},{5,1},{9,5},{13,9},{2,14},{6,2},{... | collective-permute-start | bytes 199688 | tf_op jit(solution)/shard_map/ppermute | solution.py:230
  64.4 2.2 copy-start.3
  66.6 7.4 %copy-start.8 = (bf16[4,1024,4,128]{3,2,1,0:T(4,128)(2,1)S(1)}, bf16[4,1024,4,128]{3,2,1,0:T(4,128)(2,1)}, u32[]{:S(2)}) copy-start(bf16[4,1024,4,128]{3,2,1,0:T(4,128)(2,1)} %in_ref.11) | copy-start | bytes 12582916
  68.4 0.8 copy-start.23
  69.2 0.8 copy-start.24
  70.0 2.2 copy-start.4
  73.9 3.4 %copy-start.25 = (bf16[1024,2,128]{2,1,0:T(2,128)(2,1)}, bf16[1024,2,128]{2,1,0:T(2,128)(2,1)S(1)}, u32[]{:S(2)}) copy-start(bf16[1024,2,128]{2,1,0:T(2,128)(2,1)S(1)} %get-tuple-element.41) | copy-start | bytes 1572868
  73.9 3.4 %copy-start.26 = (bf16[1024,2,128]{2,1,0:T(2,128)(2,1)}, bf16[1024,2,128]{2,1,0:T(2,128)(2,1)S(1)}, u32[]{:S(2)}) copy-start(bf16[1024,2,128]{2,1,0:T(2,128)(2,1)S(1)} %get-tuple-element.40) | copy-start | bytes 1572868
  75.7 0.8 copy-start.19
  76.5 0.8 copy-start.21
  77.3 7.0 %collective-permute-start.15 = (bf16[2048,128]{1,0:T(8,128)(2,1)}, bf16[2048,128]{1,0:T(8,128)(2,1)}, u32[]{:S(2)}, u32[]{:S(2)}) collective-permute-start(bf16[2048,128]{1,0:T(8,128)(2,1)} %bitcast.35), channel_id=1, source_target_pairs={{0,1},{1,0},{4,5},{5,4},{8,9},{9,8},{12,13},{13,12},{2,3},{3,2},{6... | collective-permute-start | bytes 1572872 | tf_op jit(solution)/shard_map/ppermute | solution.py:223
  77.3 17.0 %collective-permute-start.2 = (bf16[2048,128]{1,0:T(8,128)(2,1)}, bf16[2048,128]{1,0:T(8,128)(2,1)S(1)}, u32[]{:S(2)}, u32[]{:S(2)}) collective-permute-start(bf16[2048,128]{1,0:T(8,128)(2,1)} %bitcast.13), channel_id=1, source_target_pairs={{0,4},{1,5},{4,8},{5,9},{8,12},{9,13},{12,0},{13,1},{2,6},{3,7},{6... | collective-permute-start | bytes 1572872 | tf_op jit(solution)/shard_map/ppermute | solution.py:223
  77.4 27.4 %collective-permute-start.3 = (bf16[2048,128]{1,0:T(8,128)(2,1)}, bf16[2048,128]{1,0:T(8,128)(2,1)S(1)}, u32[]{:S(2)}, u32[]{:S(2)}) collective-permute-start(bf16[2048,128]{1,0:T(8,128)(2,1)} %bitcast.86), channel_id=1, source_target_pairs={{0,5},{1,4},{4,9},{5,8},{8,13},{9,12},{12,1},{13,0},{2,7},{3,6},{6... | collective-permute-start | bytes 1572872 | tf_op jit(solution)/shard_map/ppermute | solution.py:223
  78.9 25.9 %copy-start.13 = (bf16[1024,2,128]{2,1,0:T(2,128)(2,1)S(1)}, bf16[1024,2,128]{2,1,0:T(2,128)(2,1)}, u32[]{:S(2)}) copy-start(bf16[1024,2,128]{2,1,0:T(2,128)(2,1)} %copy-done.12) | copy-start | bytes 1572868
  78.9 37.3 %copy-start.17 = (bf16[1024,2,128]{2,1,0:T(2,128)(2,1)S(1)}, bf16[1024,2,128]{2,1,0:T(2,128)(2,1)}, u32[]{:S(2)}) copy-start(bf16[1024,2,128]{2,1,0:T(2,128)(2,1)} %copy-done.16) | copy-start | bytes 1572868
  78.9 48.1 %copy-start.15 = (bf16[1024,2,128]{2,1,0:T(2,128)(2,1)S(1)}, bf16[1024,2,128]{2,1,0:T(2,128)(2,1)}, u32[]{:S(2)}) copy-start(bf16[1024,2,128]{2,1,0:T(2,128)(2,1)} %copy-done.14) | copy-start | bytes 1572868
  78.9 104.7 %copy-start.22 = (bf16[1024,2,128]{2,1,0:T(2,128)(2,1)S(1)}, bf16[1024,2,128]{2,1,0:T(2,128)(2,1)}, u32[]{:S(2)}) copy-start(bf16[1024,2,128]{2,1,0:T(2,128)(2,1)} %copy-done.21) | copy-start | bytes 1572868
  79.0 115.9 %copy-start.20 = (bf16[1024,2,128]{2,1,0:T(2,128)(2,1)S(1)}, bf16[1024,2,128]{2,1,0:T(2,128)(2,1)}, u32[]{:S(2)}) copy-start(bf16[1024,2,128]{2,1,0:T(2,128)(2,1)} %copy-done.19) | copy-start | bytes 1572868
  79.0 126.5 %copy-start.10 = (bf16[1024,2,128]{2,1,0:T(2,128)(2,1)S(1)}, bf16[1024,2,128]{2,1,0:T(2,128)(2,1)}, u32[]{:S(2)}) copy-start(bf16[1024,2,128]{2,1,0:T(2,128)(2,1)} %copy-done.9) | copy-start | bytes 1572868
  79.0 37.2 %collective-permute-start.16 = (bf16[2048,128]{1,0:T(8,128)(2,1)}, bf16[2048,128]{1,0:T(8,128)(2,1)S(1)}, u32[]{:S(2)}, u32[]{:S(2)}) collective-permute-start(bf16[2048,128]{1,0:T(8,128)(2,1)} %bitcast.92), channel_id=1, source_target_pairs={{0,12},{1,13},{4,0},{5,1},{8,4},{9,5},{12,8},{13,9},{2,14},{3,15},... | collective-permute-start | bytes 1572872 | tf_op jit(solution)/shard_map/ppermute | solution.py:223
  82.9 44.1 %collective-permute-start.17 = (bf16[2048,128]{1,0:T(8,128)(2,1)}, bf16[2048,128]{1,0:T(8,128)(2,1)S(1)}, u32[]{:S(2)}, u32[]{:S(2)}) collective-permute-start(bf16[2048,128]{1,0:T(8,128)(2,1)} %bitcast.91), channel_id=1, source_target_pairs={{0,13},{1,12},{4,1},{5,0},{8,5},{9,4},{12,9},{13,8},{2,15},{3,14},... | collective-permute-start | bytes 1572872 | tf_op jit(solution)/shard_map/ppermute | solution.py:223
  84.3 99.3 %collective-permute-start.11 = (bf16[2048,128]{1,0:T(8,128)(2,1)}, bf16[2048,128]{1,0:T(8,128)(2,1)S(1)}, u32[]{:S(2)}, u32[]{:S(2)}) collective-permute-start(bf16[2048,128]{1,0:T(8,128)(2,1)} %bitcast.90), channel_id=1, source_target_pairs={{0,8},{1,9},{4,12},{5,13},{8,0},{9,1},{12,4},{13,5},{2,10},{3,11},... | collective-permute-start | bytes 1572872 | tf_op jit(solution)/shard_map/ppermute | solution.py:223
  94.3 100.6 %collective-permute-start.12 = (bf16[2048,128]{1,0:T(8,128)(2,1)}, bf16[2048,128]{1,0:T(8,128)(2,1)S(1)}, u32[]{:S(2)}, u32[]{:S(2)}) collective-permute-start(bf16[2048,128]{1,0:T(8,128)(2,1)} %bitcast.89), channel_id=1, source_target_pairs={{0,9},{1,8},{4,13},{5,12},{8,1},{9,0},{12,5},{13,4},{2,11},{3,10},... | collective-permute-start | bytes 1572872 | tf_op jit(solution)/shard_map/ppermute | solution.py:223
  104.8 105.5 %collective-permute-start.4 = (bf16[2048,128]{1,0:T(8,128)(2,1)S(1)}, bf16[2048,128]{1,0:T(8,128)(2,1)S(1)}, u32[]{:S(2)}, u32[]{:S(2)}) collective-permute-start(bf16[2048,128]{1,0:T(8,128)(2,1)S(1)} %bitcast.83), channel_id=1, source_target_pairs={{0,1},{1,0},{4,5},{5,4},{8,9},{9,8},{12,13},{13,12},{2,3},{3,2},{6... | collective-permute-start | bytes 1572872 | tf_op jit(solution)/shard_map/ppermute | solution.py:223
  116.2 94.1 %collective-permute-start = (bf16[2048,128]{1,0:T(8,128)(2,1)S(1)}, bf16[2048,128]{1,0:T(8,128)(2,1)S(1)}, u32[]{:S(2)}, u32[]{:S(2)}) collective-permute-start(bf16[2048,128]{1,0:T(8,128)(2,1)S(1)} %bitcast.85), channel_id=1, source_target_pairs={{0,8},{1,9},{4,12},{5,13},{8,0},{9,1},{12,4},{13,5},{2,10},{3,11},... | collective-permute-start | bytes 1572872 | tf_op jit(solution)/shard_map/ppermute | solution.py:223
  127.0 90.4 %collective-permute-start.1 = (bf16[2048,128]{1,0:T(8,128)(2,1)S(1)}, bf16[2048,128]{1,0:T(8,128)(2,1)S(1)}, u32[]{:S(2)}, u32[]{:S(2)}) collective-permute-start(bf16[2048,128]{1,0:T(8,128)(2,1)S(1)} %bitcast.84), channel_id=1, source_target_pairs={{0,9},{1,8},{4,13},{5,12},{8,1},{9,0},{12,5},{13,4},{2,11},{3,10},... | collective-permute-start | bytes 1572872 | tf_op jit(solution)/shard_map/ppermute | solution.py:223
  183.6 44.9 %collective-permute-start.10 = (bf16[2048,128]{1,0:T(8,128)(2,1)S(1)}, bf16[2048,128]{1,0:T(8,128)(2,1)S(1)}, u32[]{:S(2)}, u32[]{:S(2)}) collective-permute-start(bf16[2048,128]{1,0:T(8,128)(2,1)S(1)} %bitcast.88), channel_id=1, source_target_pairs={{0,13},{1,12},{4,1},{5,0},{8,5},{9,4},{12,9},{13,8},{2,15},{3,14},... | collective-permute-start | bytes 1572872 | tf_op jit(solution)/shard_map/ppermute | solution.py:223
  194.9 44.9 %collective-permute-start.9 = (bf16[2048,128]{1,0:T(8,128)(2,1)S(1)}, bf16[2048,128]{1,0:T(8,128)(2,1)S(1)}, u32[]{:S(2)}, u32[]{:S(2)}) collective-permute-start(bf16[2048,128]{1,0:T(8,128)(2,1)S(1)} %bitcast.87), channel_id=1, source_target_pairs={{0,12},{1,13},{4,0},{5,1},{8,4},{9,5},{12,8},{13,9},{2,14},{3,15},... | collective-permute-start | bytes 1572872 | tf_op jit(solution)/shard_map/ppermute | solution.py:223

commit v3 on v2

--- a/solution.py
+++ b/solution.py
@@ -29,93 +29,137 @@
     )
 
 
-def arrange(cache, request, core, core_count, after):
-    _, shard_length, heads, head_dim = cache.shape
+def arrange(caches, request, core, after):
+    _, shard_length, heads, head_dim = caches[0].shape
+    core_count = 2
     heads_decode = heads // core_count
     steps = 4
     places = shard_length // steps
-    block = jax.ShapeDtypeStruct((shard_length, heads_decode, head_dim), cache.dtype)
-
-    def kernel(request_ref, core_ref, in_ref, *rest):
-        out_refs = rest[len(after) :]
-        for own in range(core_count):
-
-            @pl.when(core_ref[0] == own)
-            def _():
-                for f, out_ref in enumerate(out_refs):
-                    low = (own + f) % core_count * heads_decode
-                    out_ref[...] = in_ref[0, :, low : low + heads_decode, :]
+    count = len(caches)
+    pieces = [(w, i) for i in range(steps) for w in range(count)]
+
+    def kernel(where_ref, *refs):
+        in_refs = refs[:count]
+        out_ref, taken, made, in_sems, out_sems = refs[count + len(after) :]
+        rows = lambda i: pl.ds(i * places, places)
+        into = [
+            pltpu.make_async_copy(
+                in_refs[w].at[where_ref[0], rows(i)], taken.at[w, rows(i)], in_sems.at[w, i]
+            )
+            for w, i in pieces
+        ]
+        out_of = [
+            pltpu.make_async_copy(
+                made.at[w, rows(i)], out_ref.at[w, rows(i)], out_sems.at[w, i]
+            )
+            for w, i in pieces
+        ]
+        for copy in into:
+            copy.start()
+        for p, (w, i) in enumerate(pieces):
+            into[p].wait()
+            for own in range(core_count):
+
+                @pl.when(where_ref[1] == own)
+                def _():
+                    low = own * heads_decode
+                    made[w, rows(i)] = taken[w, rows(i), low : low + heads_decode, :]
+
+            out_of[p].start()
+        for copy in out_of:
+            copy.wait()
 
     blocks = pl.pallas_call(
         kernel,
-        out_shape=(block,) * core_count,
-        grid_spec=pltpu.PrefetchScalarGridSpec(
-            num_scalar_prefetch=2,
-            grid=(steps,),
-            in_specs=[
-                pl.BlockSpec((1, places, heads, head_dim), lambda i, r, c: (r[0], i, 0, 0))
-            ]
-            + [pl.BlockSpec(memory_space=pl.ANY)] * len(after),
-            out_specs=(pl.BlockSpec((places, heads_decode, head_dim), lambda i, r, c: (i, 0, 0)),)
-            * core_count,
+        out_shape=jax.ShapeDtypeStruct(
+            (count, shard_length, heads_decode, head_dim), caches[0].dtype
         ),
+        in_specs=[pl.BlockSpec(memory_space=pltpu.SMEM)]
+        + [pl.BlockSpec(memory_space=pltpu.HBM)] * count
+        + [pl.BlockSpec(memory_space=pl.ANY)] * len(after),
+        out_specs=pl.BlockSpec(memory_space=pltpu.HBM),
+        scratch_shapes=[
+            pltpu.VMEM((count, shard_length, heads, head_dim), caches[0].dtype),
+            pltpu.VMEM((count, shard_length, heads_decode, head_dim), caches[0].dtype),
+            pltpu.SemaphoreType.DMA((count, steps)),
+            pltpu.SemaphoreType.DMA((count, steps)),
+        ],
         compiler_params=pltpu.CompilerParams(vmem_limit_bytes=VMEM_BYTES),
         cost_estimate=pl.CostEstimate(
             flops=0,
             transcendentals=0,
-            bytes_accessed=4 * shard_length * heads * head_dim,
+            bytes_accessed=3 * count * shard_length * heads * head_dim,
         ),
         name="arrange",
-    )(request, core, cache, *after)
-    return [x.reshape(shard_length * heads_decode, head_dim) for x in blocks]
-
-
-def assemble(blocks, places, rows, filled=None):
-    block_rows, head_dim = blocks[0].shape
+    )(jnp.concatenate([request, core]), *caches, *after)
+    return blocks.reshape(count, shard_length * heads_decode, head_dim)
+
+
+def assemble(blocks, places, rows, filled=()):
+    arrays, block_rows, head_dim = blocks[0].shape
     count = len(blocks)
-    extra = [] if filled is None else [filled]
+    pieces = [(i, w) for i in range(count) for w in range(arrays)]
 
     def kernel(places_ref, *refs):
         in_refs = refs[:count]
-        out_ref, held, in_sems, out_sems = refs[count + len(extra) :]
+        out_refs = refs[count + len(filled) :][:arrays]
+        held, in_sems, out_sems = refs[count + len(filled) + arrays :]
         into = [
-            pltpu.make_async_copy(in_refs[i], held.at[i], in_sems.at[i]) for i in range(count)
+            pltpu.make_async_copy(in_refs[i].at[w], held.at[i, w], in_sems.at[i, w])
+            for i, w in pieces
         ]
         out_of = [
             pltpu.make_async_copy(
-                held.at[i],
-                out_ref.at[pl.ds(pl.multiple_of(places_ref[i], block_rows), block_rows)],
-                out_sems.at[i],
+                held.at[i, w],
+                out_refs[w].at[pl.ds(pl.multiple_of(places_ref[i], block_rows), block_rows)],
+                out_sems.at[i, w],
             )
-            for i in range(count)
+            for i, w in pieces
         ]
         for copy in into:
             copy.start()
-        for i in range(count):
-            into[i].wait()
-            out_of[i].start()
+        for p in range(len(pieces)):
+            into[p].wait()
+            out_of[p].start()
         for copy in out_of:
             copy.wait()
 
     return pl.pallas_call(
         kernel,
-        out_shape=jax.ShapeDtypeStruct((rows, head_dim), blocks[0].dtype),
+        out_shape=(jax.ShapeDtypeStruct((rows, head_dim), blocks[0].dtype),) * arrays,
         in_specs=[pl.BlockSpec(memory_space=pltpu.SMEM)]
         + [pl.BlockSpec(memory_space=pl.ANY)] * count
-        + [pl.BlockSpec(memory_space=pltpu.HBM)] * len(extra),
-        out_specs=pl.BlockSpec(memory_space=pltpu.HBM),
+        + [pl.BlockSpec(memory_space=pltpu.HBM)] * len(filled),
+        out_specs=(pl.BlockSpec(memory_space=pltpu.HBM),) * arrays,
         scratch_shapes=[
-            pltpu.VMEM((count, block_rows, head_dim), blocks[0].dtype),
-            pltpu.SemaphoreType.DMA((count,)),
-            pltpu.SemaphoreType.DMA((count,)),
+            pltpu.VMEM((count, arrays, block_rows, head_dim), blocks[0].dtype),
+            pltpu.SemaphoreType.DMA((count, arrays)),
+            pltpu.SemaphoreType.DMA((count, arrays)),
         ],
-        input_output_aliases={1 + count: 0} if extra else {},
+        input_output_aliases={1 + count + w: w for w in range(len(filled))},
         compiler_params=pltpu.CompilerParams(vmem_limit_bytes=VMEM_BYTES),
         cost_estimate=pl.CostEstimate(
-            flops=0, transcendentals=0, bytes_accessed=4 * count * block_rows * head_dim
+            flops=0,
+            transcendentals=0,
+            bytes_accessed=4 * count * arrays * block_rows * head_dim,
         ),
         name="assemble",
-    )(places, *blocks, *extra)
+    )(places, *blocks, *filled)
+
+
+def pair_tokens(first, second, after):
+    def kernel(first_ref, second_ref, after_ref, out_ref):
+        out_ref[0] = first_ref[...]
+        out_ref[1] = second_ref[...]
+
+    whole = pl.BlockSpec(memory_space=pltpu.VMEM)
+    return pl.pallas_call(
+        kernel,
+        out_shape=jax.ShapeDtypeStruct((2,) + first.shape, first.dtype),
+        in_specs=[whole, whole, pl.BlockSpec(memory_space=pl.ANY)],
+        out_specs=whole,
+        name="pair_tokens",
+    )(first, second, after)
 
 
 def attend_shard(queries, keys, values, lengths, first_place, score_factor):
@@ -188,15 +232,14 @@
     ctx_count = lax.axis_size("ctx")
     sub_count = lax.axis_size("sub")
     requests, shard_length, heads, head_dim = key_cache.shape
-    assert requests == ctx_count
+    assert requests == ctx_count and sub_count == 2
     heads_decode = heads // sub_count
     ctx_index = lax.axis_index("ctx")
     sub_index = lax.axis_index("sub")
     take = functools.partial(jnp.take, mode="clip")
 
     device_rows = shard_length * heads_decode
-    core = jnp.reshape(sub_index, (1,)).astype(jnp.int32)
-    received = ({}, {})
+    received = {}
 
     def place_of(shift, flip):
         source = lax.rem(ctx_index - shift + ctx_count, ctx_count) * sub_count + lax.rem(
@@ -204,24 +247,23 @@
         )
         return source * device_rows
 
-    def hand_off(which, shift, after=()):
+    def hand_off(shift, flip, after=()):
         owner = lax.rem(ctx_index + shift, ctx_count)
         request = lax.dynamic_slice_in_dim(owner_order, owner, 1)
-        blocks = arrange(
-            (key_cache, value_cache)[which], request, core, sub_count, after
-        )
-        for flip, block in enumerate(blocks):
-            if shift or flip:
-                pairs = [
-                    (
-                        c * sub_count + s,
-                        (c + shift) % ctx_count * sub_count + (s + flip) % sub_count,
-                    )
-                    for c in range(ctx_count)
-                    for s in range(sub_count)
-                ]
-                block = lax.ppermute(block, ("ctx", "sub"), pairs)
-            received[which][shift, flip] = block
+        core = jnp.reshape(lax.rem(sub_index + flip, sub_count), (1,)).astype(jnp.int32)
+        block = made = arrange((key_cache, value_cache), request, core, after)
+        if shift or flip:
+            pairs = [
+                (
+                    c * sub_count + s,
+                    (c + shift) % ctx_count * sub_count + (s + flip) % sub_count,
+                )
+                for c in range(ctx_count)
+                for s in range(sub_count)
+            ]
+            block = lax.ppermute(made, ("ctx", "sub"), pairs)
+        received[shift, flip] = block
+        return made
 
     def sum_shifted(values, combine):
         return combine(
@@ -235,7 +277,7 @@
         )
 
     middle = ctx_count // 2
-    hand_off(0, middle)
+    leading = hand_off(middle, 0)
 
     query_width = w_query.shape[1]
     key_width = w_key.shape[1]
@@ -243,7 +285,7 @@
     score_factor = head_dim ** (-0.5)
     rows_local = first_tokens.shape[0]
     tokens = lax.all_gather(
-        jnp.stack([first_tokens, second_tokens]), ("head", "sub"), axis=1, tiled=True
+        pair_tokens(first_tokens, second_tokens, leading), ("head", "sub"), axis=1, tiled=True
     )
     wide = tokens.astype(jnp.float32).reshape(2 * requests, -1)
     gained = wide * norm_gain.astype(jnp.float32)
@@ -266,10 +308,9 @@
         axis=1,
     )
     summed = sum_shifted(partial, lambda parts: functools.reduce(jnp.add, parts))
-    for which in (0, 1):
-        for shift in range(1, middle):
-            hand_off(which, shift, (partial,))
-        hand_off(which, 0, (partial,))
+    hand_off(middle, 1, (partial,))
+    hand_off(0, 1, (summed,))
+    hand_off(0, 0, (summed,))
     raw = summed[:, :-LANES] * lax.rsqrt(summed[:, -LANES:][:, :1] / width + eps_norm)
     raw = raw.reshape(2, requests, -1, head_dim)
     positions = lengths.astype(jnp.float32)[None, :] + jnp.arange(2, dtype=jnp.float32)[:, None]
@@ -332,10 +373,16 @@
     stats = send_form(*kept)
     gathered = unpack(sum_shifted(stats, jnp.stack))
     sums, maxima, totals = merge(*gathered)
-    for which in (0, 1):
-        for shift in range(middle + 1, ctx_count):
-            hand_off(which, shift, (stats,))
-    hand_off(1, middle, (stats,))
+    queue = [
+        (shift, flip)
+        for shift in range(1, ctx_count)
+        for flip in range(sub_count)
+        if shift != middle
+    ]
+    ahead = [(middle, 0), (middle, 1)]
+    hand_off(*queue[0], (stats,))
+    for key, earlier in zip(queue[1:], ahead + queue):
+        hand_off(*key, (stats, received[earlier]))
 
     grouped = own_queries.reshape(requests, heads_decode, 2, group_size, head_dim).astype(
         jnp.float32
@@ -373,21 +420,19 @@
     residual = take(tokens, own_ids, axis=1).astype(jnp.float32)
     result = (residual + jnp.sum(parts, axis=0)).astype(jnp.bfloat16)
 
-    def outcome(which, last):
-        early = [key for key in received[which] if key not in last]
-        whole = None
-        for keys in (early, last):
-            if keys:
-                whole = assemble(
-                    [received[which][key] for key in keys],
-                    jnp.stack([place_of(*key) for key in keys]).astype(jnp.int32),
-                    ctx_count * sub_count * device_rows,
-                    whole,
-                )
-        return whole.reshape(1, -1, heads_decode, head_dim)
-
-    moved_keys = outcome(0, [])
-    moved_values = outcome(1, [(middle, flip) for flip in range(sub_count)])
+    moved = ()
+    for keys in (
+        [(0, 0), (0, 1)] + ahead,
+        queue[:-2],
+        queue[-2:],
+    ):
+        moved = assemble(
+            [received[key] for key in keys],
+            jnp.stack([place_of(*key) for key in keys]).astype(jnp.int32),
+            ctx_count * sub_count * device_rows,
+            moved,
+        )
+    moved_keys, moved_values = (x.reshape(1, -1, heads_decode, head_dim) for x in moved)
     return (moved_keys, moved_values, result[0], result[1])
 
 

time: 243 us -> 227 us (0.934)
  waiting for transfers between devices: 128 us -> 61.4 us
  starting transfers between devices: 30.6 us -> 53.2 us
  Pallas kernels: 30.9 us -> 45.1 us
  other arithmetic: 4.13 us -> 17.6 us
  local copies, waits for them, and re-layouts: 24.4 us -> 21.4 us
    ppermute x14 -> x7, waiting for transfers between devices: 127 us -> 49.5 us  [hand_off(): block = lax.ppermute(made, ('ctx', 'sub'), pairs)]
    ppermute x6, starting transfers between devices: 12.4 us -> 47.3 us  [sum_shifted(): lax.ppermute(values, 'ctx', [(c, (c + shift) % ctx_count) for c in range(...]
    pallas_call x11 -> x12, Pallas kernels: 24.6 us -> 38.8 us  [the longest x8 28.7 us: arrange(): pl.pallas_call(kernel, out_shape=jax.ShapeDtypeStruct((count, shard_lengt...]
    ppermute x14 -> x7, starting transfers between devices: 18 us -> 5.49 us  [hand_off(): block = lax.ppermute(made, ('ctx', 'sub'), pairs)]
    ppermute x6, waiting for transfers between devices: 0.02 us -> 11.9 us  [sum_shifted(): lax.ppermute(values, 'ctx', [(c, (c + shift) % ctx_count) for c in range(...]
    unnamed x58 -> x26, local copies, waits for them, and re-layouts: 21.1 us -> 12 us
    concatenate x0 -> x6, other arithmetic: none -> 4.13 us  [arrange(): jnp.concatenate([request, core])]
  transfers between devices with their start and end apart: 21 -> 14, of which waited for: 9 -> 5; matrix products, arithmetic and copies ran while one was open for 4% -> 13% of each run, Pallas kernels for 12% -> 17%
where the time goes in v3:
time: 227 us; the launch traced here: 226 us
  waiting for transfers between devices  61.4 us (27%)
  starting transfers between devices  53.2 us (23%)
  Pallas kernels  45.1 us (20%)
  local copies, waits for them, and re-layouts  21.4 us (9%)
  other arithmetic  17.6 us (8%)
  blocking collectives  16 us (7%)
  matrix products  9.87 us (4%)
    ppermute x7, waiting for transfers between devices, hand_off(): block = lax.ppermute(made, ('ctx', 'sub'), pairs)  49.5 us
    ppermute x6, starting transfers between devices, sum_shifted(): lax.ppermute(values, 'ctx', [(c, (c + shift) % ctx_count) for c in range(...  47.3 us
    pallas_call x8, Pallas kernels, arrange(): pl.pallas_call(kernel, out_shape=jax.ShapeDtypeStruct((count, shard_lengt...  28.7 us
    unnamed x26, local copies, waits for them, and re-layouts  12 us
    ppermute x6, waiting for transfers between devices, sum_shifted(): lax.ppermute(values, 'ctx', [(c, (c + shift) % ctx_count) for c in range(...  11.9 us
    pallas_call x3, Pallas kernels, assemble(): pl.pallas_call(kernel, out_shape=(jax.ShapeDtypeStruct((rows, head_dim),...  8.85 us
    all_gather x1, blocking collectives, local(): parts = lax.all_gather(branch, ('head', 'sub'), axis=0)  6.68 us
    pallas_call x1, Pallas kernels, attend_shard(): pl.pallas_call(kernel, out_shape=(result, result, result), grid_spec=pltp...  6.29 us
  transfers between devices with their start and end apart: 14, of which 5 were waited for; matrix products, arithmetic and copies ran while one was open for 13% of the time, Pallas kernels for 17%

profile of v3, /device:TPU:0, one launch (start us, length us, event | category | flops | bytes accessed | tf_op | source)
XLA Modules:
  0.0 225.8 jit_solution(7868633123346541629)
XLA Ops:
  0.7 1.5 fusion.26
  2.2 0.7 pad_add_fusion.5
  2.9 2.2 copy-done.1
  5.1 3.0 %arrange.8 = bf16[2,1024,2,128]{3,2,1,0:T(2,128)(2,1)} custom-call(s32[2]{0:T(128)S(1)} %get-tuple-element.69.where_ref, bf16[4,1024,4,128]{3,2,1,0:T(4,128)(2,1)S(1)} %copy-done.1, bf16[4,1024,4,128]{3,2,1,0:T(4,128)(2,1)} %refs_1_.15), custom_call_target="tpu_custom_call" | custom-call | bytes 3145728 | tf_op jit(solution)/shard_map/arrange/pallas_call | solution.py:72
  8.1 1.3 pair_tokens.1
  9.4 0.7 copy.47
  10.2 6.2 %all_gather.9 = bf16[2,4,2048]{2,0,1:T(2,128)(2,1)S(1)} all-gather(bf16[2,1,2048]{2,0,1:T(2,128)(2,1)S(1)} %copy.47), channel_id=1, replica_groups=mesh['groups'=2,'ctx'=4,'head'=2,'sub'=2] {'head','sub'}, dimensions={1}, use_global_device_ids=true | all-gather | bytes 40960 | tf_op jit(solution)/shard_map/all_gather | solution.py:287
  16.6 4.7 %fusion.9 = f32[16,2048]{1,0:T(8,128)S(1)} fusion(bf16[2048,2048]{1,0:T(8,128)(2,1)} %param.18, bf16[8,2048]{1,0:T(8,128)(2,1)S(1)} %get-tuple-element.50, bf16[8,2048]{1,0:T(8,128)(2,1)S(1)} %get-tuple-element.49), kind=kOutput, calls=%fused_computation.38 | convolution fusion | flops 134348800 | bytes 8585216 | tf_op jit(solution)/shard_map/dot_general | solution.py:297
  22.1 2.0 collective-permute-start
  24.1 2.6 %collective-permute-start.1 = (f32[8,2688]{1,0:T(8,128)S(1)}, f32[8,2688]{1,0:T(8,128)}, u32[]{:S(2)}, u32[]{:S(2)}) collective-permute-start(f32[8,2688]{1,0:T(8,128)S(1)} %pad_maximum_fusion.2.refs_2_), channel_id=1, source_target_pairs={{0,8},{4,12},{8,0},{12,4},{1,9},{5,13},{9,1},{13,5},{2,10},{6,14},... | collective-permute-start | bytes 258056 | tf_op jit(solution)/shard_map/ppermute | solution.py:272
  26.7 1.3 collective-permute-start.2
  28.3 2.2 copy-done.2
  30.4 3.3 %arrange.9 = bf16[2,1024,2,128]{3,2,1,0:T(2,128)(2,1)} custom-call(s32[2]{0:T(128)S(1)} %get-tuple-element.68.where_ref, bf16[4,1024,4,128]{3,2,1,0:T(4,128)(2,1)S(1)} %copy-done.2, bf16[4,1024,4,128]{3,2,1,0:T(4,128)(2,1)} %refs_1_.15, f32[8,2688]{1,0:T(8,128)S(1)} %pad_maximum_fusion.2.refs_2_), custom_call_target="tpu_custom_call" | custom-call | bytes 3145728 | tf_op jit(solution)/shard_map/arrange/pallas_call | solution.py:72
  33.8 1.3 collective-permute-start.4
  35.6 0.6 pad_clamp_fusion
  36.2 0.7 pad_add_fusion.7.where_ref
  36.9 0.7 pad_add_fusion.8.where_ref
  37.6 0.6 pad_add_fusion.3.where_ref
  38.3 0.6 pad_add_fusion.4.where_ref
  38.9 0.7 pad_add_fusion.9
  40.0 1.0 add_add_fusion.refs_2_
  41.5 3.1 %all_gather.10.q_ref = bf16[4,64,128]{2,1,0:T(8,128)(2,1)S(1)} all-gather(bf16[4,32,128]{2,1,0:T(8,128)(2,1)S(1)} %bitcast.92), channel_id=1, replica_groups=mesh['groups'=2,'ctx'=4,'head'=2,'sub'=2] {'sub'}, dimensions={1}, use_global_device_ids=true | all-gather | bytes 98304 | tf_op jit(solution)/shard_map/all_gather | solution.py:328
  44.6 2.2 copy-done.3
  46.8 6.3 %attend_shard.1 = (f32[4,64,128]{2,1,0:T(8,128)S(1)}, f32[4,64,128]{2,1,0:T(8,128)S(1)}, f32[4,64,128]{2,1,0:T(8,128)S(1)}) custom-call(s32[4]{0:T(128)S(1)} %copy-done.8, s32[1]{0:T(128)} %bitcast.3.place_ref, bf16[4,64,128]{2,1,0:T(8,128)(2,1)S(1)} %all_gather.10.q_ref, bf16[4,4096,128]{2,1,0:T(8,128)(2,1)S(1)} %bitcast.70, bf16[4,4096,128]{2,1,0:T(8,128)(2,1)} %bitcast.75), custom_call_target="tpu_custom_call" | custom-call | flops 536870912 | bytes 8388608 | tf_op jit(solution)/shard_map/attend_shard/pallas_call | solution.py:199
  53.1 0.7 dynamic-slice_bitcast_fusion
  54.2 0.9 pad_maximum_fusion.3
  55.5 0.6 copy.57
  56.1 2.2 copy-done.4
  58.3 3.3 %arrange.15 = bf16[2,1024,2,128]{3,2,1,0:T(2,128)(2,1)} custom-call(s32[2]{0:T(128)S(1)} %get-tuple-element.70.where_ref, bf16[4,1024,4,128]{3,2,1,0:T(4,128)(2,1)S(1)} %copy-done.4, bf16[4,1024,4,128]{3,2,1,0:T(4,128)(2,1)} %refs_1_.15, f32[8,2688]{1,0:T(8,128)S(1)} %add_add_fusion.refs_2_), custom_call_target="tpu_custom_call" | custom-call | bytes 3145728 | tf_op jit(solution)/shard_map/arrange/pallas_call | solution.py:72
  61.6 3.7 %arrange.14 = bf16[2,1024,2,128]{3,2,1,0:T(2,128)(2,1)S(1)} custom-call(s32[2]{0:T(128)S(1)} %get-tuple-element.71.where_ref, bf16[4,1024,4,128]{3,2,1,0:T(4,128)(2,1)S(1)} %copy-done.4, bf16[4,1024,4,128]{3,2,1,0:T(4,128)(2,1)} %refs_1_.15, f32[8,2688]{1,0:T(8,128)S(1)} %add_add_fusion.refs_2_), custom_call_target="tpu_custom_call" | custom-call | bytes 3145728 | tf_op jit(solution)/shard_map/arrange/pallas_call | solution.py:72
  65.4 1.0 copy-done.6
  66.4 0.7 multiply_reduce_fusion.1
  67.1 0.8 slice_reduce_fusion
  68.2 0.9 slice.109
  69.2 39.0 %collective-permute-start.11 = (f32[130,128]{1,0:T(8,128)S(1)}, f32[130,128]{1,0:T(8,128)S(1)}, u32[]{:S(2)}, u32[]{:S(2)}) collective-permute-start(f32[130,128]{1,0:T(8,128)S(1)} %get-tuple-element.54.refs_2_), channel_id=1, source_target_pairs={{0,4},{4,8},{8,12},{12,0},{1,5},{5,9},{9,13},{13,1},{2,6},{6,10},{... | collective-permute-start | bytes 199688 | tf_op jit(solution)/shard_map/ppermute | solution.py:272
  108.2 2.1 collective-permute-start.12
  110.6 1.4 fusion.11
  112.0 2.2 copy-done.5
  114.2 3.0 %arrange.11 = bf16[2,1024,2,128]{3,2,1,0:T(2,128)(2,1)} custom-call(s32[2]{0:T(128)S(1)} %pad_add_fusion.8.where_ref, bf16[4,1024,4,128]{3,2,1,0:T(4,128)(2,1)S(1)} %copy-done.5, bf16[4,1024,4,128]{3,2,1,0:T(4,128)(2,1)} %refs_1_.15, f32[130,128]{1,0:T(8,128)S(1)} %get-tuple-element.54.refs_2_), custom_call_target="tpu_custom_call" | custom-call | bytes 3145728 | tf_op jit(solution)/shard_map/arrange/pallas_call | solution.py:72
  117.4 11.7 %collective-permute-done.12 = f32[130,128]{1,0:T(8,128)S(1)} collective-permute-done((f32[130,128]{1,0:T(8,128)S(1)}, f32[130,128]{1,0:T(8,128)S(1)}, u32[]{:S(2)}, u32[]{:S(2)}) %collective-permute-start.12) | collective-permute-done | bytes 66592 | tf_op jit(solution)/shard_map/ppermute | solution.py:272
  130.1 1.3 reshape.294
  131.4 1.2 fusion.17
  132.6 1.4 reshape.295
  134.0 0.7 copy_maximum_fusion
  134.7 0.8 fusion.21
  135.6 0.7 copy_add_fusion
  136.4 0.6 subtract_exponential_fusion.1
  137.1 0.8 multiply_reduce_fusion
  138.0 0.7 gather_fusion
  138.8 4.2 %arrange.13 = bf16[2,1024,2,128]{3,2,1,0:T(2,128)(2,1)S(1)} custom-call(s32[2]{0:T(128)S(1)} %pad_add_fusion.7.where_ref, bf16[4,1024,4,128]{3,2,1,0:T(4,128)(2,1)} %refs_0_.15, bf16[4,1024,4,128]{3,2,1,0:T(4,128)(2,1)} %refs_1_.15, f32[130,128]{1,0:T(8,128)S(1)} %get-tuple-element.54.refs_2_, bf16[2,2048,128]{2,1,0:T(8,128)(2,1)S(1)} %collective-permute-done.8.refs_3_.refs_2_), custom_call_target="tpu_custom_call" | custom-call | bytes 3145728 | tf_op jit(solution)/shard_map/arrange/pallas_call | solution.py:72
  143.0 0.9 collective-permute-start.9
  143.9 3.8 %arrange.10 = bf16[2,1024,2,128]{3,2,1,0:T(2,128)(2,1)S(1)} custom-call(s32[2]{0:T(128)S(1)} %pad_add_fusion.4.where_ref, bf16[4,1024,4,128]{3,2,1,0:T(4,128)(2,1)} %refs_0_.15, bf16[4,1024,4,128]{3,2,1,0:T(4,128)(2,1)} %refs_1_.15, f32[130,128]{1,0:T(8,128)S(1)} %get-tuple-element.54.refs_2_, bf16[2,2048,128]{2,1,0:T(8,128)(2,1)S(1)} %collective-permute-done.4.refs_3_), custom_call_target="tpu_custom_call" | custom-call | bytes 3145728 | tf_op jit(solution)/shard_map/arrange/pallas_call | solution.py:72
  147.7 2.6 %collective-permute-start.5 = (bf16[2,2048,128]{2,1,0:T(8,128)(2,1)S(1)}, bf16[2,2048,128]{2,1,0:T(8,128)(2,1)S(1)}, u32[]{:S(2)}, u32[]{:S(2)}) collective-permute-start(bf16[2,2048,128]{2,1,0:T(8,128)(2,1)S(1)} %bitcast.72), channel_id=1, source_target_pairs={{0,12},{1,13},{4,0},{5,1},{8,4},{9,5},{12,8},{13,9},{2,14},{3,15},... | collective-permute-start | bytes 3145736 | tf_op jit(solution)/shard_map/ppermute | solution.py:264
  150.3 7.1 %collective-permute-done.6.refs_3_.refs_0_ = bf16[2,2048,128]{2,1,0:T(8,128)(2,1)} collective-permute-done((bf16[2,2048,128]{2,1,0:T(8,128)(2,1)}, bf16[2,2048,128]{2,1,0:T(8,128)(2,1)}, u32[]{:S(2)}, u32[]{:S(2)}) %collective-permute-start.6) | collective-permute-done | bytes 1048608 | tf_op jit(solution)/shard_map/ppermute | solution.py:264
  157.5 4.2 %arrange.12 = bf16[2,1024,2,128]{3,2,1,0:T(2,128)(2,1)S(1)} custom-call(s32[2]{0:T(128)S(1)} %pad_add_fusion.3.where_ref, bf16[4,1024,4,128]{3,2,1,0:T(4,128)(2,1)} %refs_0_.15, bf16[4,1024,4,128]{3,2,1,0:T(4,128)(2,1)} %refs_1_.15, f32[130,128]{1,0:T(8,128)S(1)} %get-tuple-element.54.refs_2_, bf16[2,2048,128]{2,1,0:T(8,128)(2,1)} %collective-permute-done.6.refs_3_.refs_0_), custom_call_target="tpu_custom_call" | custom-call | bytes 3145728 | tf_op jit(solution)/shard_map/arrange/pallas_call | solution.py:72
  161.7 4.7 %fusion = f32[2,4,2048]{2,1,0:T(4,128)S(1)} fusion(bf16[2,4,2048]{2,1,0:T(4,128)(2,1)S(1)} %reshape.296, bf16[2048,2048]{1,0:T(8,128)(2,1)} %param.21), kind=kOutput, calls=%fused_computation.1 | convolution fusion | flops 67108864 | bytes 8486912 | tf_op jit(solution)/shard_map/dot_general | solution.py:414
  166.4 6.7 %all-gather = f32[8,4,2048]{2,1,0:T(4,128)S(1)} all-gather(f32[2,4,2048]{2,1,0:T(4,128)S(1)} %fusion), channel_id=2, replica_groups=mesh['groups'=2,'ctx'=4,'head'=2,'sub'=2] {'head','sub'}, dimensions={0}, use_global_device_ids=true | all-gather | bytes 327680 | tf_op jit(solution)/shard_map/all_gather | solution.py:417
  173.2 0.6 fusion.10
  173.9 0.6 slice_bitcast_fusion
  174.5 3.8 %assemble.3 = (bf16[16384,128]{1,0:T(8,128)(2,1)}, bf16[16384,128]{1,0:T(8,128)(2,1)}) custom-call(s32[4]{0:T(128)S(1)} %pad_add_fusion.2.places_ref, bf16[2,2048,128]{2,1,0:T(8,128)(2,1)S(1)} %bitcast.71, bf16[2,2048,128]{2,1,0:T(8,128)(2,1)} %collective-permute-done.10.refs_1_, bf16[2,2048,128]{2,1,0:T(8,128)(2,1)S(1)} %collective-permute-done.8.refs_3_.refs_2_, ...), custom_call_target="tpu_custom_call" | custom-call | bytes 8388608 | tf_op jit(solution)/shard_map/assemble/pallas_call | solution.py:127
  178.3 3.0 %assemble.4 = (bf16[16384,128]{1,0:T(8,128)(2,1)}, bf16[16384,128]{1,0:T(8,128)(2,1)}) custom-call(s32[2]{0:T(128)S(1)} %pad_add_fusion.1.places_ref, bf16[2,2048,128]{2,1,0:T(8,128)(2,1)} %collective-permute-done.6.refs_3_.refs_0_, bf16[2,2048,128]{2,1,0:T(8,128)(2,1)S(1)} %collective-permute-done.9.refs_1_, ...), custom_call_target="tpu_custom_call", output_to_operand_aliasing={{0}: (3, {}), {1}: (4, {})} | custom-call | bytes 4194304 | tf_op jit(solution)/shard_map/assemble/pallas_call | solution.py:127
  181.3 19.8 %collective-permute-done.5.refs_0_ = bf16[2,2048,128]{2,1,0:T(8,128)(2,1)S(1)} collective-permute-done((bf16[2,2048,128]{2,1,0:T(8,128)(2,1)S(1)}, bf16[2,2048,128]{2,1,0:T(8,128)(2,1)S(1)}, u32[]{:S(2)}, u32[]{:S(2)}) %collective-permute-start.5) | collective-permute-done | bytes 1048608 | tf_op jit(solution)/shard_map/ppermute | solution.py:264
  201.1 22.5 %collective-permute-done.7.refs_1_ = bf16[2,2048,128]{2,1,0:T(8,128)(2,1)S(1)} collective-permute-done((bf16[2,2048,128]{2,1,0:T(8,128)(2,1)S(1)}, bf16[2,2048,128]{2,1,0:T(8,128)(2,1)S(1)}, u32[]{:S(2)}, u32[]{:S(2)}) %collective-permute-start.7) | collective-permute-done | bytes 1048608 | tf_op jit(solution)/shard_map/ppermute | solution.py:264
  223.6 2.1 assemble.5
  (88 shorter events, 5.8 us)
Async XLA Ops:
  0.6 20.7 %copy-start = (bf16[2048,256]{1,0:T(8,128)(2,1)S(1)}, bf16[2048,256]{1,0:T(8,128)(2,1)}, u32[]{:S(2)}) copy-start(bf16[2048,256]{1,0:T(8,128)(2,1)} %param.19) | copy-start | bytes 3145732
  0.6 15.9 %copy-start.12 = (bf16[2048]{0:T(1024)(128)(2,1)S(1)}, bf16[2048]{0:T(1024)(128)(2,1)}, u32[]{:S(2)}) copy-start(bf16[2048]{0:T(1024)(128)(2,1)} %param.17) | copy-start | bytes 12292
  2.9 2.2 copy-start.1
  16.6 4.9 %copy-start.9 = (bf16[2048,256]{1,0:T(8,128)(2,1)S(1)}, bf16[2048,256]{1,0:T(8,128)(2,1)}, u32[]{:S(2)}) copy-start(bf16[2048,256]{1,0:T(8,128)(2,1)} %param.20) | copy-start | bytes 3145732
  21.3 14.3 %copy-start.11 = (s32[4]{0:T(128)S(1)}, s32[4]{0:T(128)}, u32[]{:S(2)}) copy-start(s32[4]{0:T(128)} %param.14) | copy-start | bytes 52
  21.3 17.6 %copy-start.8 = (s32[4]{0:T(128)S(1)}, s32[4]{0:T(128)}, u32[]{:S(2)}) copy-start(s32[4]{0:T(128)} %lengths_ref.1) | copy-start | bytes 52
  22.1 17.9 %collective-permute-start = (f32[8,2688]{1,0:T(8,128)S(1)}, f32[8,2688]{1,0:T(8,128)S(1)}, u32[]{:S(2)}, u32[]{:S(2)}) collective-permute-start(f32[8,2688]{1,0:T(8,128)S(1)} %pad_maximum_fusion.2.refs_2_), channel_id=1, source_target_pairs={{0,4},{4,8},{8,12},{12,0},{1,5},{5,9},{9,13},{13,1},{2,6},{6,10},{... | collective-permute-start | bytes 258056 | tf_op jit(solution)/shard_map/ppermute | solution.py:272
  24.1 15.9 %collective-permute-start.1 = (f32[8,2688]{1,0:T(8,128)S(1)}, f32[8,2688]{1,0:T(8,128)}, u32[]{:S(2)}, u32[]{:S(2)}) collective-permute-start(f32[8,2688]{1,0:T(8,128)S(1)} %pad_maximum_fusion.2.refs_2_), channel_id=1, source_target_pairs={{0,8},{4,12},{8,0},{12,4},{1,9},{5,13},{9,1},{13,5},{2,10},{6,14},... | collective-permute-start | bytes 258056 | tf_op jit(solution)/shard_map/ppermute | solution.py:272
  26.7 13.3 %collective-permute-start.2 = (f32[8,2688]{1,0:T(8,128)S(1)}, f32[8,2688]{1,0:T(8,128)}, u32[]{:S(2)}, u32[]{:S(2)}) collective-permute-start(f32[8,2688]{1,0:T(8,128)S(1)} %pad_maximum_fusion.2.refs_2_), channel_id=1, source_target_pairs={{0,12},{4,0},{8,4},{12,8},{1,13},{5,1},{9,5},{13,9},{2,14},{6,2},{... | collective-permute-start | bytes 258056 | tf_op jit(solution)/shard_map/ppermute | solution.py:272
  28.1 110.7 %collective-permute-start.8 = (bf16[2,2048,128]{2,1,0:T(8,128)(2,1)}, bf16[2,2048,128]{2,1,0:T(8,128)(2,1)S(1)}, u32[]{:S(2)}, u32[]{:S(2)}) collective-permute-start(bf16[2,2048,128]{2,1,0:T(8,128)(2,1)} %bitcast.4.after_ref), channel_id=1, source_target_pairs={{0,8},{1,9},{4,12},{5,13},{8,0},{9,1},{12,4},{13,5},{2,10},{3,11},... | collective-permute-start | bytes 3145736 | tf_op jit(solution)/shard_map/ppermute | solution.py:264
  28.3 2.2 copy-start.2
  33.8 110.1 %collective-permute-start.4 = (bf16[2,2048,128]{2,1,0:T(8,128)(2,1)}, bf16[2,2048,128]{2,1,0:T(8,128)(2,1)S(1)}, u32[]{:S(2)}, u32[]{:S(2)}) collective-permute-start(bf16[2,2048,128]{2,1,0:T(8,128)(2,1)} %bitcast.15), channel_id=1, source_target_pairs={{0,9},{1,8},{4,13},{5,12},{8,1},{9,0},{12,5},{13,4},{2,11},{3,10},... | collective-permute-start | bytes 3145736 | tf_op jit(solution)/shard_map/ppermute | solution.py:264
  44.6 2.2 copy-start.3
  55.0 12.1 %collective-permute-start.3 = (f32[130,128]{1,0:T(8,128)S(1)}, f32[130,128]{1,0:T(8,128)}, u32[]{:S(2)}, u32[]{:S(2)}) collective-permute-start(f32[130,128]{1,0:T(8,128)S(1)} %pad_maximum_fusion.3), channel_id=1, source_target_pairs={{0,1},{1,0},{2,3},{3,2},{4,5},{5,4},{6,7},{7,6},{8,9},{9,8},{10,11... | collective-permute-start | bytes 199688 | tf_op jit(solution)/shard_map/ppermute | solution.py:371
  56.1 2.2 copy-start.4
  58.3 10.8 %copy-start.10 = (f32[1,4,32,128]{3,2,1,0:T(8,128)S(1)}, f32[1,4,32,128]{3,2,1,0:T(8,128)}, u32[]{:S(2)}) copy-start(f32[1,4,32,128]{3,2,1,0:T(8,128)} %get-tuple-element.45) | copy-start | bytes 196612
  65.4 1.0 copy-start.6
  69.2 48.0 %collective-permute-start.11 = (f32[130,128]{1,0:T(8,128)S(1)}, f32[130,128]{1,0:T(8,128)S(1)}, u32[]{:S(2)}, u32[]{:S(2)}) collective-permute-start(f32[130,128]{1,0:T(8,128)S(1)} %get-tuple-element.54.refs_2_), channel_id=1, source_target_pairs={{0,4},{4,8},{8,12},{12,0},{1,5},{5,9},{9,13},{13,1},{2,6},{6,10},{... | collective-permute-start | bytes 199688 | tf_op jit(solution)/shard_map/ppermute | solution.py:272
  108.2 21.0 %collective-permute-start.12 = (f32[130,128]{1,0:T(8,128)S(1)}, f32[130,128]{1,0:T(8,128)S(1)}, u32[]{:S(2)}, u32[]{:S(2)}) collective-permute-start(f32[130,128]{1,0:T(8,128)S(1)} %get-tuple-element.54.refs_2_), channel_id=1, source_target_pairs={{0,8},{4,12},{8,0},{12,4},{1,9},{5,13},{9,1},{13,5},{2,10},{6,14},... | collective-permute-start | bytes 199688 | tf_op jit(solution)/shard_map/ppermute | solution.py:272
  110.3 19.3 %collective-permute-start.13 = (f32[130,128]{1,0:T(8,128)S(1)}, f32[130,128]{1,0:T(8,128)S(1)}, u32[]{:S(2)}, u32[]{:S(2)}) collective-permute-start(f32[130,128]{1,0:T(8,128)S(1)} %get-tuple-element.54.refs_2_), channel_id=1, source_target_pairs={{0,12},{4,0},{8,4},{12,8},{1,13},{5,1},{9,5},{13,9},{2,14},{6,2},{... | collective-permute-start | bytes 199688 | tf_op jit(solution)/shard_map/ppermute | solution.py:272
  112.0 2.2 copy-start.5
  117.3 57.2 %collective-permute-start.10 = (bf16[2,2048,128]{2,1,0:T(8,128)(2,1)}, bf16[2,2048,128]{2,1,0:T(8,128)(2,1)}, u32[]{:S(2)}, u32[]{:S(2)}) collective-permute-start(bf16[2,2048,128]{2,1,0:T(8,128)(2,1)} %bitcast.27), channel_id=1, source_target_pairs={{0,1},{1,0},{4,5},{5,4},{8,9},{9,8},{12,13},{13,12},{2,3},{3,2},{6... | collective-permute-start | bytes 3145736 | tf_op jit(solution)/shard_map/ppermute | solution.py:264
  129.2 28.3 %collective-permute-start.6 = (bf16[2,2048,128]{2,1,0:T(8,128)(2,1)}, bf16[2,2048,128]{2,1,0:T(8,128)(2,1)}, u32[]{:S(2)}, u32[]{:S(2)}) collective-permute-start(bf16[2,2048,128]{2,1,0:T(8,128)(2,1)} %bitcast.17), channel_id=1, source_target_pairs={{0,4},{1,5},{4,8},{5,9},{8,12},{9,13},{12,0},{13,1},{2,6},{3,7},{6... | collective-permute-start | bytes 3145736 | tf_op jit(solution)/shard_map/ppermute | solution.py:264
  143.0 35.4 %collective-permute-start.9 = (bf16[2,2048,128]{2,1,0:T(8,128)(2,1)S(1)}, bf16[2,2048,128]{2,1,0:T(8,128)(2,1)S(1)}, u32[]{:S(2)}, u32[]{:S(2)}) collective-permute-start(bf16[2,2048,128]{2,1,0:T(8,128)(2,1)S(1)} %bitcast.73), channel_id=1, source_target_pairs={{0,5},{1,4},{4,9},{5,8},{8,13},{9,12},{12,1},{13,0},{2,7},{3,6},{6... | collective-permute-start | bytes 3145736 | tf_op jit(solution)/shard_map/ppermute | solution.py:264
  147.7 53.3 %collective-permute-start.5 = (bf16[2,2048,128]{2,1,0:T(8,128)(2,1)S(1)}, bf16[2,2048,128]{2,1,0:T(8,128)(2,1)S(1)}, u32[]{:S(2)}, u32[]{:S(2)}) collective-permute-start(bf16[2,2048,128]{2,1,0:T(8,128)(2,1)S(1)} %bitcast.72), channel_id=1, source_target_pairs={{0,12},{1,13},{4,0},{5,1},{8,4},{9,5},{12,8},{13,9},{2,14},{3,15},... | collective-permute-start | bytes 3145736 | tf_op jit(solution)/shard_map/ppermute | solution.py:264
  161.7 12.8 %copy-start.7 = (bf16[2,1024,2,128]{3,2,1,0:T(2,128)(2,1)S(1)}, bf16[2,1024,2,128]{3,2,1,0:T(2,128)(2,1)}, u32[]{:S(2)}) copy-start(bf16[2,1024,2,128]{3,2,1,0:T(2,128)(2,1)} %copy-done.6) | copy-start | bytes 3145732
  161.7 61.9 %collective-permute-start.7 = (bf16[2,2048,128]{2,1,0:T(8,128)(2,1)S(1)}, bf16[2,2048,128]{2,1,0:T(8,128)(2,1)S(1)}, u32[]{:S(2)}, u32[]{:S(2)}) collective-permute-start(bf16[2,2048,128]{2,1,0:T(8,128)(2,1)S(1)} %bitcast.74), channel_id=1, source_target_pairs={{0,13},{1,12},{4,1},{5,0},{8,5},{9,4},{12,9},{13,8},{2,15},{3,14},... | collective-permute-start | bytes 3145736 | tf_op jit(solution)/shard_map/ppermute | solution.py:264

commit v4 on v3

--- a/solution.py
+++ b/solution.py
@@ -29,22 +29,29 @@
     )
 
 
-def arrange(caches, request, core, after):
+def in_hbm(x):
+    return pltpu.with_memory_space_constraint(x, pltpu.HBM)
+
+
+def arrange(caches, owner_order, shift, flip, after):
     _, shard_length, heads, head_dim = caches[0].shape
-    core_count = 2
+    ctx_count = lax.axis_size("ctx")
+    core_count = lax.axis_size("sub")
     heads_decode = heads // core_count
     steps = 4
     places = shard_length // steps
     count = len(caches)
     pieces = [(w, i) for i in range(steps) for w in range(count)]
 
-    def kernel(where_ref, *refs):
+    def kernel(order_ref, *refs):
+        request = order_ref[lax.rem(lax.axis_index("ctx") + shift, ctx_count)]
+        core = lax.rem(lax.axis_index("sub") + flip, core_count)
         in_refs = refs[:count]
         out_ref, taken, made, in_sems, out_sems = refs[count + len(after) :]
         rows = lambda i: pl.ds(i * places, places)
         into = [
             pltpu.make_async_copy(
-                in_refs[w].at[where_ref[0], rows(i)], taken.at[w, rows(i)], in_sems.at[w, i]
+                in_refs[w].at[request, rows(i)], taken.at[w, rows(i)], in_sems.at[w, i]
             )
             for w, i in pieces
         ]
@@ -60,7 +67,7 @@
             into[p].wait()
             for own in range(core_count):
 
-                @pl.when(where_ref[1] == own)
+                @pl.when(core == own)
                 def _():
                     low = own * heads_decode
                     made[w, rows(i)] = taken[w, rows(i), low : low + heads_decode, :]
@@ -71,9 +78,7 @@
 
     blocks = pl.pallas_call(
         kernel,
-        out_shape=jax.ShapeDtypeStruct(
-            (count, shard_length, heads_decode, head_dim), caches[0].dtype
-        ),
+        out_shape=pltpu.HBM((count, shard_length, heads_decode, head_dim), caches[0].dtype),
         in_specs=[pl.BlockSpec(memory_space=pltpu.SMEM)]
         + [pl.BlockSpec(memory_space=pltpu.HBM)] * count
         + [pl.BlockSpec(memory_space=pl.ANY)] * len(after),
@@ -91,16 +96,29 @@
             bytes_accessed=3 * count * shard_length * heads * head_dim,
         ),
         name="arrange",
-    )(jnp.concatenate([request, core]), *caches, *after)
+    )(owner_order, *(in_hbm(x) for x in caches), *after)
     return blocks.reshape(count, shard_length * heads_decode, head_dim)
 
 
-def assemble(blocks, places, rows, filled=()):
+def assemble(blocks, keys, filled=()):
+    ctx_count = lax.axis_size("ctx")
+    core_count = lax.axis_size("sub")
     arrays, block_rows, head_dim = blocks[0].shape
     count = len(blocks)
+    rows = ctx_count * core_count * block_rows
     pieces = [(i, w) for i in range(count) for w in range(arrays)]
 
-    def kernel(places_ref, *refs):
+    def kernel(*refs):
+        ctx = lax.axis_index("ctx")
+        core = lax.axis_index("sub")
+        places = [
+            (
+                lax.rem(ctx + (ctx_count - shift), ctx_count) * core_count
+                + lax.rem(core + (core_count - flip), core_count)
+            )
+            * block_rows
+            for shift, flip in keys
+        ]
         in_refs = refs[:count]
         out_refs = refs[count + len(filled) :][:arrays]
         held, in_sems, out_sems = refs[count + len(filled) + arrays :]
@@ -111,7 +129,7 @@
         out_of = [
             pltpu.make_async_copy(
                 held.at[i, w],
-                out_refs[w].at[pl.ds(pl.multiple_of(places_ref[i], block_rows), block_rows)],
+                out_refs[w].at[pl.ds(pl.multiple_of(places[i], block_rows), block_rows)],
                 out_sems.at[i, w],
             )
             for i, w in pieces
@@ -126,9 +144,8 @@
 
     return pl.pallas_call(
         kernel,
-        out_shape=(jax.ShapeDtypeStruct((rows, head_dim), blocks[0].dtype),) * arrays,
-        in_specs=[pl.BlockSpec(memory_space=pltpu.SMEM)]
-        + [pl.BlockSpec(memory_space=pl.ANY)] * count
+        out_shape=(pltpu.HBM((rows, head_dim), blocks[0].dtype),) * arrays,
+        in_specs=[pl.BlockSpec(memory_space=pl.ANY)] * count
         + [pl.BlockSpec(memory_space=pltpu.HBM)] * len(filled),
         out_specs=(pl.BlockSpec(memory_space=pltpu.HBM),) * arrays,
         scratch_shapes=[
@@ -136,7 +153,7 @@
             pltpu.SemaphoreType.DMA((count, arrays)),
             pltpu.SemaphoreType.DMA((count, arrays)),
         ],
-        input_output_aliases={1 + count + w: w for w in range(len(filled))},
+        input_output_aliases={count + w: w for w in range(len(filled))},
         compiler_params=pltpu.CompilerParams(vmem_limit_bytes=VMEM_BYTES),
         cost_estimate=pl.CostEstimate(
             flops=0,
@@ -144,25 +161,25 @@
             bytes_accessed=4 * count * arrays * block_rows * head_dim,
         ),
         name="assemble",
-    )(places, *blocks, *filled)
+    )(*blocks, *filled)
 
 
 def pair_tokens(first, second, after):
     def kernel(first_ref, second_ref, after_ref, out_ref):
-        out_ref[0] = first_ref[...]
-        out_ref[1] = second_ref[...]
+        out_ref[:, 0] = first_ref[...]
+        out_ref[:, 1] = second_ref[...]
 
     whole = pl.BlockSpec(memory_space=pltpu.VMEM)
     return pl.pallas_call(
         kernel,
-        out_shape=jax.ShapeDtypeStruct((2,) + first.shape, first.dtype),
+        out_shape=jax.ShapeDtypeStruct((first.shape[0], 2, first.shape[1]), first.dtype),
         in_specs=[whole, whole, pl.BlockSpec(memory_space=pl.ANY)],
         out_specs=whole,
         name="pair_tokens",
-    )(first, second, after)
-
-
-def attend_shard(queries, keys, values, lengths, first_place, score_factor):
+    )(first, second, in_hbm(after))
+
+
+def attend_shard(queries, keys, values, lengths, score_factor, after):
     requests, shard_length, heads, head_dim = keys.shape
     rows = queries.shape[1]
     per_head = rows // heads
@@ -170,8 +187,12 @@
     flat_keys = keys.reshape(requests, columns, head_dim)
     flat_values = values.reshape(requests, columns, head_dim)
 
-    def kernel(lengths_ref, place_ref, q_ref, k_ref, v_ref, acc_ref, max_ref, sum_ref):
+    core_count = lax.axis_size("sub")
+
+    def kernel(lengths_ref, q_ref, k_ref, v_ref, *refs):
+        acc_ref, max_ref, sum_ref = refs[len(after) :]
         request = pl.program_id(0)
+        shard = lax.axis_index("ctx") * core_count + lax.axis_index("sub")
         scores = (
             lax.dot_general(
                 q_ref[0], k_ref[0], (((1,), (1,)), ((), ())), preferred_element_type=jnp.float32
@@ -180,7 +201,7 @@
         )
         row = lax.broadcasted_iota(jnp.int32, (rows, columns), 0)
         column = lax.broadcasted_iota(jnp.int32, (rows, columns), 1)
-        live_columns = (lengths_ref[request] - place_ref[0]) * heads
+        live_columns = (lengths_ref[request] - shard * shard_length) * heads
         live = (lax.rem(column, heads) == lax.div(row, per_head)) & (column < live_columns)
         scores = jnp.where(live, scores, masked_score)
         row_max = jnp.max(scores, axis=1, keepdims=True)
@@ -200,9 +221,10 @@
         kernel,
         out_shape=(result, result, result),
         grid_spec=pltpu.PrefetchScalarGridSpec(
-            num_scalar_prefetch=2,
+            num_scalar_prefetch=1,
             grid=(requests,),
-            in_specs=[small, large, large],
+            in_specs=[small, large, large]
+            + [pl.BlockSpec(memory_space=pl.ANY)] * len(after),
             out_specs=(small, small, small),
         ),
         compiler_params=pltpu.CompilerParams(vmem_limit_bytes=VMEM_BYTES),
@@ -212,7 +234,7 @@
             bytes_accessed=4 * keys.size,
         ),
         name="attend_shard",
-    )(lengths, first_place, queries, flat_keys, flat_values)
+    )(lengths, queries, in_hbm(flat_keys), in_hbm(flat_values), *after)
 
 
 def local(
@@ -234,24 +256,13 @@
     requests, shard_length, heads, head_dim = key_cache.shape
     assert requests == ctx_count and sub_count == 2
     heads_decode = heads // sub_count
-    ctx_index = lax.axis_index("ctx")
     sub_index = lax.axis_index("sub")
     take = functools.partial(jnp.take, mode="clip")
 
-    device_rows = shard_length * heads_decode
     received = {}
 
-    def place_of(shift, flip):
-        source = lax.rem(ctx_index - shift + ctx_count, ctx_count) * sub_count + lax.rem(
-            sub_index - flip + sub_count, sub_count
-        )
-        return source * device_rows
-
     def hand_off(shift, flip, after=()):
-        owner = lax.rem(ctx_index + shift, ctx_count)
-        request = lax.dynamic_slice_in_dim(owner_order, owner, 1)
-        core = jnp.reshape(lax.rem(sub_index + flip, sub_count), (1,)).astype(jnp.int32)
-        block = made = arrange((key_cache, value_cache), request, core, after)
+        block = made = arrange((key_cache, value_cache), owner_order, shift, flip, after)
         if shift or flip:
             pairs = [
                 (
@@ -285,7 +296,7 @@
     score_factor = head_dim ** (-0.5)
     rows_local = first_tokens.shape[0]
     tokens = lax.all_gather(
-        pair_tokens(first_tokens, second_tokens, leading), ("head", "sub"), axis=1, tiled=True
+        pair_tokens(first_tokens, second_tokens, leading), ("head", "sub"), axis=0, tiled=True
     )
     wide = tokens.astype(jnp.float32).reshape(2 * requests, -1)
     gained = wide * norm_gain.astype(jnp.float32)
@@ -309,27 +320,29 @@
     )
     summed = sum_shifted(partial, lambda parts: functools.reduce(jnp.add, parts))
     hand_off(middle, 1, (partial,))
-    hand_off(0, 1, (summed,))
     hand_off(0, 0, (summed,))
     raw = summed[:, :-LANES] * lax.rsqrt(summed[:, -LANES:][:, :1] / width + eps_norm)
-    raw = raw.reshape(2, requests, -1, head_dim)
-    positions = lengths.astype(jnp.float32)[None, :] + jnp.arange(2, dtype=jnp.float32)[:, None]
+    raw = raw.reshape(requests, 2, -1, head_dim)
+    positions = lengths.astype(jnp.float32)[:, None] + jnp.arange(2, dtype=jnp.float32)
     query_heads = query_width // head_dim
     key_heads = key_width // head_dim
     rotated = rotate(raw[:, :, : query_heads + key_heads], positions).astype(jnp.bfloat16)
-    queries = rotated[:, :, :query_heads].reshape(2, requests, heads_decode, group_size, head_dim)
+    queries = rotated[:, :, :query_heads].reshape(requests, 2, heads_decode, group_size, head_dim)
     fresh_keys = rotated[:, :, query_heads:]
     fresh_values = raw[:, :, query_heads + key_heads :].astype(jnp.bfloat16)
 
     per_head = 2 * group_size
-    own_queries = jnp.transpose(queries, (1, 2, 0, 3, 4)).reshape(
+    own_queries = jnp.transpose(queries, (0, 2, 1, 3, 4)).reshape(
         requests, heads_decode * per_head, head_dim
     )
     all_queries = lax.all_gather(own_queries, "sub", axis=1, tiled=True)
-    shard_index = ctx_index * sub_count + sub_index
-    first_place = jnp.reshape(shard_index * shard_length, (1,)).astype(jnp.int32)
     sums, maxima, totals = attend_shard(
-        all_queries, key_cache, value_cache, lengths, first_place, score_factor
+        all_queries,
+        key_cache,
+        value_cache,
+        lengths,
+        score_factor,
+        (received[middle, 0],),
     )
 
     own_rows = heads_decode * per_head
@@ -383,12 +396,13 @@
     hand_off(*queue[0], (stats,))
     for key, earlier in zip(queue[1:], ahead + queue):
         hand_off(*key, (stats, received[earlier]))
+    hand_off(0, 1, (stats, received[middle, 1]))
 
     grouped = own_queries.reshape(requests, heads_decode, 2, group_size, head_dim).astype(
         jnp.float32
     )
-    keys_wide = jnp.transpose(fresh_keys, (1, 2, 0, 3)).astype(jnp.float32)
-    values_wide = jnp.transpose(fresh_values, (1, 2, 0, 3)).astype(jnp.float32)
+    keys_wide = jnp.transpose(fresh_keys, (0, 2, 1, 3)).astype(jnp.float32)
+    values_wide = jnp.transpose(fresh_values, (0, 2, 1, 3)).astype(jnp.float32)
     fresh_scores = (
         jnp.sum(grouped[:, :, :, :, None, :] * keys_wide[:, :, None, None, :, :], axis=-1)
         * score_factor
@@ -410,14 +424,14 @@
     attended = (numerator / denominator[..., None]).astype(jnp.bfloat16)
 
     attended = take(attended, owner_order, axis=0)
-    attended = jnp.transpose(attended, (2, 0, 1, 3, 4)).reshape(2 * requests, query_width)
+    attended = jnp.transpose(attended, (0, 2, 1, 3, 4)).reshape(2 * requests, query_width)
     branch = jnp.dot(attended, w_out, preferred_element_type=jnp.float32)
-    branch = branch.reshape(2, requests, -1)
+    branch = branch.reshape(requests, 2, -1)
     row_start = lax.axis_index(("head", "sub")) * rows_local
     parts = lax.all_gather(branch, ("head", "sub"), axis=0)
-    parts = lax.dynamic_slice_in_dim(parts, row_start, rows_local, 2)
+    parts = lax.dynamic_slice_in_dim(parts, row_start, rows_local, 1)
     own_ids = lax.dynamic_slice_in_dim(owner_order, row_start, rows_local)
-    residual = take(tokens, own_ids, axis=1).astype(jnp.float32)
+    residual = take(tokens, own_ids, axis=0).astype(jnp.float32)
     result = (residual + jnp.sum(parts, axis=0)).astype(jnp.bfloat16)
 
     moved = ()
@@ -428,12 +442,11 @@
     ):
         moved = assemble(
             [received[key] for key in keys],
-            jnp.stack([place_of(*key) for key in keys]).astype(jnp.int32),
-            ctx_count * sub_count * device_rows,
+            keys,
             moved,
         )
     moved_keys, moved_values = (x.reshape(1, -1, heads_decode, head_dim) for x in moved)
-    return (moved_keys, moved_values, result[0], result[1])
+    return (moved_keys, moved_values, result[:, 0], result[:, 1])
 
 
 def solution(mesh):

time: 227 us -> 228 us (level)
  waiting for transfers between devices: 61.4 us -> 125 us
  starting transfers between devices: 53.2 us -> 15.3 us
  local copies, waits for them, and re-layouts: 21.4 us -> 6.91 us
  other arithmetic: 17.6 us -> 11 us
  Pallas kernels: 45.1 us -> 42.7 us
    ppermute x7, waiting for transfers between devices: 49.5 us -> 124 us  [hand_off(): block = lax.ppermute(made, ('ctx', 'sub'), pairs)]
    ppermute x6, starting transfers between devices: 47.3 us -> 9.77 us  [sum_shifted(): lax.ppermute(values, 'ctx', [(c, (c + shift) % ctx_count) for c in range(...]
    ppermute x6, waiting for transfers between devices: 11.9 us -> 0.02 us  [sum_shifted(): lax.ppermute(values, 'ctx', [(c, (c + shift) % ctx_count) for c in range(...]
    unnamed x26 -> x14, local copies, waits for them, and re-layouts: 12 us -> 0.77 us
    concatenate x6 -> x0, other arithmetic: 4.13 us -> none  [arrange(): jnp.concatenate([request, core])]
    pallas_call x12, Pallas kernels: 38.8 us -> 35.6 us  [the longest x8 26.2 us: arrange(): pl.pallas_call(kernel, out_shape=pltpu.HBM((count, shard_length, heads_de...]
  transfers between devices with their start and end apart: 14 -> 14, of which waited for: 5 -> 6; matrix products, arithmetic and copies ran while one was open for 13% -> 9% of each run, Pallas kernels for 17% -> 16%
where the time goes in v4:
time: 228 us
  waiting for transfers between devices  125 us (55%)
  Pallas kernels  42.7 us (19%)
  blocking collectives  15.8 us (7%)
  starting transfers between devices  15.3 us (7%)
  other arithmetic  11 us (5%)
  matrix products  9.95 us (4%)
  local copies, waits for them, and re-layouts  6.91 us (3%)
    ppermute x7, waiting for transfers between devices, hand_off(): block = lax.ppermute(made, ('ctx', 'sub'), pairs)  124 us
    pallas_call x8, Pallas kernels, arrange(): pl.pallas_call(kernel, out_shape=pltpu.HBM((count, shard_length, heads_de...  26.2 us
    ppermute x6, starting transfers between devices, sum_shifted(): lax.ppermute(values, 'ctx', [(c, (c + shift) % ctx_count) for c in range(...  9.77 us
    pallas_call x3, Pallas kernels, assemble(): pl.pallas_call(kernel, out_shape=(pltpu.HBM((rows, head_dim), blocks[0].d...  8.12 us
    pallas_call x1, Pallas kernels, attend_shard(): pl.pallas_call(kernel, out_shape=(result, result, result), grid_spec=pltp...  7.02 us
    all_gather x1, blocking collectives, local(): lax.all_gather(pair_tokens(first_tokens, second_tokens, leading), ('head'...  6.47 us
    all_gather x1, blocking collectives, local(): parts = lax.all_gather(branch, ('head', 'sub'), axis=0)  5.79 us
    ppermute x7, starting transfers between devices, hand_off(): block = lax.ppermute(made, ('ctx', 'sub'), pairs)  5.5 us
  transfers between devices with their start and end apart: 14, of which 6 were waited for; matrix products, arithmetic and copies ran while one was open for 9% of the time, Pallas kernels for 16%

profile of v4, /device:TPU:0, one launch (start us, length us, event | category | flops | bytes accessed | tf_op | source)
XLA Modules:
  0.0 227.6 jit_solution(14038646168386732591)
XLA Ops:
  0.7 0.7 copy-done.2
  1.4 3.1 %arrange.8 = bf16[2,1024,2,128]{3,2,1,0:T(2,128)(2,1)} custom-call(s32[4]{0:T(128)S(1)} %copy-done.2, bf16[4,1024,4,128]{3,2,1,0:T(4,128)(2,1)} %refs_0_.15, bf16[4,1024,4,128]{3,2,1,0:T(4,128)(2,1)} %refs_1_.15), custom_call_target="tpu_custom_call" | custom-call | bytes 3145728 | tf_op jit(solution)/shard_map/arrange/pallas_call | solution.py:79
  4.5 1.3 pair_tokens.1
  5.8 6.5 %all_gather.9 = bf16[4,2,2048]{2,1,0:T(2,128)(2,1)S(1)} all-gather(bf16[1,2,2048]{2,1,0:T(2,128)(2,1)} %pair_tokens.1), channel_id=1, replica_groups=mesh['groups'=2,'ctx'=4,'head'=2,'sub'=2] {'head','sub'}, dimensions={0}, use_global_device_ids=true | all-gather | bytes 40960 | tf_op jit(solution)/shard_map/all_gather | solution.py:298
  12.3 0.1 multiply_reduce_fusion.2
  12.5 4.7 %fusion.9 = f32[16,2048]{1,0:T(8,128)S(1)} fusion(bf16[2048,2048]{1,0:T(8,128)(2,1)} %param.18, bf16[8,2048]{1,0:T(8,128)(2,1)S(1)} %get-tuple-element.50, bf16[8,2048]{1,0:T(8,128)(2,1)S(1)} %get-tuple-element.49), kind=kOutput, calls=%fused_computation.38 | convolution fusion | flops 134348800 | bytes 8585216 | tf_op jit(solution)/shard_map/dot_general | solution.py:308
  17.1 0.3 fusion.8
  17.4 0.3 fusion.7
  17.9 2.0 collective-permute-start
  19.8 2.6 %collective-permute-start.1 = (f32[8,2688]{1,0:T(8,128)S(1)}, f32[8,2688]{1,0:T(8,128)S(1)}, u32[]{:S(2)}, u32[]{:S(2)}) collective-permute-start(f32[8,2688]{1,0:T(8,128)S(1)} %pad_maximum_fusion.2.refs_2_), channel_id=1, source_target_pairs={{0,8},{4,12},{8,0},{12,4},{1,9},{5,13},{9,1},{13,5},{2,10},{6,14},... | collective-permute-start | bytes 258056 | tf_op jit(solution)/shard_map/ppermute | solution.py:283
  22.4 1.3 collective-permute-start.2
  23.7 0.2 collective-permute-start.3
  23.9 3.4 %arrange.9 = bf16[2,1024,2,128]{3,2,1,0:T(2,128)(2,1)} custom-call(s32[4]{0:T(128)S(1)} %copy-done.3, bf16[4,1024,4,128]{3,2,1,0:T(4,128)(2,1)} %refs_0_.15, bf16[4,1024,4,128]{3,2,1,0:T(4,128)(2,1)} %refs_1_.15, f32[8,2688]{1,0:T(8,128)S(1)} %pad_maximum_fusion.2.refs_2_), custom_call_target="tpu_custom_call" | custom-call | bytes 3145728 | tf_op jit(solution)/shard_map/arrange/pallas_call | solution.py:79
  27.4 1.2 collective-permute-start.5
  28.6 0.6 pad_clamp_fusion
  29.3 0.6 dynamic_slice.30
  29.9 0.1 multiply_cosine_fusion
  30.0 0.6 iota_compare_fusion
  30.6 0.9 add_add_fusion.refs_2_
  31.5 0.1 fusion.14
  31.6 3.1 %arrange.14 = bf16[2,1024,2,128]{3,2,1,0:T(2,128)(2,1)} custom-call(s32[4]{0:T(128)S(1)} %copy-done.3, bf16[4,1024,4,128]{3,2,1,0:T(4,128)(2,1)} %refs_0_.15, bf16[4,1024,4,128]{3,2,1,0:T(4,128)(2,1)} %refs_1_.15, f32[8,2688]{1,0:T(8,128)S(1)} %add_add_fusion.refs_2_), custom_call_target="tpu_custom_call" | custom-call | bytes 3145728 | tf_op jit(solution)/shard_map/arrange/pallas_call | solution.py:79
  34.8 0.1 add_convert_fusion
  35.0 0.6 copy.43
  35.7 3.5 %all_gather.10.q_ref = bf16[4,64,128]{2,1,0:T(8,128)(2,1)S(1)} all-gather(bf16[4,32,128]{2,1,0:T(8,128)(2,1)S(1)} %bitcast.83), channel_id=1, replica_groups=mesh['groups'=2,'ctx'=4,'head'=2,'sub'=2] {'sub'}, dimensions={1}, use_global_device_ids=true | all-gather | bytes 98304 | tf_op jit(solution)/shard_map/all_gather | solution.py:338
  39.3 58.6 %collective-permute-done.3.refs_0_.refs_3_.refs_2_ = bf16[2,2048,128]{2,1,0:T(8,128)(2,1)S(1)} collective-permute-done((bf16[2,2048,128]{2,1,0:T(8,128)(2,1)}, bf16[2,2048,128]{2,1,0:T(8,128)(2,1)S(1)}, u32[]{:S(2)}, u32[]{:S(2)}) %collective-permute-start.3) | collective-permute-done | bytes 1048608 | tf_op jit(solution)/shard_map/ppermute | solution.py:275
  97.9 7.0 %attend_shard.1 = (f32[4,64,128]{2,1,0:T(8,128)S(1)}, f32[4,64,128]{2,1,0:T(8,128)S(1)}, f32[4,64,128]{2,1,0:T(8,128)S(1)}) custom-call(s32[4]{0:T(128)S(1)} %copy-done.4, bf16[4,64,128]{2,1,0:T(8,128)(2,1)S(1)} %all_gather.10.q_ref, bf16[4,4096,128]{2,1,0:T(8,128)(2,1)} %bitcast.60, bf16[4,4096,128]{2,1,0:T(8,128)(2,1)} %bitcast.61, ...), custom_call_target="tpu_custom_call" | custom-call | flops 536870912 | bytes 8388608 | tf_op jit(solution)/shard_map/attend_shard/pallas_call | solution.py:220
  104.9 0.2 dynamic-slice_reduce_fusion
  105.4 0.1 multiply_reduce_fusion.1
  105.6 1.0 collective-permute-done.4
  106.9 0.1 reshape.267
  107.0 0.1 fusion.3
  107.2 2.7 %collective-permute-start.12 = (f32[130,128]{1,0:T(8,128)S(1)}, f32[130,128]{1,0:T(8,128)S(1)}, u32[]{:S(2)}, u32[]{:S(2)}) collective-permute-start(f32[130,128]{1,0:T(8,128)S(1)} %get-tuple-element.54.refs_2_), channel_id=1, source_target_pairs={{0,8},{4,12},{8,0},{12,4},{1,9},{5,13},{9,1},{13,5},{2,10},{6,14},... | collective-permute-start | bytes 199688 | tf_op jit(solution)/shard_map/ppermute | solution.py:283
  109.9 1.1 collective-permute-start.13
  111.0 0.8 fusion.11
  111.8 3.3 %arrange.11 = bf16[2,1024,2,128]{3,2,1,0:T(2,128)(2,1)} custom-call(s32[4]{0:T(128)S(1)} %copy-done.3, bf16[4,1024,4,128]{3,2,1,0:T(4,128)(2,1)} %refs_0_.15, bf16[4,1024,4,128]{3,2,1,0:T(4,128)(2,1)} %refs_1_.15, f32[130,128]{1,0:T(8,128)S(1)} %get-tuple-element.54.refs_2_), custom_call_target="tpu_custom_call" | custom-call | bytes 3145728 | tf_op jit(solution)/shard_map/arrange/pallas_call | solution.py:79
  115.0 8.1 %collective-permute-done.5.refs_3_ = bf16[2,2048,128]{2,1,0:T(8,128)(2,1)S(1)} collective-permute-done((bf16[2,2048,128]{2,1,0:T(8,128)(2,1)}, bf16[2,2048,128]{2,1,0:T(8,128)(2,1)S(1)}, u32[]{:S(2)}, u32[]{:S(2)}) %collective-permute-start.5) | collective-permute-done | bytes 1048608 | tf_op jit(solution)/shard_map/ppermute | solution.py:275
  123.2 3.4 %arrange.15 = bf16[2,1024,2,128]{3,2,1,0:T(2,128)(2,1)} custom-call(s32[4]{0:T(128)S(1)} %copy-done.3, bf16[4,1024,4,128]{3,2,1,0:T(4,128)(2,1)} %refs_0_.15, bf16[4,1024,4,128]{3,2,1,0:T(4,128)(2,1)} %refs_1_.15, f32[130,128]{1,0:T(8,128)S(1)} %get-tuple-element.54.refs_2_, bf16[2,2048,128]{2,1,0:T(8,128)(2,1)S(1)} %collective-permute-done.5.refs_3_), custom_call_target="tpu_custom_call" | custom-call | bytes 3145728 | tf_op jit(solution)/shard_map/arrange/pallas_call | solution.py:79
  126.7 3.4 %arrange.13 = bf16[2,1024,2,128]{3,2,1,0:T(2,128)(2,1)} custom-call(s32[4]{0:T(128)S(1)} %copy-done.3, bf16[4,1024,4,128]{3,2,1,0:T(4,128)(2,1)} %refs_0_.15, bf16[4,1024,4,128]{3,2,1,0:T(4,128)(2,1)} %refs_1_.15, f32[130,128]{1,0:T(8,128)S(1)} %get-tuple-element.54.refs_2_, bf16[2,2048,128]{2,1,0:T(8,128)(2,1)S(1)} %collective-permute-done.3.refs_0_.refs_3_.refs_2_), custom_call_target="tpu_custom_call" | custom-call | bytes 3145728 | tf_op jit(solution)/shard_map/arrange/pallas_call | solution.py:79
  130.2 3.1 %arrange.10 = bf16[2,1024,2,128]{3,2,1,0:T(2,128)(2,1)} custom-call(s32[4]{0:T(128)S(1)} %copy-done.3, bf16[4,1024,4,128]{3,2,1,0:T(4,128)(2,1)} %refs_0_.15, bf16[4,1024,4,128]{3,2,1,0:T(4,128)(2,1)} %refs_1_.15, f32[130,128]{1,0:T(8,128)S(1)} %get-tuple-element.54.refs_2_, bf16[2,2048,128]{2,1,0:T(8,128)(2,1)S(1)} %collective-permute-done.5.refs_3_), custom_call_target="tpu_custom_call" | custom-call | bytes 3145728 | tf_op jit(solution)/shard_map/arrange/pallas_call | solution.py:79
  133.3 0.2 collective-permute-start.7
  133.4 3.7 %collective-permute-start.6 = (bf16[2,2048,128]{2,1,0:T(8,128)(2,1)}, bf16[2,2048,128]{2,1,0:T(8,128)(2,1)}, u32[]{:S(2)}, u32[]{:S(2)}) collective-permute-start(bf16[2,2048,128]{2,1,0:T(8,128)(2,1)} %bitcast.65), channel_id=1, source_target_pairs={{0,12},{1,13},{4,0},{5,1},{8,4},{9,5},{12,8},{13,9},{2,14},{3,15},... | collective-permute-start | bytes 3145736 | tf_op jit(solution)/shard_map/ppermute | solution.py:275
  137.2 1.2 fusion.24
  138.3 1.4 reshape.279
  139.7 1.2 fusion.17
  140.9 1.3 reshape.280
  142.2 0.7 copy_maximum_fusion
  143.0 0.8 fusion.21
  143.7 0.7 copy_add_fusion
  144.5 0.7 subtract_exponential_fusion.1
  145.2 0.1 fusion.2
  145.4 0.8 multiply_reduce_fusion
  146.2 0.1 divide_convert_fusion
  146.3 0.7 gather_fusion
  147.0 33.6 %collective-permute-done.7.refs_3_.refs_0_ = bf16[2,2048,128]{2,1,0:T(8,128)(2,1)} collective-permute-done((bf16[2,2048,128]{2,1,0:T(8,128)(2,1)}, bf16[2,2048,128]{2,1,0:T(8,128)(2,1)}, u32[]{:S(2)}, u32[]{:S(2)}) %collective-permute-start.7) | collective-permute-done | bytes 1048608 | tf_op jit(solution)/shard_map/ppermute | solution.py:275
  180.6 3.4 %arrange.12 = bf16[2,1024,2,128]{3,2,1,0:T(2,128)(2,1)} custom-call(s32[4]{0:T(128)S(1)} %copy-done.3, bf16[4,1024,4,128]{3,2,1,0:T(4,128)(2,1)} %refs_0_.15, bf16[4,1024,4,128]{3,2,1,0:T(4,128)(2,1)} %refs_1_.15, f32[130,128]{1,0:T(8,128)S(1)} %get-tuple-element.54.refs_2_, bf16[2,2048,128]{2,1,0:T(8,128)(2,1)} %collective-permute-done.7.refs_3_.refs_0_), custom_call_target="tpu_custom_call" | custom-call | bytes 3145728 | tf_op jit(solution)/shard_map/arrange/pallas_call | solution.py:79
  184.1 4.8 %fusion = f32[4,2,2048]{2,1,0:T(2,128)S(1)} fusion(bf16[4,2,2048]{2,1,0:T(2,128)(2,1)S(1)} %reshape.316, bf16[2048,2048]{1,0:T(8,128)(2,1)} %param.21), kind=kOutput, calls=%fused_computation.1 | convolution fusion | flops 67108864 | bytes 8486912 | tf_op jit(solution)/shard_map/dot_general | solution.py:428
  188.9 5.8 %all-gather = f32[16,2,2048]{2,1,0:T(2,128)S(1)} all-gather(f32[4,2,2048]{2,1,0:T(2,128)S(1)} %fusion), channel_id=2, replica_groups=mesh['groups'=2,'ctx'=4,'head'=2,'sub'=2] {'head','sub'}, dimensions={0}, use_global_device_ids=true | all-gather | bytes 327680 | tf_op jit(solution)/shard_map/all_gather | solution.py:431
  194.7 0.6 fusion.10
  195.3 0.6 slice_bitcast_fusion
  195.9 3.3 %assemble.3 = (bf16[16384,128]{1,0:T(8,128)(2,1)}, bf16[16384,128]{1,0:T(8,128)(2,1)}) custom-call(bf16[2,2048,128]{2,1,0:T(8,128)(2,1)S(1)} %bitcast.59, bf16[2,2048,128]{2,1,0:T(8,128)(2,1)} %collective-permute-done.10.refs_1_, bf16[2,2048,128]{2,1,0:T(8,128)(2,1)S(1)} %collective-permute-done.3.refs_0_.refs_3_.refs_2_, ...), custom_call_target="tpu_custom_call" | custom-call | bytes 8388608 | tf_op jit(solution)/shard_map/assemble/pallas_call | solution.py:145
  199.2 2.4 %assemble.4 = (bf16[16384,128]{1,0:T(8,128)(2,1)}, bf16[16384,128]{1,0:T(8,128)(2,1)}) custom-call(bf16[2,2048,128]{2,1,0:T(8,128)(2,1)} %collective-permute-done.7.refs_3_.refs_0_, bf16[2,2048,128]{2,1,0:T(8,128)(2,1)} %collective-permute-done.9.refs_1_, ...), custom_call_target="tpu_custom_call", output_to_operand_aliasing={{0}: (2, {}), {1}: (3, {})} | custom-call | bytes 4194304 | tf_op jit(solution)/shard_map/assemble/pallas_call | solution.py:145
  201.7 1.0 collective-permute-done.6.refs_0_
  202.7 22.4 %collective-permute-done.8.refs_1_ = bf16[2,2048,128]{2,1,0:T(8,128)(2,1)S(1)} collective-permute-done((bf16[2,2048,128]{2,1,0:T(8,128)(2,1)}, bf16[2,2048,128]{2,1,0:T(8,128)(2,1)S(1)}, u32[]{:S(2)}, u32[]{:S(2)}) %collective-permute-start.8) | collective-permute-done | bytes 1048608 | tf_op jit(solution)/shard_map/ppermute | solution.py:275
  225.1 2.4 %assemble.5 = (bf16[16384,128]{1,0:T(8,128)(2,1)}, bf16[16384,128]{1,0:T(8,128)(2,1)}) custom-call(bf16[2,2048,128]{2,1,0:T(8,128)(2,1)} %collective-permute-done.6.refs_0_, bf16[2,2048,128]{2,1,0:T(8,128)(2,1)S(1)} %collective-permute-done.8.refs_1_, bf16[16384,128]{1,0:T(8,128)(2,1)} %get-tuple-element.18.refs_2_, ...), custom_call_target="tpu_custom_call", output_to_operand_aliasing={{0}: (2, {}), {1}: (3, {})} | custom-call | bytes 4194304 | tf_op jit(solution)/shard_map/assemble/pallas_call | solution.py:145
  (63 shorter events, 1.6 us)
Async XLA Ops:
  0.6 16.5 %copy-start = (bf16[2048,256]{1,0:T(8,128)(2,1)S(1)}, bf16[2048,256]{1,0:T(8,128)(2,1)}, u32[]{:S(2)}) copy-start(bf16[2048,256]{1,0:T(8,128)(2,1)} %param.19) | copy-start | bytes 3145732
  0.6 0.7 copy-start.2
  1.4 11.0 %copy-start.6 = (bf16[2048]{0:T(1024)(128)(2,1)S(1)}, bf16[2048]{0:T(1024)(128)(2,1)}, u32[]{:S(2)}) copy-start(bf16[2048]{0:T(1024)(128)(2,1)} %param.17) | copy-start | bytes 12292
  12.4 4.9 %copy-start.5 = (bf16[2048,256]{1,0:T(8,128)(2,1)S(1)}, bf16[2048,256]{1,0:T(8,128)(2,1)}, u32[]{:S(2)}) copy-start(bf16[2048,256]{1,0:T(8,128)(2,1)} %param.20) | copy-start | bytes 3145732
  12.5 11.5 %copy-start.3 = (s32[4]{0:T(128)S(1)}, s32[4]{0:T(128)}, u32[]{:S(2)}) copy-start(s32[4]{0:T(128)} %order_ref.15) | copy-start | bytes 52
  17.1 12.1 %copy-start.4 = (s32[4]{0:T(128)S(1)}, s32[4]{0:T(128)}, u32[]{:S(2)}) copy-start(s32[4]{0:T(128)} %lengths_ref.1) | copy-start | bytes 52
  17.9 12.7 %collective-permute-start = (f32[8,2688]{1,0:T(8,128)S(1)}, f32[8,2688]{1,0:T(8,128)S(1)}, u32[]{:S(2)}, u32[]{:S(2)}) collective-permute-start(f32[8,2688]{1,0:T(8,128)S(1)} %pad_maximum_fusion.2.refs_2_), channel_id=1, source_target_pairs={{0,4},{4,8},{8,12},{12,0},{1,5},{5,9},{9,13},{13,1},{2,6},{6,10},{... | collective-permute-start | bytes 258056 | tf_op jit(solution)/shard_map/ppermute | solution.py:283
  19.8 10.8 %collective-permute-start.1 = (f32[8,2688]{1,0:T(8,128)S(1)}, f32[8,2688]{1,0:T(8,128)S(1)}, u32[]{:S(2)}, u32[]{:S(2)}) collective-permute-start(f32[8,2688]{1,0:T(8,128)S(1)} %pad_maximum_fusion.2.refs_2_), channel_id=1, source_target_pairs={{0,8},{4,12},{8,0},{12,4},{1,9},{5,13},{9,1},{13,5},{2,10},{6,14},... | collective-permute-start | bytes 258056 | tf_op jit(solution)/shard_map/ppermute | solution.py:283
  22.4 8.2 %collective-permute-start.2 = (f32[8,2688]{1,0:T(8,128)S(1)}, f32[8,2688]{1,0:T(8,128)}, u32[]{:S(2)}, u32[]{:S(2)}) collective-permute-start(f32[8,2688]{1,0:T(8,128)S(1)} %pad_maximum_fusion.2.refs_2_), channel_id=1, source_target_pairs={{0,12},{4,0},{8,4},{12,8},{1,13},{5,1},{9,5},{13,9},{2,14},{6,2},{... | collective-permute-start | bytes 258056 | tf_op jit(solution)/shard_map/ppermute | solution.py:283
  23.7 74.1 %collective-permute-start.3 = (bf16[2,2048,128]{2,1,0:T(8,128)(2,1)}, bf16[2,2048,128]{2,1,0:T(8,128)(2,1)S(1)}, u32[]{:S(2)}, u32[]{:S(2)}) collective-permute-start(bf16[2,2048,128]{2,1,0:T(8,128)(2,1)} %bitcast.after_ref), channel_id=1, source_target_pairs={{0,8},{1,9},{4,12},{5,13},{8,0},{9,1},{12,4},{13,5},{2,10},{3,11},... | collective-permute-start | bytes 3145736 | tf_op jit(solution)/shard_map/ppermute | solution.py:275
  27.4 95.8 %collective-permute-start.5 = (bf16[2,2048,128]{2,1,0:T(8,128)(2,1)}, bf16[2,2048,128]{2,1,0:T(8,128)(2,1)S(1)}, u32[]{:S(2)}, u32[]{:S(2)}) collective-permute-start(bf16[2,2048,128]{2,1,0:T(8,128)(2,1)} %bitcast.64), channel_id=1, source_target_pairs={{0,9},{1,8},{4,13},{5,12},{8,1},{9,0},{12,5},{13,4},{2,11},{3,10},... | collective-permute-start | bytes 3145736 | tf_op jit(solution)/shard_map/ppermute | solution.py:275
  105.3 1.3 collective-permute-start.4
  107.1 26.1 %collective-permute-start.11 = (f32[130,128]{1,0:T(8,128)S(1)}, f32[130,128]{1,0:T(8,128)S(1)}, u32[]{:S(2)}, u32[]{:S(2)}) collective-permute-start(f32[130,128]{1,0:T(8,128)S(1)} %get-tuple-element.54.refs_2_), channel_id=1, source_target_pairs={{0,4},{4,8},{8,12},{12,0},{1,5},{5,9},{9,13},{13,1},{2,6},{6,10},{... | collective-permute-start | bytes 199688 | tf_op jit(solution)/shard_map/ppermute | solution.py:283
  107.2 26.2 %collective-permute-start.12 = (f32[130,128]{1,0:T(8,128)S(1)}, f32[130,128]{1,0:T(8,128)S(1)}, u32[]{:S(2)}, u32[]{:S(2)}) collective-permute-start(f32[130,128]{1,0:T(8,128)S(1)} %get-tuple-element.54.refs_2_), channel_id=1, source_target_pairs={{0,8},{4,12},{8,0},{12,4},{1,9},{5,13},{9,1},{13,5},{2,10},{6,14},... | collective-permute-start | bytes 199688 | tf_op jit(solution)/shard_map/ppermute | solution.py:283
  109.9 27.3 %collective-permute-start.13 = (f32[130,128]{1,0:T(8,128)S(1)}, f32[130,128]{1,0:T(8,128)S(1)}, u32[]{:S(2)}, u32[]{:S(2)}) collective-permute-start(f32[130,128]{1,0:T(8,128)S(1)} %get-tuple-element.54.refs_2_), channel_id=1, source_target_pairs={{0,12},{4,0},{8,4},{12,8},{1,13},{5,1},{9,5},{13,9},{2,14},{6,2},{... | collective-permute-start | bytes 199688 | tf_op jit(solution)/shard_map/ppermute | solution.py:283
  126.6 69.3 %collective-permute-start.10 = (bf16[2,2048,128]{2,1,0:T(8,128)(2,1)}, bf16[2,2048,128]{2,1,0:T(8,128)(2,1)}, u32[]{:S(2)}, u32[]{:S(2)}) collective-permute-start(bf16[2,2048,128]{2,1,0:T(8,128)(2,1)} %bitcast.67), channel_id=1, source_target_pairs={{0,1},{1,0},{4,5},{5,4},{8,9},{9,8},{12,13},{13,12},{2,3},{3,2},{6... | collective-permute-start | bytes 3145736 | tf_op jit(solution)/shard_map/ppermute | solution.py:275
  130.1 69.1 %collective-permute-start.9 = (bf16[2,2048,128]{2,1,0:T(8,128)(2,1)}, bf16[2,2048,128]{2,1,0:T(8,128)(2,1)}, u32[]{:S(2)}, u32[]{:S(2)}) collective-permute-start(bf16[2,2048,128]{2,1,0:T(8,128)(2,1)} %bitcast.66), channel_id=1, source_target_pairs={{0,5},{1,4},{4,9},{5,8},{8,13},{9,12},{12,1},{13,0},{2,7},{3,6},{6... | collective-permute-start | bytes 3145736 | tf_op jit(solution)/shard_map/ppermute | solution.py:275
  133.3 47.3 %collective-permute-start.7 = (bf16[2,2048,128]{2,1,0:T(8,128)(2,1)}, bf16[2,2048,128]{2,1,0:T(8,128)(2,1)}, u32[]{:S(2)}, u32[]{:S(2)}) collective-permute-start(bf16[2,2048,128]{2,1,0:T(8,128)(2,1)} %bitcast.12), channel_id=1, source_target_pairs={{0,4},{1,5},{4,8},{5,9},{8,12},{9,13},{12,0},{13,1},{2,6},{3,7},{6... | collective-permute-start | bytes 3145736 | tf_op jit(solution)/shard_map/ppermute | solution.py:275
  133.4 69.2 %collective-permute-start.6 = (bf16[2,2048,128]{2,1,0:T(8,128)(2,1)}, bf16[2,2048,128]{2,1,0:T(8,128)(2,1)}, u32[]{:S(2)}, u32[]{:S(2)}) collective-permute-start(bf16[2,2048,128]{2,1,0:T(8,128)(2,1)} %bitcast.65), channel_id=1, source_target_pairs={{0,12},{1,13},{4,0},{5,1},{8,4},{9,5},{12,8},{13,9},{2,14},{3,15},... | collective-permute-start | bytes 3145736 | tf_op jit(solution)/shard_map/ppermute | solution.py:275
  184.0 11.9 %copy-start.1 = (bf16[2,1024,2,128]{3,2,1,0:T(2,128)(2,1)S(1)}, bf16[2,1024,2,128]{3,2,1,0:T(2,128)(2,1)}, u32[]{:S(2)}) copy-start(bf16[2,1024,2,128]{3,2,1,0:T(2,128)(2,1)} %arrange.14) | copy-start | bytes 3145732
  184.1 41.0 %collective-permute-start.8 = (bf16[2,2048,128]{2,1,0:T(8,128)(2,1)}, bf16[2,2048,128]{2,1,0:T(8,128)(2,1)S(1)}, u32[]{:S(2)}, u32[]{:S(2)}) collective-permute-start(bf16[2,2048,128]{2,1,0:T(8,128)(2,1)} %bitcast.68), channel_id=1, source_target_pairs={{0,13},{1,12},{4,1},{5,0},{8,5},{9,4},{12,9},{13,8},{2,15},{3,14},... | collective-permute-start | bytes 3145736 | tf_op jit(solution)/shard_map/ppermute | solution.py:275

commit v5 on v4

--- a/solution.py
+++ b/solution.py
@@ -100,43 +100,36 @@
     return blocks.reshape(count, shard_length * heads_decode, head_dim)
 
 
-def assemble(blocks, keys, filled=()):
+def assemble(blocks, pieces, filled=()):
     ctx_count = lax.axis_size("ctx")
     core_count = lax.axis_size("sub")
-    arrays, block_rows, head_dim = blocks[0].shape
+    _, block_rows, head_dim = blocks[0].shape
+    rows = ctx_count * core_count * block_rows
+    arrays = 2
     count = len(blocks)
-    rows = ctx_count * core_count * block_rows
-    pieces = [(i, w) for i in range(count) for w in range(arrays)]
+    total = len(pieces)
 
     def kernel(*refs):
         ctx = lax.axis_index("ctx")
         core = lax.axis_index("sub")
-        places = [
-            (
-                lax.rem(ctx + (ctx_count - shift), ctx_count) * core_count
-                + lax.rem(core + (core_count - flip), core_count)
-            )
-            * block_rows
-            for shift, flip in keys
-        ]
         in_refs = refs[:count]
         out_refs = refs[count + len(filled) :][:arrays]
         held, in_sems, out_sems = refs[count + len(filled) + arrays :]
-        into = [
-            pltpu.make_async_copy(in_refs[i].at[w], held.at[i, w], in_sems.at[i, w])
-            for i, w in pieces
-        ]
-        out_of = [
-            pltpu.make_async_copy(
-                held.at[i, w],
-                out_refs[w].at[pl.ds(pl.multiple_of(places[i], block_rows), block_rows)],
-                out_sems.at[i, w],
-            )
-            for i, w in pieces
-        ]
+        into, out_of = [], []
+        for p, (block, entry, output, shift, flip) in enumerate(pieces):
+            source = lax.rem(ctx + (ctx_count - shift), ctx_count) * core_count + lax.rem(
+                core + (core_count - flip), core_count
+            )
+            place = pl.ds(pl.multiple_of(source * block_rows, block_rows), block_rows)
+            into.append(
+                pltpu.make_async_copy(in_refs[block].at[entry], held.at[p], in_sems.at[p])
+            )
+            out_of.append(
+                pltpu.make_async_copy(held.at[p], out_refs[output].at[place], out_sems.at[p])
+            )
         for copy in into:
             copy.start()
-        for p in range(len(pieces)):
+        for p in range(total):
             into[p].wait()
             out_of[p].start()
         for copy in out_of:
@@ -149,16 +142,14 @@
         + [pl.BlockSpec(memory_space=pltpu.HBM)] * len(filled),
         out_specs=(pl.BlockSpec(memory_space=pltpu.HBM),) * arrays,
         scratch_shapes=[
-            pltpu.VMEM((count, arrays, block_rows, head_dim), blocks[0].dtype),
-            pltpu.SemaphoreType.DMA((count, arrays)),
-            pltpu.SemaphoreType.DMA((count, arrays)),
+            pltpu.VMEM((total, block_rows, head_dim), blocks[0].dtype),
+            pltpu.SemaphoreType.DMA((total,)),
+            pltpu.SemaphoreType.DMA((total,)),
         ],
         input_output_aliases={count + w: w for w in range(len(filled))},
         compiler_params=pltpu.CompilerParams(vmem_limit_bytes=VMEM_BYTES),
         cost_estimate=pl.CostEstimate(
-            flops=0,
-            transcendentals=0,
-            bytes_accessed=4 * count * arrays * block_rows * head_dim,
+            flops=0, transcendentals=0, bytes_accessed=4 * total * block_rows * head_dim
         ),
         name="assemble",
     )(*blocks, *filled)
@@ -177,6 +168,29 @@
         out_specs=whole,
         name="pair_tokens",
     )(first, second, in_hbm(after))
+
+
+def pack_products(products, wide, after):
+    rows = wide.shape[0]
+    widths = [x.shape[1] for x in products]
+
+    def kernel(*refs):
+        wide_ref, out_ref = refs[len(products)], refs[-1]
+        low = 0
+        for ref, columns in zip(refs, widths):
+            out_ref[:, low : low + columns] = ref[:rows] + ref[rows:]
+            low += columns
+        squares = jnp.sum(wide_ref[...] * wide_ref[...], axis=1, keepdims=True)
+        out_ref[:, low:] = jnp.broadcast_to(squares, (rows, LANES))
+
+    whole = pl.BlockSpec(memory_space=pltpu.VMEM)
+    return pl.pallas_call(
+        kernel,
+        out_shape=jax.ShapeDtypeStruct((rows, sum(widths) + LANES), jnp.float32),
+        in_specs=[whole] * (len(products) + 1) + [pl.BlockSpec(memory_space=pl.ANY)] * len(after),
+        out_specs=whole,
+        name="pack_products",
+    )(*products, wide, *after)
 
 
 def attend_shard(queries, keys, values, lengths, score_factor, after):
@@ -259,10 +273,12 @@
     sub_index = lax.axis_index("sub")
     take = functools.partial(jnp.take, mode="clip")
 
+    both = (0, 1)
     received = {}
 
-    def hand_off(shift, flip, after=()):
-        block = made = arrange((key_cache, value_cache), owner_order, shift, flip, after)
+    def hand_off(which, shift, flip, after=()):
+        caches = [(key_cache, value_cache)[w] for w in which]
+        block = made = arrange(caches, owner_order, shift, flip, after)
         if shift or flip:
             pairs = [
                 (
@@ -273,7 +289,7 @@
                 for s in range(sub_count)
             ]
             block = lax.ppermute(made, ("ctx", "sub"), pairs)
-        received[shift, flip] = block
+        received[which, shift, flip] = block
         return made
 
     def sum_shifted(values, combine):
@@ -288,7 +304,8 @@
         )
 
     middle = ctx_count // 2
-    leading = hand_off(middle, 0)
+    ahead = ((0,), 1, 0)
+    leading = hand_off(*ahead)
 
     query_width = w_query.shape[1]
     key_width = w_key.shape[1]
@@ -303,24 +320,20 @@
     upper = lax.reduce_precision(gained, 8, 7)
     lower = gained - upper
     halves = jnp.concatenate([upper, lower]).astype(jnp.bfloat16)
-    products = jnp.concatenate(
+    partial = pack_products(
         [
             jnp.dot(halves, weight, preferred_element_type=jnp.float32)
             for weight in (w_query, w_key, w_value)
         ],
-        axis=1,
-    )
-    squares = jnp.sum(wide * wide, axis=1, keepdims=True)
-    partial = jnp.concatenate(
-        [
-            products[: 2 * requests] + products[2 * requests :],
-            jnp.broadcast_to(squares, (2 * requests, LANES)),
-        ],
-        axis=1,
+        wide,
+        (received[ahead],),
     )
     summed = sum_shifted(partial, lambda parts: functools.reduce(jnp.add, parts))
-    hand_off(middle, 1, (partial,))
-    hand_off(0, 0, (summed,))
+    first = (both, middle, 0)
+    second = (both, 1, 1)
+    hand_off(*first, (summed,))
+    hand_off(*second, (summed,))
+    hand_off(both, 0, 0, (summed,))
     raw = summed[:, :-LANES] * lax.rsqrt(summed[:, -LANES:][:, :1] / width + eps_norm)
     raw = raw.reshape(requests, 2, -1, head_dim)
     positions = lengths.astype(jnp.float32)[:, None] + jnp.arange(2, dtype=jnp.float32)
@@ -342,7 +355,7 @@
         value_cache,
         lengths,
         score_factor,
-        (received[middle, 0],),
+        (),
     )
 
     own_rows = heads_decode * per_head
@@ -386,17 +399,17 @@
     stats = send_form(*kept)
     gathered = unpack(sum_shifted(stats, jnp.stack))
     sums, maxima, totals = merge(*gathered)
-    queue = [
-        (shift, flip)
-        for shift in range(1, ctx_count)
+    third = (both, middle, 1)
+    hand_off(*third, (stats, received[second]))
+    rest = [
+        (both, shift, flip)
+        for shift in range(2, ctx_count)
         for flip in range(sub_count)
         if shift != middle
-    ]
-    ahead = [(middle, 0), (middle, 1)]
-    hand_off(*queue[0], (stats,))
-    for key, earlier in zip(queue[1:], ahead + queue):
-        hand_off(*key, (stats, received[earlier]))
-    hand_off(0, 1, (stats, received[middle, 1]))
+    ] + [((1,), 1, 0)]
+    for key in rest:
+        hand_off(*key, (stats, received[first]))
+    hand_off(both, 0, 1, (stats, received[first]))
 
     grouped = own_queries.reshape(requests, heads_decode, 2, group_size, head_dim).astype(
         jnp.float32
@@ -435,16 +448,14 @@
     result = (residual + jnp.sum(parts, axis=0)).astype(jnp.bfloat16)
 
     moved = ()
-    for keys in (
-        [(0, 0), (0, 1)] + ahead,
-        queue[:-2],
-        queue[-2:],
-    ):
-        moved = assemble(
-            [received[key] for key in keys],
-            keys,
-            moved,
-        )
+    groups = [[ahead, (both, 0, 0), (both, 0, 1), first, second], [third] + rest]
+    for keys in groups:
+        pieces = [
+            (block, entry, output, shift, flip)
+            for block, (which, shift, flip) in enumerate(keys)
+            for entry, output in enumerate(which)
+        ]
+        moved = assemble([received[key] for key in keys], pieces, moved)
     moved_keys, moved_values = (x.reshape(1, -1, heads_decode, head_dim) for x in moved)
     return (moved_keys, moved_values, result[:, 0], result[:, 1])
 

time: 228 us -> 257 us (1.13)
  the two profiles are of different devices: /device:TPU:0 before, /device:TPU:13 now
where the time goes in v5:
time: 257 us; the launch traced here: 256 us
  waiting for transfers between devices  148 us (58%)
  Pallas kernels  43 us (17%)
  starting transfers between devices  16.9 us (7%)
  blocking collectives  13.7 us (5%)
  matrix products  12.9 us (5%)
  other arithmetic  12.6 us (5%)
  local copies, waits for them, and re-layouts  8.28 us (3%)
    ppermute x6, waiting for transfers between devices, sum_shifted(): lax.ppermute(values, 'ctx', [(c, (c + shift) % ctx_count) for c in range(...  75.8 us
    ppermute x8, waiting for transfers between devices, hand_off(): block = lax.ppermute(made, ('ctx', 'sub'), pairs)  72 us
    pallas_call x9, Pallas kernels, arrange(): pl.pallas_call(kernel, out_shape=pltpu.HBM((count, shard_length, heads_de...  28.1 us
    ppermute x8, starting transfers between devices, hand_off(): block = lax.ppermute(made, ('ctx', 'sub'), pairs)  10.7 us
    dot_general x3, matrix products, local(): jnp.dot(halves, weight, preferred_element_type=jnp.float32)  8.18 us
    pallas_call x1, Pallas kernels, attend_shard(): pl.pallas_call(kernel, out_shape=(result, result, result), grid_spec=pltp...  7.02 us
    ppermute x6, starting transfers between devices, sum_shifted(): lax.ppermute(values, 'ctx', [(c, (c + shift) % ctx_count) for c in range(...  6.02 us
    all_gather x1, blocking collectives, local(): lax.all_gather(pair_tokens(first_tokens, second_tokens, leading), ('head'...  5.98 us
  transfers between devices with their start and end apart: 15, of which 8 were waited for; matrix products, arithmetic and copies ran while one was open for 12% of the time, Pallas kernels for 8%

profile of v5, /device:TPU:13, one launch (start us, length us, event | category | flops | bytes accessed | tf_op | source)
XLA Modules:
  0.0 256.4 jit_solution(11999729706843199099)
XLA Ops:
  0.7 0.7 copy-done.4
  1.4 2.8 %arrange.9 = bf16[1,1024,2,128]{3,2,1,0:T(2,128)(2,1)} custom-call(s32[4]{0:T(128)S(1)} %copy-done.4, bf16[4,1024,4,128]{3,2,1,0:T(4,128)(2,1)} %refs_0_.17), custom_call_target="tpu_custom_call" | custom-call | bytes 1572864 | tf_op jit(solution)/shard_map/arrange/pallas_call | solution.py:79
  4.2 1.3 collective-permute-start
  5.5 1.3 pad_clamp_fusion
  6.8 1.3 dynamic_slice.30
  8.1 0.7 convert_element_type.51
  8.8 0.7 convert_element_type.50
  9.5 1.3 pair_tokens.1
  10.8 6.0 %all_gather.9 = bf16[4,2,2048]{2,1,0:T(2,128)(2,1)S(1)} all-gather(bf16[1,2,2048]{2,1,0:T(2,128)(2,1)} %pair_tokens.1), channel_id=1, replica_groups=mesh['groups'=2,'ctx'=4,'head'=2,'sub'=2] {'head','sub'}, dimensions={0}, use_global_device_ids=true | all-gather | bytes 40960 | tf_op jit(solution)/shard_map/all_gather | solution.py:315
  16.9 0.9 fusion.8.refs_1_
  17.7 2.1 fusion.7.refs_2_
  19.9 5.2 %fusion.9.refs_0_ = f32[16,2048]{1,0:T(8,128)} fusion(bf16[2048,2048]{1,0:T(8,128)(2,1)} %param.18, bf16[8,2048]{1,0:T(8,128)(2,1)S(1)} %get-tuple-element.46, bf16[8,2048]{1,0:T(8,128)(2,1)S(1)} %get-tuple-element.45), kind=kOutput, calls=%fused_computation.34 | convolution fusion | flops 134348800 | bytes 8585216 | tf_op jit(solution)/shard_map/dot_general | solution.py:325
  25.2 0.8 copy-done.2
  26.0 1.7 pack_products.1
  27.6 0.2 collective-permute-start.3
  27.8 2.3 collective-permute-start.2
  30.1 0.8 collective-permute-start.1
  31.0 0.5 iota_compare_fusion
  31.5 0.4 collective-permute-done.3
  31.8 4.0 %collective-permute-done.2 = f32[8,2688]{1,0:T(8,128)S(1)} collective-permute-done((f32[8,2688]{1,0:T(8,128)}, f32[8,2688]{1,0:T(8,128)S(1)}, u32[]{:S(2)}, u32[]{:S(2)}) %collective-permute-start.2) | collective-permute-done | bytes 86048 | tf_op jit(solution)/shard_map/ppermute | solution.py:299
  35.8 1.8 collective-permute-done.1
  37.6 0.9 add_add_fusion.refs_2_
  39.1 3.4 %arrange.16 = bf16[2,1024,2,128]{3,2,1,0:T(2,128)(2,1)} custom-call(s32[4]{0:T(128)S(1)} %copy-done.5, bf16[4,1024,4,128]{3,2,1,0:T(4,128)(2,1)} %refs_0_.17, bf16[4,1024,4,128]{3,2,1,0:T(4,128)(2,1)} %refs_1_.13, f32[8,2688]{1,0:T(8,128)S(1)} %add_add_fusion.refs_2_), custom_call_target="tpu_custom_call" | custom-call | bytes 3145728 | tf_op jit(solution)/shard_map/arrange/pallas_call | solution.py:79
  42.5 3.4 %arrange.12 = bf16[2,1024,2,128]{3,2,1,0:T(2,128)(2,1)} custom-call(s32[4]{0:T(128)S(1)} %copy-done.5, bf16[4,1024,4,128]{3,2,1,0:T(4,128)(2,1)} %refs_0_.17, bf16[4,1024,4,128]{3,2,1,0:T(4,128)(2,1)} %refs_1_.13, f32[8,2688]{1,0:T(8,128)S(1)} %add_add_fusion.refs_2_), custom_call_target="tpu_custom_call" | custom-call | bytes 3145728 | tf_op jit(solution)/shard_map/arrange/pallas_call | solution.py:79
  46.0 3.1 %arrange.10 = bf16[2,1024,2,128]{3,2,1,0:T(2,128)(2,1)} custom-call(s32[4]{0:T(128)S(1)} %copy-done.5, bf16[4,1024,4,128]{3,2,1,0:T(4,128)(2,1)} %refs_0_.17, bf16[4,1024,4,128]{3,2,1,0:T(4,128)(2,1)} %refs_1_.13, f32[8,2688]{1,0:T(8,128)S(1)} %add_add_fusion.refs_2_), custom_call_target="tpu_custom_call" | custom-call | bytes 3145728 | tf_op jit(solution)/shard_map/arrange/pallas_call | solution.py:79
  49.0 0.6 copy.41
  49.6 1.8 all_gather.10.q_ref
  51.5 7.0 %attend_shard.1 = (f32[4,64,128]{2,1,0:T(8,128)S(1)}, f32[4,64,128]{2,1,0:T(8,128)S(1)}, f32[4,64,128]{2,1,0:T(8,128)S(1)}) custom-call(s32[4]{0:T(128)S(1)} %copy-done.6, bf16[4,64,128]{2,1,0:T(8,128)(2,1)S(1)} %all_gather.10.q_ref, bf16[4,4096,128]{2,1,0:T(8,128)(2,1)} %bitcast.61, bf16[4,4096,128]{2,1,0:T(8,128)(2,1)} %bitcast.62), custom_call_target="tpu_custom_call" | custom-call | flops 536870912 | bytes 8388608 | tf_op jit(solution)/shard_map/attend_shard/pallas_call | solution.py:234
  59.0 0.2 collective-permute-start.4
  59.2 2.3 collective-permute-start.5
  61.5 1.2 collective-permute-start.7
  63.4 1.2 collective-permute-start.13
  64.6 1.5 collective-permute-start.14
  66.1 0.7 fusion.11
  66.8 67.0 %collective-permute-done.13 = f32[130,128]{1,0:T(8,128)S(1)} collective-permute-done((f32[130,128]{1,0:T(8,128)S(1)}, f32[130,128]{1,0:T(8,128)S(1)}, u32[]{:S(2)}, u32[]{:S(2)}) %collective-permute-start.13) | collective-permute-done | bytes 66592 | tf_op jit(solution)/shard_map/ppermute | solution.py:299
  133.8 1.5 collective-permute-done.12
  135.3 1.1 collective-permute-done.14
  136.4 1.1 fusion.24
  137.5 1.4 reshape.283
  138.9 1.3 fusion.17
  140.2 1.4 reshape.284
  141.5 0.7 copy_maximum_fusion
  142.2 0.7 fusion.21
  142.9 0.7 copy_add_fusion
  143.7 0.7 subtract_exponential_fusion.1
  144.5 0.8 multiply_reduce_fusion
  145.4 0.7 gather_fusion
  146.2 3.1 %arrange.11 = bf16[2,1024,2,128]{3,2,1,0:T(2,128)(2,1)} custom-call(s32[4]{0:T(128)S(1)} %copy-done.5, bf16[4,1024,4,128]{3,2,1,0:T(4,128)(2,1)} %refs_0_.17, bf16[4,1024,4,128]{3,2,1,0:T(4,128)(2,1)} %refs_1_.13, f32[130,128]{1,0:T(8,128)S(1)} %get-tuple-element.50.refs_2_.refs_1_, bf16[2,2048,128]{2,1,0:T(8,128)(2,1)S(1)} %collective-permute-done.5.refs_3_.refs_4_), custom_call_target="tpu_custom_call" | custom-call | bytes 3145728 | tf_op jit(solution)/shard_map/arrange/pallas_call | solution.py:79
  149.2 1.9 collective-permute-start.6
  151.1 3.4 %arrange.13 = bf16[2,1024,2,128]{3,2,1,0:T(2,128)(2,1)} custom-call(s32[4]{0:T(128)S(1)} %copy-done.5, bf16[4,1024,4,128]{3,2,1,0:T(4,128)(2,1)} %refs_0_.17, bf16[4,1024,4,128]{3,2,1,0:T(4,128)(2,1)} %refs_1_.13, f32[130,128]{1,0:T(8,128)S(1)} %get-tuple-element.50.refs_2_.refs_1_, bf16[2,2048,128]{2,1,0:T(8,128)(2,1)S(1)} %collective-permute-done.7.refs_3_.refs_2_), custom_call_target="tpu_custom_call" | custom-call | bytes 3145728 | tf_op jit(solution)/shard_map/arrange/pallas_call | solution.py:79
  154.6 1.5 collective-permute-start.8
  156.1 3.1 %arrange.14 = bf16[2,1024,2,128]{3,2,1,0:T(2,128)(2,1)} custom-call(s32[4]{0:T(128)S(1)} %copy-done.5, bf16[4,1024,4,128]{3,2,1,0:T(4,128)(2,1)} %refs_0_.17, bf16[4,1024,4,128]{3,2,1,0:T(4,128)(2,1)} %refs_1_.13, f32[130,128]{1,0:T(8,128)S(1)} %get-tuple-element.50.refs_2_.refs_1_, bf16[2,2048,128]{2,1,0:T(8,128)(2,1)S(1)} %collective-permute-done.7.refs_3_.refs_2_), custom_call_target="tpu_custom_call" | custom-call | bytes 3145728 | tf_op jit(solution)/shard_map/arrange/pallas_call | solution.py:79
  159.1 0.9 collective-permute-start.9
  160.0 3.1 %arrange.17 = bf16[2,1024,2,128]{3,2,1,0:T(2,128)(2,1)} custom-call(s32[4]{0:T(128)S(1)} %copy-done.5, bf16[4,1024,4,128]{3,2,1,0:T(4,128)(2,1)} %refs_0_.17, bf16[4,1024,4,128]{3,2,1,0:T(4,128)(2,1)} %refs_1_.13, f32[130,128]{1,0:T(8,128)S(1)} %get-tuple-element.50.refs_2_.refs_1_, bf16[2,2048,128]{2,1,0:T(8,128)(2,1)S(1)} %collective-permute-done.7.refs_3_.refs_2_), custom_call_target="tpu_custom_call" | custom-call | bytes 3145728 | tf_op jit(solution)/shard_map/arrange/pallas_call | solution.py:79
  163.1 1.5 collective-permute-start.11
  164.6 4.7 %fusion = f32[4,2,2048]{2,1,0:T(2,128)S(1)} fusion(bf16[4,2,2048]{2,1,0:T(2,128)(2,1)S(1)} %reshape.322, bf16[2048,2048]{1,0:T(8,128)(2,1)} %param.21), kind=kOutput, calls=%fused_computation.1 | convolution fusion | flops 67108864 | bytes 8486912 | tf_op jit(solution)/shard_map/dot_general | solution.py:441
  169.3 5.9 %all-gather = f32[16,2,2048]{2,1,0:T(2,128)S(1)} all-gather(f32[4,2,2048]{2,1,0:T(2,128)S(1)} %fusion), channel_id=2, replica_groups=mesh['groups'=2,'ctx'=4,'head'=2,'sub'=2] {'head','sub'}, dimensions={0}, use_global_device_ids=true | all-gather | bytes 327680 | tf_op jit(solution)/shard_map/all_gather | solution.py:444
  175.2 2.8 %arrange.15 = bf16[1,1024,2,128]{3,2,1,0:T(2,128)(2,1)} custom-call(s32[4]{0:T(128)S(1)} %copy-done.5, bf16[4,1024,4,128]{3,2,1,0:T(4,128)(2,1)} %refs_1_.13, f32[130,128]{1,0:T(8,128)S(1)} %get-tuple-element.50.refs_2_.refs_1_, bf16[2,2048,128]{2,1,0:T(8,128)(2,1)S(1)} %collective-permute-done.7.refs_3_.refs_2_), custom_call_target="tpu_custom_call" | custom-call | bytes 1572864 | tf_op jit(solution)/shard_map/arrange/pallas_call | solution.py:79
  178.1 0.6 fusion.10
  178.7 0.6 slice_bitcast_fusion
  179.4 2.7 %assemble.2 = (bf16[16384,128]{1,0:T(8,128)(2,1)}, bf16[16384,128]{1,0:T(8,128)(2,1)}) custom-call(bf16[1,2048,128]{2,1,0:T(8,128)(2,1)S(1)} %copy-done.3, bf16[2,2048,128]{2,1,0:T(8,128)(2,1)S(1)} %bitcast.60, bf16[2,2048,128]{2,1,0:T(8,128)(2,1)S(1)} %collective-permute-done.11.refs_2_, bf16[2,2048,128]{2,1,0:T(8,128)(2,1)S(1)} %collective-permute-done.7.refs_3_.refs_2_, ...), custom_call_target="tpu_custom_call" | custom-call | bytes 9437184 | tf_op jit(solution)/shard_map/assemble/pallas_call | solution.py:138
  182.1 70.8 %collective-permute-done.10.refs_3_ = bf16[1,2048,128]{2,1,0:T(8,128)(2,1)S(1)} collective-permute-done((bf16[1,2048,128]{2,1,0:T(8,128)(2,1)}, bf16[1,2048,128]{2,1,0:T(8,128)(2,1)S(1)}, u32[]{:S(2)}, u32[]{:S(2)}) %collective-permute-start.10) | collective-permute-done | bytes 524320 | tf_op jit(solution)/shard_map/ppermute | solution.py:291
  252.8 1.2 collective-permute-done.9.refs_2_
  254.0 2.2 assemble.3
  (62 shorter events, 2.2 us)
Async XLA Ops:
  0.6 16.2 %copy-start = (bf16[2048,256]{1,0:T(8,128)(2,1)S(1)}, bf16[2048,256]{1,0:T(8,128)(2,1)}, u32[]{:S(2)}) copy-start(bf16[2048,256]{1,0:T(8,128)(2,1)} %param.19) | copy-start | bytes 3145732
  0.6 0.7 copy-start.4
  4.2 21.0 %collective-permute-start = (bf16[1,2048,128]{2,1,0:T(8,128)(2,1)}, bf16[1,2048,128]{2,1,0:T(8,128)(2,1)S(1)}, u32[]{:S(2)}, u32[]{:S(2)}) collective-permute-start(bf16[1,2048,128]{2,1,0:T(8,128)(2,1)} %bitcast.65), channel_id=1, source_target_pairs={{0,4},{1,5},{4,8},{5,9},{8,12},{9,13},{12,0},{13,1},{2,6},{3,7},{6... | collective-permute-start | bytes 1572872 | tf_op jit(solution)/shard_map/ppermute | solution.py:291
  16.8 8.4 %copy-start.7 = (f32[8,2048]{1,0:T(8,128)}, f32[8,2048]{1,0:T(8,128)S(1)}, u32[]{:S(2)}) copy-start(f32[8,2048]{1,0:T(8,128)S(1)} %reshape.308.refs_3_) | copy-start | bytes 196612
  19.9 19.1 %copy-start.5 = (s32[4]{0:T(128)S(1)}, s32[4]{0:T(128)}, u32[]{:S(2)}) copy-start(s32[4]{0:T(128)} %order_ref.17) | copy-start | bytes 52
  25.2 0.8 copy-start.2
  27.6 4.2 %collective-permute-start.3 = (f32[8,2688]{1,0:T(8,128)}, f32[8,2688]{1,0:T(8,128)S(1)}, u32[]{:S(2)}, u32[]{:S(2)}) collective-permute-start(f32[8,2688]{1,0:T(8,128)} %pack_products.1), channel_id=1, source_target_pairs={{0,12},{4,0},{8,4},{12,8},{1,13},{5,1},{9,5},{13,9},{2,14},{6,2},{... | collective-permute-start | bytes 258056 | tf_op jit(solution)/shard_map/ppermute | solution.py:299
  27.8 8.0 %collective-permute-start.2 = (f32[8,2688]{1,0:T(8,128)}, f32[8,2688]{1,0:T(8,128)S(1)}, u32[]{:S(2)}, u32[]{:S(2)}) collective-permute-start(f32[8,2688]{1,0:T(8,128)} %pack_products.1), channel_id=1, source_target_pairs={{0,8},{4,12},{8,0},{12,4},{1,9},{5,13},{9,1},{13,5},{2,10},{6,14},... | collective-permute-start | bytes 258056 | tf_op jit(solution)/shard_map/ppermute | solution.py:299
  30.1 7.5 %collective-permute-start.1 = (f32[8,2688]{1,0:T(8,128)}, f32[8,2688]{1,0:T(8,128)S(1)}, u32[]{:S(2)}, u32[]{:S(2)}) collective-permute-start(f32[8,2688]{1,0:T(8,128)} %pack_products.1), channel_id=1, source_target_pairs={{0,4},{4,8},{8,12},{12,0},{1,5},{5,9},{9,13},{13,1},{2,6},{6,10},{... | collective-permute-start | bytes 258056 | tf_op jit(solution)/shard_map/ppermute | solution.py:299
  42.5 9.0 %copy-start.6 = (s32[4]{0:T(128)S(1)}, s32[4]{0:T(128)}, u32[]{:S(2)}) copy-start(s32[4]{0:T(128)} %lengths_ref.1) | copy-start | bytes 52
  59.0 3.9 %collective-permute-start.4 = (f32[130,128]{1,0:T(8,128)S(1)}, f32[130,128]{1,0:T(8,128)S(1)}, u32[]{:S(2)}, u32[]{:S(2)}) collective-permute-start(f32[130,128]{1,0:T(8,128)S(1)} %pad_maximum_fusion.1), channel_id=1, source_target_pairs={{0,1},{1,0},{2,3},{3,2},{4,5},{5,4},{6,7},{7,6},{8,9},{9,8},{10,11... | collective-permute-start | bytes 199688 | tf_op jit(solution)/shard_map/ppermute | solution.py:397
  59.2 87.0 %collective-permute-start.5 = (bf16[2,2048,128]{2,1,0:T(8,128)(2,1)}, bf16[2,2048,128]{2,1,0:T(8,128)(2,1)S(1)}, u32[]{:S(2)}, u32[]{:S(2)}) collective-permute-start(bf16[2,2048,128]{2,1,0:T(8,128)(2,1)} %bitcast.10), channel_id=1, source_target_pairs={{0,5},{1,4},{4,9},{5,8},{8,13},{9,12},{12,1},{13,0},{2,7},{3,6},{6... | collective-permute-start | bytes 3145736 | tf_op jit(solution)/shard_map/ppermute | solution.py:291
  61.5 89.6 %collective-permute-start.7 = (bf16[2,2048,128]{2,1,0:T(8,128)(2,1)}, bf16[2,2048,128]{2,1,0:T(8,128)(2,1)S(1)}, u32[]{:S(2)}, u32[]{:S(2)}) collective-permute-start(bf16[2,2048,128]{2,1,0:T(8,128)(2,1)} %bitcast.67), channel_id=1, source_target_pairs={{0,8},{1,9},{4,12},{5,13},{8,0},{9,1},{12,4},{13,5},{2,10},{3,11},... | collective-permute-start | bytes 3145736 | tf_op jit(solution)/shard_map/ppermute | solution.py:291
  63.4 70.4 %collective-permute-start.13 = (f32[130,128]{1,0:T(8,128)S(1)}, f32[130,128]{1,0:T(8,128)S(1)}, u32[]{:S(2)}, u32[]{:S(2)}) collective-permute-start(f32[130,128]{1,0:T(8,128)S(1)} %get-tuple-element.50.refs_2_.refs_1_), channel_id=1, source_target_pairs={{0,8},{4,12},{8,0},{12,4},{1,9},{5,13},{9,1},{13,5},{2,10},{6,14},... | collective-permute-start | bytes 199688 | tf_op jit(solution)/shard_map/ppermute | solution.py:299
  64.6 70.7 %collective-permute-start.12 = (f32[130,128]{1,0:T(8,128)S(1)}, f32[130,128]{1,0:T(8,128)S(1)}, u32[]{:S(2)}, u32[]{:S(2)}) collective-permute-start(f32[130,128]{1,0:T(8,128)S(1)} %get-tuple-element.50.refs_2_.refs_1_), channel_id=1, source_target_pairs={{0,4},{4,8},{8,12},{12,0},{1,5},{5,9},{9,13},{13,1},{2,6},{6,10},{... | collective-permute-start | bytes 199688 | tf_op jit(solution)/shard_map/ppermute | solution.py:299
  64.6 71.8 %collective-permute-start.14 = (f32[130,128]{1,0:T(8,128)S(1)}, f32[130,128]{1,0:T(8,128)S(1)}, u32[]{:S(2)}, u32[]{:S(2)}) collective-permute-start(f32[130,128]{1,0:T(8,128)S(1)} %get-tuple-element.50.refs_2_.refs_1_), channel_id=1, source_target_pairs={{0,12},{4,0},{8,4},{12,8},{1,13},{5,1},{9,5},{13,9},{2,14},{6,2},{... | collective-permute-start | bytes 199688 | tf_op jit(solution)/shard_map/ppermute | solution.py:299
  149.2 103.6 %collective-permute-start.6 = (bf16[2,2048,128]{2,1,0:T(8,128)(2,1)}, bf16[2,2048,128]{2,1,0:T(8,128)(2,1)S(1)}, u32[]{:S(2)}, u32[]{:S(2)}) collective-permute-start(bf16[2,2048,128]{2,1,0:T(8,128)(2,1)} %bitcast.68), channel_id=1, source_target_pairs={{0,9},{1,8},{4,13},{5,12},{8,1},{9,0},{12,5},{13,4},{2,11},{3,10},... | collective-permute-start | bytes 3145736 | tf_op jit(solution)/shard_map/ppermute | solution.py:291
  154.6 98.2 %collective-permute-start.8 = (bf16[2,2048,128]{2,1,0:T(8,128)(2,1)}, bf16[2,2048,128]{2,1,0:T(8,128)(2,1)S(1)}, u32[]{:S(2)}, u32[]{:S(2)}) collective-permute-start(bf16[2,2048,128]{2,1,0:T(8,128)(2,1)} %bitcast.69), channel_id=1, source_target_pairs={{0,12},{1,13},{4,0},{5,1},{8,4},{9,5},{12,8},{13,9},{2,14},{3,15},... | collective-permute-start | bytes 3145736 | tf_op jit(solution)/shard_map/ppermute | solution.py:291
  159.1 94.9 %collective-permute-start.9 = (bf16[2,2048,128]{2,1,0:T(8,128)(2,1)}, bf16[2,2048,128]{2,1,0:T(8,128)(2,1)S(1)}, u32[]{:S(2)}, u32[]{:S(2)}) collective-permute-start(bf16[2,2048,128]{2,1,0:T(8,128)(2,1)} %bitcast.70), channel_id=1, source_target_pairs={{0,13},{1,12},{4,1},{5,0},{8,5},{9,4},{12,9},{13,8},{2,15},{3,14},... | collective-permute-start | bytes 3145736 | tf_op jit(solution)/shard_map/ppermute | solution.py:291
  163.1 16.3 %copy-start.1 = (bf16[2,1024,2,128]{3,2,1,0:T(2,128)(2,1)S(1)}, bf16[2,1024,2,128]{3,2,1,0:T(2,128)(2,1)}, u32[]{:S(2)}) copy-start(bf16[2,1024,2,128]{3,2,1,0:T(2,128)(2,1)} %arrange.16) | copy-start | bytes 3145732
  163.1 16.2 %copy-start.3 = (bf16[1,2048,128]{2,1,0:T(8,128)(2,1)S(1)}, bf16[1,2048,128]{2,1,0:T(8,128)(2,1)}, u32[]{:S(2)}) copy-start(bf16[1,2048,128]{2,1,0:T(8,128)(2,1)} %copy-done.2) | copy-start | bytes 1572868
  163.1 16.2 %collective-permute-start.11 = (bf16[2,2048,128]{2,1,0:T(8,128)(2,1)}, bf16[2,2048,128]{2,1,0:T(8,128)(2,1)S(1)}, u32[]{:S(2)}, u32[]{:S(2)}) collective-permute-start(bf16[2,2048,128]{2,1,0:T(8,128)(2,1)} %bitcast.71), channel_id=1, source_target_pairs={{0,1},{1,0},{4,5},{5,4},{8,9},{9,8},{12,13},{13,12},{2,3},{3,2},{6... | collective-permute-start | bytes 3145736 | tf_op jit(solution)/shard_map/ppermute | solution.py:291
  178.0 74.8 %collective-permute-start.10 = (bf16[1,2048,128]{2,1,0:T(8,128)(2,1)}, bf16[1,2048,128]{2,1,0:T(8,128)(2,1)S(1)}, u32[]{:S(2)}, u32[]{:S(2)}) collective-permute-start(bf16[1,2048,128]{2,1,0:T(8,128)(2,1)} %bitcast.81), channel_id=1, source_target_pairs={{0,4},{1,5},{4,8},{5,9},{8,12},{9,13},{12,0},{13,1},{2,6},{3,7},{6... | collective-permute-start | bytes 1572872 | tf_op jit(solution)/shard_map/ppermute | solution.py:291

commit v6 on v5

--- a/solution.py
+++ b/solution.py
@@ -90,11 +90,6 @@
             pltpu.SemaphoreType.DMA((count, steps)),
         ],
         compiler_params=pltpu.CompilerParams(vmem_limit_bytes=VMEM_BYTES),
-        cost_estimate=pl.CostEstimate(
-            flops=0,
-            transcendentals=0,
-            bytes_accessed=3 * count * shard_length * heads * head_dim,
-        ),
         name="arrange",
     )(owner_order, *(in_hbm(x) for x in caches), *after)
     return blocks.reshape(count, shard_length * heads_decode, head_dim)
@@ -193,20 +188,52 @@
     )(*products, wide, *after)
 
 
-def attend_shard(queries, keys, values, lengths, score_factor, after):
+def to_rows(column_form):
+    count = column_form.shape[0] // LANES
+    return jnp.concatenate(
+        [
+            jnp.sum(
+                jnp.where(diagonal(), column_form[i * LANES : (i + 1) * LANES], 0.0),
+                axis=0,
+                keepdims=True,
+            )
+            for i in range(count)
+        ]
+    )
+
+
+def to_columns(row_form):
+    return jnp.concatenate(
+        [
+            jnp.sum(
+                jnp.where(diagonal(), row_form[i : i + 1], 0.0), axis=1, keepdims=True
+            )
+            for i in range(row_form.shape[0])
+        ]
+    )
+
+
+def diagonal():
+    row = lax.broadcasted_iota(jnp.int32, (LANES, LANES), 0)
+    return row == lax.broadcasted_iota(jnp.int32, (LANES, LANES), 1)
+
+
+def attend_shard(queries, keys, values, lengths, score_factor):
     requests, shard_length, heads, head_dim = keys.shape
     rows = queries.shape[1]
+    own_rows = rows // 2
     per_head = rows // heads
     columns = shard_length * heads
+    count = requests * own_rows
+    extra = count // LANES
     flat_keys = keys.reshape(requests, columns, head_dim)
     flat_values = values.reshape(requests, columns, head_dim)
-
     core_count = lax.axis_size("sub")
 
-    def kernel(lengths_ref, q_ref, k_ref, v_ref, *refs):
-        acc_ref, max_ref, sum_ref = refs[len(after) :]
+    def kernel(lengths_ref, q_ref, k_ref, v_ref, kept_ref, sent_ref, max_scr, sum_scr):
         request = pl.program_id(0)
-        shard = lax.axis_index("ctx") * core_count + lax.axis_index("sub")
+        core = lax.axis_index("sub")
+        shard = lax.axis_index("ctx") * core_count + core
         scores = (
             lax.dot_general(
                 q_ref[0], k_ref[0], (((1,), (1,)), ((), ())), preferred_element_type=jnp.float32
@@ -220,35 +247,117 @@
         scores = jnp.where(live, scores, masked_score)
         row_max = jnp.max(scores, axis=1, keepdims=True)
         weights = jnp.where(live, jnp.exp(scores - row_max), 0.0)
-        acc_ref[0] = jnp.dot(
+        sums = jnp.dot(
             weights.astype(jnp.bfloat16), v_ref[0], preferred_element_type=jnp.float32
         )
-        max_ref[0] = jnp.broadcast_to(row_max, (rows, head_dim))
-        sum_ref[0] = jnp.broadcast_to(
-            jnp.sum(weights, axis=1, keepdims=True), (rows, head_dim)
-        )
-
-    small = pl.BlockSpec((1, rows, head_dim), lambda r, *_: (r, 0, 0))
+        row_max = jnp.broadcast_to(row_max, (rows, head_dim))
+        row_sum = jnp.broadcast_to(jnp.sum(weights, axis=1, keepdims=True), (rows, head_dim))
+        place = pl.ds(pl.multiple_of(request * own_rows, own_rows), own_rows)
+        first = core == 0
+        for f, out_ref in enumerate((kept_ref, sent_ref)):
+            low = first if f == 0 else jnp.logical_not(first)
+            pick = lambda x: jnp.where(low, x[:own_rows], x[own_rows:])
+            out_ref[place, :] = pick(sums)
+            max_scr[f, place, :] = pick(row_max)
+            sum_scr[f, place, :] = pick(row_sum)
+
+        @pl.when(request == requests - 1)
+        def _():
+            for f, out_ref in enumerate((kept_ref, sent_ref)):
+                out_ref[count : count + extra, :] = to_rows(max_scr[f])
+                out_ref[count + extra :, :] = to_rows(sum_scr[f])
+
     large = pl.BlockSpec((1, columns, head_dim), lambda r, *_: (r, 0, 0))
-    result = jax.ShapeDtypeStruct((requests, rows, head_dim), jnp.float32)
+    packed = (count + 2 * extra, head_dim)
     return pl.pallas_call(
         kernel,
-        out_shape=(result, result, result),
+        out_shape=(jax.ShapeDtypeStruct(packed, jnp.float32),) * 2,
         grid_spec=pltpu.PrefetchScalarGridSpec(
             num_scalar_prefetch=1,
             grid=(requests,),
-            in_specs=[small, large, large]
-            + [pl.BlockSpec(memory_space=pl.ANY)] * len(after),
-            out_specs=(small, small, small),
+            in_specs=[
+                pl.BlockSpec((1, rows, head_dim), lambda r, *_: (r, 0, 0)),
+                large,
+                large,
+            ],
+            out_specs=(pl.BlockSpec(packed, lambda r, *_: (0, 0)),) * 2,
+            scratch_shapes=[pltpu.VMEM((2, count, head_dim), jnp.float32)] * 2,
         ),
         compiler_params=pltpu.CompilerParams(vmem_limit_bytes=VMEM_BYTES),
-        cost_estimate=pl.CostEstimate(
-            flops=4 * requests * rows * columns * head_dim,
-            transcendentals=requests * rows * columns,
-            bytes_accessed=4 * keys.size,
-        ),
         name="attend_shard",
-    )(lengths, queries, in_hbm(flat_keys), in_hbm(flat_values), *after)
+    )(lengths, queries, in_hbm(flat_keys), in_hbm(flat_values))
+
+
+def packed_sizes(packed_rows):
+    extra = packed_rows // (LANES + 2)
+    return extra * LANES, extra
+
+
+def merge_packed(kept, other, after):
+    count, extra = packed_sizes(kept.shape[0])
+
+    def kernel(kept_ref, other_ref, *refs):
+        out_ref = refs[-1]
+        both = (kept_ref, other_ref)
+        maxima = [ref[count : count + extra, :] for ref in both]
+        largest = jnp.maximum(*maxima)
+        scales = [jnp.exp(x - largest) for x in maxima]
+        out_ref[:count, :] = sum(
+            ref[:count, :] * to_columns(scale) for ref, scale in zip(both, scales)
+        )
+        out_ref[count : count + extra, :] = largest
+        out_ref[count + extra :, :] = sum(
+            ref[count + extra :, :] * scale for ref, scale in zip(both, scales)
+        )
+
+    whole = pl.BlockSpec(memory_space=pltpu.VMEM)
+    return pl.pallas_call(
+        kernel,
+        out_shape=jax.ShapeDtypeStruct(kept.shape, kept.dtype),
+        in_specs=[whole] * 2 + [pl.BlockSpec(memory_space=pl.ANY)] * len(after),
+        out_specs=whole,
+        name="merge_packed",
+    )(kept, other, *after)
+
+
+def finish(packed, queries, fresh_keys, fresh_values, group_size, score_factor, after):
+    count, extra = packed_sizes(packed[0].shape[0])
+    shares = len(packed)
+    head_dim = queries.shape[1]
+
+    def kernel(*refs):
+        out_ref = refs[-1]
+        packed_refs = refs[:shares]
+        q_ref, key_ref, value_ref = refs[shares : shares + 3]
+        wide = q_ref[...].astype(jnp.float32)
+        row = lax.broadcasted_iota(jnp.int32, (count, 1), 0)
+        second = lax.rem(lax.div(row, group_size), 2) == 1
+        scores = [
+            jnp.sum(wide * key_ref[u].astype(jnp.float32), axis=1, keepdims=True) * score_factor
+            for u in range(2)
+        ]
+        scores[1] = jnp.where(second, scores[1], masked_score)
+        maxima = [to_columns(ref[count : count + extra, :]) for ref in packed_refs]
+        totals = [to_columns(ref[count + extra :, :]) for ref in packed_refs]
+        largest = functools.reduce(jnp.maximum, maxima + scores)
+        scales = [jnp.exp(x - largest) for x in maxima]
+        weights = [jnp.exp(x - largest) for x in scores]
+        weights[1] = jnp.where(second, weights[1], 0.0)
+        denominator = sum(t * scale for t, scale in zip(totals, scales)) + weights[0] + weights[1]
+        numerator = sum(ref[:count, :] * scale for ref, scale in zip(packed_refs, scales))
+        for u in range(2):
+            rounded = weights[u].astype(jnp.bfloat16).astype(jnp.float32)
+            numerator = numerator + rounded * value_ref[u].astype(jnp.float32)
+        out_ref[...] = (numerator / denominator).astype(jnp.bfloat16)
+
+    whole = pl.BlockSpec(memory_space=pltpu.VMEM)
+    return pl.pallas_call(
+        kernel,
+        out_shape=jax.ShapeDtypeStruct((count, head_dim), jnp.bfloat16),
+        in_specs=[whole] * (shares + 3) + [pl.BlockSpec(memory_space=pl.ANY)] * len(after),
+        out_specs=whole,
+        name="finish",
+    )(*packed, queries, fresh_keys, fresh_values, *after)
 
 
 def local(
@@ -292,19 +401,14 @@
         received[which, shift, flip] = block
         return made
 
-    def sum_shifted(values, combine):
-        return combine(
-            [values]
-            + [
-                lax.ppermute(
-                    values, "ctx", [(c, (c + shift) % ctx_count) for c in range(ctx_count)]
-                )
-                for shift in range(1, ctx_count)
-            ]
-        )
+    def from_all(values):
+        return [values] + [
+            lax.ppermute(values, "ctx", [(c, (c + shift) % ctx_count) for c in range(ctx_count)])
+            for shift in range(1, ctx_count)
+        ]
 
     middle = ctx_count // 2
-    ahead = ((0,), 1, 0)
+    ahead = (both, 1, 0)
     leading = hand_off(*ahead)
 
     query_width = w_query.shape[1]
@@ -328,12 +432,9 @@
         wide,
         (received[ahead],),
     )
-    summed = sum_shifted(partial, lambda parts: functools.reduce(jnp.add, parts))
-    first = (both, middle, 0)
-    second = (both, 1, 1)
-    hand_off(*first, (summed,))
-    hand_off(*second, (summed,))
-    hand_off(both, 0, 0, (summed,))
+    summed = functools.reduce(jnp.add, from_all(partial))
+    behind = (both, 1, 1)
+    hand_off(*behind, (summed,))
     raw = summed[:, :-LANES] * lax.rsqrt(summed[:, -LANES:][:, :1] / width + eps_norm)
     raw = raw.reshape(requests, 2, -1, head_dim)
     positions = lengths.astype(jnp.float32)[:, None] + jnp.arange(2, dtype=jnp.float32)
@@ -349,92 +450,36 @@
         requests, heads_decode * per_head, head_dim
     )
     all_queries = lax.all_gather(own_queries, "sub", axis=1, tiled=True)
-    sums, maxima, totals = attend_shard(
-        all_queries,
-        key_cache,
-        value_cache,
-        lengths,
-        score_factor,
-        (),
-    )
-
-    own_rows = heads_decode * per_head
-
-    def pack(core):
-        part = lambda x: lax.dynamic_slice_in_dim(x, core * own_rows, own_rows, 1)
-        return (part(sums), part(maxima)[:, :, 0], part(totals)[:, :, 0])
-
-    def send_form(sums, maxima, totals):
-        return jnp.concatenate(
-            [x.reshape(-1, head_dim) for x in (sums, maxima, totals)], axis=0
-        )
-
-    count = requests * own_rows
-    extra = count // head_dim
-
-    def unpack(packed):
-        lead = packed.shape[:-2]
-        shape = lead + (requests, own_rows)
-        return (
-            packed[..., :count, :].reshape(shape + (head_dim,)),
-            packed[..., count : count + extra, :].reshape(shape),
-            packed[..., count + extra :, :].reshape(shape),
-        )
-
-    def merge(sums, maxima, totals):
-        largest = jnp.max(maxima, axis=0)
-        scale = jnp.exp(maxima - largest)
-        return (
-            jnp.sum(sums * scale[..., None], axis=0),
-            largest,
-            jnp.sum(totals * scale, axis=0),
-        )
-
-    kept = pack(sub_index)
-    for shift in range(1, sub_count):
-        pairs = [(i, (i + shift) % sub_count) for i in range(sub_count)]
-        sent = send_form(*pack(lax.rem(sub_index + shift, sub_count)))
-        other = unpack(lax.ppermute(sent, "sub", pairs))
-        kept = merge(*(jnp.stack([a, b]) for a, b in zip(kept, other)))
-    stats = send_form(*kept)
-    gathered = unpack(sum_shifted(stats, jnp.stack))
-    sums, maxima, totals = merge(*gathered)
-    third = (both, middle, 1)
-    hand_off(*third, (stats, received[second]))
+    kept, sent = attend_shard(all_queries, key_cache, value_cache, lengths, score_factor)
+
+    swap = [(i, (i + 1) % sub_count) for i in range(sub_count)]
+    stats = merge_packed(kept, lax.ppermute(sent, "sub", swap), (received[behind],))
+    hand_off(both, 0, 0, (stats,))
+    hand_off(both, 0, 1, (stats,))
+    packed = from_all(stats)
+
     rest = [
         (both, shift, flip)
-        for shift in range(2, ctx_count)
+        for shift in sorted(range(2, ctx_count), key=lambda d: -d)
         for flip in range(sub_count)
-        if shift != middle
-    ] + [((1,), 1, 0)]
-    for key in rest:
-        hand_off(*key, (stats, received[first]))
-    hand_off(both, 0, 1, (stats, received[first]))
-
-    grouped = own_queries.reshape(requests, heads_decode, 2, group_size, head_dim).astype(
-        jnp.float32
-    )
-    keys_wide = jnp.transpose(fresh_keys, (0, 2, 1, 3)).astype(jnp.float32)
-    values_wide = jnp.transpose(fresh_values, (0, 2, 1, 3)).astype(jnp.float32)
-    fresh_scores = (
-        jnp.sum(grouped[:, :, :, :, None, :] * keys_wide[:, :, None, None, :, :], axis=-1)
-        * score_factor
-    )
-    step = jnp.arange(2)
-    seen = (step[None, :] <= step[:, None])[None, None, :, None, :]
-    fresh_scores = jnp.where(seen, fresh_scores, masked_score)
-    shape = (requests, heads_decode, 2, group_size)
-    maxima = maxima.reshape(shape)
-    largest = jnp.maximum(maxima, jnp.max(fresh_scores, axis=-1))
-    old_scale = jnp.exp(maxima - largest)
-    fresh_weights = jnp.where(seen, jnp.exp(fresh_scores - largest[..., None]), 0.0)
-    denominator = totals.reshape(shape) * old_scale + jnp.sum(fresh_weights, axis=-1)
-    numerator = sums.reshape(shape + (head_dim,)) * old_scale[..., None] + jnp.sum(
-        lax.reduce_precision(fresh_weights, 8, 7)[..., None]
-        * values_wide[:, :, None, None, :, :],
-        axis=-2,
-    )
-    attended = (numerator / denominator[..., None]).astype(jnp.bfloat16)
+    ]
+    blocks = [hand_off(*key, tuple(packed[1:])) for key in rest]
+
+    def for_rows(fresh):
+        spread = jnp.broadcast_to(
+            fresh[:, :, :, None], (requests, 2, heads_decode, per_head, head_dim)
+        )
+        return jnp.swapaxes(spread, 0, 1).reshape(2, -1, head_dim)
+
+    attended = finish(
+        packed,
+        own_queries.reshape(-1, head_dim),
+        for_rows(fresh_keys),
+        for_rows(fresh_values),
+        group_size,
+        score_factor,
+        (received[rest[0]],) + tuple(in_hbm(x) for x in blocks[1:]),
+    ).reshape(requests, heads_decode, 2, group_size, head_dim)
 
     attended = take(attended, owner_order, axis=0)
     attended = jnp.transpose(attended, (0, 2, 1, 3, 4)).reshape(2 * requests, query_width)
@@ -448,7 +493,7 @@
     result = (residual + jnp.sum(parts, axis=0)).astype(jnp.bfloat16)
 
     moved = ()
-    groups = [[ahead, (both, 0, 0), (both, 0, 1), first, second], [third] + rest]
+    groups = [[ahead, (both, 0, 0), (both, 0, 1), behind], rest]
     for keys in groups:
         pieces = [
             (block, entry, output, shift, flip)

time: 257 us -> 234 us (0.911)
  the two profiles are of different devices: /device:TPU:13 before, /device:TPU:0 now
where the time goes in v6:
time: 234 us; the launch traced here: 233 us
  waiting for transfers between devices  135 us (58%)
  Pallas kernels  46.3 us (20%)
  starting transfers between devices  13.5 us (6%)
  blocking collectives  13 us (6%)
  matrix products  11.7 us (5%)
  local copies, waits for them, and re-layouts  9.03 us (4%)
  other arithmetic  3.6 us (2%)
    ppermute x7, waiting for transfers between devices, hand_off(): block = lax.ppermute(made, ('ctx', 'sub'), pairs)  125 us
    pallas_call x8, Pallas kernels, arrange(): pl.pallas_call(kernel, out_shape=pltpu.HBM((count, shard_length, heads_de...  26.2 us
    ppermute x6, waiting for transfers between devices, from_all(): lax.ppermute(values, 'ctx', [(c, (c + shift) % ctx_count) for c in range(...  9.11 us
    ppermute x7, starting transfers between devices, hand_off(): block = lax.ppermute(made, ('ctx', 'sub'), pairs)  8.58 us
    pallas_call x1, Pallas kernels, attend_shard(): pl.pallas_call(kernel, out_shape=(jax.ShapeDtypeStruct(packed, jnp.float3...  7.04 us
    dot_general x3, matrix products, local(): jnp.dot(halves, weight, preferred_element_type=jnp.float32)  6.95 us
    pallas_call x2, Pallas kernels, assemble(): pl.pallas_call(kernel, out_shape=(pltpu.HBM((rows, head_dim), blocks[0].d...  6.54 us
    all_gather x1, blocking collectives, local(): parts = lax.all_gather(branch, ('head', 'sub'), axis=0)  5.79 us
  transfers between devices with their start and end apart: 14, of which 10 were waited for; matrix products, arithmetic and copies ran while one was open for 8% of the time, Pallas kernels for 14%

profile of v6, /device:TPU:0, one launch (start us, length us, event | category | flops | bytes accessed | tf_op | source)
XLA Modules:
  0.0 233.2 jit_solution(11551155024919646841)
XLA Ops:
  0.7 0.7 copy-done.14
  1.4 3.1 %arrange.8 = bf16[2,1024,2,128]{3,2,1,0:T(2,128)(2,1)} custom-call(s32[4]{0:T(128)S(1)} %copy-done.14, bf16[4,1024,4,128]{3,2,1,0:T(4,128)(2,1)} %refs_0_.15, bf16[4,1024,4,128]{3,2,1,0:T(4,128)(2,1)} %refs_1_.15), custom_call_target="tpu_custom_call" | custom-call | tf_op jit(solution)/shard_map/arrange/pallas_call | solution.py:79
  4.5 3.1 %collective-permute-start = (bf16[2,2048,128]{2,1,0:T(8,128)(2,1)}, bf16[2,2048,128]{2,1,0:T(8,128)(2,1)S(1)}, u32[]{:S(2)}, u32[]{:S(2)}) collective-permute-start(bf16[2,2048,128]{2,1,0:T(8,128)(2,1)} %bitcast.50), channel_id=1, source_target_pairs={{0,4},{1,5},{4,8},{5,9},{8,12},{9,13},{12,0},{13,1},{2,6},{3,7},{6... | collective-permute-start | bytes 3145736 | tf_op jit(solution)/shard_map/ppermute | solution.py:400
  7.6 0.1 iota_add_fusion
  7.6 1.3 pair_tokens.1
  9.0 5.4 %all_gather.9 = bf16[4,2,2048]{2,1,0:T(2,128)(2,1)S(1)} all-gather(bf16[1,2,2048]{2,1,0:T(2,128)(2,1)} %pair_tokens.1), channel_id=1, replica_groups=mesh['groups'=2,'ctx'=4,'head'=2,'sub'=2] {'head','sub'}, dimensions={0}, use_global_device_ids=true | all-gather | bytes 40960 | tf_op jit(solution)/shard_map/all_gather | solution.py:419
  14.4 0.6 copy-done.20
  15.0 0.9 fusion.6.refs_1_
  15.9 0.8 fusion.5.refs_2_
  16.7 5.3 %fusion.7.refs_0_ = f32[16,2048]{1,0:T(8,128)} fusion(bf16[2048,2048]{1,0:T(8,128)(2,1)} %param.18, bf16[8,2048]{1,0:T(8,128)(2,1)S(1)} %get-tuple-element.30, bf16[8,2048]{1,0:T(8,128)(2,1)S(1)} %get-tuple-element.29), kind=kOutput, calls=%fused_computation.18 | convolution fusion | flops 134348800 | bytes 8585216 | tf_op jit(solution)/shard_map/dot_general | solution.py:429
  22.0 11.3 %collective-permute-done.refs_4_.refs_0_ = bf16[2,2048,128]{2,1,0:T(8,128)(2,1)S(1)} collective-permute-done((bf16[2,2048,128]{2,1,0:T(8,128)(2,1)}, bf16[2,2048,128]{2,1,0:T(8,128)(2,1)S(1)}, u32[]{:S(2)}, u32[]{:S(2)}) %collective-permute-start) | collective-permute-done | bytes 1048608 | tf_op jit(solution)/shard_map/ppermute | solution.py:400
  33.3 1.0 copy-done.4
  34.3 1.7 pack_products.1
  35.9 1.7 collective-permute-start.3
  37.7 1.0 collective-permute-start.1
  38.7 0.1 multiply_cosine_fusion
  38.8 2.1 collective-permute-done.3
  41.0 5.0 %collective-permute-done.2 = f32[8,2688]{1,0:T(8,128)S(1)} collective-permute-done((f32[8,2688]{1,0:T(8,128)}, f32[8,2688]{1,0:T(8,128)S(1)}, u32[]{:S(2)}, u32[]{:S(2)}) %collective-permute-start.2) | collective-permute-done | bytes 86048 | tf_op jit(solution)/shard_map/ppermute | solution.py:406
  46.0 0.9 add_add_fusion.refs_2_
  46.9 0.1 fusion.11
  47.0 3.4 %arrange.9 = bf16[2,1024,2,128]{3,2,1,0:T(2,128)(2,1)} custom-call(s32[4]{0:T(128)S(1)} %copy-done.15, bf16[4,1024,4,128]{3,2,1,0:T(4,128)(2,1)} %refs_0_.15, bf16[4,1024,4,128]{3,2,1,0:T(4,128)(2,1)} %refs_1_.15, f32[8,2688]{1,0:T(8,128)S(1)} %add_add_fusion.refs_2_), custom_call_target="tpu_custom_call" | custom-call | tf_op jit(solution)/shard_map/arrange/pallas_call | solution.py:79
  50.5 0.1 collective-permute-start.5
  50.6 0.1 slice_multiply_fusion
  50.7 0.1 add_convert_fusion
  50.8 0.1 fusion.4
  50.9 1.9 all_gather.10.q_ref
  52.7 7.0 %attend_shard.1 = (f32[130,128]{1,0:T(8,128)S(1)}, f32[130,128]{1,0:T(8,128)S(1)}) custom-call(s32[4]{0:T(128)S(1)} %copy-done.16, bf16[4,64,128]{2,1,0:T(8,128)(2,1)S(1)} %all_gather.10.q_ref, bf16[4,4096,128]{2,1,0:T(8,128)(2,1)} %bitcast.46, bf16[4,4096,128]{2,1,0:T(8,128)(2,1)} %bitcast.47), custom_call_target="tpu_custom_call" | custom-call | tf_op jit(solution)/shard_map/attend_shard/pallas_call | solution.py:272
  59.8 0.6 copy-done.13
  60.4 0.2 collective-permute-start.4
  60.6 1.1 collective-permute-done.4.other_ref
  61.7 15.9 %collective-permute-done.5.refs_0_.refs_3_ = bf16[2,2048,128]{2,1,0:T(8,128)(2,1)S(1)} collective-permute-done((bf16[2,2048,128]{2,1,0:T(8,128)(2,1)}, bf16[2,2048,128]{2,1,0:T(8,128)(2,1)S(1)}, u32[]{:S(2)}, u32[]{:S(2)}) %collective-permute-start.5) | collective-permute-done | bytes 1048608 | tf_op jit(solution)/shard_map/ppermute | solution.py:400
  77.6 1.0 copy-done.6
  78.6 1.7 merge_packed.1.refs_2_.refs_0_
  80.3 2.0 collective-permute-start.6
  82.3 0.9 copy-done.11
  83.2 3.4 %arrange.15 = bf16[2,1024,2,128]{3,2,1,0:T(2,128)(2,1)} custom-call(s32[4]{0:T(128)S(1)} %copy-done.15, bf16[4,1024,4,128]{3,2,1,0:T(4,128)(2,1)} %refs_0_.15, bf16[4,1024,4,128]{3,2,1,0:T(4,128)(2,1)} %refs_1_.15, f32[130,128]{1,0:T(8,128)S(1)} %copy-done.11), custom_call_target="tpu_custom_call" | custom-call | tf_op jit(solution)/shard_map/arrange/pallas_call | solution.py:79
  86.6 0.1 collective-permute-start.13
  86.7 1.9 collective-permute-done.7.refs_3_.refs_2_
  88.7 3.3 %arrange.10 = bf16[2,1024,2,128]{3,2,1,0:T(2,128)(2,1)} custom-call(s32[4]{0:T(128)S(1)} %copy-done.15, bf16[4,1024,4,128]{3,2,1,0:T(4,128)(2,1)} %refs_0_.15, bf16[4,1024,4,128]{3,2,1,0:T(4,128)(2,1)} %refs_1_.15, f32[130,128]{1,0:T(8,128)S(1)} %collective-permute-done.6.refs_2_.refs_1_, f32[130,128]{1,0:T(8,128)S(1)} %collective-permute-done.7.refs_3_.refs_2_, ...), custom_call_target="tpu_custom_call" | custom-call | tf_op jit(solution)/shard_map/arrange/pallas_call | solution.py:79
  91.9 1.3 collective-permute-start.9
  93.3 0.6 dynamic_slice.6
  93.9 0.6 pad_clamp_fusion
  94.5 0.1 pad_maximum_fusion.4
  94.6 3.1 %arrange.14 = bf16[2,1024,2,128]{3,2,1,0:T(2,128)(2,1)} custom-call(s32[4]{0:T(128)S(1)} %copy-done.15, bf16[4,1024,4,128]{3,2,1,0:T(4,128)(2,1)} %refs_0_.15, bf16[4,1024,4,128]{3,2,1,0:T(4,128)(2,1)} %refs_1_.15, f32[130,128]{1,0:T(8,128)S(1)} %copy-done.12), custom_call_target="tpu_custom_call" | custom-call | tf_op jit(solution)/shard_map/arrange/pallas_call | solution.py:79
  97.6 3.4 %arrange.11 = bf16[2,1024,2,128]{3,2,1,0:T(2,128)(2,1)} custom-call(s32[4]{0:T(128)S(1)} %copy-done.15, bf16[4,1024,4,128]{3,2,1,0:T(4,128)(2,1)} %refs_0_.15, bf16[4,1024,4,128]{3,2,1,0:T(4,128)(2,1)} %refs_1_.15, f32[130,128]{1,0:T(8,128)S(1)} %collective-permute-done.6.refs_2_.refs_1_, f32[130,128]{1,0:T(8,128)S(1)} %collective-permute-done.7.refs_3_.refs_2_, ...), custom_call_target="tpu_custom_call" | custom-call | tf_op jit(solution)/shard_map/arrange/pallas_call | solution.py:79
  101.1 1.4 collective-permute-start.10
  102.5 3.1 %arrange.12 = bf16[2,1024,2,128]{3,2,1,0:T(2,128)(2,1)} custom-call(s32[4]{0:T(128)S(1)} %copy-done.15, bf16[4,1024,4,128]{3,2,1,0:T(4,128)(2,1)} %refs_0_.15, bf16[4,1024,4,128]{3,2,1,0:T(4,128)(2,1)} %refs_1_.15, f32[130,128]{1,0:T(8,128)S(1)} %collective-permute-done.6.refs_2_.refs_1_, f32[130,128]{1,0:T(8,128)S(1)} %collective-permute-done.7.refs_3_.refs_2_, ...), custom_call_target="tpu_custom_call" | custom-call | tf_op jit(solution)/shard_map/arrange/pallas_call | solution.py:79
  105.6 0.1 collective-permute-start.11
  105.7 3.4 %arrange.13 = bf16[2,1024,2,128]{3,2,1,0:T(2,128)(2,1)} custom-call(s32[4]{0:T(128)S(1)} %copy-done.15, bf16[4,1024,4,128]{3,2,1,0:T(4,128)(2,1)} %refs_0_.15, bf16[4,1024,4,128]{3,2,1,0:T(4,128)(2,1)} %refs_1_.15, f32[130,128]{1,0:T(8,128)S(1)} %collective-permute-done.6.refs_2_.refs_1_, f32[130,128]{1,0:T(8,128)S(1)} %collective-permute-done.7.refs_3_.refs_2_, ...), custom_call_target="tpu_custom_call" | custom-call | tf_op jit(solution)/shard_map/arrange/pallas_call | solution.py:79
  109.2 2.6 %collective-permute-start.12 = (bf16[2,2048,128]{2,1,0:T(8,128)(2,1)}, bf16[2,2048,128]{2,1,0:T(8,128)(2,1)}, u32[]{:S(2)}, u32[]{:S(2)}) collective-permute-start(bf16[2,2048,128]{2,1,0:T(8,128)(2,1)} %bitcast.56), channel_id=1, source_target_pairs={{0,9},{1,8},{4,13},{5,12},{8,1},{9,0},{12,5},{13,4},{2,11},{3,10},... | collective-permute-start | bytes 3145736 | tf_op jit(solution)/shard_map/ppermute | solution.py:400
  111.7 3.2 %assemble.2 = (bf16[16384,128]{1,0:T(8,128)(2,1)}, bf16[16384,128]{1,0:T(8,128)(2,1)}) custom-call(bf16[2,2048,128]{2,1,0:T(8,128)(2,1)S(1)} %copy-done.5, bf16[2,2048,128]{2,1,0:T(8,128)(2,1)S(1)} %bitcast.45, bf16[2,2048,128]{2,1,0:T(8,128)(2,1)} %collective-permute-done.13.refs_2_, bf16[2,2048,128]{2,1,0:T(8,128)(2,1)S(1)} %copy-done.7), custom_call_target="tpu_custom_call" | custom-call | bytes 8388608 | tf_op jit(solution)/shard_map/assemble/pallas_call | solution.py:133
  114.9 3.4 %collective-permute-done.9.refs_0_.refs_7_ = bf16[2,2048,128]{2,1,0:T(8,128)(2,1)S(1)} collective-permute-done((bf16[2,2048,128]{2,1,0:T(8,128)(2,1)}, bf16[2,2048,128]{2,1,0:T(8,128)(2,1)S(1)}, u32[]{:S(2)}, u32[]{:S(2)}) %collective-permute-start.9) | collective-permute-done | bytes 1048608 | tf_op jit(solution)/shard_map/ppermute | solution.py:400
  118.3 0.7 broadcast_in_dim.11
  119.0 0.6 broadcast_in_dim.12
  119.6 1.9 finish.1
  121.5 1.5 gather_fusion
  123.1 4.7 %fusion = f32[4,2,2048]{2,1,0:T(2,128)S(1)} fusion(bf16[4,2,2048]{2,1,0:T(2,128)(2,1)S(1)} %reshape.192, bf16[2048,2048]{1,0:T(8,128)(2,1)} %param.21), kind=kOutput, calls=%fused_computation.1 | convolution fusion | flops 67108864 | bytes 8486912 | tf_op jit(solution)/shard_map/dot_general | solution.py:486
  127.8 5.8 %all-gather = f32[16,2,2048]{2,1,0:T(2,128)S(1)} all-gather(f32[4,2,2048]{2,1,0:T(2,128)S(1)} %fusion), channel_id=2, replica_groups=mesh['groups'=2,'ctx'=4,'head'=2,'sub'=2] {'head','sub'}, dimensions={0}, use_global_device_ids=true | all-gather | bytes 327680 | tf_op jit(solution)/shard_map/all_gather | solution.py:489
  133.6 1.4 fusion.8
  135.0 0.6 slice_bitcast_fusion
  135.6 4.0 %collective-permute-done.10.refs_1_ = bf16[2,2048,128]{2,1,0:T(8,128)(2,1)S(1)} collective-permute-done((bf16[2,2048,128]{2,1,0:T(8,128)(2,1)}, bf16[2,2048,128]{2,1,0:T(8,128)(2,1)S(1)}, u32[]{:S(2)}, u32[]{:S(2)}) %collective-permute-start.10) | collective-permute-done | bytes 1048608 | tf_op jit(solution)/shard_map/ppermute | solution.py:400
  139.6 67.9 %collective-permute-done.11.refs_2_ = bf16[2,2048,128]{2,1,0:T(8,128)(2,1)} collective-permute-done((bf16[2,2048,128]{2,1,0:T(8,128)(2,1)}, bf16[2,2048,128]{2,1,0:T(8,128)(2,1)}, u32[]{:S(2)}, u32[]{:S(2)}) %collective-permute-start.11) | collective-permute-done | bytes 1048608 | tf_op jit(solution)/shard_map/ppermute | solution.py:400
  207.5 22.1 %collective-permute-done.12.refs_3_ = bf16[2,2048,128]{2,1,0:T(8,128)(2,1)} collective-permute-done((bf16[2,2048,128]{2,1,0:T(8,128)(2,1)}, bf16[2,2048,128]{2,1,0:T(8,128)(2,1)}, u32[]{:S(2)}, u32[]{:S(2)}) %collective-permute-start.12) | collective-permute-done | bytes 1048608 | tf_op jit(solution)/shard_map/ppermute | solution.py:400
  229.7 3.4 %assemble.3 = (bf16[16384,128]{1,0:T(8,128)(2,1)}, bf16[16384,128]{1,0:T(8,128)(2,1)}) custom-call(bf16[2,2048,128]{2,1,0:T(8,128)(2,1)S(1)} %copy-done.2, bf16[2,2048,128]{2,1,0:T(8,128)(2,1)S(1)} %collective-permute-done.10.refs_1_, bf16[2,2048,128]{2,1,0:T(8,128)(2,1)} %collective-permute-done.11.refs_2_, ...), custom_call_target="tpu_custom_call", output_to_operand_aliasing={{0}: (4, {}), {1}: (5, {})} | custom-call | bytes 8388608 | tf_op jit(solution)/shard_map/assemble/pallas_call | solution.py:133
  (60 shorter events, 0.2 us)
Async XLA Ops:
  0.6 14.4 %copy-start = (bf16[2048,256]{1,0:T(8,128)(2,1)S(1)}, bf16[2048,256]{1,0:T(8,128)(2,1)}, u32[]{:S(2)}) copy-start(bf16[2048,256]{1,0:T(8,128)(2,1)} %param.19) | copy-start | bytes 3145732
  0.6 0.7 copy-start.14
  1.4 6.2 %copy-start.16 = (s32[4]{0:T(128)S(1)}, s32[4]{0:T(128)}, u32[]{:S(2)}) copy-start(s32[4]{0:T(128)} %lengths_ref.1) | copy-start | bytes 52
  1.4 6.2 %copy-start.22 = (bf16[2048]{0:T(1024)(128)(2,1)S(1)}, bf16[2048]{0:T(1024)(128)(2,1)}, u32[]{:S(2)}) copy-start(bf16[2048]{0:T(1024)(128)(2,1)} %param.17) | copy-start | bytes 12292
  1.4 14.5 %copy-start.17 = (bf16[2048,256]{1,0:T(8,128)(2,1)S(1)}, bf16[2048,256]{1,0:T(8,128)(2,1)}, u32[]{:S(2)}) copy-start(bf16[2048,256]{1,0:T(8,128)(2,1)} %param.20) | copy-start | bytes 3145732
  4.5 28.8 %collective-permute-start = (bf16[2,2048,128]{2,1,0:T(8,128)(2,1)}, bf16[2,2048,128]{2,1,0:T(8,128)(2,1)S(1)}, u32[]{:S(2)}, u32[]{:S(2)}) collective-permute-start(bf16[2,2048,128]{2,1,0:T(8,128)(2,1)} %bitcast.50), channel_id=1, source_target_pairs={{0,4},{1,5},{4,8},{5,9},{8,12},{9,13},{12,0},{13,1},{2,6},{3,7},{6... | collective-permute-start | bytes 3145736 | tf_op jit(solution)/shard_map/ppermute | solution.py:400
  14.4 0.6 copy-start.20
  15.0 7.0 %copy-start.18 = (f32[8,2048]{1,0:T(8,128)}, f32[8,2048]{1,0:T(8,128)S(1)}, u32[]{:S(2)}) copy-start(f32[8,2048]{1,0:T(8,128)S(1)} %reshape.179.refs_3_) | copy-start | bytes 196612
  16.7 30.3 %copy-start.15 = (s32[4]{0:T(128)S(1)}, s32[4]{0:T(128)}, u32[]{:S(2)}) copy-start(s32[4]{0:T(128)} %order_ref.15) | copy-start | bytes 52
  33.3 1.0 copy-start.4
  35.9 5.0 %collective-permute-start.3 = (f32[8,2688]{1,0:T(8,128)}, f32[8,2688]{1,0:T(8,128)S(1)}, u32[]{:S(2)}, u32[]{:S(2)}) collective-permute-start(f32[8,2688]{1,0:T(8,128)} %pack_products.1), channel_id=1, source_target_pairs={{0,12},{4,0},{8,4},{12,8},{1,13},{5,1},{9,5},{13,9},{2,14},{6,2},{... | collective-permute-start | bytes 258056 | tf_op jit(solution)/shard_map/ppermute | solution.py:406
  37.7 8.3 %collective-permute-start.2 = (f32[8,2688]{1,0:T(8,128)}, f32[8,2688]{1,0:T(8,128)S(1)}, u32[]{:S(2)}, u32[]{:S(2)}) collective-permute-start(f32[8,2688]{1,0:T(8,128)} %pack_products.1), channel_id=1, source_target_pairs={{0,8},{4,12},{8,0},{12,4},{1,9},{5,13},{9,1},{13,5},{2,10},{6,14},... | collective-permute-start | bytes 258056 | tf_op jit(solution)/shard_map/ppermute | solution.py:406
  37.7 8.3 %collective-permute-start.1 = (f32[8,2688]{1,0:T(8,128)}, f32[8,2688]{1,0:T(8,128)S(1)}, u32[]{:S(2)}, u32[]{:S(2)}) collective-permute-start(f32[8,2688]{1,0:T(8,128)} %pack_products.1), channel_id=1, source_target_pairs={{0,4},{4,8},{8,12},{12,0},{1,5},{5,9},{9,13},{13,1},{2,6},{6,10},{... | collective-permute-start | bytes 258056 | tf_op jit(solution)/shard_map/ppermute | solution.py:406
  50.5 27.1 %collective-permute-start.5 = (bf16[2,2048,128]{2,1,0:T(8,128)(2,1)}, bf16[2,2048,128]{2,1,0:T(8,128)(2,1)S(1)}, u32[]{:S(2)}, u32[]{:S(2)}) collective-permute-start(bf16[2,2048,128]{2,1,0:T(8,128)(2,1)} %bitcast.59), channel_id=1, source_target_pairs={{0,5},{1,4},{4,9},{5,8},{8,13},{9,12},{12,1},{13,0},{2,7},{3,6},{6... | collective-permute-start | bytes 3145736 | tf_op jit(solution)/shard_map/ppermute | solution.py:400
  50.9 1.9 copy-start.19
  59.8 0.6 copy-start.13
  60.4 1.3 collective-permute-start.4
  61.7 16.0 %copy-start.21 = (f32[130,128]{1,0:T(8,128)}, f32[130,128]{1,0:T(8,128)S(1)}, u32[]{:S(2)}) copy-start(f32[130,128]{1,0:T(8,128)S(1)} %collective-permute-done.4.other_ref) | copy-start | bytes 199684
  77.6 1.0 copy-start.6
  80.2 6.5 %collective-permute-start.8 = (f32[130,128]{1,0:T(8,128)}, f32[130,128]{1,0:T(8,128)S(1)}, u32[]{:S(2)}, u32[]{:S(2)}) collective-permute-start(f32[130,128]{1,0:T(8,128)} %merge_packed.1.refs_2_.refs_0_), channel_id=1, source_target_pairs={{0,12},{4,0},{8,4},{12,8},{1,13},{5,1},{9,5},{13,9},{2,14},{6,2},{... | collective-permute-start | bytes 199688 | tf_op jit(solution)/shard_map/ppermute | solution.py:406
  80.3 8.4 %collective-permute-start.7 = (f32[130,128]{1,0:T(8,128)}, f32[130,128]{1,0:T(8,128)S(1)}, u32[]{:S(2)}, u32[]{:S(2)}) collective-permute-start(f32[130,128]{1,0:T(8,128)} %merge_packed.1.refs_2_.refs_0_), channel_id=1, source_target_pairs={{0,8},{4,12},{8,0},{12,4},{1,9},{5,13},{9,1},{13,5},{2,10},{6,14},... | collective-permute-start | bytes 199688 | tf_op jit(solution)/shard_map/ppermute | solution.py:406
  80.3 8.4 %collective-permute-start.6 = (f32[130,128]{1,0:T(8,128)}, f32[130,128]{1,0:T(8,128)S(1)}, u32[]{:S(2)}, u32[]{:S(2)}) collective-permute-start(f32[130,128]{1,0:T(8,128)} %merge_packed.1.refs_2_.refs_0_), channel_id=1, source_target_pairs={{0,4},{4,8},{8,12},{12,0},{1,5},{5,9},{9,13},{13,1},{2,6},{6,10},{... | collective-permute-start | bytes 199688 | tf_op jit(solution)/shard_map/ppermute | solution.py:406
  82.3 0.9 copy-start.11
  83.2 11.4 %copy-start.12 = (f32[130,128]{1,0:T(8,128)S(1)}, f32[130,128]{1,0:T(8,128)}, u32[]{:S(2)}) copy-start(f32[130,128]{1,0:T(8,128)} %merge_packed.1.refs_2_.refs_0_) | copy-start | bytes 199684
  86.6 25.1 %collective-permute-start.13 = (bf16[2,2048,128]{2,1,0:T(8,128)(2,1)}, bf16[2,2048,128]{2,1,0:T(8,128)(2,1)}, u32[]{:S(2)}, u32[]{:S(2)}) collective-permute-start(bf16[2,2048,128]{2,1,0:T(8,128)(2,1)} %bitcast.58), channel_id=1, source_target_pairs={{0,1},{1,0},{4,5},{5,4},{8,9},{9,8},{12,13},{13,12},{2,3},{3,2},{6... | collective-permute-start | bytes 3145736 | tf_op jit(solution)/shard_map/ppermute | solution.py:400
  86.7 19.0 %copy-start.8 = (f32[130,128]{1,0:T(8,128)}, f32[130,128]{1,0:T(8,128)S(1)}, u32[]{:S(2)}) copy-start(f32[130,128]{1,0:T(8,128)S(1)} %collective-permute-done.8.refs_4_.refs_3_) | copy-start | bytes 199684
  88.7 17.0 %copy-start.9 = (f32[130,128]{1,0:T(8,128)}, f32[130,128]{1,0:T(8,128)S(1)}, u32[]{:S(2)}) copy-start(f32[130,128]{1,0:T(8,128)S(1)} %collective-permute-done.7.refs_3_.refs_2_) | copy-start | bytes 199684
  88.7 17.0 %copy-start.10 = (f32[130,128]{1,0:T(8,128)}, f32[130,128]{1,0:T(8,128)S(1)}, u32[]{:S(2)}) copy-start(f32[130,128]{1,0:T(8,128)S(1)} %collective-permute-done.6.refs_2_.refs_1_) | copy-start | bytes 199684
  91.9 26.4 %collective-permute-start.9 = (bf16[2,2048,128]{2,1,0:T(8,128)(2,1)}, bf16[2,2048,128]{2,1,0:T(8,128)(2,1)S(1)}, u32[]{:S(2)}, u32[]{:S(2)}) collective-permute-start(bf16[2,2048,128]{2,1,0:T(8,128)(2,1)} %bitcast.60), channel_id=1, source_target_pairs={{0,12},{1,13},{4,0},{5,1},{8,4},{9,5},{12,8},{13,9},{2,14},{3,15},... | collective-permute-start | bytes 3145736 | tf_op jit(solution)/shard_map/ppermute | solution.py:400
  101.1 10.6 %copy-start.3 = (bf16[2,1024,2,128]{3,2,1,0:T(2,128)(2,1)S(1)}, bf16[2,1024,2,128]{3,2,1,0:T(2,128)(2,1)}, u32[]{:S(2)}) copy-start(bf16[2,1024,2,128]{3,2,1,0:T(2,128)(2,1)} %arrange.14) | copy-start | bytes 3145732
  101.1 10.6 %copy-start.5 = (bf16[2,2048,128]{2,1,0:T(8,128)(2,1)S(1)}, bf16[2,2048,128]{2,1,0:T(8,128)(2,1)}, u32[]{:S(2)}) copy-start(bf16[2,2048,128]{2,1,0:T(8,128)(2,1)} %copy-done.4) | copy-start | bytes 3145732
  101.1 10.6 %copy-start.7 = (bf16[2,2048,128]{2,1,0:T(8,128)(2,1)S(1)}, bf16[2,2048,128]{2,1,0:T(8,128)(2,1)}, u32[]{:S(2)}) copy-start(bf16[2,2048,128]{2,1,0:T(8,128)(2,1)} %copy-done.6) | copy-start | bytes 3145732
  101.1 38.5 %collective-permute-start.10 = (bf16[2,2048,128]{2,1,0:T(8,128)(2,1)}, bf16[2,2048,128]{2,1,0:T(8,128)(2,1)S(1)}, u32[]{:S(2)}, u32[]{:S(2)}) collective-permute-start(bf16[2,2048,128]{2,1,0:T(8,128)(2,1)} %bitcast.52), channel_id=1, source_target_pairs={{0,13},{1,12},{4,1},{5,0},{8,5},{9,4},{12,9},{13,8},{2,15},{3,14},... | collective-permute-start | bytes 3145736 | tf_op jit(solution)/shard_map/ppermute | solution.py:400
  105.6 101.9 %collective-permute-start.11 = (bf16[2,2048,128]{2,1,0:T(8,128)(2,1)}, bf16[2,2048,128]{2,1,0:T(8,128)(2,1)}, u32[]{:S(2)}, u32[]{:S(2)}) collective-permute-start(bf16[2,2048,128]{2,1,0:T(8,128)(2,1)} %bitcast.54), channel_id=1, source_target_pairs={{0,8},{1,9},{4,12},{5,13},{8,0},{9,1},{12,4},{13,5},{2,10},{3,11},... | collective-permute-start | bytes 3145736 | tf_op jit(solution)/shard_map/ppermute | solution.py:400
  109.2 120.5 %collective-permute-start.12 = (bf16[2,2048,128]{2,1,0:T(8,128)(2,1)}, bf16[2,2048,128]{2,1,0:T(8,128)(2,1)}, u32[]{:S(2)}, u32[]{:S(2)}) collective-permute-start(bf16[2,2048,128]{2,1,0:T(8,128)(2,1)} %bitcast.56), channel_id=1, source_target_pairs={{0,9},{1,8},{4,13},{5,12},{8,1},{9,0},{12,5},{13,4},{2,11},{3,10},... | collective-permute-start | bytes 3145736 | tf_op jit(solution)/shard_map/ppermute | solution.py:400
  118.3 1.3 copy-start.1
  121.5 108.1 %copy-start.2 = (bf16[2,2048,128]{2,1,0:T(8,128)(2,1)S(1)}, bf16[2,2048,128]{2,1,0:T(8,128)(2,1)}, u32[]{:S(2)}) copy-start(bf16[2,2048,128]{2,1,0:T(8,128)(2,1)} %copy-done.1) | copy-start | bytes 3145732

commit v7 on v6

--- a/solution.py
+++ b/solution.py
@@ -33,7 +33,7 @@
     return pltpu.with_memory_space_constraint(x, pltpu.HBM)
 
 
-def arrange(caches, owner_order, shift, flip, after):
+def arrange(caches, owner_order, shift, flip, after, apart):
     _, shard_length, heads, head_dim = caches[0].shape
     ctx_count = lax.axis_size("ctx")
     core_count = lax.axis_size("sub")
@@ -42,12 +42,15 @@
     places = shard_length // steps
     count = len(caches)
     pieces = [(w, i) for i in range(steps) for w in range(count)]
+    outputs = count if apart else 1
+    shape = (count // outputs, shard_length, heads_decode, head_dim)
 
     def kernel(order_ref, *refs):
         request = order_ref[lax.rem(lax.axis_index("ctx") + shift, ctx_count)]
         core = lax.rem(lax.axis_index("sub") + flip, core_count)
         in_refs = refs[:count]
-        out_ref, taken, made, in_sems, out_sems = refs[count + len(after) :]
+        out_refs = refs[count + len(after) : -4]
+        taken, made, in_sems, out_sems = refs[-4:]
         rows = lambda i: pl.ds(i * places, places)
         into = [
             pltpu.make_async_copy(
@@ -57,7 +60,9 @@
         ]
         out_of = [
             pltpu.make_async_copy(
-                made.at[w, rows(i)], out_ref.at[w, rows(i)], out_sems.at[w, i]
+                made.at[w, rows(i)],
+                out_refs[w].at[0, rows(i)] if apart else out_refs[0].at[w, rows(i)],
+                out_sems.at[w, i],
             )
             for w, i in pieces
         ]
@@ -78,11 +83,11 @@
 
     blocks = pl.pallas_call(
         kernel,
-        out_shape=pltpu.HBM((count, shard_length, heads_decode, head_dim), caches[0].dtype),
+        out_shape=(pltpu.HBM(shape, caches[0].dtype),) * outputs,
         in_specs=[pl.BlockSpec(memory_space=pltpu.SMEM)]
         + [pl.BlockSpec(memory_space=pltpu.HBM)] * count
         + [pl.BlockSpec(memory_space=pl.ANY)] * len(after),
-        out_specs=pl.BlockSpec(memory_space=pltpu.HBM),
+        out_specs=(pl.BlockSpec(memory_space=pltpu.HBM),) * outputs,
         scratch_shapes=[
             pltpu.VMEM((count, shard_length, heads, head_dim), caches[0].dtype),
             pltpu.VMEM((count, shard_length, heads_decode, head_dim), caches[0].dtype),
@@ -92,7 +97,23 @@
         compiler_params=pltpu.CompilerParams(vmem_limit_bytes=VMEM_BYTES),
         name="arrange",
     )(owner_order, *(in_hbm(x) for x in caches), *after)
-    return blocks.reshape(count, shard_length * heads_decode, head_dim)
+    blocks = [x.reshape(shape[0], shard_length * heads_decode, head_dim) for x in blocks]
+    return blocks if apart else blocks[0]
+
+
+def hold(blocks, after):
+    def kernel(*refs):
+        pass
+
+    in_place = pl.BlockSpec(memory_space=pltpu.HBM)
+    return pl.pallas_call(
+        kernel,
+        out_shape=tuple(pltpu.HBM(x.shape, x.dtype) for x in blocks),
+        in_specs=[in_place] * len(blocks) + [pl.BlockSpec(memory_space=pl.ANY)] * len(after),
+        out_specs=(in_place,) * len(blocks),
+        input_output_aliases={i: i for i in range(len(blocks))},
+        name="hold",
+    )(*(in_hbm(x) for x in blocks), *after)
 
 
 def assemble(blocks, pieces, filled=()):
@@ -186,6 +207,20 @@
         out_specs=whole,
         name="pack_products",
     )(*products, wide, *after)
+
+
+def add_all(parts, after):
+    def kernel(*refs):
+        refs[-1][...] = functools.reduce(jnp.add, [ref[...] for ref in refs[: len(parts)]])
+
+    whole = pl.BlockSpec(memory_space=pltpu.VMEM)
+    return pl.pallas_call(
+        kernel,
+        out_shape=jax.ShapeDtypeStruct(parts[0].shape, parts[0].dtype),
+        in_specs=[whole] * len(parts) + [pl.BlockSpec(memory_space=pl.ANY)] * len(after),
+        out_specs=whole,
+        name="add_all",
+    )(*parts, *after)
 
 
 def to_rows(column_form):
@@ -385,21 +420,21 @@
     both = (0, 1)
     received = {}
 
-    def hand_off(which, shift, flip, after=()):
-        caches = [(key_cache, value_cache)[w] for w in which]
-        block = made = arrange(caches, owner_order, shift, flip, after)
-        if shift or flip:
-            pairs = [
-                (
-                    c * sub_count + s,
-                    (c + shift) % ctx_count * sub_count + (s + flip) % sub_count,
-                )
-                for c in range(ctx_count)
-                for s in range(sub_count)
-            ]
-            block = lax.ppermute(made, ("ctx", "sub"), pairs)
-        received[which, shift, flip] = block
-        return made
+    def make(shift, flip, after=(), apart=False):
+        return arrange((key_cache, value_cache), owner_order, shift, flip, after, apart)
+
+    def send(block, which, shift, flip):
+        pairs = [
+            (
+                c * sub_count + s,
+                (c + shift) % ctx_count * sub_count + (s + flip) % sub_count,
+            )
+            for c in range(ctx_count)
+            for s in range(sub_count)
+        ]
+        moved = lax.ppermute(block, ("ctx", "sub"), pairs)
+        received[which, shift, flip] = moved
+        return moved
 
     def from_all(values):
         return [values] + [
@@ -408,8 +443,8 @@
         ]
 
     middle = ctx_count // 2
-    ahead = (both, 1, 0)
-    leading = hand_off(*ahead)
+    leading = make(1, 0, apart=True)
+    ahead = [send(leading[w], (w,), 1, 0) for w in both]
 
     query_width = w_query.shape[1]
     key_width = w_key.shape[1]
@@ -417,7 +452,7 @@
     score_factor = head_dim ** (-0.5)
     rows_local = first_tokens.shape[0]
     tokens = lax.all_gather(
-        pair_tokens(first_tokens, second_tokens, leading), ("head", "sub"), axis=0, tiled=True
+        pair_tokens(first_tokens, second_tokens, leading[0]), ("head", "sub"), axis=0, tiled=True
     )
     wide = tokens.astype(jnp.float32).reshape(2 * requests, -1)
     gained = wide * norm_gain.astype(jnp.float32)
@@ -430,11 +465,11 @@
             for weight in (w_query, w_key, w_value)
         ],
         wide,
-        (received[ahead],),
-    )
-    summed = functools.reduce(jnp.add, from_all(partial))
-    behind = (both, 1, 1)
-    hand_off(*behind, (summed,))
+        (ahead[0],),
+    )
+    summed = add_all(from_all(partial), (ahead[1],))
+    waiting = hold(make(1, 1, (partial,), apart=True), (summed,))
+    behind = [send(waiting[w], (w,), 1, 1) for w in both]
     raw = summed[:, :-LANES] * lax.rsqrt(summed[:, -LANES:][:, :1] / width + eps_norm)
     raw = raw.reshape(requests, 2, -1, head_dim)
     positions = lengths.astype(jnp.float32)[:, None] + jnp.arange(2, dtype=jnp.float32)
@@ -453,17 +488,21 @@
     kept, sent = attend_shard(all_queries, key_cache, value_cache, lengths, score_factor)
 
     swap = [(i, (i + 1) % sub_count) for i in range(sub_count)]
-    stats = merge_packed(kept, lax.ppermute(sent, "sub", swap), (received[behind],))
-    hand_off(both, 0, 0, (stats,))
-    hand_off(both, 0, 1, (stats,))
+    stats = merge_packed(kept, lax.ppermute(sent, "sub", swap), (behind[0],))
     packed = from_all(stats)
 
     rest = [
-        (both, shift, flip)
+        (shift, flip)
         for shift in sorted(range(2, ctx_count), key=lambda d: -d)
         for flip in range(sub_count)
     ]
-    blocks = [hand_off(*key, tuple(packed[1:])) for key in rest]
+    blocks = hold(
+        [make(*key, (stats,)) for key in rest], tuple(packed[1:]) + (behind[1],)
+    )
+    for block, key in zip(blocks, rest):
+        send(block, both, *key)
+    received[both, 0, 0] = make(0, 0, tuple(packed[1:]))
+    send(make(0, 1, tuple(packed[1:])), both, 0, 1)
 
     def for_rows(fresh):
         spread = jnp.broadcast_to(
@@ -478,7 +517,7 @@
         for_rows(fresh_values),
         group_size,
         score_factor,
-        (received[rest[0]],) + tuple(in_hbm(x) for x in blocks[1:]),
+        (received[both, *rest[0]],) + tuple(in_hbm(x) for x in blocks[1:]),
     ).reshape(requests, heads_decode, 2, group_size, head_dim)
 
     attended = take(attended, owner_order, axis=0)
@@ -493,7 +532,11 @@
     result = (residual + jnp.sum(parts, axis=0)).astype(jnp.bfloat16)
 
     moved = ()
-    groups = [[ahead, (both, 0, 0), (both, 0, 1), behind], rest]
+    early = [((w,), 1, flip) for flip in range(sub_count) for w in both]
+    groups = [
+        early + [(both, 0, 0), (both, 0, 1)],
+        [(both, *key) for key in rest],
+    ]
     for keys in groups:
         pieces = [
             (block, entry, output, shift, flip)

time: 234 us -> 227 us (0.970)
  waiting for transfers between devices: 135 us -> 117 us
  local copies, waits for them, and re-layouts: 9.03 us -> 13.6 us
  starting transfers between devices: 13.5 us -> 17.6 us
    ppermute x8 -> x10, waiting for transfers between devices: 126 us -> 115 us  [the longest x9 113 us: send(): moved = lax.ppermute(block, ('ctx', 'sub'), pairs)]
    ppermute x6, waiting for transfers between devices: 9.11 us -> 2.8 us  [from_all(): lax.ppermute(values, 'ctx', [(c, (c + shift) % ctx_count) for c in range(...]
    unnamed x46 -> x70, local copies, waits for them, and re-layouts: 4.89 us -> 9.58 us
    ppermute x8 -> x10, starting transfers between devices: 8.75 us -> 12.8 us  [the longest x9 12.6 us: send(): moved = lax.ppermute(block, ('ctx', 'sub'), pairs)]
    pallas_call x8 -> x11, Pallas kernels: 26.2 us -> 27.9 us  [the longest x8 26.2 us: arrange(): pl.pallas_call(kernel, out_shape=(pltpu.HBM(shape, caches[0].dtype),) * o...]
  transfers between devices with their start and end apart: 14 -> 16, of which waited for: 10 -> 8; matrix products, arithmetic and copies ran while one was open for 8% -> 8% of each run, Pallas kernels for 14% -> 18%
where the time goes in v7:
time: 227 us; the launch traced here: 225 us
  waiting for transfers between devices  117 us (52%)
  Pallas kernels  47.8 us (21%)
  starting transfers between devices  17.6 us (8%)
  local copies, waits for them, and re-layouts  13.6 us (6%)
  blocking collectives  13 us (6%)
  matrix products  11.8 us (5%)
  other arithmetic  2.95 us (1%)
    ppermute x9, waiting for transfers between devices, send(): moved = lax.ppermute(block, ('ctx', 'sub'), pairs)  113 us
    pallas_call x8, Pallas kernels, arrange(): pl.pallas_call(kernel, out_shape=(pltpu.HBM(shape, caches[0].dtype),) * o...  26.2 us
    ppermute x9, starting transfers between devices, send(): moved = lax.ppermute(block, ('ctx', 'sub'), pairs)  12.6 us
    unnamed x70, local copies, waits for them, and re-layouts  9.58 us
    pallas_call x1, Pallas kernels, attend_shard(): pl.pallas_call(kernel, out_shape=(jax.ShapeDtypeStruct(packed, jnp.float3...  7.04 us
    dot_general x3, matrix products, local(): jnp.dot(halves, weight, preferred_element_type=jnp.float32)  6.97 us
    pallas_call x2, Pallas kernels, assemble(): pl.pallas_call(kernel, out_shape=(pltpu.HBM((rows, head_dim), blocks[0].d...  6.37 us
    all_gather x1, blocking collectives, local(): parts = lax.all_gather(branch, ('head', 'sub'), axis=0)  5.79 us
  transfers between devices with their start and end apart: 16, of which 8 were waited for; matrix products, arithmetic and copies ran while one was open for 8% of the time, Pallas kernels for 18%

profile of v7, /device:TPU:0, one launch (start us, length us, event | category | flops | bytes accessed | tf_op | source)
XLA Modules:
  0.0 225.4 jit_solution(2576008223770531900)
XLA Ops:
  0.7 0.7 copy-done.24
  1.4 3.1 %arrange.8 = (bf16[1,1024,2,128]{3,2,1,0:T(2,128)(2,1)}, bf16[1,1024,2,128]{3,2,1,0:T(2,128)(2,1)}) custom-call(s32[4]{0:T(128)S(1)} %copy-done.24, bf16[4,1024,4,128]{3,2,1,0:T(4,128)(2,1)} %refs_0_.15, bf16[4,1024,4,128]{3,2,1,0:T(4,128)(2,1)} %refs_1_.15), custom_call_target="tpu_custom_call" | custom-call | tf_op jit(solution)/shard_map/arrange/pallas_call | solution.py:84
  4.5 3.1 %collective-permute-start.4 = (bf16[1,2048,128]{2,1,0:T(8,128)(2,1)}, bf16[1,2048,128]{2,1,0:T(8,128)(2,1)S(1)}, u32[]{:S(2)}, u32[]{:S(2)}) collective-permute-start(bf16[1,2048,128]{2,1,0:T(8,128)(2,1)} %bitcast.65), channel_id=1, source_target_pairs={{0,4},{1,5},{4,8},{5,9},{8,12},{9,13},{12,0},{13,1},{2,6},{3,7},{6... | collective-permute-start | bytes 1572872 | tf_op jit(solution)/shard_map/ppermute | solution.py:435
  7.5 1.6 collective-permute-start
  9.1 1.3 pair_tokens.1
  10.5 5.4 %all_gather.9 = bf16[4,2,2048]{2,1,0:T(2,128)(2,1)S(1)} all-gather(bf16[1,2,2048]{2,1,0:T(2,128)(2,1)} %pair_tokens.1), channel_id=1, replica_groups=mesh['groups'=2,'ctx'=4,'head'=2,'sub'=2] {'head','sub'}, dimensions={0}, use_global_device_ids=true | all-gather | bytes 40960 | tf_op jit(solution)/shard_map/all_gather | solution.py:454
  15.9 0.9 fusion.6.refs_1_
  16.8 5.3 %fusion.7.refs_0_ = f32[16,2048]{1,0:T(8,128)} fusion(bf16[2048,2048]{1,0:T(8,128)(2,1)} %param.18, bf16[8,2048]{1,0:T(8,128)(2,1)S(1)} %get-tuple-element.50, bf16[8,2048]{1,0:T(8,128)(2,1)S(1)} %get-tuple-element.49), kind=kOutput, calls=%fused_computation.17 | convolution fusion | flops 134348800 | bytes 8585216 | tf_op jit(solution)/shard_map/dot_general | solution.py:464
  22.1 0.9 fusion.5.refs_2_
  23.0 10.3 %collective-permute-done.refs_4_.refs_0_ = bf16[1,2048,128]{2,1,0:T(8,128)(2,1)S(1)} collective-permute-done((bf16[1,2048,128]{2,1,0:T(8,128)(2,1)}, bf16[1,2048,128]{2,1,0:T(8,128)(2,1)S(1)}, u32[]{:S(2)}, u32[]{:S(2)}) %collective-permute-start) | collective-permute-done | bytes 524320 | tf_op jit(solution)/shard_map/ppermute | solution.py:435
  33.3 0.8 copy-done.7
  34.1 1.7 pack_products.1.refs_0_.refs_2_
  35.8 1.7 collective-permute-start.3
  37.5 1.0 collective-permute-start.1
  38.5 0.1 multiply_cosine_fusion
  38.7 0.9 copy-done.22
  39.6 3.4 %arrange.9 = (bf16[1,1024,2,128]{3,2,1,0:T(2,128)(2,1)}, bf16[1,1024,2,128]{3,2,1,0:T(2,128)(2,1)}) custom-call(s32[4]{0:T(128)S(1)} %copy-done.25, bf16[4,1024,4,128]{3,2,1,0:T(4,128)(2,1)} %refs_0_.15, bf16[4,1024,4,128]{3,2,1,0:T(4,128)(2,1)} %refs_1_.15, f32[8,2688]{1,0:T(8,128)S(1)} %copy-done.22), custom_call_target="tpu_custom_call" | custom-call | tf_op jit(solution)/shard_map/arrange/pallas_call | solution.py:84
  43.1 2.8 %collective-permute-done.2.refs_2_ = f32[8,2688]{1,0:T(8,128)S(1)} collective-permute-done((f32[8,2688]{1,0:T(8,128)}, f32[8,2688]{1,0:T(8,128)S(1)}, u32[]{:S(2)}, u32[]{:S(2)}) %collective-permute-start.2) | collective-permute-done | bytes 86048 | tf_op jit(solution)/shard_map/ppermute | solution.py:441
  45.9 0.6 copy-done.31
  46.5 0.6 copy-done.32
  47.1 1.7 add_all.1.refs_2_
  48.8 0.8 fusion.11
  49.6 1.0 collective-permute-start.10
  50.7 1.0 slice_multiply_fusion
  51.7 0.1 add_convert_fusion
  51.8 0.1 fusion.4
  51.9 1.9 all_gather.10.q_ref
  53.8 7.0 %attend_shard.1 = (f32[130,128]{1,0:T(8,128)S(1)}, f32[130,128]{1,0:T(8,128)S(1)}) custom-call(s32[4]{0:T(128)S(1)} %copy-done.26, bf16[4,64,128]{2,1,0:T(8,128)(2,1)S(1)} %all_gather.10.q_ref, bf16[4,4096,128]{2,1,0:T(8,128)(2,1)} %bitcast.48, bf16[4,4096,128]{2,1,0:T(8,128)(2,1)} %bitcast.49), custom_call_target="tpu_custom_call" | custom-call | tf_op jit(solution)/shard_map/attend_shard/pallas_call | solution.py:307
  60.8 0.6 copy-done.23
  61.4 0.2 collective-permute-start.5
  61.6 1.1 collective-permute-done.5.other_ref
  62.7 3.2 %collective-permute-done.6.refs_0_.refs_2_ = bf16[1,2048,128]{2,1,0:T(8,128)(2,1)S(1)} collective-permute-done((bf16[1,2048,128]{2,1,0:T(8,128)(2,1)}, bf16[1,2048,128]{2,1,0:T(8,128)(2,1)S(1)}, u32[]{:S(2)}, u32[]{:S(2)}) %collective-permute-start.6) | collective-permute-done | bytes 524320 | tf_op jit(solution)/shard_map/ppermute | solution.py:435
  65.9 0.8 copy-done.9
  66.7 1.7 merge_packed.1.refs_2_.refs_0_
  68.3 2.0 collective-permute-start.7
  70.4 0.9 copy-done.4
  71.3 3.4 %arrange.13 = bf16[2,1024,2,128]{3,2,1,0:T(2,128)(2,1)} custom-call(s32[4]{0:T(128)S(1)} %copy-done.25, bf16[4,1024,4,128]{3,2,1,0:T(4,128)(2,1)} %refs_0_.15, bf16[4,1024,4,128]{3,2,1,0:T(4,128)(2,1)} %refs_1_.15, f32[130,128]{1,0:T(8,128)S(1)} %copy-done.4), custom_call_target="tpu_custom_call" | custom-call | tf_op jit(solution)/shard_map/arrange/pallas_call | solution.py:84
  74.7 3.3 %arrange.12 = bf16[2,1024,2,128]{3,2,1,0:T(2,128)(2,1)} custom-call(s32[4]{0:T(128)S(1)} %copy-done.25, bf16[4,1024,4,128]{3,2,1,0:T(4,128)(2,1)} %refs_0_.15, bf16[4,1024,4,128]{3,2,1,0:T(4,128)(2,1)} %refs_1_.15, f32[130,128]{1,0:T(8,128)S(1)} %copy-done.4), custom_call_target="tpu_custom_call" | custom-call | tf_op jit(solution)/shard_map/arrange/pallas_call | solution.py:84
  78.0 3.4 %arrange.11 = bf16[2,1024,2,128]{3,2,1,0:T(2,128)(2,1)} custom-call(s32[4]{0:T(128)S(1)} %copy-done.25, bf16[4,1024,4,128]{3,2,1,0:T(4,128)(2,1)} %refs_0_.15, bf16[4,1024,4,128]{3,2,1,0:T(4,128)(2,1)} %refs_1_.15, f32[130,128]{1,0:T(8,128)S(1)} %copy-done.4), custom_call_target="tpu_custom_call" | custom-call | tf_op jit(solution)/shard_map/arrange/pallas_call | solution.py:84
  81.4 3.1 %arrange.10 = bf16[2,1024,2,128]{3,2,1,0:T(2,128)(2,1)} custom-call(s32[4]{0:T(128)S(1)} %copy-done.25, bf16[4,1024,4,128]{3,2,1,0:T(4,128)(2,1)} %refs_0_.15, bf16[4,1024,4,128]{3,2,1,0:T(4,128)(2,1)} %refs_1_.15, f32[130,128]{1,0:T(8,128)S(1)} %copy-done.4), custom_call_target="tpu_custom_call" | custom-call | tf_op jit(solution)/shard_map/arrange/pallas_call | solution.py:84
  84.6 0.7 copy-done.11
  85.4 2.4 %collective-permute-start.11 = (bf16[2,2048,128]{2,1,0:T(8,128)(2,1)}, bf16[2,2048,128]{2,1,0:T(8,128)(2,1)S(1)}, u32[]{:S(2)}, u32[]{:S(2)}) collective-permute-start(bf16[2,2048,128]{2,1,0:T(8,128)(2,1)} %get-tuple-element.28), channel_id=1, source_target_pairs={{0,12},{1,13},{4,0},{5,1},{8,4},{9,5},{12,8},{13,9},{2,14},{3,15},... | collective-permute-start | bytes 3145736 | tf_op jit(solution)/shard_map/ppermute | solution.py:435
  87.8 0.9 copy-done.14
  88.7 0.9 copy-done.17
  89.6 0.9 copy-done.20
  90.5 3.4 %arrange.15 = bf16[2,1024,2,128]{3,2,1,0:T(2,128)(2,1)} custom-call(s32[4]{0:T(128)S(1)} %copy-done.25, bf16[4,1024,4,128]{3,2,1,0:T(4,128)(2,1)} %refs_0_.15, bf16[4,1024,4,128]{3,2,1,0:T(4,128)(2,1)} %refs_1_.15, f32[130,128]{1,0:T(8,128)S(1)} %copy-done.20, f32[130,128]{1,0:T(8,128)S(1)} %copy-done.17, f32[130,128]{1,0:T(8,128)S(1)} %copy-done.14), custom_call_target="tpu_custom_call" | custom-call | tf_op jit(solution)/shard_map/arrange/pallas_call | solution.py:84
  94.0 0.6 dynamic_slice.6
  94.7 2.1 collective-permute-start.12
  96.8 2.3 %collective-permute-start.14 = (bf16[2,2048,128]{2,1,0:T(8,128)(2,1)}, bf16[2,2048,128]{2,1,0:T(8,128)(2,1)}, u32[]{:S(2)}, u32[]{:S(2)}) collective-permute-start(bf16[2,2048,128]{2,1,0:T(8,128)(2,1)} %get-tuple-element.31.refs_10_), channel_id=1, source_target_pairs={{0,9},{1,8},{4,13},{5,12},{8,1},{9,0},{12,5},{13,4},{2,11},{3,10},... | collective-permute-start | bytes 3145736 | tf_op jit(solution)/shard_map/ppermute | solution.py:435
  99.1 3.1 %arrange.14 = bf16[2,1024,2,128]{3,2,1,0:T(2,128)(2,1)} custom-call(s32[4]{0:T(128)S(1)} %copy-done.25, bf16[4,1024,4,128]{3,2,1,0:T(4,128)(2,1)} %refs_0_.15, bf16[4,1024,4,128]{3,2,1,0:T(4,128)(2,1)} %refs_1_.15, f32[130,128]{1,0:T(8,128)S(1)} %copy-done.21, f32[130,128]{1,0:T(8,128)S(1)} %copy-done.18, f32[130,128]{1,0:T(8,128)S(1)} %copy-done.15), custom_call_target="tpu_custom_call" | custom-call | tf_op jit(solution)/shard_map/arrange/pallas_call | solution.py:84
  102.2 9.6 %collective-permute-done.11.refs_0_.refs_7_ = bf16[2,2048,128]{2,1,0:T(8,128)(2,1)S(1)} collective-permute-done((bf16[2,2048,128]{2,1,0:T(8,128)(2,1)}, bf16[2,2048,128]{2,1,0:T(8,128)(2,1)S(1)}, u32[]{:S(2)}, u32[]{:S(2)}) %collective-permute-start.11) | collective-permute-done | bytes 1048608 | tf_op jit(solution)/shard_map/ppermute | solution.py:435
  111.8 0.7 broadcast_in_dim.11
  112.5 0.6 broadcast_in_dim.12
  113.1 1.9 finish.1
  115.0 1.4 gather_fusion
  116.5 4.9 %fusion = f32[4,2,2048]{2,1,0:T(2,128)S(1)} fusion(bf16[4,2,2048]{2,1,0:T(2,128)(2,1)S(1)} %reshape.200, bf16[2048,2048]{1,0:T(8,128)(2,1)} %param.21), kind=kOutput, calls=%fused_computation.1 | convolution fusion | flops 67108864 | bytes 8486912 | tf_op jit(solution)/shard_map/dot_general | solution.py:525
  121.4 3.1 %assemble.2 = (bf16[16384,128]{1,0:T(8,128)(2,1)}, bf16[16384,128]{1,0:T(8,128)(2,1)}) custom-call(bf16[1,2048,128]{2,1,0:T(8,128)(2,1)S(1)} %copy-done.8, bf16[1,2048,128]{2,1,0:T(8,128)(2,1)S(1)} %copy-done.6, bf16[1,2048,128]{2,1,0:T(8,128)(2,1)S(1)} %copy-done.10, bf16[1,2048,128]{2,1,0:T(8,128)(2,1)S(1)} %copy-done.12, ...), custom_call_target="tpu_custom_call" | custom-call | bytes 8388608 | tf_op jit(solution)/shard_map/assemble/pallas_call | solution.py:154
  124.5 5.8 %all-gather = f32[16,2,2048]{2,1,0:T(2,128)S(1)} all-gather(f32[4,2,2048]{2,1,0:T(2,128)S(1)} %fusion), channel_id=2, replica_groups=mesh['groups'=2,'ctx'=4,'head'=2,'sub'=2] {'head','sub'}, dimensions={0}, use_global_device_ids=true | all-gather | bytes 327680 | tf_op jit(solution)/shard_map/all_gather | solution.py:528
  130.3 0.7 fusion.8
  131.0 0.6 slice_bitcast_fusion
  131.6 2.6 %collective-permute-done.12.refs_1_ = bf16[2,2048,128]{2,1,0:T(8,128)(2,1)} collective-permute-done((bf16[2,2048,128]{2,1,0:T(8,128)(2,1)}, bf16[2,2048,128]{2,1,0:T(8,128)(2,1)}, u32[]{:S(2)}, u32[]{:S(2)}) %collective-permute-start.12) | collective-permute-done | bytes 1048608 | tf_op jit(solution)/shard_map/ppermute | solution.py:435
  134.2 68.4 %collective-permute-done.13.refs_2_ = bf16[2,2048,128]{2,1,0:T(8,128)(2,1)} collective-permute-done((bf16[2,2048,128]{2,1,0:T(8,128)(2,1)}, bf16[2,2048,128]{2,1,0:T(8,128)(2,1)}, u32[]{:S(2)}, u32[]{:S(2)}) %collective-permute-start.13) | collective-permute-done | bytes 1048608 | tf_op jit(solution)/shard_map/ppermute | solution.py:435
  202.6 19.4 %collective-permute-done.14.refs_3_ = bf16[2,2048,128]{2,1,0:T(8,128)(2,1)} collective-permute-done((bf16[2,2048,128]{2,1,0:T(8,128)(2,1)}, bf16[2,2048,128]{2,1,0:T(8,128)(2,1)}, u32[]{:S(2)}, u32[]{:S(2)}) %collective-permute-start.14) | collective-permute-done | bytes 1048608 | tf_op jit(solution)/shard_map/ppermute | solution.py:435
  222.0 3.3 %assemble.3 = (bf16[16384,128]{1,0:T(8,128)(2,1)}, bf16[16384,128]{1,0:T(8,128)(2,1)}) custom-call(bf16[2,2048,128]{2,1,0:T(8,128)(2,1)S(1)} %copy-done.2, bf16[2,2048,128]{2,1,0:T(8,128)(2,1)} %collective-permute-done.12.refs_1_, bf16[2,2048,128]{2,1,0:T(8,128)(2,1)} %collective-permute-done.13.refs_2_, ...), custom_call_target="tpu_custom_call", output_to_operand_aliasing={{0}: (4, {}), {1}: (5, {})} | custom-call | bytes 8388608 | tf_op jit(solution)/shard_map/assemble/pallas_call | solution.py:154
  (90 shorter events, 0.7 us)
Async XLA Ops:
  0.6 15.3 %copy-start = (bf16[2048,256]{1,0:T(8,128)(2,1)S(1)}, bf16[2048,256]{1,0:T(8,128)(2,1)}, u32[]{:S(2)}) copy-start(bf16[2048,256]{1,0:T(8,128)(2,1)} %param.19) | copy-start | bytes 3145732
  0.6 0.7 copy-start.24
  1.4 7.7 %copy-start.26 = (s32[4]{0:T(128)S(1)}, s32[4]{0:T(128)}, u32[]{:S(2)}) copy-start(s32[4]{0:T(128)} %lengths_ref.1) | copy-start | bytes 52
  1.4 7.7 %copy-start.34 = (bf16[2048]{0:T(1024)(128)(2,1)S(1)}, bf16[2048]{0:T(1024)(128)(2,1)}, u32[]{:S(2)}) copy-start(bf16[2048]{0:T(1024)(128)(2,1)} %param.17) | copy-start | bytes 12292
  4.5 38.6 %collective-permute-start.4 = (bf16[1,2048,128]{2,1,0:T(8,128)(2,1)}, bf16[1,2048,128]{2,1,0:T(8,128)(2,1)S(1)}, u32[]{:S(2)}, u32[]{:S(2)}) collective-permute-start(bf16[1,2048,128]{2,1,0:T(8,128)(2,1)} %bitcast.65), channel_id=1, source_target_pairs={{0,4},{1,5},{4,8},{5,9},{8,12},{9,13},{12,0},{13,1},{2,6},{3,7},{6... | collective-permute-start | bytes 1572872 | tf_op jit(solution)/shard_map/ppermute | solution.py:435
  7.5 25.8 %collective-permute-start = (bf16[1,2048,128]{2,1,0:T(8,128)(2,1)}, bf16[1,2048,128]{2,1,0:T(8,128)(2,1)S(1)}, u32[]{:S(2)}, u32[]{:S(2)}) collective-permute-start(bf16[1,2048,128]{2,1,0:T(8,128)(2,1)} %bitcast.54), channel_id=1, source_target_pairs={{0,4},{1,5},{4,8},{5,9},{8,12},{9,13},{12,0},{13,1},{2,6},{3,7},{6... | collective-permute-start | bytes 1572872 | tf_op jit(solution)/shard_map/ppermute | solution.py:435
  15.9 6.2 %copy-start.28 = (f32[8,2048]{1,0:T(8,128)}, f32[8,2048]{1,0:T(8,128)S(1)}, u32[]{:S(2)}) copy-start(f32[8,2048]{1,0:T(8,128)S(1)} %reshape.187.refs_3_) | copy-start | bytes 196612
  15.9 6.2 %copy-start.27 = (bf16[2048,256]{1,0:T(8,128)(2,1)S(1)}, bf16[2048,256]{1,0:T(8,128)(2,1)}, u32[]{:S(2)}) copy-start(bf16[2048,256]{1,0:T(8,128)(2,1)} %param.20) | copy-start | bytes 3145732
  16.8 21.9 %copy-start.25 = (s32[4]{0:T(128)S(1)}, s32[4]{0:T(128)}, u32[]{:S(2)}) copy-start(s32[4]{0:T(128)} %order_ref.15) | copy-start | bytes 52
  33.3 0.8 copy-start.7
  35.8 7.3 %collective-permute-start.3 = (f32[8,2688]{1,0:T(8,128)}, f32[8,2688]{1,0:T(8,128)S(1)}, u32[]{:S(2)}, u32[]{:S(2)}) collective-permute-start(f32[8,2688]{1,0:T(8,128)} %pack_products.1.refs_0_.refs_2_), channel_id=1, source_target_pairs={{0,12},{4,0},{8,4},{12,8},{1,13},{5,1},{9,5},{13,9},{2,14},{6,2},{... | collective-permute-start | bytes 258056 | tf_op jit(solution)/shard_map/ppermute | solution.py:441
  37.5 8.3 %collective-permute-start.2 = (f32[8,2688]{1,0:T(8,128)}, f32[8,2688]{1,0:T(8,128)S(1)}, u32[]{:S(2)}, u32[]{:S(2)}) collective-permute-start(f32[8,2688]{1,0:T(8,128)} %pack_products.1.refs_0_.refs_2_), channel_id=1, source_target_pairs={{0,8},{4,12},{8,0},{12,4},{1,9},{5,13},{9,1},{13,5},{2,10},{6,14},... | collective-permute-start | bytes 258056 | tf_op jit(solution)/shard_map/ppermute | solution.py:441
  37.5 8.3 %collective-permute-start.1 = (f32[8,2688]{1,0:T(8,128)}, f32[8,2688]{1,0:T(8,128)S(1)}, u32[]{:S(2)}, u32[]{:S(2)}) collective-permute-start(f32[8,2688]{1,0:T(8,128)} %pack_products.1.refs_0_.refs_2_), channel_id=1, source_target_pairs={{0,4},{4,8},{8,12},{12,0},{1,5},{5,9},{9,13},{13,1},{2,6},{6,10},{... | collective-permute-start | bytes 258056 | tf_op jit(solution)/shard_map/ppermute | solution.py:441
  38.7 0.9 copy-start.22
  43.0 2.8 %copy-start.5 = (bf16[1,2048,128]{2,1,0:T(8,128)(2,1)}, bf16[1,2048,128]{2,1,0:T(8,128)(2,1)S(1)}, u32[]{:S(2)}) copy-start(bf16[1,2048,128]{2,1,0:T(8,128)(2,1)S(1)} %collective-permute-done.4.refs_4_.refs_1_) | copy-start | bytes 1572868
  43.1 2.8 %copy-start.30 = (f32[8,2688]{1,0:T(8,128)}, f32[8,2688]{1,0:T(8,128)S(1)}, u32[]{:S(2)}) copy-start(f32[8,2688]{1,0:T(8,128)S(1)} %collective-permute-done.3.refs_3_) | copy-start | bytes 258052
  45.8 0.6 copy-start.31
  46.5 0.6 copy-start.32
  49.6 16.3 %collective-permute-start.6 = (bf16[1,2048,128]{2,1,0:T(8,128)(2,1)}, bf16[1,2048,128]{2,1,0:T(8,128)(2,1)S(1)}, u32[]{:S(2)}, u32[]{:S(2)}) collective-permute-start(bf16[1,2048,128]{2,1,0:T(8,128)(2,1)} %get-tuple-element.26), channel_id=1, source_target_pairs={{0,5},{1,4},{4,9},{5,8},{8,13},{9,12},{12,1},{13,0},{2,7},{3,6},{6... | collective-permute-start | bytes 1572872 | tf_op jit(solution)/shard_map/ppermute | solution.py:435
  49.6 34.9 %collective-permute-start.10 = (bf16[1,2048,128]{2,1,0:T(8,128)(2,1)}, bf16[1,2048,128]{2,1,0:T(8,128)(2,1)S(1)}, u32[]{:S(2)}, u32[]{:S(2)}) collective-permute-start(bf16[1,2048,128]{2,1,0:T(8,128)(2,1)} %get-tuple-element.27), channel_id=1, source_target_pairs={{0,5},{1,4},{4,9},{5,8},{8,13},{9,12},{12,1},{13,0},{2,7},{3,6},{6... | collective-permute-start | bytes 1572872 | tf_op jit(solution)/shard_map/ppermute | solution.py:435
  51.9 22.8 %copy-start.29 = (bf16[4,2,2,8,128]{4,3,2,1,0:T(8,128)(2,1)}, bf16[4,2,2,8,128]{4,3,2,1,0:T(8,128)(2,1)S(1)}, u32[]{:S(2)}) copy-start(bf16[4,2,2,8,128]{4,3,2,1,0:T(8,128)(2,1)S(1)} %copy.31) | copy-start | bytes 98308
  60.8 0.6 copy-start.23
  61.4 1.3 collective-permute-start.5
  62.7 3.2 %copy-start.33 = (f32[130,128]{1,0:T(8,128)}, f32[130,128]{1,0:T(8,128)S(1)}, u32[]{:S(2)}) copy-start(f32[130,128]{1,0:T(8,128)S(1)} %collective-permute-done.5.other_ref) | copy-start | bytes 199684
  65.9 0.8 copy-start.9
  68.3 16.2 %collective-permute-start.9 = (f32[130,128]{1,0:T(8,128)}, f32[130,128]{1,0:T(8,128)S(1)}, u32[]{:S(2)}, u32[]{:S(2)}) collective-permute-start(f32[130,128]{1,0:T(8,128)} %merge_packed.1.refs_2_.refs_0_), channel_id=1, source_target_pairs={{0,12},{4,0},{8,4},{12,8},{1,13},{5,1},{9,5},{13,9},{2,14},{6,2},{... | collective-permute-start | bytes 199688 | tf_op jit(solution)/shard_map/ppermute | solution.py:441
  68.3 16.2 %collective-permute-start.8 = (f32[130,128]{1,0:T(8,128)}, f32[130,128]{1,0:T(8,128)S(1)}, u32[]{:S(2)}, u32[]{:S(2)}) collective-permute-start(f32[130,128]{1,0:T(8,128)} %merge_packed.1.refs_2_.refs_0_), channel_id=1, source_target_pairs={{0,8},{4,12},{8,0},{12,4},{1,9},{5,13},{9,1},{13,5},{2,10},{6,14},... | collective-permute-start | bytes 199688 | tf_op jit(solution)/shard_map/ppermute | solution.py:441
  68.3 16.2 %collective-permute-start.7 = (f32[130,128]{1,0:T(8,128)}, f32[130,128]{1,0:T(8,128)S(1)}, u32[]{:S(2)}, u32[]{:S(2)}) collective-permute-start(f32[130,128]{1,0:T(8,128)} %merge_packed.1.refs_2_.refs_0_), channel_id=1, source_target_pairs={{0,4},{4,8},{8,12},{12,0},{1,5},{5,9},{9,13},{13,1},{2,6},{6,10},{... | collective-permute-start | bytes 199688 | tf_op jit(solution)/shard_map/ppermute | solution.py:441
  70.4 0.9 copy-start.4
  84.5 0.8 copy-start.11
  84.5 0.8 copy-start.13
  84.6 0.8 copy-start.16
  84.6 0.8 copy-start.19
  85.4 26.4 %collective-permute-start.11 = (bf16[2,2048,128]{2,1,0:T(8,128)(2,1)}, bf16[2,2048,128]{2,1,0:T(8,128)(2,1)S(1)}, u32[]{:S(2)}, u32[]{:S(2)}) collective-permute-start(bf16[2,2048,128]{2,1,0:T(8,128)(2,1)} %get-tuple-element.28), channel_id=1, source_target_pairs={{0,12},{1,13},{4,0},{5,1},{8,4},{9,5},{12,8},{13,9},{2,14},{3,15},... | collective-permute-start | bytes 3145736 | tf_op jit(solution)/shard_map/ppermute | solution.py:435
  87.8 0.9 copy-start.14
  88.7 0.9 copy-start.17
  89.6 0.9 copy-start.20
  90.5 8.7 %copy-start.15 = (f32[130,128]{1,0:T(8,128)S(1)}, f32[130,128]{1,0:T(8,128)}, u32[]{:S(2)}) copy-start(f32[130,128]{1,0:T(8,128)} %copy-done.13) | copy-start | bytes 199684
  90.5 8.7 %copy-start.18 = (f32[130,128]{1,0:T(8,128)S(1)}, f32[130,128]{1,0:T(8,128)}, u32[]{:S(2)}) copy-start(f32[130,128]{1,0:T(8,128)} %copy-done.16) | copy-start | bytes 199684
  90.5 8.7 %copy-start.21 = (f32[130,128]{1,0:T(8,128)S(1)}, f32[130,128]{1,0:T(8,128)}, u32[]{:S(2)}) copy-start(f32[130,128]{1,0:T(8,128)} %copy-done.19) | copy-start | bytes 199684
  93.9 27.5 %collective-permute-start.15 = (bf16[2,2048,128]{2,1,0:T(8,128)(2,1)}, bf16[2,2048,128]{2,1,0:T(8,128)(2,1)}, u32[]{:S(2)}, u32[]{:S(2)}) collective-permute-start(bf16[2,2048,128]{2,1,0:T(8,128)(2,1)} %bitcast.53), channel_id=1, source_target_pairs={{0,1},{1,0},{4,5},{5,4},{8,9},{9,8},{12,13},{13,12},{2,3},{3,2},{6... | collective-permute-start | bytes 3145736 | tf_op jit(solution)/shard_map/ppermute | solution.py:435
  94.7 39.6 %collective-permute-start.12 = (bf16[2,2048,128]{2,1,0:T(8,128)(2,1)}, bf16[2,2048,128]{2,1,0:T(8,128)(2,1)}, u32[]{:S(2)}, u32[]{:S(2)}) collective-permute-start(bf16[2,2048,128]{2,1,0:T(8,128)(2,1)} %get-tuple-element.29.refs_8_), channel_id=1, source_target_pairs={{0,13},{1,12},{4,1},{5,0},{8,5},{9,4},{12,9},{13,8},{2,15},{3,14},... | collective-permute-start | bytes 3145736 | tf_op jit(solution)/shard_map/ppermute | solution.py:435
  96.8 105.8 %collective-permute-start.13 = (bf16[2,2048,128]{2,1,0:T(8,128)(2,1)}, bf16[2,2048,128]{2,1,0:T(8,128)(2,1)}, u32[]{:S(2)}, u32[]{:S(2)}) collective-permute-start(bf16[2,2048,128]{2,1,0:T(8,128)(2,1)} %get-tuple-element.30.refs_9_), channel_id=1, source_target_pairs={{0,8},{1,9},{4,12},{5,13},{8,0},{9,1},{12,4},{13,5},{2,10},{3,11},... | collective-permute-start | bytes 3145736 | tf_op jit(solution)/shard_map/ppermute | solution.py:435
  96.8 125.1 %collective-permute-start.14 = (bf16[2,2048,128]{2,1,0:T(8,128)(2,1)}, bf16[2,2048,128]{2,1,0:T(8,128)(2,1)}, u32[]{:S(2)}, u32[]{:S(2)}) collective-permute-start(bf16[2,2048,128]{2,1,0:T(8,128)(2,1)} %get-tuple-element.31.refs_10_), channel_id=1, source_target_pairs={{0,9},{1,8},{4,13},{5,12},{8,1},{9,0},{12,5},{13,4},{2,11},{3,10},... | collective-permute-start | bytes 3145736 | tf_op jit(solution)/shard_map/ppermute | solution.py:435
  102.2 19.2 %copy-start.3 = (bf16[2,1024,2,128]{3,2,1,0:T(2,128)(2,1)S(1)}, bf16[2,1024,2,128]{3,2,1,0:T(2,128)(2,1)}, u32[]{:S(2)}) copy-start(bf16[2,1024,2,128]{3,2,1,0:T(2,128)(2,1)} %arrange.14) | copy-start | bytes 3145732
  111.8 1.3 copy-start.1
  115.0 107.0 %copy-start.2 = (bf16[2,2048,128]{2,1,0:T(8,128)(2,1)S(1)}, bf16[2,2048,128]{2,1,0:T(8,128)(2,1)}, u32[]{:S(2)}) copy-start(bf16[2,2048,128]{2,1,0:T(8,128)(2,1)} %copy-done.1) | copy-start | bytes 3145732
  116.5 4.9 %copy-start.6 = (bf16[1,2048,128]{2,1,0:T(8,128)(2,1)S(1)}, bf16[1,2048,128]{2,1,0:T(8,128)(2,1)}, u32[]{:S(2)}) copy-start(bf16[1,2048,128]{2,1,0:T(8,128)(2,1)} %copy-done.5) | copy-start | bytes 1572868
  116.5 4.9 %copy-start.8 = (bf16[1,2048,128]{2,1,0:T(8,128)(2,1)S(1)}, bf16[1,2048,128]{2,1,0:T(8,128)(2,1)}, u32[]{:S(2)}) copy-start(bf16[1,2048,128]{2,1,0:T(8,128)(2,1)} %copy-done.7) | copy-start | bytes 1572868
  116.5 4.9 %copy-start.10 = (bf16[1,2048,128]{2,1,0:T(8,128)(2,1)S(1)}, bf16[1,2048,128]{2,1,0:T(8,128)(2,1)}, u32[]{:S(2)}) copy-start(bf16[1,2048,128]{2,1,0:T(8,128)(2,1)} %copy-done.9) | copy-start | bytes 1572868
  116.5 4.9 %copy-start.12 = (bf16[1,2048,128]{2,1,0:T(8,128)(2,1)S(1)}, bf16[1,2048,128]{2,1,0:T(8,128)(2,1)}, u32[]{:S(2)}) copy-start(bf16[1,2048,128]{2,1,0:T(8,128)(2,1)} %copy-done.11) | copy-start | bytes 1572868

commit v8 on v7

--- a/solution.py
+++ b/solution.py
@@ -33,6 +33,14 @@
     return pltpu.with_memory_space_constraint(x, pltpu.HBM)
 
 
+def in_vmem(x):
+    return pltpu.with_memory_space_constraint(x, pltpu.VMEM)
+
+
+def vmem_specs(count):
+    return [pl.BlockSpec(memory_space=pltpu.VMEM)] * count
+
+
 def arrange(caches, owner_order, shift, flip, after, apart):
     _, shard_length, heads, head_dim = caches[0].shape
     ctx_count = lax.axis_size("ctx")
@@ -86,7 +94,7 @@
         out_shape=(pltpu.HBM(shape, caches[0].dtype),) * outputs,
         in_specs=[pl.BlockSpec(memory_space=pltpu.SMEM)]
         + [pl.BlockSpec(memory_space=pltpu.HBM)] * count
-        + [pl.BlockSpec(memory_space=pl.ANY)] * len(after),
+        + vmem_specs(len(after)),
         out_specs=(pl.BlockSpec(memory_space=pltpu.HBM),) * outputs,
         scratch_shapes=[
             pltpu.VMEM((count, shard_length, heads, head_dim), caches[0].dtype),
@@ -96,7 +104,7 @@
         ],
         compiler_params=pltpu.CompilerParams(vmem_limit_bytes=VMEM_BYTES),
         name="arrange",
-    )(owner_order, *(in_hbm(x) for x in caches), *after)
+    )(owner_order, *(in_hbm(x) for x in caches), *(in_vmem(x) for x in after))
     blocks = [x.reshape(shape[0], shard_length * heads_decode, head_dim) for x in blocks]
     return blocks if apart else blocks[0]
 
@@ -109,11 +117,11 @@
     return pl.pallas_call(
         kernel,
         out_shape=tuple(pltpu.HBM(x.shape, x.dtype) for x in blocks),
-        in_specs=[in_place] * len(blocks) + [pl.BlockSpec(memory_space=pl.ANY)] * len(after),
+        in_specs=[in_place] * len(blocks) + vmem_specs(len(after)),
         out_specs=(in_place,) * len(blocks),
         input_output_aliases={i: i for i in range(len(blocks))},
         name="hold",
-    )(*(in_hbm(x) for x in blocks), *after)
+    )(*(in_hbm(x) for x in blocks), *(in_vmem(x) for x in after))
 
 
 def assemble(blocks, pieces, filled=()):
@@ -202,25 +210,11 @@
     whole = pl.BlockSpec(memory_space=pltpu.VMEM)
     return pl.pallas_call(
         kernel,
-        out_shape=jax.ShapeDtypeStruct((rows, sum(widths) + LANES), jnp.float32),
-        in_specs=[whole] * (len(products) + 1) + [pl.BlockSpec(memory_space=pl.ANY)] * len(after),
+        out_shape=pltpu.VMEM((rows, sum(widths) + LANES), jnp.float32),
+        in_specs=[whole] * (len(products) + 1 + len(after)),
         out_specs=whole,
         name="pack_products",
-    )(*products, wide, *after)
-
-
-def add_all(parts, after):
-    def kernel(*refs):
-        refs[-1][...] = functools.reduce(jnp.add, [ref[...] for ref in refs[: len(parts)]])
-
-    whole = pl.BlockSpec(memory_space=pltpu.VMEM)
-    return pl.pallas_call(
-        kernel,
-        out_shape=jax.ShapeDtypeStruct(parts[0].shape, parts[0].dtype),
-        in_specs=[whole] * len(parts) + [pl.BlockSpec(memory_space=pl.ANY)] * len(after),
-        out_specs=whole,
-        name="add_all",
-    )(*parts, *after)
+    )(*(in_vmem(x) for x in (*products, wide, *after)))
 
 
 def to_rows(column_form):
@@ -306,7 +300,7 @@
     packed = (count + 2 * extra, head_dim)
     return pl.pallas_call(
         kernel,
-        out_shape=(jax.ShapeDtypeStruct(packed, jnp.float32),) * 2,
+        out_shape=(pltpu.VMEM(packed, jnp.float32),) * 2,
         grid_spec=pltpu.PrefetchScalarGridSpec(
             num_scalar_prefetch=1,
             grid=(requests,),
@@ -315,7 +309,7 @@
                 large,
                 large,
             ],
-            out_specs=(pl.BlockSpec(packed, lambda r, *_: (0, 0)),) * 2,
+            out_specs=tuple(vmem_specs(2)),
             scratch_shapes=[pltpu.VMEM((2, count, head_dim), jnp.float32)] * 2,
         ),
         compiler_params=pltpu.CompilerParams(vmem_limit_bytes=VMEM_BYTES),
@@ -348,14 +342,14 @@
     whole = pl.BlockSpec(memory_space=pltpu.VMEM)
     return pl.pallas_call(
         kernel,
-        out_shape=jax.ShapeDtypeStruct(kept.shape, kept.dtype),
-        in_specs=[whole] * 2 + [pl.BlockSpec(memory_space=pl.ANY)] * len(after),
+        out_shape=pltpu.VMEM(kept.shape, kept.dtype),
+        in_specs=[whole] * (2 + len(after)),
         out_specs=whole,
         name="merge_packed",
-    )(kept, other, *after)
-
-
-def finish(packed, queries, fresh_keys, fresh_values, group_size, score_factor, after):
+    )(*(in_vmem(x) for x in (kept, other, *after)))
+
+
+def finish(packed, queries, fresh_keys, fresh_values, group_size, score_factor, after, made):
     count, extra = packed_sizes(packed[0].shape[0])
     shares = len(packed)
     head_dim = queries.shape[1]
@@ -388,11 +382,15 @@
     whole = pl.BlockSpec(memory_space=pltpu.VMEM)
     return pl.pallas_call(
         kernel,
-        out_shape=jax.ShapeDtypeStruct((count, head_dim), jnp.bfloat16),
-        in_specs=[whole] * (shares + 3) + [pl.BlockSpec(memory_space=pl.ANY)] * len(after),
+        out_shape=pltpu.VMEM((count, head_dim), jnp.bfloat16),
+        in_specs=[whole] * (shares + 3 + len(after))
+        + [pl.BlockSpec(memory_space=pltpu.HBM)] * len(made),
         out_specs=whole,
         name="finish",
-    )(*packed, queries, fresh_keys, fresh_values, *after)
+    )(
+        *(in_vmem(x) for x in (*packed, queries, fresh_keys, fresh_values, *after)),
+        *(in_hbm(x) for x in made),
+    )
 
 
 def local(
@@ -444,7 +442,9 @@
 
     middle = ctx_count // 2
     leading = make(1, 0, apart=True)
-    ahead = [send(leading[w], (w,), 1, 0) for w in both]
+    paired = pair_tokens(first_tokens, second_tokens, leading[0])
+    later = hold(leading[1:], (paired,))
+    ahead = [send(block, (w,), 1, 0) for w, block in enumerate([leading[0], *later])]
 
     query_width = w_query.shape[1]
     key_width = w_key.shape[1]
@@ -452,7 +452,7 @@
     score_factor = head_dim ** (-0.5)
     rows_local = first_tokens.shape[0]
     tokens = lax.all_gather(
-        pair_tokens(first_tokens, second_tokens, leading[0]), ("head", "sub"), axis=0, tiled=True
+        paired, ("head", "sub"), axis=0, tiled=True
     )
     wide = tokens.astype(jnp.float32).reshape(2 * requests, -1)
     gained = wide * norm_gain.astype(jnp.float32)
@@ -467,8 +467,8 @@
         wide,
         (ahead[0],),
     )
-    summed = add_all(from_all(partial), (ahead[1],))
-    waiting = hold(make(1, 1, (partial,), apart=True), (summed,))
+    summed = functools.reduce(jnp.add, from_all(partial))
+    waiting = hold(make(1, 1, (partial,), apart=True), (summed, ahead[1]))
     behind = [send(waiting[w], (w,), 1, 1) for w in both]
     raw = summed[:, :-LANES] * lax.rsqrt(summed[:, -LANES:][:, :1] / width + eps_norm)
     raw = raw.reshape(requests, 2, -1, head_dim)
@@ -496,9 +496,8 @@
         for shift in sorted(range(2, ctx_count), key=lambda d: -d)
         for flip in range(sub_count)
     ]
-    blocks = hold(
-        [make(*key, (stats,)) for key in rest], tuple(packed[1:]) + (behind[1],)
-    )
+    blocks = hold([make(*rest[0], (partial,))], (*packed[1:], behind[1]))
+    blocks = [*blocks, *(make(*key, tuple(packed[1:])) for key in rest[1:])]
     for block, key in zip(blocks, rest):
         send(block, both, *key)
     received[both, 0, 0] = make(0, 0, tuple(packed[1:]))
@@ -517,7 +516,8 @@
         for_rows(fresh_values),
         group_size,
         score_factor,
-        (received[both, *rest[0]],) + tuple(in_hbm(x) for x in blocks[1:]),
+        (received[both, *rest[0]],),
+        blocks[1:],
     ).reshape(requests, heads_decode, 2, group_size, head_dim)
 
     attended = take(attended, owner_order, axis=0)
@@ -535,7 +535,8 @@
     early = [((w,), 1, flip) for flip in range(sub_count) for w in both]
     groups = [
         early + [(both, 0, 0), (both, 0, 1)],
-        [(both, *key) for key in rest],
+        [(both, *key) for key in rest[:-1]],
+        [(both, *rest[-1])],
     ]
     for keys in groups:
         pieces = [

time: 227 us -> 214 us (0.943)
  local copies, waits for them, and re-layouts: 13.6 us -> 7.35 us
  waiting for transfers between devices: 117 us -> 121 us
  Pallas kernels: 47.8 us -> 44 us
  starting transfers between devices: 17.6 us -> 14.7 us
    ppermute x6, waiting for transfers between devices: 2.8 us -> 17.3 us  [from_all(): lax.ppermute(values, 'ctx', [(c, (c + shift) % ctx_count) for c in range(...]
    ppermute x9, waiting for transfers between devices: 113 us -> 103 us  [send(): moved = lax.ppermute(block, ('ctx', 'sub'), pairs)]
    pallas_call x5 -> x4, Pallas kernels: 13.9 us -> 7.54 us  [the longest x1 7.04 us: attend_shard(): pl.pallas_call(kernel, out_shape=(pltpu.VMEM(packed, jnp.float32),) * 2,...]
    unnamed x70 -> x30, local copies, waits for them, and re-layouts: 9.58 us -> 5.48 us
    ppermute x9, starting transfers between devices: 12.6 us -> 9.33 us  [send(): moved = lax.ppermute(block, ('ctx', 'sub'), pairs)]
    pallas_call x2 -> x3, Pallas kernels: 6.37 us -> 7.93 us  [assemble(): pl.pallas_call(kernel, out_shape=(pltpu.HBM((rows, head_dim), blocks[0].d...]
  transfers between devices with their start and end apart: 16 -> 16, of which waited for: 8 -> 12; matrix products, arithmetic and copies ran while one was open for 8% -> 6% of each run, Pallas kernels for 18% -> 18%
where the time goes in v8:
time: 214 us; the launch traced here: 213 us
  waiting for transfers between devices  121 us (57%)
  Pallas kernels  44 us (21%)
  starting transfers between devices  14.7 us (7%)
  blocking collectives  12.8 us (6%)
  matrix products  9.95 us (5%)
  local copies, waits for them, and re-layouts  7.35 us (3%)
    ppermute x9, waiting for transfers between devices, send(): moved = lax.ppermute(block, ('ctx', 'sub'), pairs)  103 us
    pallas_call x8, Pallas kernels, arrange(): pl.pallas_call(kernel, out_shape=(pltpu.HBM(shape, caches[0].dtype),) * o...  26.2 us
    ppermute x6, waiting for transfers between devices, from_all(): lax.ppermute(values, 'ctx', [(c, (c + shift) % ctx_count) for c in range(...  17.3 us
    ppermute x9, starting transfers between devices, send(): moved = lax.ppermute(block, ('ctx', 'sub'), pairs)  9.33 us
    pallas_call x3, Pallas kernels, assemble(): pl.pallas_call(kernel, out_shape=(pltpu.HBM((rows, head_dim), blocks[0].d...  7.93 us
    pallas_call x1, Pallas kernels, attend_shard(): pl.pallas_call(kernel, out_shape=(pltpu.VMEM(packed, jnp.float32),) * 2,...  7.04 us
    all_gather x1, blocking collectives, local(): parts = lax.all_gather(branch, ('head', 'sub'), axis=0)  5.79 us
    unnamed x30, local copies, waits for them, and re-layouts  5.48 us
  transfers between devices with their start and end apart: 16, of which 12 were waited for; matrix products, arithmetic and copies ran while one was open for 6% of the time, Pallas kernels for 18%

profile of v8, /device:TPU:0, one launch (start us, length us, event | category | flops | bytes accessed | tf_op | source)
XLA Modules:
  0.0 212.8 jit_solution(17531789763894971772)
XLA Ops:
  0.7 0.7 copy-done.10
  1.4 3.1 %arrange.8 = (bf16[1,1024,2,128]{3,2,1,0:T(2,128)(2,1)}, bf16[1,1024,2,128]{3,2,1,0:T(2,128)(2,1)}) custom-call(s32[4]{0:T(128)S(1)} %copy-done.10, bf16[4,1024,4,128]{3,2,1,0:T(4,128)(2,1)} %refs_0_.15, bf16[4,1024,4,128]{3,2,1,0:T(4,128)(2,1)} %refs_1_.15), custom_call_target="tpu_custom_call" | custom-call | tf_op jit(solution)/shard_map/arrange/pallas_call | solution.py:92
  4.5 3.1 %collective-permute-start = (bf16[1,2048,128]{2,1,0:T(8,128)(2,1)}, bf16[1,2048,128]{2,1,0:T(8,128)(2,1)S(1)}, u32[]{:S(2)}, u32[]{:S(2)}) collective-permute-start(bf16[1,2048,128]{2,1,0:T(8,128)(2,1)} %bitcast.67), channel_id=1, source_target_pairs={{0,4},{1,5},{4,8},{5,9},{8,12},{9,13},{12,0},{13,1},{2,6},{3,7},{6... | collective-permute-start | bytes 1572872 | tf_op jit(solution)/shard_map/ppermute | solution.py:433
  7.6 1.3 pair_tokens.1.refs_1_
  8.9 0.7 copy-done.9
  9.6 1.6 collective-permute-start.5
  11.2 5.2 %all_gather.9 = bf16[4,2,2048]{2,1,0:T(2,128)(2,1)S(1)} all-gather(bf16[1,2,2048]{2,1,0:T(2,128)(2,1)S(1)} %copy-done.9), channel_id=1, replica_groups=mesh['groups'=2,'ctx'=4,'head'=2,'sub'=2] {'head','sub'}, dimensions={0}, use_global_device_ids=true | all-gather | bytes 40960 | tf_op jit(solution)/shard_map/all_gather | solution.py:454
  16.5 0.2 fusion.6.refs_1_
  16.7 0.3 fusion.5.refs_2_
  17.0 4.6 %fusion.7.refs_0_ = f32[16,2048]{1,0:T(8,128)S(1)} fusion(bf16[2048,2048]{1,0:T(8,128)(2,1)} %param.18, bf16[8,2048]{1,0:T(8,128)(2,1)S(1)} %get-tuple-element.46, bf16[8,2048]{1,0:T(8,128)(2,1)S(1)} %get-tuple-element.45), kind=kOutput, calls=%fused_computation.18 | convolution fusion | flops 134348800 | bytes 8585216 | tf_op jit(solution)/shard_map/dot_general | solution.py:464
  21.6 0.9 collective-permute-done.refs_4_.refs_0_
  22.5 0.1 pack_products.1.refs_2_
  22.6 2.1 collective-permute-start.3
  24.7 0.1 collective-permute-start.2
  24.7 0.9 collective-permute-start.1
  25.7 0.1 multiply_cosine_fusion
  25.8 3.4 %arrange.9 = (bf16[1,1024,2,128]{3,2,1,0:T(2,128)(2,1)}, bf16[1,1024,2,128]{3,2,1,0:T(2,128)(2,1)}) custom-call(s32[4]{0:T(128)S(1)} %copy-done.11, bf16[4,1024,4,128]{3,2,1,0:T(4,128)(2,1)} %refs_0_.15, bf16[4,1024,4,128]{3,2,1,0:T(4,128)(2,1)} %refs_1_.15, f32[8,2688]{1,0:T(8,128)S(1)} %pack_products.1.refs_2_), custom_call_target="tpu_custom_call" | custom-call | tf_op jit(solution)/shard_map/arrange/pallas_call | solution.py:92
  29.3 5.9 %collective-permute-done.3 = f32[8,2688]{1,0:T(8,128)S(1)} collective-permute-done((f32[8,2688]{1,0:T(8,128)S(1)}, f32[8,2688]{1,0:T(8,128)S(1)}, u32[]{:S(2)}, u32[]{:S(2)}) %collective-permute-start.3) | collective-permute-done | bytes 86048 | tf_op jit(solution)/shard_map/ppermute | solution.py:439
  35.1 5.5 %collective-permute-done.2 = f32[8,2688]{1,0:T(8,128)S(1)} collective-permute-done((f32[8,2688]{1,0:T(8,128)S(1)}, f32[8,2688]{1,0:T(8,128)S(1)}, u32[]{:S(2)}, u32[]{:S(2)}) %collective-permute-start.2) | collective-permute-done | bytes 86048 | tf_op jit(solution)/shard_map/ppermute | solution.py:439
  40.7 0.1 fusion.11
  40.9 1.0 collective-permute-start.11
  41.9 0.1 slice_multiply_fusion
  42.0 0.1 add_convert_fusion
  42.1 0.1 fusion.4
  42.2 1.9 all_gather.10.q_ref
  44.1 7.0 %attend_shard.1 = (f32[130,128]{1,0:T(8,128)S(1)}, f32[130,128]{1,0:T(8,128)S(1)}) custom-call(s32[4]{0:T(128)S(1)} %copy-done.12, bf16[4,64,128]{2,1,0:T(8,128)(2,1)S(1)} %all_gather.10.q_ref, bf16[4,4096,128]{2,1,0:T(8,128)(2,1)} %bitcast.53, bf16[4,4096,128]{2,1,0:T(8,128)(2,1)} %bitcast.54), custom_call_target="tpu_custom_call" | custom-call | tf_op jit(solution)/shard_map/attend_shard/pallas_call | solution.py:301
  51.1 0.2 collective-permute-start.4
  51.4 1.1 collective-permute-done.4.other_ref
  52.5 4.4 %collective-permute-done.6.refs_0_.refs_2_ = bf16[1,2048,128]{2,1,0:T(8,128)(2,1)S(1)} collective-permute-done((bf16[1,2048,128]{2,1,0:T(8,128)(2,1)}, bf16[1,2048,128]{2,1,0:T(8,128)(2,1)S(1)}, u32[]{:S(2)}, u32[]{:S(2)}) %collective-permute-start.6) | collective-permute-done | bytes 524320 | tf_op jit(solution)/shard_map/ppermute | solution.py:433
  56.9 0.8 copy-done.6
  57.7 1.0 copy-done.7
  58.7 0.1 merge_packed.1.refs_0_
  58.8 0.2 collective-permute-start.9
  59.0 1.9 collective-permute-start.7
  60.9 3.1 %arrange.11 = bf16[2,1024,2,128]{3,2,1,0:T(2,128)(2,1)} custom-call(s32[4]{0:T(128)S(1)} %copy-done.11, bf16[4,1024,4,128]{3,2,1,0:T(4,128)(2,1)} %refs_0_.15, bf16[4,1024,4,128]{3,2,1,0:T(4,128)(2,1)} %refs_1_.15, f32[8,2688]{1,0:T(8,128)S(1)} %pack_products.1.refs_2_), custom_call_target="tpu_custom_call" | custom-call | tf_op jit(solution)/shard_map/arrange/pallas_call | solution.py:92
  64.0 4.4 %collective-permute-done.11.refs_4_.refs_3_ = bf16[1,2048,128]{2,1,0:T(8,128)(2,1)} collective-permute-done((bf16[1,2048,128]{2,1,0:T(8,128)(2,1)}, bf16[1,2048,128]{2,1,0:T(8,128)(2,1)}, u32[]{:S(2)}, u32[]{:S(2)}) %collective-permute-start.11) | collective-permute-done | bytes 524320 | tf_op jit(solution)/shard_map/ppermute | solution.py:433
  68.4 1.5 collective-permute-done.9.refs_4_.refs_3_
  70.0 4.3 %collective-permute-done.8.refs_3_.refs_2_ = f32[130,128]{1,0:T(8,128)S(1)} collective-permute-done((f32[130,128]{1,0:T(8,128)S(1)}, f32[130,128]{1,0:T(8,128)S(1)}, u32[]{:S(2)}, u32[]{:S(2)}) %collective-permute-start.8) | collective-permute-done | bytes 66592 | tf_op jit(solution)/shard_map/ppermute | solution.py:439
  74.3 1.0 hold.5
  75.4 3.6 %arrange.15 = bf16[2,1024,2,128]{3,2,1,0:T(2,128)(2,1)} custom-call(s32[4]{0:T(128)S(1)} %copy-done.11, bf16[4,1024,4,128]{3,2,1,0:T(4,128)(2,1)} %refs_0_.15, bf16[4,1024,4,128]{3,2,1,0:T(4,128)(2,1)} %refs_1_.15, f32[130,128]{1,0:T(8,128)S(1)} %collective-permute-done.7.refs_2_.refs_1_, f32[130,128]{1,0:T(8,128)S(1)} %collective-permute-done.8.refs_3_.refs_2_, ...), custom_call_target="tpu_custom_call" | custom-call | tf_op jit(solution)/shard_map/arrange/pallas_call | solution.py:92
  79.1 3.4 %arrange.12 = bf16[2,1024,2,128]{3,2,1,0:T(2,128)(2,1)} custom-call(s32[4]{0:T(128)S(1)} %copy-done.11, bf16[4,1024,4,128]{3,2,1,0:T(4,128)(2,1)} %refs_0_.15, bf16[4,1024,4,128]{3,2,1,0:T(4,128)(2,1)} %refs_1_.15, f32[130,128]{1,0:T(8,128)S(1)} %collective-permute-done.7.refs_2_.refs_1_, f32[130,128]{1,0:T(8,128)S(1)} %collective-permute-done.8.refs_3_.refs_2_, ...), custom_call_target="tpu_custom_call" | custom-call | tf_op jit(solution)/shard_map/arrange/pallas_call | solution.py:92
  82.5 0.8 collective-permute-start.13
  83.3 3.1 %arrange.13 = bf16[2,1024,2,128]{3,2,1,0:T(2,128)(2,1)} custom-call(s32[4]{0:T(128)S(1)} %copy-done.11, bf16[4,1024,4,128]{3,2,1,0:T(4,128)(2,1)} %refs_0_.15, bf16[4,1024,4,128]{3,2,1,0:T(4,128)(2,1)} %refs_1_.15, f32[130,128]{1,0:T(8,128)S(1)} %collective-permute-done.7.refs_2_.refs_1_, f32[130,128]{1,0:T(8,128)S(1)} %collective-permute-done.8.refs_3_.refs_2_, ...), custom_call_target="tpu_custom_call" | custom-call | tf_op jit(solution)/shard_map/arrange/pallas_call | solution.py:92
  86.4 2.5 %collective-permute-start.14 = (bf16[2,2048,128]{2,1,0:T(8,128)(2,1)}, bf16[2,2048,128]{2,1,0:T(8,128)(2,1)}, u32[]{:S(2)}, u32[]{:S(2)}) collective-permute-start(bf16[2,2048,128]{2,1,0:T(8,128)(2,1)} %bitcast.60), channel_id=1, source_target_pairs={{0,8},{1,9},{4,12},{5,13},{8,0},{9,1},{12,4},{13,5},{2,10},{3,11},... | collective-permute-start | bytes 3145736 | tf_op jit(solution)/shard_map/ppermute | solution.py:433
  88.9 0.6 dynamic_slice.6
  89.5 0.1 pad_maximum_fusion.4
  89.6 3.4 %arrange.10 = bf16[2,1024,2,128]{3,2,1,0:T(2,128)(2,1)} custom-call(s32[4]{0:T(128)S(1)} %copy-done.11, bf16[4,1024,4,128]{3,2,1,0:T(4,128)(2,1)} %refs_0_.15, bf16[4,1024,4,128]{3,2,1,0:T(4,128)(2,1)} %refs_1_.15, f32[130,128]{1,0:T(8,128)S(1)} %collective-permute-done.7.refs_2_.refs_1_, f32[130,128]{1,0:T(8,128)S(1)} %collective-permute-done.8.refs_3_.refs_2_, ...), custom_call_target="tpu_custom_call" | custom-call | tf_op jit(solution)/shard_map/arrange/pallas_call | solution.py:92
  93.0 0.2 collective-permute-start.10
  93.3 3.1 %arrange.14 = bf16[2,1024,2,128]{3,2,1,0:T(2,128)(2,1)} custom-call(s32[4]{0:T(128)S(1)} %copy-done.11, bf16[4,1024,4,128]{3,2,1,0:T(4,128)(2,1)} %refs_0_.15, bf16[4,1024,4,128]{3,2,1,0:T(4,128)(2,1)} %refs_1_.15, f32[130,128]{1,0:T(8,128)S(1)} %collective-permute-done.7.refs_2_.refs_1_, f32[130,128]{1,0:T(8,128)S(1)} %collective-permute-done.8.refs_3_.refs_2_, ...), custom_call_target="tpu_custom_call" | custom-call | tf_op jit(solution)/shard_map/arrange/pallas_call | solution.py:92
  96.3 5.2 %collective-permute-done.12.refs_0_.refs_7_ = bf16[2,2048,128]{2,1,0:T(8,128)(2,1)S(1)} collective-permute-done((bf16[2,2048,128]{2,1,0:T(8,128)(2,1)}, bf16[2,2048,128]{2,1,0:T(8,128)(2,1)S(1)}, u32[]{:S(2)}, u32[]{:S(2)}) %collective-permute-start.12) | collective-permute-done | bytes 1048608 | tf_op jit(solution)/shard_map/ppermute | solution.py:433
  101.6 1.0 copy-done.1
  102.6 1.2 copy-done.2
  103.8 0.3 finish.1
  104.1 0.6 gather_fusion
  104.7 4.9 %fusion = f32[4,2,2048]{2,1,0:T(2,128)S(1)} fusion(bf16[4,2,2048]{2,1,0:T(2,128)(2,1)S(1)} %reshape.200, bf16[2048,2048]{1,0:T(8,128)(2,1)} %param.21), kind=kOutput, calls=%fused_computation.1 | convolution fusion | flops 67108864 | bytes 8486912 | tf_op jit(solution)/shard_map/dot_general | solution.py:525
  109.6 3.0 %assemble.3 = (bf16[16384,128]{1,0:T(8,128)(2,1)}, bf16[16384,128]{1,0:T(8,128)(2,1)}) custom-call(bf16[1,2048,128]{2,1,0:T(8,128)(2,1)S(1)} %copy-done.5, bf16[1,2048,128]{2,1,0:T(8,128)(2,1)S(1)} %collective-permute-done.5.refs_3_.refs_1_, bf16[1,2048,128]{2,1,0:T(8,128)(2,1)S(1)} %copy-done.8, ...), custom_call_target="tpu_custom_call" | custom-call | bytes 8388608 | tf_op jit(solution)/shard_map/assemble/pallas_call | solution.py:162
  112.6 11.1 %collective-permute-done.13.refs_1_ = bf16[2,2048,128]{2,1,0:T(8,128)(2,1)} collective-permute-done((bf16[2,2048,128]{2,1,0:T(8,128)(2,1)}, bf16[2,2048,128]{2,1,0:T(8,128)(2,1)}, u32[]{:S(2)}, u32[]{:S(2)}) %collective-permute-start.13) | collective-permute-done | bytes 1048608 | tf_op jit(solution)/shard_map/ppermute | solution.py:433
  123.8 65.3 %collective-permute-done.14.refs_2_ = bf16[2,2048,128]{2,1,0:T(8,128)(2,1)} collective-permute-done((bf16[2,2048,128]{2,1,0:T(8,128)(2,1)}, bf16[2,2048,128]{2,1,0:T(8,128)(2,1)}, u32[]{:S(2)}, u32[]{:S(2)}) %collective-permute-start.14) | collective-permute-done | bytes 1048608 | tf_op jit(solution)/shard_map/ppermute | solution.py:433
  189.0 2.9 %assemble.4 = (bf16[16384,128]{1,0:T(8,128)(2,1)}, bf16[16384,128]{1,0:T(8,128)(2,1)}) custom-call(bf16[2,2048,128]{2,1,0:T(8,128)(2,1)S(1)} %copy-done.2, bf16[2,2048,128]{2,1,0:T(8,128)(2,1)} %collective-permute-done.13.refs_1_, bf16[2,2048,128]{2,1,0:T(8,128)(2,1)} %collective-permute-done.14.refs_2_, ...), custom_call_target="tpu_custom_call", output_to_operand_aliasing={{0}: (3, {}), {1}: (4, {})} | custom-call | bytes 6291456 | tf_op jit(solution)/shard_map/assemble/pallas_call | solution.py:162
  191.9 5.8 %all-gather = f32[16,2,2048]{2,1,0:T(2,128)S(1)} all-gather(f32[4,2,2048]{2,1,0:T(2,128)S(1)} %fusion), channel_id=2, replica_groups=mesh['groups'=2,'ctx'=4,'head'=2,'sub'=2] {'head','sub'}, dimensions={0}, use_global_device_ids=true | all-gather | bytes 327680 | tf_op jit(solution)/shard_map/all_gather | solution.py:528
  197.7 0.7 fusion.8
  198.4 0.6 slice_bitcast_fusion
  199.0 11.6 %collective-permute-done.10.refs_0_ = bf16[2,2048,128]{2,1,0:T(8,128)(2,1)} collective-permute-done((bf16[2,2048,128]{2,1,0:T(8,128)(2,1)}, bf16[2,2048,128]{2,1,0:T(8,128)(2,1)}, u32[]{:S(2)}, u32[]{:S(2)}) %collective-permute-start.10) | collective-permute-done | bytes 1048608 | tf_op jit(solution)/shard_map/ppermute | solution.py:433
  210.6 2.0 assemble.5
  (52 shorter events, 0.5 us)
Async XLA Ops:
  0.6 15.8 %copy-start = (bf16[2048,256]{1,0:T(8,128)(2,1)S(1)}, bf16[2048,256]{1,0:T(8,128)(2,1)}, u32[]{:S(2)}) copy-start(bf16[2048,256]{1,0:T(8,128)(2,1)} %param.19) | copy-start | bytes 3145732
  0.6 0.7 copy-start.10
  1.4 15.0 %copy-start.12 = (s32[4]{0:T(128)S(1)}, s32[4]{0:T(128)}, u32[]{:S(2)}) copy-start(s32[4]{0:T(128)} %lengths_ref.1) | copy-start | bytes 52
  1.4 15.0 %copy-start.14 = (bf16[2048]{0:T(1024)(128)(2,1)S(1)}, bf16[2048]{0:T(1024)(128)(2,1)}, u32[]{:S(2)}) copy-start(bf16[2048]{0:T(1024)(128)(2,1)} %param.17) | copy-start | bytes 12292
  1.4 15.3 %copy-start.13 = (bf16[2048,256]{1,0:T(8,128)(2,1)S(1)}, bf16[2048,256]{1,0:T(8,128)(2,1)}, u32[]{:S(2)}) copy-start(bf16[2048,256]{1,0:T(8,128)(2,1)} %param.20) | copy-start | bytes 3145732
  4.5 18.0 %collective-permute-start = (bf16[1,2048,128]{2,1,0:T(8,128)(2,1)}, bf16[1,2048,128]{2,1,0:T(8,128)(2,1)S(1)}, u32[]{:S(2)}, u32[]{:S(2)}) collective-permute-start(bf16[1,2048,128]{2,1,0:T(8,128)(2,1)} %bitcast.67), channel_id=1, source_target_pairs={{0,4},{1,5},{4,8},{5,9},{8,12},{9,13},{12,0},{13,1},{2,6},{3,7},{6... | collective-permute-start | bytes 1572872 | tf_op jit(solution)/shard_map/ppermute | solution.py:433
  8.9 0.7 copy-start.9
  9.6 31.3 %collective-permute-start.5 = (bf16[1,2048,128]{2,1,0:T(8,128)(2,1)}, bf16[1,2048,128]{2,1,0:T(8,128)(2,1)S(1)}, u32[]{:S(2)}, u32[]{:S(2)}) collective-permute-start(bf16[1,2048,128]{2,1,0:T(8,128)(2,1)} %hold.3), channel_id=1, source_target_pairs={{0,4},{1,5},{4,8},{5,9},{8,12},{9,13},{12,0},{13,1},{2,6},{3,7},{6... | collective-permute-start | bytes 1572872 | tf_op jit(solution)/shard_map/ppermute | solution.py:433
  17.0 8.8 %copy-start.11 = (s32[4]{0:T(128)S(1)}, s32[4]{0:T(128)}, u32[]{:S(2)}) copy-start(s32[4]{0:T(128)} %order_ref.15) | copy-start | bytes 52
  22.5 28.6 %copy-start.4 = (bf16[1,2048,128]{2,1,0:T(8,128)(2,1)}, bf16[1,2048,128]{2,1,0:T(8,128)(2,1)S(1)}, u32[]{:S(2)}) copy-start(bf16[1,2048,128]{2,1,0:T(8,128)(2,1)S(1)} %collective-permute-done.refs_4_.refs_0_) | copy-start | bytes 1572868
  22.6 12.6 %collective-permute-start.3 = (f32[8,2688]{1,0:T(8,128)S(1)}, f32[8,2688]{1,0:T(8,128)S(1)}, u32[]{:S(2)}, u32[]{:S(2)}) collective-permute-start(f32[8,2688]{1,0:T(8,128)S(1)} %pack_products.1.refs_2_), channel_id=1, source_target_pairs={{0,12},{4,0},{8,4},{12,8},{1,13},{5,1},{9,5},{13,9},{2,14},{6,2},{... | collective-permute-start | bytes 258056 | tf_op jit(solution)/shard_map/ppermute | solution.py:439
  24.7 16.0 %collective-permute-start.2 = (f32[8,2688]{1,0:T(8,128)S(1)}, f32[8,2688]{1,0:T(8,128)S(1)}, u32[]{:S(2)}, u32[]{:S(2)}) collective-permute-start(f32[8,2688]{1,0:T(8,128)S(1)} %pack_products.1.refs_2_), channel_id=1, source_target_pairs={{0,8},{4,12},{8,0},{12,4},{1,9},{5,13},{9,1},{13,5},{2,10},{6,14},... | collective-permute-start | bytes 258056 | tf_op jit(solution)/shard_map/ppermute | solution.py:439
  24.7 15.9 %collective-permute-start.1 = (f32[8,2688]{1,0:T(8,128)S(1)}, f32[8,2688]{1,0:T(8,128)S(1)}, u32[]{:S(2)}, u32[]{:S(2)}) collective-permute-start(f32[8,2688]{1,0:T(8,128)S(1)} %pack_products.1.refs_2_), channel_id=1, source_target_pairs={{0,4},{4,8},{8,12},{12,0},{1,5},{5,9},{9,13},{13,1},{2,6},{6,10},{... | collective-permute-start | bytes 258056 | tf_op jit(solution)/shard_map/ppermute | solution.py:439
  40.9 16.0 %collective-permute-start.6 = (bf16[1,2048,128]{2,1,0:T(8,128)(2,1)}, bf16[1,2048,128]{2,1,0:T(8,128)(2,1)S(1)}, u32[]{:S(2)}, u32[]{:S(2)}) collective-permute-start(bf16[1,2048,128]{2,1,0:T(8,128)(2,1)} %get-tuple-element.24), channel_id=1, source_target_pairs={{0,5},{1,4},{4,9},{5,8},{8,13},{9,12},{12,1},{13,0},{2,7},{3,6},{6... | collective-permute-start | bytes 1572872 | tf_op jit(solution)/shard_map/ppermute | solution.py:433
  40.9 27.5 %collective-permute-start.11 = (bf16[1,2048,128]{2,1,0:T(8,128)(2,1)}, bf16[1,2048,128]{2,1,0:T(8,128)(2,1)}, u32[]{:S(2)}, u32[]{:S(2)}) collective-permute-start(bf16[1,2048,128]{2,1,0:T(8,128)(2,1)} %get-tuple-element.25), channel_id=1, source_target_pairs={{0,5},{1,4},{4,9},{5,8},{8,13},{9,12},{12,1},{13,0},{2,7},{3,6},{6... | collective-permute-start | bytes 1572872 | tf_op jit(solution)/shard_map/ppermute | solution.py:433
  51.1 1.3 collective-permute-start.4
  56.9 0.8 copy-start.6
  57.7 1.0 copy-start.7
  58.8 11.1 %collective-permute-start.9 = (f32[130,128]{1,0:T(8,128)S(1)}, f32[130,128]{1,0:T(8,128)S(1)}, u32[]{:S(2)}, u32[]{:S(2)}) collective-permute-start(f32[130,128]{1,0:T(8,128)S(1)} %merge_packed.1.refs_0_), channel_id=1, source_target_pairs={{0,12},{4,0},{8,4},{12,8},{1,13},{5,1},{9,5},{13,9},{2,14},{6,2},{... | collective-permute-start | bytes 199688 | tf_op jit(solution)/shard_map/ppermute | solution.py:439
  59.0 15.3 %collective-permute-start.8 = (f32[130,128]{1,0:T(8,128)S(1)}, f32[130,128]{1,0:T(8,128)S(1)}, u32[]{:S(2)}, u32[]{:S(2)}) collective-permute-start(f32[130,128]{1,0:T(8,128)S(1)} %merge_packed.1.refs_0_), channel_id=1, source_target_pairs={{0,8},{4,12},{8,0},{12,4},{1,9},{5,13},{9,1},{13,5},{2,10},{6,14},... | collective-permute-start | bytes 199688 | tf_op jit(solution)/shard_map/ppermute | solution.py:439
  59.0 15.3 %collective-permute-start.7 = (f32[130,128]{1,0:T(8,128)S(1)}, f32[130,128]{1,0:T(8,128)S(1)}, u32[]{:S(2)}, u32[]{:S(2)}) collective-permute-start(f32[130,128]{1,0:T(8,128)S(1)} %merge_packed.1.refs_0_), channel_id=1, source_target_pairs={{0,4},{4,8},{8,12},{12,0},{1,5},{5,9},{9,13},{13,1},{2,6},{6,10},{... | collective-permute-start | bytes 199688 | tf_op jit(solution)/shard_map/ppermute | solution.py:439
  75.3 26.2 %collective-permute-start.12 = (bf16[2,2048,128]{2,1,0:T(8,128)(2,1)}, bf16[2,2048,128]{2,1,0:T(8,128)(2,1)S(1)}, u32[]{:S(2)}, u32[]{:S(2)}) collective-permute-start(bf16[2,2048,128]{2,1,0:T(8,128)(2,1)} %hold.5), channel_id=1, source_target_pairs={{0,12},{1,13},{4,0},{5,1},{8,4},{9,5},{12,8},{13,9},{2,14},{3,15},... | collective-permute-start | bytes 3145736 | tf_op jit(solution)/shard_map/ppermute | solution.py:433
  79.0 30.6 %collective-permute-start.15 = (bf16[2,2048,128]{2,1,0:T(8,128)(2,1)}, bf16[2,2048,128]{2,1,0:T(8,128)(2,1)}, u32[]{:S(2)}, u32[]{:S(2)}) collective-permute-start(bf16[2,2048,128]{2,1,0:T(8,128)(2,1)} %bitcast.64), channel_id=1, source_target_pairs={{0,1},{1,0},{4,5},{5,4},{8,9},{9,8},{12,13},{13,12},{2,3},{3,2},{6... | collective-permute-start | bytes 3145736 | tf_op jit(solution)/shard_map/ppermute | solution.py:433
  82.5 41.3 %collective-permute-start.13 = (bf16[2,2048,128]{2,1,0:T(8,128)(2,1)}, bf16[2,2048,128]{2,1,0:T(8,128)(2,1)}, u32[]{:S(2)}, u32[]{:S(2)}) collective-permute-start(bf16[2,2048,128]{2,1,0:T(8,128)(2,1)} %bitcast.58), channel_id=1, source_target_pairs={{0,13},{1,12},{4,1},{5,0},{8,5},{9,4},{12,9},{13,8},{2,15},{3,14},... | collective-permute-start | bytes 3145736 | tf_op jit(solution)/shard_map/ppermute | solution.py:433
  86.4 102.7 %collective-permute-start.14 = (bf16[2,2048,128]{2,1,0:T(8,128)(2,1)}, bf16[2,2048,128]{2,1,0:T(8,128)(2,1)}, u32[]{:S(2)}, u32[]{:S(2)}) collective-permute-start(bf16[2,2048,128]{2,1,0:T(8,128)(2,1)} %bitcast.60), channel_id=1, source_target_pairs={{0,8},{1,9},{4,12},{5,13},{8,0},{9,1},{12,4},{13,5},{2,10},{3,11},... | collective-permute-start | bytes 3145736 | tf_op jit(solution)/shard_map/ppermute | solution.py:433
  93.0 117.6 %collective-permute-start.10 = (bf16[2,2048,128]{2,1,0:T(8,128)(2,1)}, bf16[2,2048,128]{2,1,0:T(8,128)(2,1)}, u32[]{:S(2)}, u32[]{:S(2)}) collective-permute-start(bf16[2,2048,128]{2,1,0:T(8,128)(2,1)} %bitcast.62), channel_id=1, source_target_pairs={{0,9},{1,8},{4,13},{5,12},{8,1},{9,0},{12,5},{13,4},{2,11},{3,10},... | collective-permute-start | bytes 3145736 | tf_op jit(solution)/shard_map/ppermute | solution.py:433
  101.6 1.0 copy-start.1
  102.6 1.2 copy-start.2
  104.7 4.9 %copy-start.3 = (bf16[2,1024,2,128]{3,2,1,0:T(2,128)(2,1)S(1)}, bf16[2,1024,2,128]{3,2,1,0:T(2,128)(2,1)}, u32[]{:S(2)}) copy-start(bf16[2,1024,2,128]{3,2,1,0:T(2,128)(2,1)} %arrange.14) | copy-start | bytes 3145732
  104.7 4.9 %copy-start.5 = (bf16[1,2048,128]{2,1,0:T(8,128)(2,1)S(1)}, bf16[1,2048,128]{2,1,0:T(8,128)(2,1)}, u32[]{:S(2)}) copy-start(bf16[1,2048,128]{2,1,0:T(8,128)(2,1)} %copy-done.4) | copy-start | bytes 1572868
  104.7 4.9 %copy-start.8 = (bf16[1,2048,128]{2,1,0:T(8,128)(2,1)S(1)}, bf16[1,2048,128]{2,1,0:T(8,128)(2,1)}, u32[]{:S(2)}) copy-start(bf16[1,2048,128]{2,1,0:T(8,128)(2,1)} %copy-done.6) | copy-start | bytes 1572868

commit v9 on v8

--- a/solution.py
+++ b/solution.py
@@ -194,23 +194,40 @@
     )(first, second, in_hbm(after))
 
 
+def in_parts(x, count):
+    parts = []
+    for _ in range(count):
+        part = x.astype(jnp.bfloat16).astype(jnp.float32)
+        parts.append(part)
+        x = x - part
+    return parts
+
+
 def pack_products(products, wide, after):
     rows = wide.shape[0]
     widths = [x.shape[1] for x in products]
+    total = sum(widths) + LANES
+    columns = 2 * total - widths[0]
 
     def kernel(*refs):
         wide_ref, out_ref = refs[len(products)], refs[-1]
+        squares = jnp.sum(wide_ref[...] * wide_ref[...], axis=1, keepdims=True)
+        values = [ref[:rows] + ref[rows:] for ref in refs[: len(products)]]
+        values.append(jnp.broadcast_to(squares, (rows, LANES)))
         low = 0
-        for ref, columns in zip(refs, widths):
-            out_ref[:, low : low + columns] = ref[:rows] + ref[rows:]
-            low += columns
-        squares = jnp.sum(wide_ref[...] * wide_ref[...], axis=1, keepdims=True)
-        out_ref[:, low:] = jnp.broadcast_to(squares, (rows, LANES))
+        for i, value in enumerate(values):
+            first, second = in_parts(value, 2)
+            high = low + value.shape[1]
+            out_ref[:, low:high] = first.astype(jnp.bfloat16)
+            if i:
+                shift = total - widths[0]
+                out_ref[:, low + shift : high + shift] = second.astype(jnp.bfloat16)
+            low = high
 
     whole = pl.BlockSpec(memory_space=pltpu.VMEM)
     return pl.pallas_call(
         kernel,
-        out_shape=pltpu.VMEM((rows, sum(widths) + LANES), jnp.float32),
+        out_shape=pltpu.VMEM((rows, columns), jnp.bfloat16),
         in_specs=[whole] * (len(products) + 1 + len(after)),
         out_specs=whole,
         name="pack_products",
@@ -317,13 +334,10 @@
     )(lengths, queries, in_hbm(flat_keys), in_hbm(flat_values))
 
 
-def packed_sizes(packed_rows):
-    extra = packed_rows // (LANES + 2)
-    return extra * LANES, extra
-
-
 def merge_packed(kept, other, after):
-    count, extra = packed_sizes(kept.shape[0])
+    extra = kept.shape[0] // (LANES + 2)
+    count = extra * LANES
+    tail = -(-5 * extra // 16) * 16
 
     def kernel(kept_ref, other_ref, *refs):
         out_ref = refs[-1]
@@ -333,16 +347,16 @@
         scales = [jnp.exp(x - largest) for x in maxima]
         out_ref[:count, :] = sum(
             ref[:count, :] * to_columns(scale) for ref, scale in zip(both, scales)
-        )
-        out_ref[count : count + extra, :] = largest
-        out_ref[count + extra :, :] = sum(
-            ref[count + extra :, :] * scale for ref, scale in zip(both, scales)
-        )
+        ).astype(jnp.bfloat16)
+        totals = sum(ref[count + extra :, :] * scale for ref, scale in zip(both, scales))
+        rest = in_parts(largest, 3) + in_parts(totals, 2)
+        rest.append(jnp.zeros((tail - 5 * extra, LANES), jnp.float32))
+        out_ref[count:, :] = jnp.concatenate(rest).astype(jnp.bfloat16)
 
     whole = pl.BlockSpec(memory_space=pltpu.VMEM)
     return pl.pallas_call(
         kernel,
-        out_shape=pltpu.VMEM(kept.shape, kept.dtype),
+        out_shape=pltpu.VMEM((count + tail, LANES), jnp.bfloat16),
         in_specs=[whole] * (2 + len(after)),
         out_specs=whole,
         name="merge_packed",
@@ -350,9 +364,9 @@
 
 
 def finish(packed, queries, fresh_keys, fresh_values, group_size, score_factor, after, made):
-    count, extra = packed_sizes(packed[0].shape[0])
     shares = len(packed)
-    head_dim = queries.shape[1]
+    count, head_dim = queries.shape
+    extra = count // LANES
 
     def kernel(*refs):
         out_ref = refs[-1]
@@ -366,14 +380,18 @@
             for u in range(2)
         ]
         scores[1] = jnp.where(second, scores[1], masked_score)
-        maxima = [to_columns(ref[count : count + extra, :]) for ref in packed_refs]
-        totals = [to_columns(ref[count + extra :, :]) for ref in packed_refs]
+        tails = [ref[count:, :].astype(jnp.float32) for ref in packed_refs]
+        part = lambda tail, i: tail[i * extra : (i + 1) * extra]
+        maxima = [to_columns(part(t, 0) + part(t, 1) + part(t, 2)) for t in tails]
+        totals = [to_columns(part(t, 3) + part(t, 4)) for t in tails]
         largest = functools.reduce(jnp.maximum, maxima + scores)
         scales = [jnp.exp(x - largest) for x in maxima]
         weights = [jnp.exp(x - largest) for x in scores]
         weights[1] = jnp.where(second, weights[1], 0.0)
         denominator = sum(t * scale for t, scale in zip(totals, scales)) + weights[0] + weights[1]
-        numerator = sum(ref[:count, :] * scale for ref, scale in zip(packed_refs, scales))
+        numerator = sum(
+            ref[:count, :].astype(jnp.float32) * scale for ref, scale in zip(packed_refs, scales)
+        )
         for u in range(2):
             rounded = weights[u].astype(jnp.bfloat16).astype(jnp.float32)
             numerator = numerator + rounded * value_ref[u].astype(jnp.float32)
@@ -467,10 +485,13 @@
         wide,
         (ahead[0],),
     )
-    summed = functools.reduce(jnp.add, from_all(partial))
+    summed = functools.reduce(jnp.add, [x.astype(jnp.float32) for x in from_all(partial)])
     waiting = hold(make(1, 1, (partial,), apart=True), (summed, ahead[1]))
     behind = [send(waiting[w], (w,), 1, 1) for w in both]
-    raw = summed[:, :-LANES] * lax.rsqrt(summed[:, -LANES:][:, :1] / width + eps_norm)
+    others = 2 * key_width + LANES
+    tail = summed[:, query_width : query_width + others] + summed[:, query_width + others :]
+    raw = jnp.concatenate([summed[:, :query_width], tail[:, :-LANES]], axis=1)
+    raw = raw * lax.rsqrt(tail[:, -LANES:][:, :1] / width + eps_norm)
     raw = raw.reshape(requests, 2, -1, head_dim)
     positions = lengths.astype(jnp.float32)[:, None] + jnp.arange(2, dtype=jnp.float32)
     query_heads = query_width // head_dim

time: 214 us -> 208 us (0.972)
  waiting for transfers between devices: 121 us -> 112 us
  local copies, waits for them, and re-layouts: 7.35 us -> 10.1 us
    ppermute x6, waiting for transfers between devices: 17.3 us -> 11 us  [from_all(): lax.ppermute(values, 'ctx', [(c, (c + shift) % ctx_count) for c in range(...]
    ppermute x9, waiting for transfers between devices: 103 us -> 99.5 us  [send(): moved = lax.ppermute(block, ('ctx', 'sub'), pairs)]
    unnamed x30 -> x62, local copies, waits for them, and re-layouts: 5.48 us -> 7.35 us
  transfers between devices with their start and end apart: 16 -> 16, of which waited for: 12 -> 11; matrix products, arithmetic and copies ran while one was open for 6% -> 8% of each run, Pallas kernels for 18% -> 18%
where the time goes in v9:
time: 208 us; the launch traced here: 207 us
  waiting for transfers between devices  112 us (54%)
  Pallas kernels  43.1 us (21%)
  starting transfers between devices  14.6 us (7%)
  blocking collectives  12.8 us (6%)
  matrix products  11.2 us (5%)
  local copies, waits for them, and re-layouts  10.1 us (5%)
  other arithmetic  2.13 us (1%)
    ppermute x9, waiting for transfers between devices, send(): moved = lax.ppermute(block, ('ctx', 'sub'), pairs)  99.5 us
    pallas_call x8, Pallas kernels, arrange(): pl.pallas_call(kernel, out_shape=(pltpu.HBM(shape, caches[0].dtype),) * o...  26.2 us
    ppermute x6, waiting for transfers between devices, from_all(): lax.ppermute(values, 'ctx', [(c, (c + shift) % ctx_count) for c in range(...  11 us
    ppermute x9, starting transfers between devices, send(): moved = lax.ppermute(block, ('ctx', 'sub'), pairs)  9.19 us
    pallas_call x3, Pallas kernels, assemble(): pl.pallas_call(kernel, out_shape=(pltpu.HBM((rows, head_dim), blocks[0].d...  8.03 us
    unnamed x62, local copies, waits for them, and re-layouts  7.35 us
    pallas_call x1, Pallas kernels, attend_shard(): pl.pallas_call(kernel, out_shape=(pltpu.VMEM(packed, jnp.float32),) * 2,...  7.04 us
    dot_general x3, matrix products, local(): jnp.dot(halves, weight, preferred_element_type=jnp.float32)  6.32 us
  transfers between devices with their start and end apart: 16, of which 11 were waited for; matrix products, arithmetic and copies ran while one was open for 8% of the time, Pallas kernels for 18%

profile of v9, /device:TPU:0, one launch (start us, length us, event | category | flops | bytes accessed | tf_op | source)
XLA Modules:
  0.0 206.7 jit_solution(16134361575473678657)
XLA Ops:
  0.7 0.7 copy-done.21
  1.4 3.1 %arrange.8 = (bf16[1,1024,2,128]{3,2,1,0:T(2,128)(2,1)}, bf16[1,1024,2,128]{3,2,1,0:T(2,128)(2,1)}) custom-call(s32[4]{0:T(128)S(1)} %copy-done.21, bf16[4,1024,4,128]{3,2,1,0:T(4,128)(2,1)} %refs_0_.15, bf16[4,1024,4,128]{3,2,1,0:T(4,128)(2,1)} %refs_1_.15), custom_call_target="tpu_custom_call" | custom-call | tf_op jit(solution)/shard_map/arrange/pallas_call | solution.py:92
  4.5 3.1 %collective-permute-start = (bf16[1,2048,128]{2,1,0:T(8,128)(2,1)}, bf16[1,2048,128]{2,1,0:T(8,128)(2,1)S(1)}, u32[]{:S(2)}, u32[]{:S(2)}) collective-permute-start(bf16[1,2048,128]{2,1,0:T(8,128)(2,1)} %bitcast.67), channel_id=1, source_target_pairs={{0,4},{1,5},{4,8},{5,9},{8,12},{9,13},{12,0},{13,1},{2,6},{3,7},{6... | collective-permute-start | bytes 1572872 | tf_op jit(solution)/shard_map/ppermute | solution.py:451
  7.5 1.3 pair_tokens.1.refs_1_
  8.9 0.7 copy-done.20
  9.6 1.6 collective-permute-start.5
  11.2 5.2 %all_gather.9 = bf16[4,2,2048]{2,1,0:T(2,128)(2,1)S(1)} all-gather(bf16[1,2,2048]{2,1,0:T(2,128)(2,1)S(1)} %copy-done.20), channel_id=1, replica_groups=mesh['groups'=2,'ctx'=4,'head'=2,'sub'=2] {'head','sub'}, dimensions={0}, use_global_device_ids=true | all-gather | bytes 40960 | tf_op jit(solution)/shard_map/all_gather | solution.py:472
  16.4 0.5 copy-done.29
  17.0 0.2 fusion.6.refs_1_
  17.3 1.5 fusion.5.refs_2_
  18.7 4.6 %fusion.7.refs_0_ = f32[16,2048]{1,0:T(8,128)S(1)} fusion(bf16[2048,2048]{1,0:T(8,128)(2,1)} %param.18, bf16[8,2048]{1,0:T(8,128)(2,1)S(1)} %get-tuple-element.46, bf16[8,2048]{1,0:T(8,128)(2,1)S(1)} %get-tuple-element.45), kind=kOutput, calls=%fused_computation.20 | convolution fusion | flops 134348800 | bytes 8585216 | tf_op jit(solution)/shard_map/dot_general | solution.py:482
  23.3 0.1 pack_products.1.refs_2_
  23.4 2.3 %collective-permute-start.3 = (bf16[8,3328]{1,0:T(8,128)(2,1)S(1)}, bf16[8,3328]{1,0:T(8,128)(2,1)S(1)}, u32[]{:S(2)}, u32[]{:S(2)}) collective-permute-start(bf16[8,3328]{1,0:T(8,128)(2,1)S(1)} %pack_products.1.refs_2_), channel_id=1, source_target_pairs={{0,12},{4,0},{8,4},{12,8},{1,13},{5,1},{9,5},{13,9},{2,14},{6,2},{... | collective-permute-start | bytes 159752 | tf_op jit(solution)/shard_map/ppermute | solution.py:457
  25.7 0.8 collective-permute-start.2
  26.5 0.1 multiply_cosine_fusion
  26.7 3.4 %arrange.9 = (bf16[1,1024,2,128]{3,2,1,0:T(2,128)(2,1)}, bf16[1,1024,2,128]{3,2,1,0:T(2,128)(2,1)}) custom-call(s32[4]{0:T(128)S(1)} %copy-done.22, bf16[4,1024,4,128]{3,2,1,0:T(4,128)(2,1)} %refs_0_.15, bf16[4,1024,4,128]{3,2,1,0:T(4,128)(2,1)} %refs_1_.15, bf16[8,3328]{1,0:T(8,128)(2,1)S(1)} %pack_products.1.refs_2_), custom_call_target="tpu_custom_call" | custom-call | tf_op jit(solution)/shard_map/arrange/pallas_call | solution.py:92
  30.1 4.4 %collective-permute-done.3 = bf16[8,3328]{1,0:T(8,128)(2,1)S(1)} collective-permute-done((bf16[8,3328]{1,0:T(8,128)(2,1)S(1)}, bf16[8,3328]{1,0:T(8,128)(2,1)S(1)}, u32[]{:S(2)}, u32[]{:S(2)}) %collective-permute-start.3) | collective-permute-done | bytes 53280 | tf_op jit(solution)/shard_map/ppermute | solution.py:457
  34.4 3.4 %collective-permute-done.2 = bf16[8,3328]{1,0:T(8,128)(2,1)S(1)} collective-permute-done((bf16[8,3328]{1,0:T(8,128)(2,1)S(1)}, bf16[8,3328]{1,0:T(8,128)(2,1)S(1)}, u32[]{:S(2)}, u32[]{:S(2)}) %collective-permute-start.2) | collective-permute-done | bytes 53280 | tf_op jit(solution)/shard_map/ppermute | solution.py:457
  37.9 0.1 fusion.11
  38.1 0.1 mul.83
  38.3 1.0 collective-permute-start.11
  39.4 0.1 add_convert_fusion
  39.5 0.1 fusion.4
  39.6 1.9 all_gather.10.q_ref
  41.5 7.0 %attend_shard.1 = (f32[130,128]{1,0:T(8,128)S(1)}, f32[130,128]{1,0:T(8,128)S(1)}) custom-call(s32[4]{0:T(128)S(1)} %copy-done.23, bf16[4,64,128]{2,1,0:T(8,128)(2,1)S(1)} %all_gather.10.q_ref, bf16[4,4096,128]{2,1,0:T(8,128)(2,1)} %bitcast.53, bf16[4,4096,128]{2,1,0:T(8,128)(2,1)} %bitcast.54), custom_call_target="tpu_custom_call" | custom-call | tf_op jit(solution)/shard_map/attend_shard/pallas_call | solution.py:318
  48.5 0.2 collective-permute-start.4
  48.7 1.1 collective-permute-done.4.other_ref
  49.8 4.4 %collective-permute-done.6.refs_0_.refs_2_ = bf16[1,2048,128]{2,1,0:T(8,128)(2,1)S(1)} collective-permute-done((bf16[1,2048,128]{2,1,0:T(8,128)(2,1)}, bf16[1,2048,128]{2,1,0:T(8,128)(2,1)S(1)}, u32[]{:S(2)}, u32[]{:S(2)}) %collective-permute-start.6) | collective-permute-done | bytes 524320 | tf_op jit(solution)/shard_map/ppermute | solution.py:451
  54.3 0.1 merge_packed.1.refs_0_
  54.4 0.2 collective-permute-start.9
  54.6 1.9 collective-permute-start.7
  56.5 3.1 %arrange.11 = bf16[2,1024,2,128]{3,2,1,0:T(2,128)(2,1)} custom-call(s32[4]{0:T(128)S(1)} %copy-done.22, bf16[4,1024,4,128]{3,2,1,0:T(4,128)(2,1)} %refs_0_.15, bf16[4,1024,4,128]{3,2,1,0:T(4,128)(2,1)} %refs_1_.15, bf16[8,3328]{1,0:T(8,128)(2,1)S(1)} %pack_products.1.refs_2_), custom_call_target="tpu_custom_call" | custom-call | tf_op jit(solution)/shard_map/arrange/pallas_call | solution.py:92
  59.6 6.1 %collective-permute-done.11.refs_4_.refs_3_ = bf16[1,2048,128]{2,1,0:T(8,128)(2,1)S(1)} collective-permute-done((bf16[1,2048,128]{2,1,0:T(8,128)(2,1)}, bf16[1,2048,128]{2,1,0:T(8,128)(2,1)S(1)}, u32[]{:S(2)}, u32[]{:S(2)}) %collective-permute-start.11) | collective-permute-done | bytes 524320 | tf_op jit(solution)/shard_map/ppermute | solution.py:451
  65.7 0.9 collective-permute-done.9.refs_4_.refs_3_
  66.6 2.2 %collective-permute-done.8.refs_3_.refs_2_ = bf16[144,128]{1,0:T(8,128)(2,1)S(1)} collective-permute-done((bf16[144,128]{1,0:T(8,128)(2,1)S(1)}, bf16[144,128]{1,0:T(8,128)(2,1)S(1)}, u32[]{:S(2)}, u32[]{:S(2)}) %collective-permute-start.8) | collective-permute-done | bytes 36896 | tf_op jit(solution)/shard_map/ppermute | solution.py:457
  68.9 0.8 copy-done.10
  69.7 3.6 %arrange.15 = bf16[2,1024,2,128]{3,2,1,0:T(2,128)(2,1)} custom-call(s32[4]{0:T(128)S(1)} %copy-done.22, bf16[4,1024,4,128]{3,2,1,0:T(4,128)(2,1)} %refs_0_.15, bf16[4,1024,4,128]{3,2,1,0:T(4,128)(2,1)} %refs_1_.15, bf16[144,128]{1,0:T(8,128)(2,1)S(1)} %collective-permute-done.7.refs_2_.refs_1_, bf16[144,128]{1,0:T(8,128)(2,1)S(1)} %collective-permute-done.8.refs_3_.refs_2_, ...), custom_call_target="tpu_custom_call" | custom-call | tf_op jit(solution)/shard_map/arrange/pallas_call | solution.py:92
  73.4 3.4 %arrange.12 = bf16[2,1024,2,128]{3,2,1,0:T(2,128)(2,1)} custom-call(s32[4]{0:T(128)S(1)} %copy-done.22, bf16[4,1024,4,128]{3,2,1,0:T(4,128)(2,1)} %refs_0_.15, bf16[4,1024,4,128]{3,2,1,0:T(4,128)(2,1)} %refs_1_.15, bf16[144,128]{1,0:T(8,128)(2,1)S(1)} %collective-permute-done.7.refs_2_.refs_1_, bf16[144,128]{1,0:T(8,128)(2,1)S(1)} %collective-permute-done.8.refs_3_.refs_2_, ...), custom_call_target="tpu_custom_call" | custom-call | tf_op jit(solution)/shard_map/arrange/pallas_call | solution.py:92
  76.9 0.6 collective-permute-start.13
  77.5 3.1 %arrange.13 = bf16[2,1024,2,128]{3,2,1,0:T(2,128)(2,1)} custom-call(s32[4]{0:T(128)S(1)} %copy-done.22, bf16[4,1024,4,128]{3,2,1,0:T(4,128)(2,1)} %refs_0_.15, bf16[4,1024,4,128]{3,2,1,0:T(4,128)(2,1)} %refs_1_.15, bf16[144,128]{1,0:T(8,128)(2,1)S(1)} %collective-permute-done.7.refs_2_.refs_1_, bf16[144,128]{1,0:T(8,128)(2,1)S(1)} %collective-permute-done.8.refs_3_.refs_2_, ...), custom_call_target="tpu_custom_call" | custom-call | tf_op jit(solution)/shard_map/arrange/pallas_call | solution.py:92
  80.6 2.7 %collective-permute-start.14 = (bf16[2,2048,128]{2,1,0:T(8,128)(2,1)}, bf16[2,2048,128]{2,1,0:T(8,128)(2,1)}, u32[]{:S(2)}, u32[]{:S(2)}) collective-permute-start(bf16[2,2048,128]{2,1,0:T(8,128)(2,1)} %bitcast.59), channel_id=1, source_target_pairs={{0,8},{1,9},{4,12},{5,13},{8,0},{9,1},{12,4},{13,5},{2,10},{3,11},... | collective-permute-start | bytes 3145736 | tf_op jit(solution)/shard_map/ppermute | solution.py:451
  83.3 0.6 dynamic_slice.6
  83.9 0.8 slice.101
  84.7 0.1 pad_maximum_fusion.5
  84.8 3.4 %arrange.10 = bf16[2,1024,2,128]{3,2,1,0:T(2,128)(2,1)} custom-call(s32[4]{0:T(128)S(1)} %copy-done.22, bf16[4,1024,4,128]{3,2,1,0:T(4,128)(2,1)} %refs_0_.15, bf16[4,1024,4,128]{3,2,1,0:T(4,128)(2,1)} %refs_1_.15, bf16[144,128]{1,0:T(8,128)(2,1)S(1)} %collective-permute-done.7.refs_2_.refs_1_, bf16[144,128]{1,0:T(8,128)(2,1)S(1)} %collective-permute-done.8.refs_3_.refs_2_, ...), custom_call_target="tpu_custom_call" | custom-call | tf_op jit(solution)/shard_map/arrange/pallas_call | solution.py:92
  88.3 3.1 %arrange.14 = bf16[2,1024,2,128]{3,2,1,0:T(2,128)(2,1)} custom-call(s32[4]{0:T(128)S(1)} %copy-done.22, bf16[4,1024,4,128]{3,2,1,0:T(4,128)(2,1)} %refs_0_.15, bf16[4,1024,4,128]{3,2,1,0:T(4,128)(2,1)} %refs_1_.15, bf16[144,128]{1,0:T(8,128)(2,1)S(1)} %collective-permute-done.7.refs_2_.refs_1_, bf16[144,128]{1,0:T(8,128)(2,1)S(1)} %collective-permute-done.8.refs_3_.refs_2_, ...), custom_call_target="tpu_custom_call" | custom-call | tf_op jit(solution)/shard_map/arrange/pallas_call | solution.py:92
  91.4 4.5 %collective-permute-done.12.refs_0_.refs_7_ = bf16[2,2048,128]{2,1,0:T(8,128)(2,1)S(1)} collective-permute-done((bf16[2,2048,128]{2,1,0:T(8,128)(2,1)}, bf16[2,2048,128]{2,1,0:T(8,128)(2,1)S(1)}, u32[]{:S(2)}, u32[]{:S(2)}) %collective-permute-start.12) | collective-permute-done | bytes 1048608 | tf_op jit(solution)/shard_map/ppermute | solution.py:451
  95.9 1.0 copy-done.2
  97.0 1.2 copy-done.3
  98.2 0.8 copy-done.13
  98.9 0.8 copy-done.15
  99.7 0.8 copy-done.19
  100.5 0.3 finish.1
  100.8 0.6 gather_fusion
  101.4 4.8 %fusion = f32[4,2,2048]{2,1,0:T(2,128)S(1)} fusion(bf16[4,2,2048]{2,1,0:T(2,128)(2,1)S(1)} %reshape.203, bf16[2048,2048]{1,0:T(8,128)(2,1)} %param.21), kind=kOutput, calls=%fused_computation.1 | convolution fusion | flops 67108864 | bytes 8486912 | tf_op jit(solution)/shard_map/dot_general | solution.py:546
  106.3 3.1 %assemble.3 = (bf16[16384,128]{1,0:T(8,128)(2,1)}, bf16[16384,128]{1,0:T(8,128)(2,1)}) custom-call(bf16[1,2048,128]{2,1,0:T(8,128)(2,1)S(1)} %copy-done.7, bf16[1,2048,128]{2,1,0:T(8,128)(2,1)S(1)} %copy-done.5, bf16[1,2048,128]{2,1,0:T(8,128)(2,1)S(1)} %copy-done.9, bf16[1,2048,128]{2,1,0:T(8,128)(2,1)S(1)} %copy-done.11, ...), custom_call_target="tpu_custom_call" | custom-call | bytes 8388608 | tf_op jit(solution)/shard_map/assemble/pallas_call | solution.py:162
  109.4 8.4 %collective-permute-done.13.refs_1_ = bf16[2,2048,128]{2,1,0:T(8,128)(2,1)} collective-permute-done((bf16[2,2048,128]{2,1,0:T(8,128)(2,1)}, bf16[2,2048,128]{2,1,0:T(8,128)(2,1)}, u32[]{:S(2)}, u32[]{:S(2)}) %collective-permute-start.13) | collective-permute-done | bytes 1048608 | tf_op jit(solution)/shard_map/ppermute | solution.py:451
  117.9 66.9 %collective-permute-done.14.refs_2_ = bf16[2,2048,128]{2,1,0:T(8,128)(2,1)} collective-permute-done((bf16[2,2048,128]{2,1,0:T(8,128)(2,1)}, bf16[2,2048,128]{2,1,0:T(8,128)(2,1)}, u32[]{:S(2)}, u32[]{:S(2)}) %collective-permute-start.14) | collective-permute-done | bytes 1048608 | tf_op jit(solution)/shard_map/ppermute | solution.py:451
  184.7 2.9 %assemble.4 = (bf16[16384,128]{1,0:T(8,128)(2,1)}, bf16[16384,128]{1,0:T(8,128)(2,1)}) custom-call(bf16[2,2048,128]{2,1,0:T(8,128)(2,1)S(1)} %copy-done.3, bf16[2,2048,128]{2,1,0:T(8,128)(2,1)} %collective-permute-done.13.refs_1_, bf16[2,2048,128]{2,1,0:T(8,128)(2,1)} %collective-permute-done.14.refs_2_, ...), custom_call_target="tpu_custom_call", output_to_operand_aliasing={{0}: (3, {}), {1}: (4, {})} | custom-call | bytes 6291456 | tf_op jit(solution)/shard_map/assemble/pallas_call | solution.py:162
  187.6 5.8 %all-gather = f32[16,2,2048]{2,1,0:T(2,128)S(1)} all-gather(f32[4,2,2048]{2,1,0:T(2,128)S(1)} %fusion), channel_id=2, replica_groups=mesh['groups'=2,'ctx'=4,'head'=2,'sub'=2] {'head','sub'}, dimensions={0}, use_global_device_ids=true | all-gather | bytes 327680 | tf_op jit(solution)/shard_map/all_gather | solution.py:549
  193.5 1.4 fusion.8
  194.8 0.6 slice_bitcast_fusion
  195.4 9.1 %collective-permute-done.10.refs_0_ = bf16[2,2048,128]{2,1,0:T(8,128)(2,1)} collective-permute-done((bf16[2,2048,128]{2,1,0:T(8,128)(2,1)}, bf16[2,2048,128]{2,1,0:T(8,128)(2,1)}, u32[]{:S(2)}, u32[]{:S(2)}) %collective-permute-start.10) | collective-permute-done | bytes 1048608 | tf_op jit(solution)/shard_map/ppermute | solution.py:451
  204.5 2.0 assemble.5
  (89 shorter events, 0.7 us)
Async XLA Ops:
  0.6 16.4 %copy-start = (bf16[2048,256]{1,0:T(8,128)(2,1)S(1)}, bf16[2048,256]{1,0:T(8,128)(2,1)}, u32[]{:S(2)}) copy-start(bf16[2048,256]{1,0:T(8,128)(2,1)} %param.19) | copy-start | bytes 3145732
  0.6 0.7 copy-start.21
  1.4 15.0 %copy-start.23 = (s32[4]{0:T(128)S(1)}, s32[4]{0:T(128)}, u32[]{:S(2)}) copy-start(s32[4]{0:T(128)} %lengths_ref.1) | copy-start | bytes 52
  1.4 15.0 %copy-start.30 = (bf16[2048]{0:T(1024)(128)(2,1)S(1)}, bf16[2048]{0:T(1024)(128)(2,1)}, u32[]{:S(2)}) copy-start(bf16[2048]{0:T(1024)(128)(2,1)} %param.17) | copy-start | bytes 12292
  4.5 18.9 %collective-permute-start = (bf16[1,2048,128]{2,1,0:T(8,128)(2,1)}, bf16[1,2048,128]{2,1,0:T(8,128)(2,1)S(1)}, u32[]{:S(2)}, u32[]{:S(2)}) collective-permute-start(bf16[1,2048,128]{2,1,0:T(8,128)(2,1)} %bitcast.67), channel_id=1, source_target_pairs={{0,4},{1,5},{4,8},{5,9},{8,12},{9,13},{12,0},{13,1},{2,6},{3,7},{6... | collective-permute-start | bytes 1572872 | tf_op jit(solution)/shard_map/ppermute | solution.py:451
  8.9 0.7 copy-start.20
  9.6 28.6 %collective-permute-start.5 = (bf16[1,2048,128]{2,1,0:T(8,128)(2,1)}, bf16[1,2048,128]{2,1,0:T(8,128)(2,1)S(1)}, u32[]{:S(2)}, u32[]{:S(2)}) collective-permute-start(bf16[1,2048,128]{2,1,0:T(8,128)(2,1)} %hold.3), channel_id=1, source_target_pairs={{0,4},{1,5},{4,8},{5,9},{8,12},{9,13},{12,0},{13,1},{2,6},{3,7},{6... | collective-permute-start | bytes 1572872 | tf_op jit(solution)/shard_map/ppermute | solution.py:451
  16.4 0.6 copy-start.29
  18.7 7.9 %copy-start.22 = (s32[4]{0:T(128)S(1)}, s32[4]{0:T(128)}, u32[]{:S(2)}) copy-start(s32[4]{0:T(128)} %order_ref.15) | copy-start | bytes 52
  23.3 25.2 %copy-start.6 = (bf16[1,2048,128]{2,1,0:T(8,128)(2,1)}, bf16[1,2048,128]{2,1,0:T(8,128)(2,1)S(1)}, u32[]{:S(2)}) copy-start(bf16[1,2048,128]{2,1,0:T(8,128)(2,1)S(1)} %collective-permute-done.refs_4_.refs_0_) | copy-start | bytes 1572868
  23.4 11.0 %collective-permute-start.3 = (bf16[8,3328]{1,0:T(8,128)(2,1)S(1)}, bf16[8,3328]{1,0:T(8,128)(2,1)S(1)}, u32[]{:S(2)}, u32[]{:S(2)}) collective-permute-start(bf16[8,3328]{1,0:T(8,128)(2,1)S(1)} %pack_products.1.refs_2_), channel_id=1, source_target_pairs={{0,12},{4,0},{8,4},{12,8},{1,13},{5,1},{9,5},{13,9},{2,14},{6,2},{... | collective-permute-start | bytes 159752 | tf_op jit(solution)/shard_map/ppermute | solution.py:457
  25.7 12.2 %collective-permute-start.2 = (bf16[8,3328]{1,0:T(8,128)(2,1)S(1)}, bf16[8,3328]{1,0:T(8,128)(2,1)S(1)}, u32[]{:S(2)}, u32[]{:S(2)}) collective-permute-start(bf16[8,3328]{1,0:T(8,128)(2,1)S(1)} %pack_products.1.refs_2_), channel_id=1, source_target_pairs={{0,8},{4,12},{8,0},{12,4},{1,9},{5,13},{9,1},{13,5},{2,10},{6,14},... | collective-permute-start | bytes 159752 | tf_op jit(solution)/shard_map/ppermute | solution.py:457
  26.5 11.4 %collective-permute-start.1 = (bf16[8,3328]{1,0:T(8,128)(2,1)S(1)}, bf16[8,3328]{1,0:T(8,128)(2,1)S(1)}, u32[]{:S(2)}, u32[]{:S(2)}) collective-permute-start(bf16[8,3328]{1,0:T(8,128)(2,1)S(1)} %pack_products.1.refs_2_), channel_id=1, source_target_pairs={{0,4},{4,8},{8,12},{12,0},{1,5},{5,9},{9,13},{13,1},{2,6},{6,10},{... | collective-permute-start | bytes 159752 | tf_op jit(solution)/shard_map/ppermute | solution.py:457
  38.2 21.4 %copy-start.4 = (bf16[1,2048,128]{2,1,0:T(8,128)(2,1)}, bf16[1,2048,128]{2,1,0:T(8,128)(2,1)S(1)}, u32[]{:S(2)}) copy-start(bf16[1,2048,128]{2,1,0:T(8,128)(2,1)S(1)} %collective-permute-done.5.refs_3_.refs_1_) | copy-start | bytes 1572868
  38.2 16.0 %collective-permute-start.6 = (bf16[1,2048,128]{2,1,0:T(8,128)(2,1)}, bf16[1,2048,128]{2,1,0:T(8,128)(2,1)S(1)}, u32[]{:S(2)}, u32[]{:S(2)}) collective-permute-start(bf16[1,2048,128]{2,1,0:T(8,128)(2,1)} %get-tuple-element.24), channel_id=1, source_target_pairs={{0,5},{1,4},{4,9},{5,8},{8,13},{9,12},{12,1},{13,0},{2,7},{3,6},{6... | collective-permute-start | bytes 1572872 | tf_op jit(solution)/shard_map/ppermute | solution.py:451
  38.3 27.4 %collective-permute-start.11 = (bf16[1,2048,128]{2,1,0:T(8,128)(2,1)}, bf16[1,2048,128]{2,1,0:T(8,128)(2,1)S(1)}, u32[]{:S(2)}, u32[]{:S(2)}) collective-permute-start(bf16[1,2048,128]{2,1,0:T(8,128)(2,1)} %get-tuple-element.25), channel_id=1, source_target_pairs={{0,5},{1,4},{4,9},{5,8},{8,13},{9,12},{12,1},{13,0},{2,7},{3,6},{6... | collective-permute-start | bytes 1572872 | tf_op jit(solution)/shard_map/ppermute | solution.py:451
  39.4 2.1 %copy-start.24 = (f32[4,2,20,128]{3,2,1,0:T(8,128)}, f32[4,2,20,128]{3,2,1,0:T(8,128)S(1)}, u32[]{:S(2)}) copy-start(f32[4,2,20,128]{3,2,1,0:T(8,128)S(1)} %broadcast_multiply_fusion) | copy-start | bytes 245764
  39.5 2.0 copy-start.27
  39.5 20.1 %copy-start.25 = (bf16[4,2,18,64]{3,2,1,0:T(8,128)(2,1)}, bf16[4,2,18,64]{3,2,1,0:T(8,128)(2,1)S(1)}, u32[]{:S(2)}) copy-start(bf16[4,2,18,64]{3,2,1,0:T(8,128)(2,1)S(1)} %get-tuple-element.43) | copy-start | bytes 55300
  39.6 14.7 %copy-start.16 = (bf16[4,2,2,8,128]{4,3,2,1,0:T(8,128)(2,1)}, bf16[4,2,2,8,128]{4,3,2,1,0:T(8,128)(2,1)S(1)}, u32[]{:S(2)}) copy-start(bf16[4,2,2,8,128]{4,3,2,1,0:T(8,128)(2,1)S(1)} %copy.31) | copy-start | bytes 98308
  48.5 1.3 collective-permute-start.4
  54.3 19.1 %copy-start.8 = (bf16[1,2048,128]{2,1,0:T(8,128)(2,1)}, bf16[1,2048,128]{2,1,0:T(8,128)(2,1)S(1)}, u32[]{:S(2)}) copy-start(bf16[1,2048,128]{2,1,0:T(8,128)(2,1)S(1)} %collective-permute-done.6.refs_0_.refs_2_) | copy-start | bytes 1572868
  54.4 14.5 %copy-start.18 = (bf16[144,128]{1,0:T(8,128)(2,1)}, bf16[144,128]{1,0:T(8,128)(2,1)S(1)}, u32[]{:S(2)}) copy-start(bf16[144,128]{1,0:T(8,128)(2,1)S(1)} %merge_packed.1.refs_0_) | copy-start | bytes 110596
  54.4 12.2 %collective-permute-start.9 = (bf16[144,128]{1,0:T(8,128)(2,1)S(1)}, bf16[144,128]{1,0:T(8,128)(2,1)S(1)}, u32[]{:S(2)}, u32[]{:S(2)}) collective-permute-start(bf16[144,128]{1,0:T(8,128)(2,1)S(1)} %merge_packed.1.refs_0_), channel_id=1, source_target_pairs={{0,12},{4,0},{8,4},{12,8},{1,13},{5,1},{9,5},{13,9},{2,14},{6,2},{... | collective-permute-start | bytes 110600 | tf_op jit(solution)/shard_map/ppermute | solution.py:457
  54.6 14.3 %collective-permute-start.8 = (bf16[144,128]{1,0:T(8,128)(2,1)S(1)}, bf16[144,128]{1,0:T(8,128)(2,1)S(1)}, u32[]{:S(2)}, u32[]{:S(2)}) collective-permute-start(bf16[144,128]{1,0:T(8,128)(2,1)S(1)} %merge_packed.1.refs_0_), channel_id=1, source_target_pairs={{0,8},{4,12},{8,0},{12,4},{1,9},{5,13},{9,1},{13,5},{2,10},{6,14},... | collective-permute-start | bytes 110600 | tf_op jit(solution)/shard_map/ppermute | solution.py:457
  54.6 14.3 %collective-permute-start.7 = (bf16[144,128]{1,0:T(8,128)(2,1)S(1)}, bf16[144,128]{1,0:T(8,128)(2,1)S(1)}, u32[]{:S(2)}, u32[]{:S(2)}) collective-permute-start(bf16[144,128]{1,0:T(8,128)(2,1)S(1)} %merge_packed.1.refs_0_), channel_id=1, source_target_pairs={{0,4},{4,8},{8,12},{12,0},{1,5},{5,9},{9,13},{13,1},{2,6},{6,10},{... | collective-permute-start | bytes 110600 | tf_op jit(solution)/shard_map/ppermute | solution.py:457
  68.9 19.4 %copy-start.12 = (bf16[144,128]{1,0:T(8,128)(2,1)}, bf16[144,128]{1,0:T(8,128)(2,1)S(1)}, u32[]{:S(2)}) copy-start(bf16[144,128]{1,0:T(8,128)(2,1)S(1)} %collective-permute-done.8.refs_3_.refs_2_) | copy-start | bytes 110596
  68.9 19.4 %copy-start.14 = (bf16[144,128]{1,0:T(8,128)(2,1)}, bf16[144,128]{1,0:T(8,128)(2,1)S(1)}, u32[]{:S(2)}) copy-start(bf16[144,128]{1,0:T(8,128)(2,1)S(1)} %collective-permute-done.7.refs_2_.refs_1_) | copy-start | bytes 110596
  68.9 0.8 copy-start.10
  69.7 26.2 %collective-permute-start.12 = (bf16[2,2048,128]{2,1,0:T(8,128)(2,1)}, bf16[2,2048,128]{2,1,0:T(8,128)(2,1)S(1)}, u32[]{:S(2)}, u32[]{:S(2)}) collective-permute-start(bf16[2,2048,128]{2,1,0:T(8,128)(2,1)} %hold.5), channel_id=1, source_target_pairs={{0,12},{1,13},{4,0},{5,1},{8,4},{9,5},{12,8},{13,9},{2,14},{3,15},... | collective-permute-start | bytes 3145736 | tf_op jit(solution)/shard_map/ppermute | solution.py:451
  73.3 11.3 %copy-start.26 = (bf16[4,2,18,64]{3,2,1,0:T(8,128)(2,1)S(1)}, bf16[4,2,18,64]{3,2,1,0:T(8,128)(2,1)}, u32[]{:S(2)}) copy-start(bf16[4,2,18,64]{3,2,1,0:T(8,128)(2,1)} %copy-done.25) | copy-start | bytes 55300
  73.3 11.3 %copy-start.28 = (bf16[4,2,18,64]{3,2,1,0:T(8,128)(2,1)S(1)}, bf16[4,2,18,64]{3,2,1,0:T(8,128)(2,1)}, u32[]{:S(2)}) copy-start(bf16[4,2,18,64]{3,2,1,0:T(8,128)(2,1)} %copy-done.27) | copy-start | bytes 55300
  73.3 32.9 %collective-permute-start.15 = (bf16[2,2048,128]{2,1,0:T(8,128)(2,1)}, bf16[2,2048,128]{2,1,0:T(8,128)(2,1)}, u32[]{:S(2)}, u32[]{:S(2)}) collective-permute-start(bf16[2,2048,128]{2,1,0:T(8,128)(2,1)} %bitcast.64), channel_id=1, source_target_pairs={{0,1},{1,0},{4,5},{5,4},{8,9},{9,8},{12,13},{13,12},{2,3},{3,2},{6... | collective-permute-start | bytes 3145736 | tf_op jit(solution)/shard_map/ppermute | solution.py:451
  76.9 41.0 %collective-permute-start.13 = (bf16[2,2048,128]{2,1,0:T(8,128)(2,1)}, bf16[2,2048,128]{2,1,0:T(8,128)(2,1)}, u32[]{:S(2)}, u32[]{:S(2)}) collective-permute-start(bf16[2,2048,128]{2,1,0:T(8,128)(2,1)} %bitcast.57), channel_id=1, source_target_pairs={{0,13},{1,12},{4,1},{5,0},{8,5},{9,4},{12,9},{13,8},{2,15},{3,14},... | collective-permute-start | bytes 3145736 | tf_op jit(solution)/shard_map/ppermute | solution.py:451
  80.6 104.1 %collective-permute-start.14 = (bf16[2,2048,128]{2,1,0:T(8,128)(2,1)}, bf16[2,2048,128]{2,1,0:T(8,128)(2,1)}, u32[]{:S(2)}, u32[]{:S(2)}) collective-permute-start(bf16[2,2048,128]{2,1,0:T(8,128)(2,1)} %bitcast.59), channel_id=1, source_target_pairs={{0,8},{1,9},{4,12},{5,13},{8,0},{9,1},{12,4},{13,5},{2,10},{3,11},... | collective-permute-start | bytes 3145736 | tf_op jit(solution)/shard_map/ppermute | solution.py:451
  84.8 12.2 %copy-start.17 = (bf16[4,2,2,8,128]{4,3,2,1,0:T(8,128)(2,1)S(1)}, bf16[4,2,2,8,128]{4,3,2,1,0:T(8,128)(2,1)}, u32[]{:S(2)}) copy-start(bf16[4,2,2,8,128]{4,3,2,1,0:T(8,128)(2,1)} %copy-done.16) | copy-start | bytes 98308
  88.2 116.3 %collective-permute-start.10 = (bf16[2,2048,128]{2,1,0:T(8,128)(2,1)}, bf16[2,2048,128]{2,1,0:T(8,128)(2,1)}, u32[]{:S(2)}, u32[]{:S(2)}) collective-permute-start(bf16[2,2048,128]{2,1,0:T(8,128)(2,1)} %bitcast.61), channel_id=1, source_target_pairs={{0,9},{1,8},{4,13},{5,12},{8,1},{9,0},{12,5},{13,4},{2,11},{3,10},... | collective-permute-start | bytes 3145736 | tf_op jit(solution)/shard_map/ppermute | solution.py:451
  91.4 14.9 %copy-start.1 = (bf16[2,1024,2,128]{3,2,1,0:T(2,128)(2,1)S(1)}, bf16[2,1024,2,128]{3,2,1,0:T(2,128)(2,1)}, u32[]{:S(2)}) copy-start(bf16[2,1024,2,128]{3,2,1,0:T(2,128)(2,1)} %arrange.14) | copy-start | bytes 3145732
  95.9 1.0 copy-start.2
  96.9 1.2 copy-start.3
  98.2 0.8 copy-start.13
  98.9 0.8 copy-start.15
  99.7 0.8 copy-start.19
  101.4 4.9 %copy-start.5 = (bf16[1,2048,128]{2,1,0:T(8,128)(2,1)S(1)}, bf16[1,2048,128]{2,1,0:T(8,128)(2,1)}, u32[]{:S(2)}) copy-start(bf16[1,2048,128]{2,1,0:T(8,128)(2,1)} %copy-done.4) | copy-start | bytes 1572868
  101.4 4.9 %copy-start.7 = (bf16[1,2048,128]{2,1,0:T(8,128)(2,1)S(1)}, bf16[1,2048,128]{2,1,0:T(8,128)(2,1)}, u32[]{:S(2)}) copy-start(bf16[1,2048,128]{2,1,0:T(8,128)(2,1)} %copy-done.6) | copy-start | bytes 1572868
  101.4 4.9 %copy-start.9 = (bf16[1,2048,128]{2,1,0:T(8,128)(2,1)S(1)}, bf16[1,2048,128]{2,1,0:T(8,128)(2,1)}, u32[]{:S(2)}) copy-start(bf16[1,2048,128]{2,1,0:T(8,128)(2,1)} %copy-done.8) | copy-start | bytes 1572868
  101.4 4.9 %copy-start.11 = (bf16[1,2048,128]{2,1,0:T(8,128)(2,1)S(1)}, bf16[1,2048,128]{2,1,0:T(8,128)(2,1)}, u32[]{:S(2)}) copy-start(bf16[1,2048,128]{2,1,0:T(8,128)(2,1)} %copy-done.10) | copy-start | bytes 1572868

commit v10 on v9

--- a/solution.py
+++ b/solution.py
@@ -109,7 +109,7 @@
     return blocks if apart else blocks[0]
 
 
-def hold(blocks, after):
+def hold(blocks, after, stored=()):
     def kernel(*refs):
         pass
 
@@ -117,14 +117,20 @@
     return pl.pallas_call(
         kernel,
         out_shape=tuple(pltpu.HBM(x.shape, x.dtype) for x in blocks),
-        in_specs=[in_place] * len(blocks) + vmem_specs(len(after)),
+        in_specs=[in_place] * len(blocks)
+        + vmem_specs(len(after))
+        + [in_place] * len(stored),
         out_specs=(in_place,) * len(blocks),
         input_output_aliases={i: i for i in range(len(blocks))},
         name="hold",
-    )(*(in_hbm(x) for x in blocks), *(in_vmem(x) for x in after))
-
-
-def assemble(blocks, pieces, filled=()):
+    )(
+        *(in_hbm(x) for x in blocks),
+        *(in_vmem(x) for x in after),
+        *(in_hbm(x) for x in stored),
+    )
+
+
+def assemble(blocks, pieces, filled, straight):
     ctx_count = lax.axis_size("ctx")
     core_count = lax.axis_size("sub")
     _, block_rows, head_dim = blocks[0].shape
@@ -145,16 +151,18 @@
                 core + (core_count - flip), core_count
             )
             place = pl.ds(pl.multiple_of(source * block_rows, block_rows), block_rows)
-            into.append(
-                pltpu.make_async_copy(in_refs[block].at[entry], held.at[p], in_sems.at[p])
-            )
+            taken = in_refs[block].at[entry]
+            if not straight:
+                into.append(pltpu.make_async_copy(taken, held.at[p], in_sems.at[p]))
+                taken = held.at[p]
             out_of.append(
-                pltpu.make_async_copy(held.at[p], out_refs[output].at[place], out_sems.at[p])
+                pltpu.make_async_copy(taken, out_refs[output].at[place], out_sems.at[p])
             )
         for copy in into:
             copy.start()
         for p in range(total):
-            into[p].wait()
+            if not straight:
+                into[p].wait()
             out_of[p].start()
         for copy in out_of:
             copy.wait()
@@ -162,11 +170,11 @@
     return pl.pallas_call(
         kernel,
         out_shape=(pltpu.HBM((rows, head_dim), blocks[0].dtype),) * arrays,
-        in_specs=[pl.BlockSpec(memory_space=pl.ANY)] * count
+        in_specs=(vmem_specs(count) if straight else [pl.BlockSpec(memory_space=pl.ANY)] * count)
         + [pl.BlockSpec(memory_space=pltpu.HBM)] * len(filled),
         out_specs=(pl.BlockSpec(memory_space=pltpu.HBM),) * arrays,
         scratch_shapes=[
-            pltpu.VMEM((total, block_rows, head_dim), blocks[0].dtype),
+            pltpu.VMEM((1 if straight else total, block_rows, head_dim), blocks[0].dtype),
             pltpu.SemaphoreType.DMA((total,)),
             pltpu.SemaphoreType.DMA((total,)),
         ],
@@ -176,7 +184,7 @@
             flops=0, transcendentals=0, bytes_accessed=4 * total * block_rows * head_dim
         ),
         name="assemble",
-    )(*blocks, *filled)
+    )(*(in_vmem(x) if straight else x for x in blocks), *filled)
 
 
 def pair_tokens(first, second, after):
@@ -517,7 +525,7 @@
         for shift in sorted(range(2, ctx_count), key=lambda d: -d)
         for flip in range(sub_count)
     ]
-    blocks = hold([make(*rest[0], (partial,))], (*packed[1:], behind[1]))
+    blocks = hold([make(*rest[0], (partial,))], tuple(packed[1:]), (behind[1],))
     blocks = [*blocks, *(make(*key, tuple(packed[1:])) for key in rest[1:])]
     for block, key in zip(blocks, rest):
         send(block, both, *key)
@@ -565,7 +573,7 @@
             for block, (which, shift, flip) in enumerate(keys)
             for entry, output in enumerate(which)
         ]
-        moved = assemble([received[key] for key in keys], pieces, moved)
+        moved = assemble([received[key] for key in keys], pieces, moved, len(keys) == 1)
     moved_keys, moved_values = (x.reshape(1, -1, heads_decode, head_dim) for x in moved)
     return (moved_keys, moved_values, result[:, 0], result[:, 1])
 

time: 208 us -> 208 us (level)
  no operation moved by 1% of the time
where the time goes in v10:
time: 208 us; the launch traced here: 206 us
  waiting for transfers between devices  112 us (54%)
  Pallas kernels  43.3 us (21%)
  starting transfers between devices  14.6 us (7%)
  blocking collectives  12.8 us (6%)
  matrix products  11.2 us (5%)
  local copies, waits for them, and re-layouts  9.27 us (4%)
  other arithmetic  2.13 us (1%)
    ppermute x9, waiting for transfers between devices, send(): moved = lax.ppermute(block, ('ctx', 'sub'), pairs)  99.5 us
    pallas_call x8, Pallas kernels, arrange(): pl.pallas_call(kernel, out_shape=(pltpu.HBM(shape, caches[0].dtype),) * o...  26.2 us
    ppermute x6, waiting for transfers between devices, from_all(): lax.ppermute(values, 'ctx', [(c, (c + shift) % ctx_count) for c in range(...  11 us
    ppermute x9, starting transfers between devices, send(): moved = lax.ppermute(block, ('ctx', 'sub'), pairs)  9.24 us
    pallas_call x3, Pallas kernels, assemble(): pl.pallas_call(kernel, out_shape=(pltpu.HBM((rows, head_dim), blocks[0].d...  8.21 us
    pallas_call x1, Pallas kernels, attend_shard(): pl.pallas_call(kernel, out_shape=(pltpu.VMEM(packed, jnp.float32),) * 2,...  7.04 us
    unnamed x62, local copies, waits for them, and re-layouts  6.55 us
    dot_general x3, matrix products, local(): jnp.dot(halves, weight, preferred_element_type=jnp.float32)  6.32 us
  transfers between devices with their start and end apart: 16, of which 11 were waited for; matrix products, arithmetic and copies ran while one was open for 8% of the time, Pallas kernels for 18%

profile of v10, /device:TPU:0, one launch (start us, length us, event | category | flops | bytes accessed | tf_op | source)
XLA Modules:
  0.0 206.1 jit_solution(13595193422176923708)
XLA Ops:
  0.7 0.7 copy-done.21
  1.4 3.1 %arrange.8 = (bf16[1,1024,2,128]{3,2,1,0:T(2,128)(2,1)}, bf16[1,1024,2,128]{3,2,1,0:T(2,128)(2,1)}) custom-call(s32[4]{0:T(128)S(1)} %copy-done.21, bf16[4,1024,4,128]{3,2,1,0:T(4,128)(2,1)} %refs_0_.15, bf16[4,1024,4,128]{3,2,1,0:T(4,128)(2,1)} %refs_1_.15), custom_call_target="tpu_custom_call" | custom-call | tf_op jit(solution)/shard_map/arrange/pallas_call | solution.py:92
  4.5 3.1 %collective-permute-start = (bf16[1,2048,128]{2,1,0:T(8,128)(2,1)}, bf16[1,2048,128]{2,1,0:T(8,128)(2,1)S(1)}, u32[]{:S(2)}, u32[]{:S(2)}) collective-permute-start(bf16[1,2048,128]{2,1,0:T(8,128)(2,1)} %bitcast.67), channel_id=1, source_target_pairs={{0,4},{1,5},{4,8},{5,9},{8,12},{9,13},{12,0},{13,1},{2,6},{3,7},{6... | collective-permute-start | bytes 1572872 | tf_op jit(solution)/shard_map/ppermute | solution.py:459
  7.5 1.3 pair_tokens.1.refs_1_
  8.9 0.7 copy-done.20
  9.6 1.6 collective-permute-start.5
  11.2 5.2 %all_gather.9 = bf16[4,2,2048]{2,1,0:T(2,128)(2,1)S(1)} all-gather(bf16[1,2,2048]{2,1,0:T(2,128)(2,1)S(1)} %copy-done.20), channel_id=1, replica_groups=mesh['groups'=2,'ctx'=4,'head'=2,'sub'=2] {'head','sub'}, dimensions={0}, use_global_device_ids=true | all-gather | bytes 40960 | tf_op jit(solution)/shard_map/all_gather | solution.py:480
  16.4 0.5 copy-done.29
  17.0 0.2 fusion.6.refs_1_
  17.3 1.5 fusion.5.refs_2_
  18.7 4.6 %fusion.7.refs_0_ = f32[16,2048]{1,0:T(8,128)S(1)} fusion(bf16[2048,2048]{1,0:T(8,128)(2,1)} %param.18, bf16[8,2048]{1,0:T(8,128)(2,1)S(1)} %get-tuple-element.46, bf16[8,2048]{1,0:T(8,128)(2,1)S(1)} %get-tuple-element.45), kind=kOutput, calls=%fused_computation.20 | convolution fusion | flops 134348800 | bytes 8585216 | tf_op jit(solution)/shard_map/dot_general | solution.py:490
  23.3 0.1 pack_products.1.refs_2_
  23.4 2.3 %collective-permute-start.3 = (bf16[8,3328]{1,0:T(8,128)(2,1)S(1)}, bf16[8,3328]{1,0:T(8,128)(2,1)S(1)}, u32[]{:S(2)}, u32[]{:S(2)}) collective-permute-start(bf16[8,3328]{1,0:T(8,128)(2,1)S(1)} %pack_products.1.refs_2_), channel_id=1, source_target_pairs={{0,12},{4,0},{8,4},{12,8},{1,13},{5,1},{9,5},{13,9},{2,14},{6,2},{... | collective-permute-start | bytes 159752 | tf_op jit(solution)/shard_map/ppermute | solution.py:465
  25.7 0.8 collective-permute-start.2
  26.5 0.1 multiply_cosine_fusion
  26.7 3.4 %arrange.9 = (bf16[1,1024,2,128]{3,2,1,0:T(2,128)(2,1)}, bf16[1,1024,2,128]{3,2,1,0:T(2,128)(2,1)}) custom-call(s32[4]{0:T(128)S(1)} %copy-done.22, bf16[4,1024,4,128]{3,2,1,0:T(4,128)(2,1)} %refs_0_.15, bf16[4,1024,4,128]{3,2,1,0:T(4,128)(2,1)} %refs_1_.15, bf16[8,3328]{1,0:T(8,128)(2,1)S(1)} %pack_products.1.refs_2_), custom_call_target="tpu_custom_call" | custom-call | tf_op jit(solution)/shard_map/arrange/pallas_call | solution.py:92
  30.1 4.4 %collective-permute-done.3 = bf16[8,3328]{1,0:T(8,128)(2,1)S(1)} collective-permute-done((bf16[8,3328]{1,0:T(8,128)(2,1)S(1)}, bf16[8,3328]{1,0:T(8,128)(2,1)S(1)}, u32[]{:S(2)}, u32[]{:S(2)}) %collective-permute-start.3) | collective-permute-done | bytes 53280 | tf_op jit(solution)/shard_map/ppermute | solution.py:465
  34.4 3.4 %collective-permute-done.2 = bf16[8,3328]{1,0:T(8,128)(2,1)S(1)} collective-permute-done((bf16[8,3328]{1,0:T(8,128)(2,1)S(1)}, bf16[8,3328]{1,0:T(8,128)(2,1)S(1)}, u32[]{:S(2)}, u32[]{:S(2)}) %collective-permute-start.2) | collective-permute-done | bytes 53280 | tf_op jit(solution)/shard_map/ppermute | solution.py:465
  37.9 0.1 fusion.11
  38.1 0.1 mul.83
  38.3 1.0 collective-permute-start.11
  39.3 0.1 broadcast_multiply_fusion
  39.4 0.1 add_convert_fusion
  39.5 0.1 fusion.4
  39.6 1.9 all_gather.10.q_ref
  41.5 7.0 %attend_shard.1 = (f32[130,128]{1,0:T(8,128)S(1)}, f32[130,128]{1,0:T(8,128)S(1)}) custom-call(s32[4]{0:T(128)S(1)} %copy-done.23, bf16[4,64,128]{2,1,0:T(8,128)(2,1)S(1)} %all_gather.10.q_ref, bf16[4,4096,128]{2,1,0:T(8,128)(2,1)} %bitcast.53, bf16[4,4096,128]{2,1,0:T(8,128)(2,1)} %bitcast.54), custom_call_target="tpu_custom_call" | custom-call | tf_op jit(solution)/shard_map/attend_shard/pallas_call | solution.py:326
  48.5 0.2 collective-permute-start.4
  48.7 1.1 collective-permute-done.4.other_ref
  49.8 4.4 %collective-permute-done.6.refs_0_.refs_2_ = bf16[1,2048,128]{2,1,0:T(8,128)(2,1)S(1)} collective-permute-done((bf16[1,2048,128]{2,1,0:T(8,128)(2,1)}, bf16[1,2048,128]{2,1,0:T(8,128)(2,1)S(1)}, u32[]{:S(2)}, u32[]{:S(2)}) %collective-permute-start.6) | collective-permute-done | bytes 524320 | tf_op jit(solution)/shard_map/ppermute | solution.py:459
  54.3 0.1 merge_packed.1.refs_0_
  54.4 0.2 collective-permute-start.9
  54.6 1.9 collective-permute-start.7
  56.5 3.1 %arrange.11 = bf16[2,1024,2,128]{3,2,1,0:T(2,128)(2,1)} custom-call(s32[4]{0:T(128)S(1)} %copy-done.22, bf16[4,1024,4,128]{3,2,1,0:T(4,128)(2,1)} %refs_0_.15, bf16[4,1024,4,128]{3,2,1,0:T(4,128)(2,1)} %refs_1_.15, bf16[8,3328]{1,0:T(8,128)(2,1)S(1)} %pack_products.1.refs_2_), custom_call_target="tpu_custom_call" | custom-call | tf_op jit(solution)/shard_map/arrange/pallas_call | solution.py:92
  59.6 6.1 %collective-permute-done.11.refs_4_.refs_3_ = bf16[1,2048,128]{2,1,0:T(8,128)(2,1)S(1)} collective-permute-done((bf16[1,2048,128]{2,1,0:T(8,128)(2,1)}, bf16[1,2048,128]{2,1,0:T(8,128)(2,1)S(1)}, u32[]{:S(2)}, u32[]{:S(2)}) %collective-permute-start.11) | collective-permute-done | bytes 524320 | tf_op jit(solution)/shard_map/ppermute | solution.py:459
  65.7 0.9 collective-permute-done.9.refs_4_.refs_3_
  66.6 2.2 %collective-permute-done.8.refs_3_.refs_2_ = bf16[144,128]{1,0:T(8,128)(2,1)S(1)} collective-permute-done((bf16[144,128]{1,0:T(8,128)(2,1)S(1)}, bf16[144,128]{1,0:T(8,128)(2,1)S(1)}, u32[]{:S(2)}, u32[]{:S(2)}) %collective-permute-start.8) | collective-permute-done | bytes 36896 | tf_op jit(solution)/shard_map/ppermute | solution.py:465
  69.0 3.6 %arrange.15 = bf16[2,1024,2,128]{3,2,1,0:T(2,128)(2,1)} custom-call(s32[4]{0:T(128)S(1)} %copy-done.22, bf16[4,1024,4,128]{3,2,1,0:T(4,128)(2,1)} %refs_0_.15, bf16[4,1024,4,128]{3,2,1,0:T(4,128)(2,1)} %refs_1_.15, bf16[144,128]{1,0:T(8,128)(2,1)S(1)} %collective-permute-done.7.refs_2_.refs_1_, bf16[144,128]{1,0:T(8,128)(2,1)S(1)} %collective-permute-done.8.refs_3_.refs_2_, ...), custom_call_target="tpu_custom_call" | custom-call | tf_op jit(solution)/shard_map/arrange/pallas_call | solution.py:92
  72.7 3.4 %arrange.12 = bf16[2,1024,2,128]{3,2,1,0:T(2,128)(2,1)} custom-call(s32[4]{0:T(128)S(1)} %copy-done.22, bf16[4,1024,4,128]{3,2,1,0:T(4,128)(2,1)} %refs_0_.15, bf16[4,1024,4,128]{3,2,1,0:T(4,128)(2,1)} %refs_1_.15, bf16[144,128]{1,0:T(8,128)(2,1)S(1)} %collective-permute-done.7.refs_2_.refs_1_, bf16[144,128]{1,0:T(8,128)(2,1)S(1)} %collective-permute-done.8.refs_3_.refs_2_, ...), custom_call_target="tpu_custom_call" | custom-call | tf_op jit(solution)/shard_map/arrange/pallas_call | solution.py:92
  76.1 0.6 collective-permute-start.13
  76.8 3.1 %arrange.13 = bf16[2,1024,2,128]{3,2,1,0:T(2,128)(2,1)} custom-call(s32[4]{0:T(128)S(1)} %copy-done.22, bf16[4,1024,4,128]{3,2,1,0:T(4,128)(2,1)} %refs_0_.15, bf16[4,1024,4,128]{3,2,1,0:T(4,128)(2,1)} %refs_1_.15, bf16[144,128]{1,0:T(8,128)(2,1)S(1)} %collective-permute-done.7.refs_2_.refs_1_, bf16[144,128]{1,0:T(8,128)(2,1)S(1)} %collective-permute-done.8.refs_3_.refs_2_, ...), custom_call_target="tpu_custom_call" | custom-call | tf_op jit(solution)/shard_map/arrange/pallas_call | solution.py:92
  79.9 2.7 %collective-permute-start.14 = (bf16[2,2048,128]{2,1,0:T(8,128)(2,1)}, bf16[2,2048,128]{2,1,0:T(8,128)(2,1)}, u32[]{:S(2)}, u32[]{:S(2)}) collective-permute-start(bf16[2,2048,128]{2,1,0:T(8,128)(2,1)} %bitcast.59), channel_id=1, source_target_pairs={{0,8},{1,9},{4,12},{5,13},{8,0},{9,1},{12,4},{13,5},{2,10},{3,11},... | collective-permute-start | bytes 3145736 | tf_op jit(solution)/shard_map/ppermute | solution.py:459
  82.6 0.6 dynamic_slice.6
  83.1 0.8 slice.101
  83.9 0.1 pad_maximum_fusion.5
  84.0 3.4 %arrange.10 = bf16[2,1024,2,128]{3,2,1,0:T(2,128)(2,1)} custom-call(s32[4]{0:T(128)S(1)} %copy-done.22, bf16[4,1024,4,128]{3,2,1,0:T(4,128)(2,1)} %refs_0_.15, bf16[4,1024,4,128]{3,2,1,0:T(4,128)(2,1)} %refs_1_.15, bf16[144,128]{1,0:T(8,128)(2,1)S(1)} %collective-permute-done.7.refs_2_.refs_1_, bf16[144,128]{1,0:T(8,128)(2,1)S(1)} %collective-permute-done.8.refs_3_.refs_2_, ...), custom_call_target="tpu_custom_call" | custom-call | tf_op jit(solution)/shard_map/arrange/pallas_call | solution.py:92
  87.6 3.1 %arrange.14 = bf16[2,1024,2,128]{3,2,1,0:T(2,128)(2,1)} custom-call(s32[4]{0:T(128)S(1)} %copy-done.22, bf16[4,1024,4,128]{3,2,1,0:T(4,128)(2,1)} %refs_0_.15, bf16[4,1024,4,128]{3,2,1,0:T(4,128)(2,1)} %refs_1_.15, bf16[144,128]{1,0:T(8,128)(2,1)S(1)} %collective-permute-done.7.refs_2_.refs_1_, bf16[144,128]{1,0:T(8,128)(2,1)S(1)} %collective-permute-done.8.refs_3_.refs_2_, ...), custom_call_target="tpu_custom_call" | custom-call | tf_op jit(solution)/shard_map/arrange/pallas_call | solution.py:92
  90.7 4.5 %collective-permute-done.12.refs_0_.refs_7_ = bf16[2,2048,128]{2,1,0:T(8,128)(2,1)S(1)} collective-permute-done((bf16[2,2048,128]{2,1,0:T(8,128)(2,1)}, bf16[2,2048,128]{2,1,0:T(8,128)(2,1)S(1)}, u32[]{:S(2)}, u32[]{:S(2)}) %collective-permute-start.12) | collective-permute-done | bytes 1048608 | tf_op jit(solution)/shard_map/ppermute | solution.py:459
  95.2 1.0 copy-done.2
  96.2 1.2 copy-done.3
  97.4 0.8 copy-done.13
  98.2 0.8 copy-done.15
  99.0 0.8 copy-done.19
  99.7 0.3 finish.1
  100.0 0.6 gather_fusion
  100.7 4.8 %fusion = f32[4,2,2048]{2,1,0:T(2,128)S(1)} fusion(bf16[4,2,2048]{2,1,0:T(2,128)(2,1)S(1)} %reshape.203, bf16[2048,2048]{1,0:T(8,128)(2,1)} %param.21), kind=kOutput, calls=%fused_computation.1 | convolution fusion | flops 67108864 | bytes 8486912 | tf_op jit(solution)/shard_map/dot_general | solution.py:554
  105.6 3.1 %assemble.3 = (bf16[16384,128]{1,0:T(8,128)(2,1)}, bf16[16384,128]{1,0:T(8,128)(2,1)}) custom-call(bf16[1,2048,128]{2,1,0:T(8,128)(2,1)S(1)} %copy-done.7, bf16[1,2048,128]{2,1,0:T(8,128)(2,1)S(1)} %copy-done.5, bf16[1,2048,128]{2,1,0:T(8,128)(2,1)S(1)} %copy-done.9, bf16[1,2048,128]{2,1,0:T(8,128)(2,1)S(1)} %copy-done.11, ...), custom_call_target="tpu_custom_call" | custom-call | bytes 8388608 | tf_op jit(solution)/shard_map/assemble/pallas_call | solution.py:170
  108.7 8.4 %collective-permute-done.13.refs_1_ = bf16[2,2048,128]{2,1,0:T(8,128)(2,1)} collective-permute-done((bf16[2,2048,128]{2,1,0:T(8,128)(2,1)}, bf16[2,2048,128]{2,1,0:T(8,128)(2,1)}, u32[]{:S(2)}, u32[]{:S(2)}) %collective-permute-start.13) | collective-permute-done | bytes 1048608 | tf_op jit(solution)/shard_map/ppermute | solution.py:459
  117.1 66.9 %collective-permute-done.14.refs_2_ = bf16[2,2048,128]{2,1,0:T(8,128)(2,1)} collective-permute-done((bf16[2,2048,128]{2,1,0:T(8,128)(2,1)}, bf16[2,2048,128]{2,1,0:T(8,128)(2,1)}, u32[]{:S(2)}, u32[]{:S(2)}) %collective-permute-start.14) | collective-permute-done | bytes 1048608 | tf_op jit(solution)/shard_map/ppermute | solution.py:459
  184.0 2.9 %assemble.4 = (bf16[16384,128]{1,0:T(8,128)(2,1)}, bf16[16384,128]{1,0:T(8,128)(2,1)}) custom-call(bf16[2,2048,128]{2,1,0:T(8,128)(2,1)S(1)} %copy-done.3, bf16[2,2048,128]{2,1,0:T(8,128)(2,1)} %collective-permute-done.13.refs_1_, bf16[2,2048,128]{2,1,0:T(8,128)(2,1)} %collective-permute-done.14.refs_2_, ...), custom_call_target="tpu_custom_call", output_to_operand_aliasing={{0}: (3, {}), {1}: (4, {})} | custom-call | bytes 6291456 | tf_op jit(solution)/shard_map/assemble/pallas_call | solution.py:170
  186.9 5.8 %all-gather = f32[16,2,2048]{2,1,0:T(2,128)S(1)} all-gather(f32[4,2,2048]{2,1,0:T(2,128)S(1)} %fusion), channel_id=2, replica_groups=mesh['groups'=2,'ctx'=4,'head'=2,'sub'=2] {'head','sub'}, dimensions={0}, use_global_device_ids=true | all-gather | bytes 327680 | tf_op jit(solution)/shard_map/all_gather | solution.py:557
  192.7 1.4 fusion.8
  194.1 0.6 slice_bitcast_fusion
  194.7 9.1 %collective-permute-done.10.refs_0_ = bf16[2,2048,128]{2,1,0:T(8,128)(2,1)} collective-permute-done((bf16[2,2048,128]{2,1,0:T(8,128)(2,1)}, bf16[2,2048,128]{2,1,0:T(8,128)(2,1)}, u32[]{:S(2)}, u32[]{:S(2)}) %collective-permute-start.10) | collective-permute-done | bytes 1048608 | tf_op jit(solution)/shard_map/ppermute | solution.py:459
  203.7 2.2 %assemble.5 = (bf16[16384,128]{1,0:T(8,128)(2,1)}, bf16[16384,128]{1,0:T(8,128)(2,1)}) custom-call(bf16[2,2048,128]{2,1,0:T(8,128)(2,1)} %collective-permute-done.10.refs_0_, bf16[16384,128]{1,0:T(8,128)(2,1)} %get-tuple-element.28.refs_1_, bf16[16384,128]{1,0:T(8,128)(2,1)} %get-tuple-element.29.refs_2_), custom_call_target="tpu_custom_call", output_to_operand_aliasing={{0}: (1, {}), {1}: (2, {})} | custom-call | bytes 2097152 | tf_op jit(solution)/shard_map/assemble/pallas_call | solution.py:170
  (89 shorter events, 0.7 us)
Async XLA Ops:
  0.6 16.4 %copy-start = (bf16[2048,256]{1,0:T(8,128)(2,1)S(1)}, bf16[2048,256]{1,0:T(8,128)(2,1)}, u32[]{:S(2)}) copy-start(bf16[2048,256]{1,0:T(8,128)(2,1)} %param.19) | copy-start | bytes 3145732
  0.6 0.7 copy-start.21
  1.4 15.0 %copy-start.23 = (s32[4]{0:T(128)S(1)}, s32[4]{0:T(128)}, u32[]{:S(2)}) copy-start(s32[4]{0:T(128)} %lengths_ref.1) | copy-start | bytes 52
  1.4 15.0 %copy-start.30 = (bf16[2048]{0:T(1024)(128)(2,1)S(1)}, bf16[2048]{0:T(1024)(128)(2,1)}, u32[]{:S(2)}) copy-start(bf16[2048]{0:T(1024)(128)(2,1)} %param.17) | copy-start | bytes 12292
  4.5 18.9 %collective-permute-start = (bf16[1,2048,128]{2,1,0:T(8,128)(2,1)}, bf16[1,2048,128]{2,1,0:T(8,128)(2,1)S(1)}, u32[]{:S(2)}, u32[]{:S(2)}) collective-permute-start(bf16[1,2048,128]{2,1,0:T(8,128)(2,1)} %bitcast.67), channel_id=1, source_target_pairs={{0,4},{1,5},{4,8},{5,9},{8,12},{9,13},{12,0},{13,1},{2,6},{3,7},{6... | collective-permute-start | bytes 1572872 | tf_op jit(solution)/shard_map/ppermute | solution.py:459
  8.9 0.7 copy-start.20
  9.6 28.6 %collective-permute-start.5 = (bf16[1,2048,128]{2,1,0:T(8,128)(2,1)}, bf16[1,2048,128]{2,1,0:T(8,128)(2,1)S(1)}, u32[]{:S(2)}, u32[]{:S(2)}) collective-permute-start(bf16[1,2048,128]{2,1,0:T(8,128)(2,1)} %hold.3), channel_id=1, source_target_pairs={{0,4},{1,5},{4,8},{5,9},{8,12},{9,13},{12,0},{13,1},{2,6},{3,7},{6... | collective-permute-start | bytes 1572872 | tf_op jit(solution)/shard_map/ppermute | solution.py:459
  16.4 0.6 copy-start.29
  18.7 7.9 %copy-start.22 = (s32[4]{0:T(128)S(1)}, s32[4]{0:T(128)}, u32[]{:S(2)}) copy-start(s32[4]{0:T(128)} %order_ref.15) | copy-start | bytes 52
  23.3 25.2 %copy-start.6 = (bf16[1,2048,128]{2,1,0:T(8,128)(2,1)}, bf16[1,2048,128]{2,1,0:T(8,128)(2,1)S(1)}, u32[]{:S(2)}) copy-start(bf16[1,2048,128]{2,1,0:T(8,128)(2,1)S(1)} %collective-permute-done.refs_4_.refs_0_) | copy-start | bytes 1572868
  23.4 11.0 %collective-permute-start.3 = (bf16[8,3328]{1,0:T(8,128)(2,1)S(1)}, bf16[8,3328]{1,0:T(8,128)(2,1)S(1)}, u32[]{:S(2)}, u32[]{:S(2)}) collective-permute-start(bf16[8,3328]{1,0:T(8,128)(2,1)S(1)} %pack_products.1.refs_2_), channel_id=1, source_target_pairs={{0,12},{4,0},{8,4},{12,8},{1,13},{5,1},{9,5},{13,9},{2,14},{6,2},{... | collective-permute-start | bytes 159752 | tf_op jit(solution)/shard_map/ppermute | solution.py:465
  25.7 12.2 %collective-permute-start.2 = (bf16[8,3328]{1,0:T(8,128)(2,1)S(1)}, bf16[8,3328]{1,0:T(8,128)(2,1)S(1)}, u32[]{:S(2)}, u32[]{:S(2)}) collective-permute-start(bf16[8,3328]{1,0:T(8,128)(2,1)S(1)} %pack_products.1.refs_2_), channel_id=1, source_target_pairs={{0,8},{4,12},{8,0},{12,4},{1,9},{5,13},{9,1},{13,5},{2,10},{6,14},... | collective-permute-start | bytes 159752 | tf_op jit(solution)/shard_map/ppermute | solution.py:465
  26.5 11.4 %collective-permute-start.1 = (bf16[8,3328]{1,0:T(8,128)(2,1)S(1)}, bf16[8,3328]{1,0:T(8,128)(2,1)S(1)}, u32[]{:S(2)}, u32[]{:S(2)}) collective-permute-start(bf16[8,3328]{1,0:T(8,128)(2,1)S(1)} %pack_products.1.refs_2_), channel_id=1, source_target_pairs={{0,4},{4,8},{8,12},{12,0},{1,5},{5,9},{9,13},{13,1},{2,6},{6,10},{... | collective-permute-start | bytes 159752 | tf_op jit(solution)/shard_map/ppermute | solution.py:465
  38.2 21.4 %copy-start.4 = (bf16[1,2048,128]{2,1,0:T(8,128)(2,1)}, bf16[1,2048,128]{2,1,0:T(8,128)(2,1)S(1)}, u32[]{:S(2)}) copy-start(bf16[1,2048,128]{2,1,0:T(8,128)(2,1)S(1)} %collective-permute-done.5.refs_3_.refs_1_) | copy-start | bytes 1572868
  38.2 16.0 %collective-permute-start.6 = (bf16[1,2048,128]{2,1,0:T(8,128)(2,1)}, bf16[1,2048,128]{2,1,0:T(8,128)(2,1)S(1)}, u32[]{:S(2)}, u32[]{:S(2)}) collective-permute-start(bf16[1,2048,128]{2,1,0:T(8,128)(2,1)} %get-tuple-element.24), channel_id=1, source_target_pairs={{0,5},{1,4},{4,9},{5,8},{8,13},{9,12},{12,1},{13,0},{2,7},{3,6},{6... | collective-permute-start | bytes 1572872 | tf_op jit(solution)/shard_map/ppermute | solution.py:459
  38.3 27.4 %collective-permute-start.11 = (bf16[1,2048,128]{2,1,0:T(8,128)(2,1)}, bf16[1,2048,128]{2,1,0:T(8,128)(2,1)S(1)}, u32[]{:S(2)}, u32[]{:S(2)}) collective-permute-start(bf16[1,2048,128]{2,1,0:T(8,128)(2,1)} %get-tuple-element.25), channel_id=1, source_target_pairs={{0,5},{1,4},{4,9},{5,8},{8,13},{9,12},{12,1},{13,0},{2,7},{3,6},{6... | collective-permute-start | bytes 1572872 | tf_op jit(solution)/shard_map/ppermute | solution.py:459
  39.4 2.1 %copy-start.24 = (f32[4,2,20,128]{3,2,1,0:T(8,128)}, f32[4,2,20,128]{3,2,1,0:T(8,128)S(1)}, u32[]{:S(2)}) copy-start(f32[4,2,20,128]{3,2,1,0:T(8,128)S(1)} %broadcast_multiply_fusion) | copy-start | bytes 245764
  39.5 2.0 copy-start.27
  39.5 20.1 %copy-start.25 = (bf16[4,2,18,64]{3,2,1,0:T(8,128)(2,1)}, bf16[4,2,18,64]{3,2,1,0:T(8,128)(2,1)S(1)}, u32[]{:S(2)}) copy-start(bf16[4,2,18,64]{3,2,1,0:T(8,128)(2,1)S(1)} %get-tuple-element.43) | copy-start | bytes 55300
  39.6 14.7 %copy-start.16 = (bf16[4,2,2,8,128]{4,3,2,1,0:T(8,128)(2,1)}, bf16[4,2,2,8,128]{4,3,2,1,0:T(8,128)(2,1)S(1)}, u32[]{:S(2)}) copy-start(bf16[4,2,2,8,128]{4,3,2,1,0:T(8,128)(2,1)S(1)} %copy.31) | copy-start | bytes 98308
  48.5 1.3 collective-permute-start.4
  54.3 18.3 %copy-start.8 = (bf16[1,2048,128]{2,1,0:T(8,128)(2,1)}, bf16[1,2048,128]{2,1,0:T(8,128)(2,1)S(1)}, u32[]{:S(2)}) copy-start(bf16[1,2048,128]{2,1,0:T(8,128)(2,1)S(1)} %collective-permute-done.6.refs_0_.refs_2_) | copy-start | bytes 1572868
  54.4 14.5 %copy-start.18 = (bf16[144,128]{1,0:T(8,128)(2,1)}, bf16[144,128]{1,0:T(8,128)(2,1)S(1)}, u32[]{:S(2)}) copy-start(bf16[144,128]{1,0:T(8,128)(2,1)S(1)} %merge_packed.1.refs_0_) | copy-start | bytes 110596
  54.4 12.2 %collective-permute-start.9 = (bf16[144,128]{1,0:T(8,128)(2,1)S(1)}, bf16[144,128]{1,0:T(8,128)(2,1)S(1)}, u32[]{:S(2)}, u32[]{:S(2)}) collective-permute-start(bf16[144,128]{1,0:T(8,128)(2,1)S(1)} %merge_packed.1.refs_0_), channel_id=1, source_target_pairs={{0,12},{4,0},{8,4},{12,8},{1,13},{5,1},{9,5},{13,9},{2,14},{6,2},{... | collective-permute-start | bytes 110600 | tf_op jit(solution)/shard_map/ppermute | solution.py:465
  54.6 14.3 %collective-permute-start.8 = (bf16[144,128]{1,0:T(8,128)(2,1)S(1)}, bf16[144,128]{1,0:T(8,128)(2,1)S(1)}, u32[]{:S(2)}, u32[]{:S(2)}) collective-permute-start(bf16[144,128]{1,0:T(8,128)(2,1)S(1)} %merge_packed.1.refs_0_), channel_id=1, source_target_pairs={{0,8},{4,12},{8,0},{12,4},{1,9},{5,13},{9,1},{13,5},{2,10},{6,14},... | collective-permute-start | bytes 110600 | tf_op jit(solution)/shard_map/ppermute | solution.py:465
  54.6 14.3 %collective-permute-start.7 = (bf16[144,128]{1,0:T(8,128)(2,1)S(1)}, bf16[144,128]{1,0:T(8,128)(2,1)S(1)}, u32[]{:S(2)}, u32[]{:S(2)}) collective-permute-start(bf16[144,128]{1,0:T(8,128)(2,1)S(1)} %merge_packed.1.refs_0_), channel_id=1, source_target_pairs={{0,4},{4,8},{8,12},{12,0},{1,5},{5,9},{9,13},{13,1},{2,6},{6,10},{... | collective-permute-start | bytes 110600 | tf_op jit(solution)/shard_map/ppermute | solution.py:465
  65.7 3.2 %copy-start.10 = (bf16[1,2048,128]{2,1,0:T(8,128)(2,1)}, bf16[1,2048,128]{2,1,0:T(8,128)(2,1)S(1)}, u32[]{:S(2)}) copy-start(bf16[1,2048,128]{2,1,0:T(8,128)(2,1)S(1)} %collective-permute-done.11.refs_4_.refs_3_) | copy-start | bytes 1572868
  68.9 18.7 %copy-start.12 = (bf16[144,128]{1,0:T(8,128)(2,1)}, bf16[144,128]{1,0:T(8,128)(2,1)S(1)}, u32[]{:S(2)}) copy-start(bf16[144,128]{1,0:T(8,128)(2,1)S(1)} %collective-permute-done.8.refs_3_.refs_2_) | copy-start | bytes 110596
  68.9 18.7 %copy-start.14 = (bf16[144,128]{1,0:T(8,128)(2,1)}, bf16[144,128]{1,0:T(8,128)(2,1)S(1)}, u32[]{:S(2)}) copy-start(bf16[144,128]{1,0:T(8,128)(2,1)S(1)} %collective-permute-done.7.refs_2_.refs_1_) | copy-start | bytes 110596
  68.9 26.3 %collective-permute-start.12 = (bf16[2,2048,128]{2,1,0:T(8,128)(2,1)}, bf16[2,2048,128]{2,1,0:T(8,128)(2,1)S(1)}, u32[]{:S(2)}, u32[]{:S(2)}) collective-permute-start(bf16[2,2048,128]{2,1,0:T(8,128)(2,1)} %hold.5), channel_id=1, source_target_pairs={{0,12},{1,13},{4,0},{5,1},{8,4},{9,5},{12,8},{13,9},{2,14},{3,15},... | collective-permute-start | bytes 3145736 | tf_op jit(solution)/shard_map/ppermute | solution.py:459
  72.6 11.3 %copy-start.26 = (bf16[4,2,18,64]{3,2,1,0:T(8,128)(2,1)S(1)}, bf16[4,2,18,64]{3,2,1,0:T(8,128)(2,1)}, u32[]{:S(2)}) copy-start(bf16[4,2,18,64]{3,2,1,0:T(8,128)(2,1)} %copy-done.25) | copy-start | bytes 55300
  72.6 11.3 %copy-start.28 = (bf16[4,2,18,64]{3,2,1,0:T(8,128)(2,1)S(1)}, bf16[4,2,18,64]{3,2,1,0:T(8,128)(2,1)}, u32[]{:S(2)}) copy-start(bf16[4,2,18,64]{3,2,1,0:T(8,128)(2,1)} %copy-done.27) | copy-start | bytes 55300
  72.6 32.9 %collective-permute-start.15 = (bf16[2,2048,128]{2,1,0:T(8,128)(2,1)}, bf16[2,2048,128]{2,1,0:T(8,128)(2,1)}, u32[]{:S(2)}, u32[]{:S(2)}) collective-permute-start(bf16[2,2048,128]{2,1,0:T(8,128)(2,1)} %bitcast.64), channel_id=1, source_target_pairs={{0,1},{1,0},{4,5},{5,4},{8,9},{9,8},{12,13},{13,12},{2,3},{3,2},{6... | collective-permute-start | bytes 3145736 | tf_op jit(solution)/shard_map/ppermute | solution.py:459
  76.1 41.0 %collective-permute-start.13 = (bf16[2,2048,128]{2,1,0:T(8,128)(2,1)}, bf16[2,2048,128]{2,1,0:T(8,128)(2,1)}, u32[]{:S(2)}, u32[]{:S(2)}) collective-permute-start(bf16[2,2048,128]{2,1,0:T(8,128)(2,1)} %bitcast.57), channel_id=1, source_target_pairs={{0,13},{1,12},{4,1},{5,0},{8,5},{9,4},{12,9},{13,8},{2,15},{3,14},... | collective-permute-start | bytes 3145736 | tf_op jit(solution)/shard_map/ppermute | solution.py:459
  79.9 104.1 %collective-permute-start.14 = (bf16[2,2048,128]{2,1,0:T(8,128)(2,1)}, bf16[2,2048,128]{2,1,0:T(8,128)(2,1)}, u32[]{:S(2)}, u32[]{:S(2)}) collective-permute-start(bf16[2,2048,128]{2,1,0:T(8,128)(2,1)} %bitcast.59), channel_id=1, source_target_pairs={{0,8},{1,9},{4,12},{5,13},{8,0},{9,1},{12,4},{13,5},{2,10},{3,11},... | collective-permute-start | bytes 3145736 | tf_op jit(solution)/shard_map/ppermute | solution.py:459
  84.0 12.2 %copy-start.17 = (bf16[4,2,2,8,128]{4,3,2,1,0:T(8,128)(2,1)S(1)}, bf16[4,2,2,8,128]{4,3,2,1,0:T(8,128)(2,1)}, u32[]{:S(2)}) copy-start(bf16[4,2,2,8,128]{4,3,2,1,0:T(8,128)(2,1)} %copy-done.16) | copy-start | bytes 98308
  87.5 116.3 %collective-permute-start.10 = (bf16[2,2048,128]{2,1,0:T(8,128)(2,1)}, bf16[2,2048,128]{2,1,0:T(8,128)(2,1)}, u32[]{:S(2)}, u32[]{:S(2)}) collective-permute-start(bf16[2,2048,128]{2,1,0:T(8,128)(2,1)} %bitcast.61), channel_id=1, source_target_pairs={{0,9},{1,8},{4,13},{5,12},{8,1},{9,0},{12,5},{13,4},{2,11},{3,10},... | collective-permute-start | bytes 3145736 | tf_op jit(solution)/shard_map/ppermute | solution.py:459
  90.6 14.9 %copy-start.1 = (bf16[2,1024,2,128]{3,2,1,0:T(2,128)(2,1)S(1)}, bf16[2,1024,2,128]{3,2,1,0:T(2,128)(2,1)}, u32[]{:S(2)}) copy-start(bf16[2,1024,2,128]{3,2,1,0:T(2,128)(2,1)} %arrange.14) | copy-start | bytes 3145732
  95.2 1.0 copy-start.2
  96.2 1.2 copy-start.3
  97.4 0.8 copy-start.13
  98.2 0.8 copy-start.15
  99.0 0.8 copy-start.19
  100.6 4.9 %copy-start.5 = (bf16[1,2048,128]{2,1,0:T(8,128)(2,1)S(1)}, bf16[1,2048,128]{2,1,0:T(8,128)(2,1)}, u32[]{:S(2)}) copy-start(bf16[1,2048,128]{2,1,0:T(8,128)(2,1)} %copy-done.4) | copy-start | bytes 1572868
  100.6 4.9 %copy-start.7 = (bf16[1,2048,128]{2,1,0:T(8,128)(2,1)S(1)}, bf16[1,2048,128]{2,1,0:T(8,128)(2,1)}, u32[]{:S(2)}) copy-start(bf16[1,2048,128]{2,1,0:T(8,128)(2,1)} %copy-done.6) | copy-start | bytes 1572868
  100.6 4.9 %copy-start.9 = (bf16[1,2048,128]{2,1,0:T(8,128)(2,1)S(1)}, bf16[1,2048,128]{2,1,0:T(8,128)(2,1)}, u32[]{:S(2)}) copy-start(bf16[1,2048,128]{2,1,0:T(8,128)(2,1)} %copy-done.8) | copy-start | bytes 1572868
  100.6 4.9 %copy-start.11 = (bf16[1,2048,128]{2,1,0:T(8,128)(2,1)S(1)}, bf16[1,2048,128]{2,1,0:T(8,128)(2,1)}, u32[]{:S(2)}) copy-start(bf16[1,2048,128]{2,1,0:T(8,128)(2,1)} %copy-done.10) | copy-start | bytes 1572868

commit v11 on v10

--- a/solution.py
+++ b/solution.py
@@ -469,8 +469,9 @@
     middle = ctx_count // 2
     leading = make(1, 0, apart=True)
     paired = pair_tokens(first_tokens, second_tokens, leading[0])
-    later = hold(leading[1:], (paired,))
-    ahead = [send(block, (w,), 1, 0) for w, block in enumerate([leading[0], *later])]
+    last = ctx_count - 1
+    later = make(last, 0, (paired,), apart=True)
+    ahead = [send(leading[0], (0,), 1, 0), send(later[0], (0,), last, 0)]
 
     query_width = w_query.shape[1]
     key_width = w_key.shape[1]
@@ -494,8 +495,8 @@
         (ahead[0],),
     )
     summed = functools.reduce(jnp.add, [x.astype(jnp.float32) for x in from_all(partial)])
-    waiting = hold(make(1, 1, (partial,), apart=True), (summed, ahead[1]))
-    behind = [send(waiting[w], (w,), 1, 1) for w in both]
+    waiting = hold([leading[1], later[1]], (summed, ahead[1]))
+    behind = [send(block, (1,), shift, 0) for block, shift in zip(waiting, (1, last))]
     others = 2 * key_width + LANES
     tail = summed[:, query_width : query_width + others] + summed[:, query_width + others :]
     raw = jnp.concatenate([summed[:, :query_width], tail[:, :-LANES]], axis=1)
@@ -522,8 +523,9 @@
 
     rest = [
         (shift, flip)
-        for shift in sorted(range(2, ctx_count), key=lambda d: -d)
+        for shift in sorted(range(1, ctx_count), key=lambda d: -abs(d - middle))
         for flip in range(sub_count)
+        if flip or shift not in (1, last)
     ]
     blocks = hold([make(*rest[0], (partial,))], tuple(packed[1:]), (behind[1],))
     blocks = [*blocks, *(make(*key, tuple(packed[1:])) for key in rest[1:])]
@@ -561,7 +563,7 @@
     result = (residual + jnp.sum(parts, axis=0)).astype(jnp.bfloat16)
 
     moved = ()
-    early = [((w,), 1, flip) for flip in range(sub_count) for w in both]
+    early = [((w,), shift, 0) for shift in (1, last) for w in both]
     groups = [
         early + [(both, 0, 0), (both, 0, 1)],
         [(both, *key) for key in rest[:-1]],

time: 208 us -> 213 us (1.024)
  starting transfers between devices: 14.6 us -> 29.1 us
  waiting for transfers between devices: 112 us -> 103 us
    ppermute x9, waiting for transfers between devices: 99.5 us -> 90.4 us  [send(): moved = lax.ppermute(block, ('ctx', 'sub'), pairs)]
    ppermute x6, starting transfers between devices: 5.14 us -> 13.6 us  [from_all(): lax.ppermute(values, 'ctx', [(c, (c + shift) % ctx_count) for c in range(...]
    ppermute x9, starting transfers between devices: 9.24 us -> 15.2 us  [send(): moved = lax.ppermute(block, ('ctx', 'sub'), pairs)]
    unnamed x62 -> x64, local copies, waits for them, and re-layouts: 6.55 us -> 8.46 us
  transfers between devices with their start and end apart: 16 -> 16, of which waited for: 11 -> 8; matrix products, arithmetic and copies ran while one was open for 8% -> 7% of each run, Pallas kernels for 18% -> 18%
where the time goes in v11:
time: 213 us; the launch traced here: 212 us
  waiting for transfers between devices  103 us (48%)
  Pallas kernels  43.2 us (20%)
  starting transfers between devices  29.1 us (14%)
  blocking collectives  12.8 us (6%)
  local copies, waits for them, and re-layouts  10.4 us (5%)
  matrix products  9.93 us (5%)
  other arithmetic  2.13 us (1%)
    ppermute x9, waiting for transfers between devices, send(): moved = lax.ppermute(block, ('ctx', 'sub'), pairs)  90.4 us
    pallas_call x8, Pallas kernels, arrange(): pl.pallas_call(kernel, out_shape=(pltpu.HBM(shape, caches[0].dtype),) * o...  26.1 us
    ppermute x9, starting transfers between devices, send(): moved = lax.ppermute(block, ('ctx', 'sub'), pairs)  15.2 us
    ppermute x6, starting transfers between devices, from_all(): lax.ppermute(values, 'ctx', [(c, (c + shift) % ctx_count) for c in range(...  13.6 us
    ppermute x6, waiting for transfers between devices, from_all(): lax.ppermute(values, 'ctx', [(c, (c + shift) % ctx_count) for c in range(...  11.2 us
    unnamed x64, local copies, waits for them, and re-layouts  8.46 us
    pallas_call x3, Pallas kernels, assemble(): pl.pallas_call(kernel, out_shape=(pltpu.HBM((rows, head_dim), blocks[0].d...  8.21 us
    pallas_call x1, Pallas kernels, attend_shard(): pl.pallas_call(kernel, out_shape=(pltpu.VMEM(packed, jnp.float32),) * 2,...  7.04 us
  transfers between devices with their start and end apart: 16, of which 8 were waited for; matrix products, arithmetic and copies ran while one was open for 7% of the time, Pallas kernels for 18%

profile of v11, /device:TPU:0, one launch (start us, length us, event | category | flops | bytes accessed | tf_op | source)
XLA Modules:
  0.0 211.7 jit_solution(893960329567010179)
XLA Ops:
  0.7 0.7 copy-done.22
  1.4 3.1 %arrange.8 = (bf16[1,1024,2,128]{3,2,1,0:T(2,128)(2,1)}, bf16[1,1024,2,128]{3,2,1,0:T(2,128)(2,1)}) custom-call(s32[4]{0:T(128)S(1)} %copy-done.22, bf16[4,1024,4,128]{3,2,1,0:T(4,128)(2,1)} %refs_0_.15, bf16[4,1024,4,128]{3,2,1,0:T(4,128)(2,1)} %refs_1_.15), custom_call_target="tpu_custom_call" | custom-call | tf_op jit(solution)/shard_map/arrange/pallas_call | solution.py:92
  4.5 3.1 %collective-permute-start = (bf16[1,2048,128]{2,1,0:T(8,128)(2,1)}, bf16[1,2048,128]{2,1,0:T(8,128)(2,1)S(1)}, u32[]{:S(2)}, u32[]{:S(2)}) collective-permute-start(bf16[1,2048,128]{2,1,0:T(8,128)(2,1)} %bitcast.67), channel_id=1, source_target_pairs={{0,4},{1,5},{4,8},{5,9},{8,12},{9,13},{12,0},{13,1},{2,6},{3,7},{6... | collective-permute-start | bytes 1572872 | tf_op jit(solution)/shard_map/ppermute | solution.py:459
  7.6 1.3 pair_tokens.1.refs_2_
  8.9 0.7 copy-done.21
  9.6 3.1 %arrange.9 = (bf16[1,1024,2,128]{3,2,1,0:T(2,128)(2,1)}, bf16[1,1024,2,128]{3,2,1,0:T(2,128)(2,1)}) custom-call(s32[4]{0:T(128)S(1)} %copy-done.23, bf16[4,1024,4,128]{3,2,1,0:T(4,128)(2,1)} %refs_0_.15, bf16[4,1024,4,128]{3,2,1,0:T(4,128)(2,1)} %refs_1_.15, bf16[1,2,2048]{2,1,0:T(2,128)(2,1)S(1)} %copy-done.21), custom_call_target="tpu_custom_call" | custom-call | tf_op jit(solution)/shard_map/arrange/pallas_call | solution.py:92
  12.6 2.1 collective-permute-start.5
  14.8 5.2 %all_gather.9 = bf16[4,2,2048]{2,1,0:T(2,128)(2,1)S(1)} all-gather(bf16[1,2,2048]{2,1,0:T(2,128)(2,1)S(1)} %copy-done.21), channel_id=1, replica_groups=mesh['groups'=2,'ctx'=4,'head'=2,'sub'=2] {'head','sub'}, dimensions={0}, use_global_device_ids=true | all-gather | bytes 40960 | tf_op jit(solution)/shard_map/all_gather | solution.py:481
  20.1 0.5 copy-done.30
  20.5 0.2 fusion.6.refs_1_
  20.8 0.3 fusion.5.refs_2_
  21.1 4.6 %fusion.7.refs_0_ = f32[16,2048]{1,0:T(8,128)S(1)} fusion(bf16[2048,2048]{1,0:T(8,128)(2,1)} %param.18, bf16[8,2048]{1,0:T(8,128)(2,1)S(1)} %get-tuple-element.46, bf16[8,2048]{1,0:T(8,128)(2,1)S(1)} %get-tuple-element.45), kind=kOutput, calls=%fused_computation.20 | convolution fusion | flops 134348800 | bytes 8585216 | tf_op jit(solution)/shard_map/dot_general | solution.py:491
  25.6 0.1 pack_products.1.refs_2_
  25.7 9.9 %collective-permute-start.3 = (bf16[8,3328]{1,0:T(8,128)(2,1)S(1)}, bf16[8,3328]{1,0:T(8,128)(2,1)S(1)}, u32[]{:S(2)}, u32[]{:S(2)}) collective-permute-start(bf16[8,3328]{1,0:T(8,128)(2,1)S(1)} %pack_products.1.refs_2_), channel_id=1, source_target_pairs={{0,12},{4,0},{8,4},{12,8},{1,13},{5,1},{9,5},{13,9},{2,14},{6,2},{... | collective-permute-start | bytes 159752 | tf_op jit(solution)/shard_map/ppermute | solution.py:465
  35.7 1.6 collective-permute-start.1
  37.3 0.1 multiply_cosine_fusion
  37.5 0.4 collective-permute-done.3
  37.9 9.6 %collective-permute-done.2 = bf16[8,3328]{1,0:T(8,128)(2,1)S(1)} collective-permute-done((bf16[8,3328]{1,0:T(8,128)(2,1)S(1)}, bf16[8,3328]{1,0:T(8,128)(2,1)S(1)}, u32[]{:S(2)}, u32[]{:S(2)}) %collective-permute-start.2) | collective-permute-done | bytes 53280 | tf_op jit(solution)/shard_map/ppermute | solution.py:465
  47.6 0.1 fusion.11
  47.7 0.1 mul.83
  47.9 3.8 %collective-permute-start.11 = (bf16[1,2048,128]{2,1,0:T(8,128)(2,1)}, bf16[1,2048,128]{2,1,0:T(8,128)(2,1)S(1)}, u32[]{:S(2)}, u32[]{:S(2)}) collective-permute-start(bf16[1,2048,128]{2,1,0:T(8,128)(2,1)} %get-tuple-element.25), channel_id=1, source_target_pairs={{0,12},{1,13},{4,0},{5,1},{8,4},{9,5},{12,8},{13,9},{2,14},{3,15},... | collective-permute-start | bytes 1572872 | tf_op jit(solution)/shard_map/ppermute | solution.py:459
  51.7 0.1 broadcast_multiply_fusion
  51.8 0.1 add_convert_fusion
  51.9 0.6 copy-done.26
  52.5 0.1 fusion.4
  52.6 1.9 all_gather.10.q_ref
  54.5 7.0 %attend_shard.1 = (f32[130,128]{1,0:T(8,128)S(1)}, f32[130,128]{1,0:T(8,128)S(1)}) custom-call(s32[4]{0:T(128)S(1)} %copy-done.24, bf16[4,64,128]{2,1,0:T(8,128)(2,1)S(1)} %all_gather.10.q_ref, bf16[4,4096,128]{2,1,0:T(8,128)(2,1)} %bitcast.53, bf16[4,4096,128]{2,1,0:T(8,128)(2,1)} %bitcast.54), custom_call_target="tpu_custom_call" | custom-call | tf_op jit(solution)/shard_map/attend_shard/pallas_call | solution.py:326
  61.5 0.2 collective-permute-start.4
  61.8 1.1 collective-permute-done.4.other_ref
  62.9 0.1 merge_packed.1.refs_0_
  63.1 1.9 collective-permute-start.7
  65.1 3.4 %arrange.11 = bf16[2,1024,2,128]{3,2,1,0:T(2,128)(2,1)} custom-call(s32[4]{0:T(128)S(1)} %copy-done.23, bf16[4,1024,4,128]{3,2,1,0:T(4,128)(2,1)} %refs_0_.15, bf16[4,1024,4,128]{3,2,1,0:T(4,128)(2,1)} %refs_1_.15, bf16[8,3328]{1,0:T(8,128)(2,1)S(1)} %pack_products.1.refs_2_), custom_call_target="tpu_custom_call" | custom-call | tf_op jit(solution)/shard_map/arrange/pallas_call | solution.py:92
  68.6 1.2 collective-permute-done.7.refs_2_.refs_1_
  69.8 0.6 copy-done.14
  70.4 0.8 copy-done.15
  71.2 3.6 %arrange.15 = bf16[2,1024,2,128]{3,2,1,0:T(2,128)(2,1)} custom-call(s32[4]{0:T(128)S(1)} %copy-done.23, bf16[4,1024,4,128]{3,2,1,0:T(4,128)(2,1)} %refs_0_.15, bf16[4,1024,4,128]{3,2,1,0:T(4,128)(2,1)} %refs_1_.15, bf16[144,128]{1,0:T(8,128)(2,1)S(1)} %copy-done.15, bf16[144,128]{1,0:T(8,128)(2,1)S(1)} %collective-permute-done.8.refs_3_.refs_2_, ...), custom_call_target="tpu_custom_call" | custom-call | tf_op jit(solution)/shard_map/arrange/pallas_call | solution.py:92
  74.8 0.9 collective-permute-start.15
  75.7 3.4 %arrange.12 = bf16[2,1024,2,128]{3,2,1,0:T(2,128)(2,1)} custom-call(s32[4]{0:T(128)S(1)} %copy-done.23, bf16[4,1024,4,128]{3,2,1,0:T(4,128)(2,1)} %refs_0_.15, bf16[4,1024,4,128]{3,2,1,0:T(4,128)(2,1)} %refs_1_.15, bf16[144,128]{1,0:T(8,128)(2,1)S(1)} %copy-done.15, bf16[144,128]{1,0:T(8,128)(2,1)S(1)} %collective-permute-done.8.refs_3_.refs_2_, ...), custom_call_target="tpu_custom_call" | custom-call | tf_op jit(solution)/shard_map/arrange/pallas_call | solution.py:92
  79.1 2.0 collective-permute-start.13
  81.2 3.1 %arrange.13 = bf16[2,1024,2,128]{3,2,1,0:T(2,128)(2,1)} custom-call(s32[4]{0:T(128)S(1)} %copy-done.23, bf16[4,1024,4,128]{3,2,1,0:T(4,128)(2,1)} %refs_0_.15, bf16[4,1024,4,128]{3,2,1,0:T(4,128)(2,1)} %refs_1_.15, bf16[144,128]{1,0:T(8,128)(2,1)S(1)} %copy-done.15, bf16[144,128]{1,0:T(8,128)(2,1)S(1)} %collective-permute-done.8.refs_3_.refs_2_, ...), custom_call_target="tpu_custom_call" | custom-call | tf_op jit(solution)/shard_map/arrange/pallas_call | solution.py:92
  84.3 0.8 collective-permute-start.14
  85.0 0.6 dynamic_slice.6
  85.6 0.1 pad_maximum_fusion.5
  85.7 3.4 %arrange.10 = bf16[2,1024,2,128]{3,2,1,0:T(2,128)(2,1)} custom-call(s32[4]{0:T(128)S(1)} %copy-done.23, bf16[4,1024,4,128]{3,2,1,0:T(4,128)(2,1)} %refs_0_.15, bf16[4,1024,4,128]{3,2,1,0:T(4,128)(2,1)} %refs_1_.15, bf16[144,128]{1,0:T(8,128)(2,1)S(1)} %copy-done.15, bf16[144,128]{1,0:T(8,128)(2,1)S(1)} %collective-permute-done.8.refs_3_.refs_2_, ...), custom_call_target="tpu_custom_call" | custom-call | tf_op jit(solution)/shard_map/arrange/pallas_call | solution.py:92
  89.2 2.5 %collective-permute-start.10 = (bf16[2,2048,128]{2,1,0:T(8,128)(2,1)}, bf16[2,2048,128]{2,1,0:T(8,128)(2,1)}, u32[]{:S(2)}, u32[]{:S(2)}) collective-permute-start(bf16[2,2048,128]{2,1,0:T(8,128)(2,1)} %bitcast.61), channel_id=1, source_target_pairs={{0,9},{1,8},{4,13},{5,12},{8,1},{9,0},{12,5},{13,4},{2,11},{3,10},... | collective-permute-start | bytes 3145736 | tf_op jit(solution)/shard_map/ppermute | solution.py:459
  91.7 3.1 %arrange.14 = bf16[2,1024,2,128]{3,2,1,0:T(2,128)(2,1)} custom-call(s32[4]{0:T(128)S(1)} %copy-done.23, bf16[4,1024,4,128]{3,2,1,0:T(4,128)(2,1)} %refs_0_.15, bf16[4,1024,4,128]{3,2,1,0:T(4,128)(2,1)} %refs_1_.15, bf16[144,128]{1,0:T(8,128)(2,1)S(1)} %copy-done.15, bf16[144,128]{1,0:T(8,128)(2,1)S(1)} %collective-permute-done.8.refs_3_.refs_2_, ...), custom_call_target="tpu_custom_call" | custom-call | tf_op jit(solution)/shard_map/arrange/pallas_call | solution.py:92
  94.8 3.1 %collective-permute-done.12.refs_0_.refs_7_ = bf16[2,2048,128]{2,1,0:T(8,128)(2,1)S(1)} collective-permute-done((bf16[2,2048,128]{2,1,0:T(8,128)(2,1)}, bf16[2,2048,128]{2,1,0:T(8,128)(2,1)S(1)}, u32[]{:S(2)}, u32[]{:S(2)}) %collective-permute-start.12) | collective-permute-done | bytes 1048608 | tf_op jit(solution)/shard_map/ppermute | solution.py:459
  97.9 1.0 copy-done.2
  98.9 1.2 copy-done.3
  100.1 0.8 copy-done.13
  100.9 0.8 copy-done.16
  101.7 0.8 copy-done.20
  102.4 0.3 finish.1
  102.7 0.6 gather_fusion
  103.4 4.8 %fusion = f32[4,2,2048]{2,1,0:T(2,128)S(1)} fusion(bf16[4,2,2048]{2,1,0:T(2,128)(2,1)S(1)} %reshape.203, bf16[2048,2048]{1,0:T(8,128)(2,1)} %param.21), kind=kOutput, calls=%fused_computation.1 | convolution fusion | flops 67108864 | bytes 8486912 | tf_op jit(solution)/shard_map/dot_general | solution.py:556
  108.3 3.1 %assemble.3 = (bf16[16384,128]{1,0:T(8,128)(2,1)}, bf16[16384,128]{1,0:T(8,128)(2,1)}) custom-call(bf16[1,2048,128]{2,1,0:T(8,128)(2,1)S(1)} %copy-done.7, bf16[1,2048,128]{2,1,0:T(8,128)(2,1)S(1)} %copy-done.9, bf16[1,2048,128]{2,1,0:T(8,128)(2,1)S(1)} %copy-done.5, bf16[1,2048,128]{2,1,0:T(8,128)(2,1)S(1)} %copy-done.11, ...), custom_call_target="tpu_custom_call" | custom-call | bytes 8388608 | tf_op jit(solution)/shard_map/assemble/pallas_call | solution.py:170
  111.4 8.0 %collective-permute-done.13.refs_1_ = bf16[2,2048,128]{2,1,0:T(8,128)(2,1)} collective-permute-done((bf16[2,2048,128]{2,1,0:T(8,128)(2,1)}, bf16[2,2048,128]{2,1,0:T(8,128)(2,1)}, u32[]{:S(2)}, u32[]{:S(2)}) %collective-permute-start.13) | collective-permute-done | bytes 1048608 | tf_op jit(solution)/shard_map/ppermute | solution.py:459
  119.4 67.5 %collective-permute-done.14.refs_2_ = bf16[2,2048,128]{2,1,0:T(8,128)(2,1)} collective-permute-done((bf16[2,2048,128]{2,1,0:T(8,128)(2,1)}, bf16[2,2048,128]{2,1,0:T(8,128)(2,1)}, u32[]{:S(2)}, u32[]{:S(2)}) %collective-permute-start.14) | collective-permute-done | bytes 1048608 | tf_op jit(solution)/shard_map/ppermute | solution.py:459
  186.8 2.9 %assemble.4 = (bf16[16384,128]{1,0:T(8,128)(2,1)}, bf16[16384,128]{1,0:T(8,128)(2,1)}) custom-call(bf16[2,2048,128]{2,1,0:T(8,128)(2,1)S(1)} %copy-done.3, bf16[2,2048,128]{2,1,0:T(8,128)(2,1)} %collective-permute-done.13.refs_1_, bf16[2,2048,128]{2,1,0:T(8,128)(2,1)} %collective-permute-done.14.refs_2_, ...), custom_call_target="tpu_custom_call", output_to_operand_aliasing={{0}: (3, {}), {1}: (4, {})} | custom-call | bytes 6291456 | tf_op jit(solution)/shard_map/assemble/pallas_call | solution.py:170
  189.7 5.8 %all-gather = f32[16,2,2048]{2,1,0:T(2,128)S(1)} all-gather(f32[4,2,2048]{2,1,0:T(2,128)S(1)} %fusion), channel_id=2, replica_groups=mesh['groups'=2,'ctx'=4,'head'=2,'sub'=2] {'head','sub'}, dimensions={0}, use_global_device_ids=true | all-gather | bytes 327680 | tf_op jit(solution)/shard_map/all_gather | solution.py:559
  195.5 1.4 fusion.8
  196.9 0.6 slice_bitcast_fusion
  197.5 11.8 %collective-permute-done.10.refs_0_ = bf16[2,2048,128]{2,1,0:T(8,128)(2,1)} collective-permute-done((bf16[2,2048,128]{2,1,0:T(8,128)(2,1)}, bf16[2,2048,128]{2,1,0:T(8,128)(2,1)}, u32[]{:S(2)}, u32[]{:S(2)}) %collective-permute-start.10) | collective-permute-done | bytes 1048608 | tf_op jit(solution)/shard_map/ppermute | solution.py:459
  209.3 2.2 %assemble.5 = (bf16[16384,128]{1,0:T(8,128)(2,1)}, bf16[16384,128]{1,0:T(8,128)(2,1)}) custom-call(bf16[2,2048,128]{2,1,0:T(8,128)(2,1)} %collective-permute-done.10.refs_0_, bf16[16384,128]{1,0:T(8,128)(2,1)} %get-tuple-element.28.refs_1_, bf16[16384,128]{1,0:T(8,128)(2,1)} %get-tuple-element.29.refs_2_), custom_call_target="tpu_custom_call", output_to_operand_aliasing={{0}: (1, {}), {1}: (2, {})} | custom-call | bytes 2097152 | tf_op jit(solution)/shard_map/assemble/pallas_call | solution.py:170
  (90 shorter events, 0.6 us)
Async XLA Ops:
  0.6 19.9 %copy-start = (bf16[2048,256]{1,0:T(8,128)(2,1)S(1)}, bf16[2048,256]{1,0:T(8,128)(2,1)}, u32[]{:S(2)}) copy-start(bf16[2048,256]{1,0:T(8,128)(2,1)} %param.19) | copy-start | bytes 3145732
  0.6 0.7 copy-start.22
  1.4 7.5 %copy-start.23 = (s32[4]{0:T(128)S(1)}, s32[4]{0:T(128)}, u32[]{:S(2)}) copy-start(s32[4]{0:T(128)} %order_ref.15) | copy-start | bytes 52
  1.4 18.5 %copy-start.24 = (s32[4]{0:T(128)S(1)}, s32[4]{0:T(128)}, u32[]{:S(2)}) copy-start(s32[4]{0:T(128)} %lengths_ref.1) | copy-start | bytes 52
  1.4 18.6 %copy-start.31 = (bf16[2048]{0:T(1024)(128)(2,1)S(1)}, bf16[2048]{0:T(1024)(128)(2,1)}, u32[]{:S(2)}) copy-start(bf16[2048]{0:T(1024)(128)(2,1)} %param.17) | copy-start | bytes 12292
  1.4 19.4 %copy-start.25 = (bf16[2048,256]{1,0:T(8,128)(2,1)S(1)}, bf16[2048,256]{1,0:T(8,128)(2,1)}, u32[]{:S(2)}) copy-start(bf16[2048,256]{1,0:T(8,128)(2,1)} %param.20) | copy-start | bytes 3145732
  4.5 21.2 %collective-permute-start = (bf16[1,2048,128]{2,1,0:T(8,128)(2,1)}, bf16[1,2048,128]{2,1,0:T(8,128)(2,1)S(1)}, u32[]{:S(2)}, u32[]{:S(2)}) collective-permute-start(bf16[1,2048,128]{2,1,0:T(8,128)(2,1)} %bitcast.67), channel_id=1, source_target_pairs={{0,4},{1,5},{4,8},{5,9},{8,12},{9,13},{12,0},{13,1},{2,6},{3,7},{6... | collective-permute-start | bytes 1572872 | tf_op jit(solution)/shard_map/ppermute | solution.py:459
  8.9 0.7 copy-start.21
  12.6 35.2 %collective-permute-start.5 = (bf16[1,2048,128]{2,1,0:T(8,128)(2,1)}, bf16[1,2048,128]{2,1,0:T(8,128)(2,1)S(1)}, u32[]{:S(2)}, u32[]{:S(2)}) collective-permute-start(bf16[1,2048,128]{2,1,0:T(8,128)(2,1)} %bitcast.71), channel_id=1, source_target_pairs={{0,12},{1,13},{4,0},{5,1},{8,4},{9,5},{12,8},{13,9},{2,14},{3,15},... | collective-permute-start | bytes 1572872 | tf_op jit(solution)/shard_map/ppermute | solution.py:459
  19.9 0.6 copy-start.30
  25.6 42.9 %copy-start.6 = (bf16[1,2048,128]{2,1,0:T(8,128)(2,1)}, bf16[1,2048,128]{2,1,0:T(8,128)(2,1)S(1)}, u32[]{:S(2)}) copy-start(bf16[1,2048,128]{2,1,0:T(8,128)(2,1)S(1)} %collective-permute-done.refs_4_.refs_0_) | copy-start | bytes 1572868
  25.7 12.2 %collective-permute-start.3 = (bf16[8,3328]{1,0:T(8,128)(2,1)S(1)}, bf16[8,3328]{1,0:T(8,128)(2,1)S(1)}, u32[]{:S(2)}, u32[]{:S(2)}) collective-permute-start(bf16[8,3328]{1,0:T(8,128)(2,1)S(1)} %pack_products.1.refs_2_), channel_id=1, source_target_pairs={{0,12},{4,0},{8,4},{12,8},{1,13},{5,1},{9,5},{13,9},{2,14},{6,2},{... | collective-permute-start | bytes 159752 | tf_op jit(solution)/shard_map/ppermute | solution.py:465
  35.7 11.8 %collective-permute-start.2 = (bf16[8,3328]{1,0:T(8,128)(2,1)S(1)}, bf16[8,3328]{1,0:T(8,128)(2,1)S(1)}, u32[]{:S(2)}, u32[]{:S(2)}) collective-permute-start(bf16[8,3328]{1,0:T(8,128)(2,1)S(1)} %pack_products.1.refs_2_), channel_id=1, source_target_pairs={{0,8},{4,12},{8,0},{12,4},{1,9},{5,13},{9,1},{13,5},{2,10},{6,14},... | collective-permute-start | bytes 159752 | tf_op jit(solution)/shard_map/ppermute | solution.py:465
  35.7 11.8 %collective-permute-start.1 = (bf16[8,3328]{1,0:T(8,128)(2,1)S(1)}, bf16[8,3328]{1,0:T(8,128)(2,1)S(1)}, u32[]{:S(2)}, u32[]{:S(2)}) collective-permute-start(bf16[8,3328]{1,0:T(8,128)(2,1)S(1)} %pack_products.1.refs_2_), channel_id=1, source_target_pairs={{0,4},{4,8},{8,12},{12,0},{1,5},{5,9},{9,13},{13,1},{2,6},{6,10},{... | collective-permute-start | bytes 159752 | tf_op jit(solution)/shard_map/ppermute | solution.py:465
  47.8 20.7 %copy-start.4 = (bf16[1,2048,128]{2,1,0:T(8,128)(2,1)}, bf16[1,2048,128]{2,1,0:T(8,128)(2,1)S(1)}, u32[]{:S(2)}) copy-start(bf16[1,2048,128]{2,1,0:T(8,128)(2,1)S(1)} %collective-permute-done.5.refs_3_.refs_2_) | copy-start | bytes 1572868
  47.8 15.0 %collective-permute-start.6 = (bf16[1,2048,128]{2,1,0:T(8,128)(2,1)}, bf16[1,2048,128]{2,1,0:T(8,128)(2,1)S(1)}, u32[]{:S(2)}, u32[]{:S(2)}) collective-permute-start(bf16[1,2048,128]{2,1,0:T(8,128)(2,1)} %get-tuple-element.24), channel_id=1, source_target_pairs={{0,4},{1,5},{4,8},{5,9},{8,12},{9,13},{12,0},{13,1},{2,6},{3,7},{6... | collective-permute-start | bytes 1572872 | tf_op jit(solution)/shard_map/ppermute | solution.py:459
  47.9 20.6 %collective-permute-start.11 = (bf16[1,2048,128]{2,1,0:T(8,128)(2,1)}, bf16[1,2048,128]{2,1,0:T(8,128)(2,1)S(1)}, u32[]{:S(2)}, u32[]{:S(2)}) collective-permute-start(bf16[1,2048,128]{2,1,0:T(8,128)(2,1)} %get-tuple-element.25), channel_id=1, source_target_pairs={{0,12},{1,13},{4,0},{5,1},{8,4},{9,5},{12,8},{13,9},{2,14},{3,15},... | collective-permute-start | bytes 1572872 | tf_op jit(solution)/shard_map/ppermute | solution.py:459
  51.9 0.6 copy-start.26
  51.9 2.6 %copy-start.28 = (bf16[4,2,18,64]{3,2,1,0:T(8,128)(2,1)}, bf16[4,2,18,64]{3,2,1,0:T(8,128)(2,1)S(1)}, u32[]{:S(2)}) copy-start(bf16[4,2,18,64]{3,2,1,0:T(8,128)(2,1)S(1)} %get-tuple-element.44) | copy-start | bytes 55300
  52.6 10.2 %copy-start.17 = (bf16[4,2,2,8,128]{4,3,2,1,0:T(8,128)(2,1)}, bf16[4,2,2,8,128]{4,3,2,1,0:T(8,128)(2,1)S(1)}, u32[]{:S(2)}) copy-start(bf16[4,2,2,8,128]{4,3,2,1,0:T(8,128)(2,1)S(1)} %copy.30) | copy-start | bytes 98308
  61.5 1.3 collective-permute-start.4
  62.9 11.9 %copy-start.8 = (bf16[1,2048,128]{2,1,0:T(8,128)(2,1)}, bf16[1,2048,128]{2,1,0:T(8,128)(2,1)S(1)}, u32[]{:S(2)}) copy-start(bf16[1,2048,128]{2,1,0:T(8,128)(2,1)S(1)} %collective-permute-done.6.refs_0_.refs_1_) | copy-start | bytes 1572868
  63.0 6.8 %copy-start.19 = (bf16[144,128]{1,0:T(8,128)(2,1)}, bf16[144,128]{1,0:T(8,128)(2,1)S(1)}, u32[]{:S(2)}) copy-start(bf16[144,128]{1,0:T(8,128)(2,1)S(1)} %merge_packed.1.refs_0_) | copy-start | bytes 110596
  63.0 5.6 %collective-permute-start.9 = (bf16[144,128]{1,0:T(8,128)(2,1)S(1)}, bf16[144,128]{1,0:T(8,128)(2,1)S(1)}, u32[]{:S(2)}, u32[]{:S(2)}) collective-permute-start(bf16[144,128]{1,0:T(8,128)(2,1)S(1)} %merge_packed.1.refs_0_), channel_id=1, source_target_pairs={{0,12},{4,0},{8,4},{12,8},{1,13},{5,1},{9,5},{13,9},{2,14},{6,2},{... | collective-permute-start | bytes 110600 | tf_op jit(solution)/shard_map/ppermute | solution.py:465
  63.1 5.5 %collective-permute-start.8 = (bf16[144,128]{1,0:T(8,128)(2,1)S(1)}, bf16[144,128]{1,0:T(8,128)(2,1)S(1)}, u32[]{:S(2)}, u32[]{:S(2)}) collective-permute-start(bf16[144,128]{1,0:T(8,128)(2,1)S(1)} %merge_packed.1.refs_0_), channel_id=1, source_target_pairs={{0,8},{4,12},{8,0},{12,4},{1,9},{5,13},{9,1},{13,5},{2,10},{6,14},... | collective-permute-start | bytes 110600 | tf_op jit(solution)/shard_map/ppermute | solution.py:465
  63.1 6.6 %collective-permute-start.7 = (bf16[144,128]{1,0:T(8,128)(2,1)S(1)}, bf16[144,128]{1,0:T(8,128)(2,1)S(1)}, u32[]{:S(2)}, u32[]{:S(2)}) collective-permute-start(bf16[144,128]{1,0:T(8,128)(2,1)S(1)} %merge_packed.1.refs_0_), channel_id=1, source_target_pairs={{0,4},{4,8},{8,12},{12,0},{1,5},{5,9},{9,13},{13,1},{2,6},{6,10},{... | collective-permute-start | bytes 110600 | tf_op jit(solution)/shard_map/ppermute | solution.py:465
  68.6 1.2 copy-start.10
  68.6 23.1 %copy-start.12 = (bf16[144,128]{1,0:T(8,128)(2,1)}, bf16[144,128]{1,0:T(8,128)(2,1)S(1)}, u32[]{:S(2)}) copy-start(bf16[144,128]{1,0:T(8,128)(2,1)S(1)} %collective-permute-done.8.refs_3_.refs_2_) | copy-start | bytes 110596
  69.8 0.6 copy-start.14
  70.4 27.5 %collective-permute-start.12 = (bf16[2,2048,128]{2,1,0:T(8,128)(2,1)}, bf16[2,2048,128]{2,1,0:T(8,128)(2,1)S(1)}, u32[]{:S(2)}, u32[]{:S(2)}) collective-permute-start(bf16[2,2048,128]{2,1,0:T(8,128)(2,1)} %hold.3), channel_id=1, source_target_pairs={{0,5},{1,4},{4,9},{5,8},{8,13},{9,12},{12,1},{13,0},{2,7},{3,6},{6... | collective-permute-start | bytes 3145736 | tf_op jit(solution)/shard_map/ppermute | solution.py:459
  70.4 0.8 copy-start.15
  74.8 10.8 %copy-start.27 = (bf16[4,2,18,64]{3,2,1,0:T(8,128)(2,1)S(1)}, bf16[4,2,18,64]{3,2,1,0:T(8,128)(2,1)}, u32[]{:S(2)}) copy-start(bf16[4,2,18,64]{3,2,1,0:T(8,128)(2,1)} %copy-done.26) | copy-start | bytes 55300
  74.8 10.8 %copy-start.29 = (bf16[4,2,18,64]{3,2,1,0:T(8,128)(2,1)S(1)}, bf16[4,2,18,64]{3,2,1,0:T(8,128)(2,1)}, u32[]{:S(2)}) copy-start(bf16[4,2,18,64]{3,2,1,0:T(8,128)(2,1)} %copy-done.28) | copy-start | bytes 55300
  74.8 33.4 %collective-permute-start.15 = (bf16[2,2048,128]{2,1,0:T(8,128)(2,1)}, bf16[2,2048,128]{2,1,0:T(8,128)(2,1)}, u32[]{:S(2)}, u32[]{:S(2)}) collective-permute-start(bf16[2,2048,128]{2,1,0:T(8,128)(2,1)} %bitcast.64), channel_id=1, source_target_pairs={{0,1},{1,0},{4,5},{5,4},{8,9},{9,8},{12,13},{13,12},{2,3},{3,2},{6... | collective-permute-start | bytes 3145736 | tf_op jit(solution)/shard_map/ppermute | solution.py:459
  79.1 40.2 %collective-permute-start.13 = (bf16[2,2048,128]{2,1,0:T(8,128)(2,1)}, bf16[2,2048,128]{2,1,0:T(8,128)(2,1)}, u32[]{:S(2)}, u32[]{:S(2)}) collective-permute-start(bf16[2,2048,128]{2,1,0:T(8,128)(2,1)} %bitcast.57), channel_id=1, source_target_pairs={{0,13},{1,12},{4,1},{5,0},{8,5},{9,4},{12,9},{13,8},{2,15},{3,14},... | collective-permute-start | bytes 3145736 | tf_op jit(solution)/shard_map/ppermute | solution.py:459
  84.3 102.6 %collective-permute-start.14 = (bf16[2,2048,128]{2,1,0:T(8,128)(2,1)}, bf16[2,2048,128]{2,1,0:T(8,128)(2,1)}, u32[]{:S(2)}, u32[]{:S(2)}) collective-permute-start(bf16[2,2048,128]{2,1,0:T(8,128)(2,1)} %bitcast.59), channel_id=1, source_target_pairs={{0,8},{1,9},{4,12},{5,13},{8,0},{9,1},{12,4},{13,5},{2,10},{3,11},... | collective-permute-start | bytes 3145736 | tf_op jit(solution)/shard_map/ppermute | solution.py:459
  85.7 13.2 %copy-start.18 = (bf16[4,2,2,8,128]{4,3,2,1,0:T(8,128)(2,1)S(1)}, bf16[4,2,2,8,128]{4,3,2,1,0:T(8,128)(2,1)}, u32[]{:S(2)}) copy-start(bf16[4,2,2,8,128]{4,3,2,1,0:T(8,128)(2,1)} %copy-done.17) | copy-start | bytes 98308
  89.2 120.1 %collective-permute-start.10 = (bf16[2,2048,128]{2,1,0:T(8,128)(2,1)}, bf16[2,2048,128]{2,1,0:T(8,128)(2,1)}, u32[]{:S(2)}, u32[]{:S(2)}) collective-permute-start(bf16[2,2048,128]{2,1,0:T(8,128)(2,1)} %bitcast.61), channel_id=1, source_target_pairs={{0,9},{1,8},{4,13},{5,12},{8,1},{9,0},{12,5},{13,4},{2,11},{3,10},... | collective-permute-start | bytes 3145736 | tf_op jit(solution)/shard_map/ppermute | solution.py:459
  94.7 13.5 %copy-start.1 = (bf16[2,1024,2,128]{3,2,1,0:T(2,128)(2,1)S(1)}, bf16[2,1024,2,128]{3,2,1,0:T(2,128)(2,1)}, u32[]{:S(2)}) copy-start(bf16[2,1024,2,128]{3,2,1,0:T(2,128)(2,1)} %arrange.14) | copy-start | bytes 3145732
  97.9 1.0 copy-start.2
  98.9 1.2 copy-start.3
  100.1 0.8 copy-start.13
  100.9 0.8 copy-start.16
  101.7 0.8 copy-start.20
  103.3 4.9 %copy-start.5 = (bf16[1,2048,128]{2,1,0:T(8,128)(2,1)S(1)}, bf16[1,2048,128]{2,1,0:T(8,128)(2,1)}, u32[]{:S(2)}) copy-start(bf16[1,2048,128]{2,1,0:T(8,128)(2,1)} %copy-done.4) | copy-start | bytes 1572868
  103.3 4.9 %copy-start.7 = (bf16[1,2048,128]{2,1,0:T(8,128)(2,1)S(1)}, bf16[1,2048,128]{2,1,0:T(8,128)(2,1)}, u32[]{:S(2)}) copy-start(bf16[1,2048,128]{2,1,0:T(8,128)(2,1)} %copy-done.6) | copy-start | bytes 1572868
  103.3 4.9 %copy-start.9 = (bf16[1,2048,128]{2,1,0:T(8,128)(2,1)S(1)}, bf16[1,2048,128]{2,1,0:T(8,128)(2,1)}, u32[]{:S(2)}) copy-start(bf16[1,2048,128]{2,1,0:T(8,128)(2,1)} %copy-done.8) | copy-start | bytes 1572868
  103.3 4.9 %copy-start.11 = (bf16[1,2048,128]{2,1,0:T(8,128)(2,1)S(1)}, bf16[1,2048,128]{2,1,0:T(8,128)(2,1)}, u32[]{:S(2)}) copy-start(bf16[1,2048,128]{2,1,0:T(8,128)(2,1)} %copy-done.10) | copy-start | bytes 1572868
